TPU v7x, 32 devices: a whole 2x2x4 slice. The times are simulated.
32 devices in a mesh: tile: 4 (over y, x), sub: 8 (over z, core).
Axes of the slice: x: 2, y: 2, z: 4, core: 2. Of those that a mesh axis runs over, the one named last changes fastest.
Arguments:
- seeds: float32 [4, 6, 16, 256, 128], P('tile', None, 'sub'), may hold values from -6 to 6
- material: int32 [4, 16, 256, 128], P('tile', 'sub'), may hold values from 0 to 3
- decay: float32 [4], replicated, may hold values from 0.5 to 1
- coupling: float32 [4], replicated, may hold values from 0.1 to 0.6
Outputs:
- gradient: float32 [4, 6, 16, 256, 128], P('tile', None, 'sub')
All inputs are finite; a program needn't handle non-finite values.
Results may differ from a plain program's by a relative error of at most 0.0003.
Values sent between devices are 32-bit elements; how exact they have to be, the bound alone decides.
No kernel may reach another device: no remote copies, remote signals or barrier semaphores. Data moves between devices by JAX's collectives and lax.ppermute only.
A program may use at most 64 MiB of HBM per device.

v0:
```python
import math

import jax
import jax.numpy as jnp
from jax import lax
from jax.sharding import PartitionSpec as P

BAND = 32
STEPS = 2


magnetic_coeff = 0.5


def passed_along(block, axis, distance):
    devices = range(lax.axis_size(axis))
    route = [(i - distance, i) for i in devices if i - distance in devices]
    return lax.ppermute(block, axis, route)


def from_behind(value, axis, steps):
    count = lax.axis_size(axis)
    pairs = [(source, (source + steps) % count) for source in range(count)]
    return lax.ppermute(value, axis, pairs)


def lookup_table(material, table):
    labels = jnp.arange(table.shape[0], dtype=jnp.int32)[:, None, None, None]
    return jnp.sum(jnp.where(material[None] == labels, table[:, None, None, None], 0.0), axis=0)


def plus_diff(values, axis_pos):
    width = values.shape[axis_pos]
    later = lax.slice_in_dim(values, 1, width, axis=axis_pos)
    padding = [(0, 0)] * values.ndim
    padding[axis_pos] = (0, 1)
    return jnp.pad(later, padding) - values


def minus_diff(values, axis_pos):
    width = values.shape[axis_pos]
    earlier = lax.slice_in_dim(values, 0, width - 1, axis=axis_pos)
    padding = [(0, 0)] * values.ndim
    padding[axis_pos] = (1, 0)
    return values - jnp.pad(earlier, padding)


def plus_depth(values, after_plane):
    return jnp.concatenate([values[1:], after_plane[None]], axis=0) - values


def minus_depth(values, before_plane):
    return values - jnp.concatenate([before_plane[None], values[:-1]], axis=0)


def curl_forward(fields, after):
    curl_x = plus_diff(fields[2], 2) - plus_depth(fields[1], after[1])
    curl_y = plus_depth(fields[0], after[0]) - plus_diff(fields[2], 1)
    curl_z = plus_diff(fields[1], 1) - plus_diff(fields[0], 2)
    return jnp.stack([curl_x, curl_y, curl_z])


def curl_backward(fields, before):
    curl_x = minus_diff(fields[2], 2) - minus_depth(fields[1], before[1])
    curl_y = minus_depth(fields[0], before[0]) - minus_diff(fields[2], 1)
    curl_z = minus_diff(fields[1], 1) - minus_diff(fields[0], 2)
    return jnp.stack([curl_x, curl_y, curl_z])


def ramp(count):
    position = jnp.arange(count).astype(jnp.float32) + 0.5
    low_part = position / BAND
    high_part = (count - position) / BAND
    return jnp.where(position < BAND, low_part, jnp.where(position > count - BAND, high_part, 1.0))


def send_back(planes):
    return passed_along(planes, "sub", 1)


def on_device(seeds, material, decay, coupling):
    seed_tile = seeds[0]
    material_tile = material[0]
    depth, size_x, size_y = (seed_tile.shape[1], seed_tile.shape[2], seed_tile.shape[3])
    decay_map = lookup_table(material_tile, decay)
    coupling_map = lookup_table(material_tile, coupling)
    field_e = seed_tile[:3]
    field_h = seed_tile[3:]
    for turn_index in range(STEPS):
        scaled = coupling_map * field_e
        after = passed_along(jnp.stack([scaled[0, 0], scaled[1, 0]]), "sub", -1)
        field_h = field_h + curl_forward(scaled, after)
        before = send_back(jnp.stack([field_h[0, -1], field_h[1, -1]]))
        field_e = decay_map * field_e - magnetic_coeff * curl_backward(field_h, before)
    adjoint = jnp.concatenate([field_e, field_h], axis=0)
    side = math.isqrt(lax.axis_size("tile"))
    weight = ramp(size_x)[:, None] * ramp(size_y)[None, :]
    weighted = adjoint * weight
    prev_band = from_behind(weighted[:, :, size_x - BAND :, :], "tile", 1)
    next_band = from_behind(weighted[:, :, :BAND, :], "tile", -1)
    combined = weighted.at[:, :, :BAND, :].add(prev_band)
    combined = combined.at[:, :, size_x - BAND :, :].add(next_band)
    flat_rows = size_x * BAND // 128
    top_slab = combined[..., size_y - BAND :].reshape(6, depth, flat_rows, 128)
    bottom_slab = combined[..., :BAND].reshape(6, depth, flat_rows, 128)
    from_below = from_behind(top_slab, "tile", side).reshape(6, depth, size_x, BAND)
    from_above = from_behind(bottom_slab, "tile", -side).reshape(6, depth, size_x, BAND)
    result = combined.at[..., :BAND].add(from_below)
    result = result.at[..., size_y - BAND :].add(from_above)
    return result[None]


def solution(mesh):
    placed = (P("tile", None, "sub", None, None), P("tile", "sub", None, None), P(), P())
    return jax.shard_map(
        on_device,
        mesh=mesh,
        in_specs=placed,
        out_specs=P("tile", None, "sub", None, None),
        check_vma=False,
    )
```

profile of v0, /device:TPU:0, one launch (start us, length us, event | category | flops | bytes accessed | tf_op | source)
XLA Modules:
  0.0 88.8 jit_solution(10331169519354940813)
XLA Ops:
  0.0 1.2 %select_reduce_fusion.1 = (f32[2,256,128]{2,1,0:T(8,128)S(1)}, f32[2,256,128]{2,1,0:T(8,128)S(1)}) fusion(f32[4]{0:T(128)} %param.14, s32[2,256,128]{2,1,0:T(8,128)} %bitcast.170, f32[4]{0:T(128)} %param.15), kind=kLoop, calls=%fused_computation.4 | loop fusion | flops 1179648 | bytes 786464 | tf_op jit(solution)/shard_map/reduce_sum | solution.py:29
  1.2 1.2 %bitcast_multiply_fusion = f32[3,2,256,128]{3,2,1,0:T(8,128)S(1)} fusion(f32[1,6,2,256,128]{4,3,2,1,0:T(8,128)} %param.12, f32[2,256,128]{2,1,0:T(8,128)S(1)} %get-tuple-element.54), kind=kLoop, calls=%fused_computation.12 | loop fusion | flops 196608 | bytes 1835008 | tf_op jit(solution)/shard_map/mul | solution.py:90
  2.5 1.3 %collective-permute-start = (f32[2,256,128]{2,1,0:T(8,128)S(1)}, f32[2,256,128]{2,1,0:T(8,128)S(1)}, u32[]{:S(2)}, u32[]{:S(2)}) collective-permute-start(f32[2,256,128]{2,1,0:T(8,128)S(1)} %pad_maximum_fusion), channel_id=1, source_target_pairs={{1,0},{2,1},{3,2},{4,3},{5,4},{6,5},{7,6},{9,8},{10,9},{11,10},{12... | collective-permute-start | bytes 786440 | tf_op jit(solution)/shard_map/ppermute | solution.py:18
  4.2 1.7 %collective-permute-done = f32[2,256,128]{2,1,0:T(8,128)S(1)} collective-permute-done((f32[2,256,128]{2,1,0:T(8,128)S(1)}, f32[2,256,128]{2,1,0:T(8,128)S(1)}, u32[]{:S(2)}, u32[]{:S(2)}) %collective-permute-start) | collective-permute-done | bytes 262176 | tf_op jit(solution)/shard_map/ppermute | solution.py:18
  6.1 1.3 %copy-done.1 = f32[1,6,2,256,128]{4,3,2,1,0:T(8,128)S(1)} copy-done((f32[1,6,2,256,128]{4,3,2,1,0:T(8,128)S(1)}, f32[1,6,2,256,128]{4,3,2,1,0:T(8,128)}, u32[]{:S(2)}) %copy-start.1) | copy-done | bytes 1572888
  7.5 7.6 %collective-permute-start.1 = (f32[2,256,128]{2,1,0:T(8,128)S(1)}, f32[2,256,128]{2,1,0:T(8,128)S(1)}, u32[]{:S(2)}, u32[]{:S(2)}) collective-permute-start(f32[2,256,128]{2,1,0:T(8,128)S(1)} %pad_maximum_fusion.1), channel_id=1, source_target_pairs={{0,1},{1,2},{2,3},{3,4},{4,5},{5,6},{6,7},{8,9},{9,10},{10,11},{11... | collective-permute-start | bytes 786440 | tf_op jit(solution)/shard_map/ppermute | solution.py:18
  15.2 1.1 %collective-permute-done.1 = f32[2,256,128]{2,1,0:T(8,128)S(1)} collective-permute-done((f32[2,256,128]{2,1,0:T(8,128)S(1)}, f32[2,256,128]{2,1,0:T(8,128)S(1)}, u32[]{:S(2)}, u32[]{:S(2)}) %collective-permute-start.1) | collective-permute-done | bytes 262176 | tf_op jit(solution)/shard_map/ppermute | solution.py:18
  16.3 0.3 fusion.8
  16.8 1.3 %collective-permute-start.2 = (f32[2,256,128]{2,1,0:T(8,128)S(1)}, f32[2,256,128]{2,1,0:T(8,128)S(1)}, u32[]{:S(2)}, u32[]{:S(2)}) collective-permute-start(f32[2,256,128]{2,1,0:T(8,128)S(1)} %pad_maximum_fusion.2), channel_id=1, source_target_pairs={{1,0},{2,1},{3,2},{4,3},{5,4},{6,5},{7,6},{9,8},{10,9},{11,10},{12... | collective-permute-start | bytes 786440 | tf_op jit(solution)/shard_map/ppermute | solution.py:18
  18.5 3.4 %collective-permute-done.2 = f32[2,256,128]{2,1,0:T(8,128)S(1)} collective-permute-done((f32[2,256,128]{2,1,0:T(8,128)S(1)}, f32[2,256,128]{2,1,0:T(8,128)S(1)}, u32[]{:S(2)}, u32[]{:S(2)}) %collective-permute-start.2) | collective-permute-done | bytes 262176 | tf_op jit(solution)/shard_map/ppermute | solution.py:18
  21.9 0.2 fusion.12
  22.3 7.4 %collective-permute-start.3 = (f32[2,256,128]{2,1,0:T(8,128)S(1)}, f32[2,256,128]{2,1,0:T(8,128)S(1)}, u32[]{:S(2)}, u32[]{:S(2)}) collective-permute-start(f32[2,256,128]{2,1,0:T(8,128)S(1)} %pad_maximum_fusion.3), channel_id=1, source_target_pairs={{0,1},{1,2},{2,3},{3,4},{4,5},{5,6},{6,7},{8,9},{9,10},{10,11},{11... | collective-permute-start | bytes 786440 | tf_op jit(solution)/shard_map/ppermute | solution.py:18
  29.9 1.0 %collective-permute-done.3 = f32[2,256,128]{2,1,0:T(8,128)S(1)} collective-permute-done((f32[2,256,128]{2,1,0:T(8,128)S(1)}, f32[2,256,128]{2,1,0:T(8,128)S(1)}, u32[]{:S(2)}, u32[]{:S(2)}) %collective-permute-start.3) | collective-permute-done | bytes 262176 | tf_op jit(solution)/shard_map/ppermute | solution.py:18
  30.8 0.3 fusion.16
  31.2 0.2 fusion.2
  31.5 1.5 %collective-permute-start.4 = (f32[6,2,32,128]{3,2,1,0:T(8,128)S(1)}, f32[6,2,32,128]{3,2,1,0:T(8,128)S(1)}, u32[]{:S(2)}, u32[]{:S(2)}) collective-permute-start(f32[6,2,32,128]{3,2,1,0:T(8,128)S(1)} %slice.459), channel_id=1, source_target_pairs={{0,8},{8,16},{16,24},{24,0},{1,9},{9,17},{17,25},{25,1},{2,10},{10... | collective-permute-start | bytes 589832 | tf_op jit(solution)/shard_map/ppermute | solution.py:24
  33.0 6.0 %collective-permute-done.4 = f32[6,2,32,128]{3,2,1,0:T(8,128)S(1)} collective-permute-done((f32[6,2,32,128]{3,2,1,0:T(8,128)S(1)}, f32[6,2,32,128]{3,2,1,0:T(8,128)S(1)}, u32[]{:S(2)}, u32[]{:S(2)}) %collective-permute-start.4) | collective-permute-done | bytes 196640 | tf_op jit(solution)/shard_map/ppermute | solution.py:24
  39.1 1.6 %collective-permute-start.5 = (f32[6,2,32,128]{3,2,1,0:T(8,128)S(1)}, f32[6,2,32,128]{3,2,1,0:T(8,128)S(1)}, u32[]{:S(2)}, u32[]{:S(2)}) collective-permute-start(f32[6,2,32,128]{3,2,1,0:T(8,128)S(1)} %get-tuple-element.57), channel_id=1, source_target_pairs={{0,24},{8,0},{16,8},{24,16},{1,25},{9,1},{17,9},{25,17},{2,26},{10... | collective-permute-start | bytes 589832 | tf_op jit(solution)/shard_map/ppermute | solution.py:24
  40.7 6.1 %collective-permute-done.5 = f32[6,2,32,128]{3,2,1,0:T(8,128)S(1)} collective-permute-done((f32[6,2,32,128]{3,2,1,0:T(8,128)S(1)}, f32[6,2,32,128]{3,2,1,0:T(8,128)S(1)}, u32[]{:S(2)}, u32[]{:S(2)}) %collective-permute-start.5) | collective-permute-done | bytes 196640 | tf_op jit(solution)/shard_map/ppermute | solution.py:24
  46.9 0.5 slice.462
  47.3 0.4 reshape.216
  47.7 1.6 %collective-permute-start.6 = (f32[6,2,64,128]{3,2,1,0:T(8,128)S(1)}, f32[6,2,64,128]{3,2,1,0:T(8,128)S(1)}, u32[]{:S(2)}, u32[]{:S(2)}) collective-permute-start(f32[6,2,64,128]{3,2,1,0:T(8,128)S(1)} %reshape.216), channel_id=1, source_target_pairs={{0,16},{8,24},{16,0},{24,8},{1,17},{9,25},{17,1},{25,9},{2,18},{10... | collective-permute-start | bytes 1179656 | tf_op jit(solution)/shard_map/ppermute | solution.py:24
  49.3 9.6 %collective-permute-done.6 = f32[6,2,64,128]{3,2,1,0:T(8,128)S(1)} collective-permute-done((f32[6,2,64,128]{3,2,1,0:T(8,128)S(1)}, f32[6,2,64,128]{3,2,1,0:T(8,128)S(1)}, u32[]{:S(2)}, u32[]{:S(2)}) %collective-permute-start.6) | collective-permute-done | bytes 393248 | tf_op jit(solution)/shard_map/ppermute | solution.py:24
  58.9 1.5 %reshape.217 = f32[6,2,256,32]{3,2,1,0:T(8,128)} reshape(f32[6,2,64,128]{3,2,1,0:T(8,128)S(1)} %collective-permute-done.6) | data formatting | bytes 786432 | tf_op jit(solution)/shard_map/reshape.115
  60.4 2.8 %fusion.20 = (f32[6,2,256,32]{3,2,1,0:T(8,128)}, f32[6,2,256,32]{3,2,1,0:T(8,128)S(1)}) fusion(f32[6,2,256,128]{3,2,1,0:T(8,128)S(1)} %fusion.19, f32[6,2,256,32]{3,2,1,0:T(8,128)} %reshape.217), kind=kLoop, calls=%fused_computation.84 | loop fusion | flops 98304 | bytes 1572864 | tf_op jit(solution)/shard_map/slice.194
  63.2 1.8 %reshape.218 = f32[6,2,64,128]{3,2,1,0:T(8,128)S(1)} reshape(f32[6,2,256,32]{3,2,1,0:T(8,128)} %get-tuple-element.55) | data formatting | bytes 786432 | tf_op jit(solution)/shard_map/reshape | solution.py:105
  65.0 1.6 %collective-permute-start.7 = (f32[6,2,64,128]{3,2,1,0:T(8,128)S(1)}, f32[6,2,64,128]{3,2,1,0:T(8,128)}, u32[]{:S(2)}, u32[]{:S(2)}) collective-permute-start(f32[6,2,64,128]{3,2,1,0:T(8,128)S(1)} %reshape.218), channel_id=1, source_target_pairs={{0,16},{8,24},{16,0},{24,8},{1,17},{9,25},{17,1},{25,9},{2,18},{10... | collective-permute-start | bytes 1179656 | tf_op jit(solution)/shard_map/ppermute | solution.py:24
  66.6 4.0 %scatter-add.16 = f32[6,2,256,128]{3,2,1,0:T(8,128)S(1)} dynamic-update-slice(f32[6,2,256,128]{3,2,1,0:T(8,128)S(1)} %fusion.19, f32[6,2,256,32]{3,2,1,0:T(8,128)S(1)} %get-tuple-element.56, s32[]{:T(128)} %constant.132.clone.1, s32[]{:T(128)} %constant.132.clone.1, s32[]{:T(128)} %constant.132.clone.1, s32[]{:T(128)} %constant.132.clone.1) | dynamic-update-slice | bytes 786436 | tf_op jit(solution)/shard_map/scatter-add | solution.py:108
  70.6 4.9 %collective-permute-done.7 = f32[6,2,64,128]{3,2,1,0:T(8,128)} collective-permute-done((f32[6,2,64,128]{3,2,1,0:T(8,128)S(1)}, f32[6,2,64,128]{3,2,1,0:T(8,128)}, u32[]{:S(2)}, u32[]{:S(2)}) %collective-permute-start.7) | collective-permute-done | bytes 393248 | tf_op jit(solution)/shard_map/ppermute | solution.py:24
  75.5 2.5 %reshape.219 = f32[6,2,256,32]{3,2,1,0:T(8,128)} reshape(f32[6,2,64,128]{3,2,1,0:T(8,128)} %collective-permute-done.7) | data formatting | bytes 786432 | tf_op jit(solution)/shard_map/reshape.127
  78.0 1.9 %fusion = f32[1,6,2,256,32]{4,3,2,1,0:T(8,128)S(1)} fusion(f32[6,2,256,32]{3,2,1,0:T(8,128)} %reshape.219, f32[6,2,256,128]{3,2,1,0:T(8,128)S(1)} %scatter-add.16), kind=kLoop, calls=%fused_computation.1 | loop fusion | flops 98304 | bytes 1179648 | tf_op jit(solution)/shard_map/broadcast_in_dim | solution.py:110
  79.9 8.8 %scatter-add.19 = f32[1,6,2,256,128]{4,3,2,1,0:T(8,128)} dynamic-update-slice(f32[1,6,2,256,128]{4,3,2,1,0:T(8,128)} %bitcast.161, f32[1,6,2,256,32]{4,3,2,1,0:T(8,128)S(1)} %fusion, s32[]{:T(128)} %constant.132.clone.1, s32[]{:T(128)} %constant.132.clone.1, s32[]{:T(128)} %constant.132.clone.1, s32[]{:T(128)} %constant.132.clone.1, s32[]{:T(128)} %constant.134.clone.1) | dynamic-update-slice | bytes 786436 | tf_op jit(solution)/shard_map/scatter-add | solution.py:109
  (38 shorter events, 1.9 us)
Async XLA Ops:
  2.5 3.4 %collective-permute-start = (f32[2,256,128]{2,1,0:T(8,128)S(1)}, f32[2,256,128]{2,1,0:T(8,128)S(1)}, u32[]{:S(2)}, u32[]{:S(2)}) collective-permute-start(f32[2,256,128]{2,1,0:T(8,128)S(1)} %pad_maximum_fusion), channel_id=1, source_target_pairs={{1,0},{2,1},{3,2},{4,3},{5,4},{6,5},{7,6},{9,8},{10,9},{11,10},{12... | collective-permute-start | bytes 786440 | tf_op jit(solution)/shard_map/ppermute | solution.py:18
  6.0 1.4 %copy-start.1 = (f32[1,6,2,256,128]{4,3,2,1,0:T(8,128)S(1)}, f32[1,6,2,256,128]{4,3,2,1,0:T(8,128)}, u32[]{:S(2)}) copy-start(f32[1,6,2,256,128]{4,3,2,1,0:T(8,128)} %param.12) | copy-start | bytes 4718596
  7.5 8.7 %collective-permute-start.1 = (f32[2,256,128]{2,1,0:T(8,128)S(1)}, f32[2,256,128]{2,1,0:T(8,128)S(1)}, u32[]{:S(2)}, u32[]{:S(2)}) collective-permute-start(f32[2,256,128]{2,1,0:T(8,128)S(1)} %pad_maximum_fusion.1), channel_id=1, source_target_pairs={{0,1},{1,2},{2,3},{3,4},{4,5},{5,6},{6,7},{8,9},{9,10},{10,11},{11... | collective-permute-start | bytes 786440 | tf_op jit(solution)/shard_map/ppermute | solution.py:18
  16.8 5.1 %collective-permute-start.2 = (f32[2,256,128]{2,1,0:T(8,128)S(1)}, f32[2,256,128]{2,1,0:T(8,128)S(1)}, u32[]{:S(2)}, u32[]{:S(2)}) collective-permute-start(f32[2,256,128]{2,1,0:T(8,128)S(1)} %pad_maximum_fusion.2), channel_id=1, source_target_pairs={{1,0},{2,1},{3,2},{4,3},{5,4},{6,5},{7,6},{9,8},{10,9},{11,10},{12... | collective-permute-start | bytes 786440 | tf_op jit(solution)/shard_map/ppermute | solution.py:18
  22.3 8.6 %collective-permute-start.3 = (f32[2,256,128]{2,1,0:T(8,128)S(1)}, f32[2,256,128]{2,1,0:T(8,128)S(1)}, u32[]{:S(2)}, u32[]{:S(2)}) collective-permute-start(f32[2,256,128]{2,1,0:T(8,128)S(1)} %pad_maximum_fusion.3), channel_id=1, source_target_pairs={{0,1},{1,2},{2,3},{3,4},{4,5},{5,6},{6,7},{8,9},{9,10},{10,11},{11... | collective-permute-start | bytes 786440 | tf_op jit(solution)/shard_map/ppermute | solution.py:18
  31.5 7.5 %collective-permute-start.4 = (f32[6,2,32,128]{3,2,1,0:T(8,128)S(1)}, f32[6,2,32,128]{3,2,1,0:T(8,128)S(1)}, u32[]{:S(2)}, u32[]{:S(2)}) collective-permute-start(f32[6,2,32,128]{3,2,1,0:T(8,128)S(1)} %slice.459), channel_id=1, source_target_pairs={{0,8},{8,16},{16,24},{24,0},{1,9},{9,17},{17,25},{25,1},{2,10},{10... | collective-permute-start | bytes 589832 | tf_op jit(solution)/shard_map/ppermute | solution.py:24
  39.1 7.7 %collective-permute-start.5 = (f32[6,2,32,128]{3,2,1,0:T(8,128)S(1)}, f32[6,2,32,128]{3,2,1,0:T(8,128)S(1)}, u32[]{:S(2)}, u32[]{:S(2)}) collective-permute-start(f32[6,2,32,128]{3,2,1,0:T(8,128)S(1)} %get-tuple-element.57), channel_id=1, source_target_pairs={{0,24},{8,0},{16,8},{24,16},{1,25},{9,1},{17,9},{25,17},{2,26},{10... | collective-permute-start | bytes 589832 | tf_op jit(solution)/shard_map/ppermute | solution.py:24
  47.7 11.2 %collective-permute-start.6 = (f32[6,2,64,128]{3,2,1,0:T(8,128)S(1)}, f32[6,2,64,128]{3,2,1,0:T(8,128)S(1)}, u32[]{:S(2)}, u32[]{:S(2)}) collective-permute-start(f32[6,2,64,128]{3,2,1,0:T(8,128)S(1)} %reshape.216), channel_id=1, source_target_pairs={{0,16},{8,24},{16,0},{24,8},{1,17},{9,25},{17,1},{25,9},{2,18},{10... | collective-permute-start | bytes 1179656 | tf_op jit(solution)/shard_map/ppermute | solution.py:24
  65.0 10.5 %collective-permute-start.7 = (f32[6,2,64,128]{3,2,1,0:T(8,128)S(1)}, f32[6,2,64,128]{3,2,1,0:T(8,128)}, u32[]{:S(2)}, u32[]{:S(2)}) collective-permute-start(f32[6,2,64,128]{3,2,1,0:T(8,128)S(1)} %reshape.218), channel_id=1, source_target_pairs={{0,16},{8,24},{16,0},{24,8},{1,17},{9,25},{17,1},{25,9},{2,18},{10... | collective-permute-start | bytes 1179656 | tf_op jit(solution)/shard_map/ppermute | solution.py:24
  70.6 9.3 %copy-start = (f32[6,2,256,128]{3,2,1,0:T(8,128)}, f32[6,2,256,128]{3,2,1,0:T(8,128)S(1)}, u32[]{:S(2)}) copy-start(f32[6,2,256,128]{3,2,1,0:T(8,128)S(1)} %scatter-add.16) | copy-start | bytes 4718596
where the time goes:
time: 89.3 us; the launch traced here: 88.8 us
  waiting for transfers between devices  33.8 us (38%)
  starting transfers between devices  23.9 us (27%)
  local copies, waits for them, and re-layouts  21.8 us (24%)
  other arithmetic  8.95 us (10%)
    ppermute x4, waiting for transfers between devices, from_behind(): return lax.ppermute(value, axis, pairs)  26.6 us
    ppermute x4, starting transfers between devices, passed_along(): return lax.ppermute(block, axis, route)  17.6 us
    scatter-add x1, local copies, waits for them, and re-layouts, on_device(): result = result.at[..., size_y - BAND:].add(from_above)  8.83 us
    ppermute x4, waiting for transfers between devices, passed_along(): return lax.ppermute(block, axis, route)  7.16 us
    ppermute x4, starting transfers between devices, from_behind(): return lax.ppermute(value, axis, pairs)  6.31 us
    another operation x2, local copies, waits for them, and re-layouts  4.04 us
    scatter-add x1, local copies, waits for them, and re-layouts, on_device(): result = combined.at[..., :BAND].add(from_below)  3.98 us
    another operation x2, other arithmetic  2.88 us
  transfers between devices with their start and end apart: 8, of which 8 were waited for; matrix products, arithmetic and copies ran while one was open for 6% of the time, Pallas kernels for 0%

commit v1 on v0

v1 whole, which is shorter than its diff:
```python
import functools
import math

import jax
import jax.numpy as jnp
from jax import lax
from jax.experimental import pallas as pl
from jax.experimental.pallas import tpu as pltpu
from jax.sharding import PartitionSpec as P

BAND = 32
STEPS = 2
HALO = 8
PLANES = 5

magnetic_coeff = 0.5


def lane_of(shape):
    return lax.broadcasted_iota(jnp.int32, shape, 1)


def row_of(shape):
    return lax.broadcasted_iota(jnp.int32, shape, 0)


def next_x(v):
    rows = v.shape[0]
    return jnp.where(row_of(v.shape) == rows - 1, 0.0, pltpu.roll(v, rows - 1, 0))


def prev_x(v):
    return jnp.where(row_of(v.shape) == 0, 0.0, pltpu.roll(v, 1, 0))


def next_y(v):
    lanes = v.shape[1]
    return jnp.where(lane_of(v.shape) == lanes - 1, 0.0, pltpu.roll(v, lanes - 1, 1))


def prev_y(v):
    return jnp.where(lane_of(v.shape) == 0, 0.0, pltpu.roll(v, 1, 1))


def plus_x(v):
    return next_x(v) - v


def plus_y(v):
    return next_y(v) - v


def minus_x(v):
    return v - prev_x(v)


def minus_y(v):
    return v - prev_y(v)


def looked_up(labels, table):
    value = jnp.full(labels.shape, table[0], jnp.float32)
    for m in range(1, table.shape[0]):
        value = jnp.where(labels == m, table[m], value)
    return value


def update_h(h, v, v_after):
    depth = len(v[0])
    new = [[], [], []]
    for p in range(depth):
        vx, vy, vz = v[0][p], v[1][p], v[2][p]
        up_x, up_y = (v[0][p + 1], v[1][p + 1]) if p + 1 < depth else v_after
        dz_x = up_x - vx if up_x is not None else -vx
        dz_y = up_y - vy if up_y is not None else -vy
        new[0].append(h[0][p] + (plus_y(vz) - dz_y))
        new[1].append(h[1][p] + (dz_x - plus_x(vz)))
        new[2].append(h[2][p] + (plus_x(vy) - plus_y(vx)))
    return new


def update_e(e, ca, h, h_before):
    depth = len(h[0])
    new = [[], [], []]
    for p in range(depth):
        hx, hy, hz = h[0][p], h[1][p], h[2][p]
        low_x, low_y = (h[0][p - 1], h[1][p - 1]) if p > 0 else h_before
        dz_x = hx - low_x if low_x is not None else hx
        dz_y = hy - low_y if low_y is not None else hy
        new[0].append(ca[p] * e[0][p] - magnetic_coeff * (minus_y(hz) - dz_y))
        new[1].append(ca[p] * e[1][p] - magnetic_coeff * (dz_x - minus_x(hz)))
        new[2].append(ca[p] * e[2][p] - magnetic_coeff * (minus_x(hy) - minus_y(hx)))
    return new


def scaled(cb, e):
    return [[cb[p] * e[c][p] for p in range(len(cb))] for c in range(3)]


def loaded(seeds, material, decay, coupling, lo, hi):
    depth = seeds.shape[2]
    e = [[seeds[0, c, p, lo:hi] for p in range(depth)] for c in range(3)]
    h = [[seeds[0, 3 + c, p, lo:hi] for p in range(depth)] for c in range(3)]
    labels = [material[0, p, lo:hi] for p in range(depth)]
    ca = [looked_up(m, decay) for m in labels]
    cb = [looked_up(m, coupling) for m in labels]
    return e, h, ca, cb


NONE = (None, None)


def halo_kernel(spans, sub, decay, coupling, seeds, material, near, far):
    odd = lax.rem(lax.axis_index(sub), 2) == 1
    at = 0
    for lo, hi in spans:
        e, h, ca, cb = loaded(seeds, material, decay, coupling, lo, hi)
        v1 = scaled(cb, e)
        h1 = update_h(h, v1, NONE)
        e1 = update_e(e, ca, h1, NONE)
        v2 = scaled(cb, e1)
        h2 = update_h(h1, v2, NONE)
        up = (h1[0][-1], h1[1][-1], h2[0][-1], h2[1][-1], cb[-1])
        down = (v1[0][0], v1[1][0], v2[0][0], v2[1][0], cb[0])
        for k in range(PLANES):
            near[k, at : at + hi - lo] = jnp.where(odd, down[k], up[k])
            far[k, at : at + hi - lo] = jnp.where(odd, up[k], down[k])
        at += hi - lo


def ramp(position, count):
    position = position.astype(jnp.float32) + 0.5
    return jnp.where(
        position < BAND,
        position / BAND,
        jnp.where(position > count - BAND, (count - position) / BAND, 1.0),
    )


def final_fields(fields, near, far, at, rows, sub, sub_size):
    e, h, ca, cb = fields
    index = lax.axis_index(sub)
    odd = lax.rem(index, 2) == 1
    below, above = index > 0, index < sub_size - 1
    a = [near[k, at : at + rows] for k in range(PLANES)]
    b = [far[k, at : at + rows] for k in range(PLANES)]
    from_below = [jnp.where(odd, a[k], b[k]) for k in range(PLANES)]
    from_above = [jnp.where(above, jnp.where(odd, b[k], a[k]), 0.0) for k in range(PLANES)]
    part_h1x, part_h1y, part_h2x, part_h2y, cb_low = from_below
    v1x_up, v1y_up, part_v2x, part_v2y, cb_up = from_above

    v1 = scaled(cb, e)
    h1 = update_h(h, v1, (v1x_up, v1y_up))
    dh1x, dh1y = -v1[1][0], v1[0][0]
    h1_low = (jnp.where(below, part_h1x + dh1x, 0.0), jnp.where(below, part_h1y + dh1y, 0.0))
    e1 = update_e(e, ca, h1, h1_low)
    v2 = scaled(cb, e1)
    v2_up = (
        part_v2x - cb_up * (magnetic_coeff * h1[1][-1]),
        part_v2y + cb_up * (magnetic_coeff * h1[0][-1]),
    )
    h2 = update_h(h1, v2, v2_up)
    dv2x = cb_low * (magnetic_coeff * dh1y)
    dv2y = cb_low * (-magnetic_coeff * dh1x)
    dv2z = cb_low * (-magnetic_coeff * (minus_x(dh1y) - minus_y(dh1x)))
    h2x_low = part_h2x + (dh1x + (plus_y(dv2z) - (v2[1][0] - dv2y)))
    h2y_low = part_h2y + (dh1y + ((v2[0][0] - dv2x) - plus_x(dv2z)))
    h2_low = (jnp.where(below, h2x_low, 0.0), jnp.where(below, h2y_low, 0.0))
    e2 = update_e(e1, ca, h2, h2_low)
    return e2 + h2


def middle_out(block):
    return pltpu.roll(block, block.shape[1] // 2, 1)


def y_packed(first, second):
    lane = lane_of(first.shape)
    lanes = first.shape[1]
    middle = (lane >= BAND) & (lane < lanes - BAND)
    return jnp.where(middle, pltpu.roll(second, lanes // 2, 1), first)


def y_unpacked(block):
    lane = lane_of(block.shape)
    lanes = block.shape[1]
    a, b = pltpu.roll(block, BAND, 1), pltpu.roll(block, lanes - BAND, 1)
    middle = (lane >= BAND) & (lane < lanes - BAND)
    first = jnp.where(middle, 0.0, jnp.where(lane < BAND, a, b))
    second = jnp.where(middle, 0.0, jnp.where(lane < BAND, b, a))
    return first, second


def weighted_planes(seeds, material, decay, coupling, near, far, at, lo, hi, keep, sub, sub_size):
    fields = loaded(seeds, material, decay, coupling, lo, hi)
    planes = final_fields(fields, near, far, at, hi - lo, sub, sub_size)
    start, stop = keep
    size_x, size_y = seeds.shape[3:]
    shape = (stop - start, size_y)
    weight = ramp(row_of(shape) + start, size_x) * ramp(lane_of(shape), size_y)
    return [[plane[start - lo : stop - lo] * weight for plane in part] for part in planes]


def edge_kernel(spans, sub, sub_size, tile, decay, coupling, seeds, material, near, far, edge, corner, strip):
    at = 0
    parts = []
    size_x = seeds.shape[3]
    for (lo, hi), keep in zip(spans, ((0, BAND), (size_x - BAND, size_x))):
        parts.append(weighted_planes(seeds, material, decay, coupling, near, far, at, lo, hi, keep, sub, sub_size))
        at += hi - lo
    odd = lax.rem(lax.axis_index(tile), 2) == 1
    low, high = parts
    half = BAND // 2
    for c in range(6):
        for p in range(seeds.shape[2]):
            edge[c, p, :BAND] = low[c][p]
            edge[c, p, BAND:] = high[c][p]
            corner[c, p] = y_packed(low[c][p], high[c][p])
            away = jnp.where(odd, high[c][p], low[c][p])
            strip[c, p] = y_packed(middle_out(away[:half]), middle_out(away[half:]))


def middle_kernel(spans, sub, sub_size, decay, coupling, seeds, material, near, far, mid, bands):
    (lo, hi), = spans
    size_x = seeds.shape[3]
    keep = (BAND, size_x - BAND)
    planes = weighted_planes(seeds, material, decay, coupling, near, far, 0, lo, hi, keep, sub, sub_size)
    half = (keep[1] - keep[0]) // 2
    for c in range(6):
        for p in range(seeds.shape[2]):
            mid[c, p] = planes[c][p]
            bands[c, p] = y_packed(planes[c][p][:half], planes[c][p][half:])


def whole_kernel(spans, sub, sub_size, decay, coupling, seeds, material, near, far, out):
    (lo, hi), = spans
    planes = weighted_planes(seeds, material, decay, coupling, near, far, 0, lo, hi, (lo, hi), sub, sub_size)
    for c in range(6):
        for p in range(seeds.shape[2]):
            out[c, p] = planes[c][p]


def corner_kernel(tile, edge, corner, summed, send):
    odd = lax.rem(lax.axis_index(tile), 2) == 1
    half = BAND // 2
    for c in range(edge.shape[0]):
        for p in range(edge.shape[1]):
            first, second = y_unpacked(corner[c, p])
            low = edge[c, p, :BAND] + first
            high = edge[c, p, BAND:] + second
            summed[c, p, :BAND] = low
            summed[c, p, BAND:] = high
            by, away = jnp.where(odd, low, high), jnp.where(odd, high, low)
            send[c, p, :BAND] = by
            send[c, p, BAND:] = y_packed(away[:half], away[half:])


def seam_kernel(tile, summed, got, strip, out):
    odd = lax.rem(lax.axis_index(tile), 2) == 1
    half = BAND // 2
    for c in range(summed.shape[0]):
        for p in range(summed.shape[1]):
            by = got[c, p, :BAND]
            corners = y_unpacked(got[c, p, BAND:])
            block = strip[c, p]
            lane = lane_of(block.shape)
            middle = (lane >= BAND) & (lane < block.shape[1] - BAND)
            first = jnp.where(middle, middle_out(block), corners[0])
            second = jnp.where(middle, block, corners[1])
            away = jnp.concatenate([first, second], axis=0)
            out[c, p, :BAND] = summed[c, p, :BAND] + jnp.where(odd, by, away)
            out[c, p, BAND:] = summed[c, p, BAND:] + jnp.where(odd, away, by)


def last_kernel(edge, mid, bands, out):
    for p in range(mid.shape[1]):
        half = bands.shape[2]
        size_x = out.shape[3]
        first, second = y_unpacked(bands[0, p])
        out[0, 0, p, :BAND] = edge[0, p, :BAND]
        out[0, 0, p, BAND : BAND + half] = mid[0, p, :half] + first
        out[0, 0, p, BAND + half : size_x - BAND] = mid[0, p, half:] + second
        out[0, 0, p, size_x - BAND :] = edge[0, p, BAND:]


SMEM = pl.BlockSpec(memory_space=pltpu.SMEM)
VMEM = pl.BlockSpec(memory_space=pltpu.VMEM)
PARAMS = pltpu.CompilerParams(vmem_limit_bytes=32 * 1024 * 1024)


def called(kernel, shapes, in_specs, *operands):
    outs = [jax.ShapeDtypeStruct(shape, jnp.float32) for shape in shapes]
    return pl.pallas_call(
        kernel,
        out_shape=outs,
        in_specs=in_specs,
        out_specs=[VMEM] * len(outs),
        compiler_params=PARAMS,
    )(*operands)


def depth_exchange(near, far, sub_size, tile_size):
    near = lax.ppermute(near, "sub", [(i, i ^ 1) for i in range(sub_size)])
    pairs = []
    for t in range(tile_size):
        for i in range(sub_size):
            other = (i + 1) ^ 1
            j = other - 1
            if 0 <= j < sub_size:
                pairs.append((t * sub_size + i, t * sub_size + j))
            else:
                pairs.append((t * sub_size + i, (t ^ 1) * sub_size + i))
    far = lax.ppermute(far, ("tile", "sub"), pairs)
    return near, far


def swapped(value, bits, tile_size):
    return lax.ppermute(value, "tile", [(t, t ^ bits) for t in range(tile_size)])


def from_behind(value, steps, count):
    return lax.ppermute(value, "tile", [(t, (t + steps) % count) for t in range(count)])


def two_by_two(seeds, material, decay, coupling, sub_size, tile_size):
    depth, size_x, size_y = seeds.shape[2:]
    edges = ((0, BAND + HALO), (size_x - BAND - HALO, size_x))
    inner = ((BAND - HALO, size_x - BAND + HALO),)
    tables = [SMEM, SMEM, VMEM, VMEM]

    def halos(spans):
        shape = (PLANES, sum(hi - lo for lo, hi in spans), size_y)
        kernel = functools.partial(halo_kernel, spans, "sub")
        return called(kernel, [shape, shape], tables, decay, coupling, seeds, material)

    edge_near, edge_far = depth_exchange(*halos(edges), sub_size, tile_size)
    inner_near, inner_far = depth_exchange(*halos(inner), sub_size, tile_size)

    edge, corner, strip = called(
        functools.partial(edge_kernel, edges, "sub", sub_size, "tile"),
        [(6, depth, 2 * BAND, size_y), (6, depth, BAND, size_y), (6, depth, BAND // 2, size_y)],
        tables + [VMEM, VMEM], decay, coupling, seeds, material, edge_near, edge_far,
    )
    corner = swapped(corner, 2, tile_size)
    strip = swapped(strip, 3, tile_size)
    rows = size_x - 2 * BAND
    mid, bands = called(
        functools.partial(middle_kernel, inner, "sub", sub_size),
        [(6, depth, rows, size_y), (6, depth, rows // 2, size_y)],
        tables + [VMEM, VMEM], decay, coupling, seeds, material, inner_near, inner_far,
    )
    bands = swapped(bands, 2, tile_size)
    summed, send = called(
        functools.partial(corner_kernel, "tile"),
        [(6, depth, 2 * BAND, size_y), (6, depth, BAND + BAND // 2, size_y)],
        [VMEM, VMEM], edge, corner,
    )
    got = swapped(send, 1, tile_size)
    edge, = called(
        functools.partial(seam_kernel, "tile"), [(6, depth, 2 * BAND, size_y)],
        [VMEM, VMEM, VMEM], summed, got, strip,
    )
    block = lambda n: pl.BlockSpec((1, depth, n, size_y), lambda c: (c, 0, 0, 0))
    return pl.pallas_call(
        last_kernel,
        grid=(6,),
        out_shape=jax.ShapeDtypeStruct(seeds.shape, jnp.float32),
        in_specs=[block(2 * BAND), block(rows), block(rows // 2)],
        out_specs=pl.BlockSpec((1, 1, depth, size_x, size_y), lambda c: (0, c, 0, 0, 0)),
        compiler_params=PARAMS,
    )(edge, mid, bands)


def any_lattice(seeds, material, decay, coupling, sub_size, tile_size):
    depth, size_x, size_y = seeds.shape[2:]
    spans = ((0, size_x),)
    tables = [SMEM, SMEM, VMEM, VMEM]
    shape = (PLANES, size_x, size_y)
    near, far = called(
        functools.partial(halo_kernel, spans, "sub"), [shape, shape], tables, decay, coupling, seeds, material
    )
    near, far = depth_exchange(near, far, sub_size, tile_size)
    weighted, = called(
        functools.partial(whole_kernel, spans, "sub", sub_size), [(6, depth, size_x, size_y)],
        tables + [VMEM, VMEM], decay, coupling, seeds, material, near, far,
    )
    side = math.isqrt(tile_size)
    prev_band = from_behind(weighted[:, :, size_x - BAND :, :], 1, tile_size)
    next_band = from_behind(weighted[:, :, :BAND, :], -1, tile_size)
    combined = weighted.at[:, :, :BAND, :].add(prev_band)
    combined = combined.at[:, :, size_x - BAND :, :].add(next_band)
    flat = (6, depth, size_x * BAND // size_y, size_y)
    thin = (6, depth, size_x, BAND)
    top_slab = combined[..., size_y - BAND :].reshape(flat)
    bottom_slab = combined[..., :BAND].reshape(flat)
    result = combined.at[..., :BAND].add(from_behind(top_slab, side, tile_size).reshape(thin))
    result = result.at[..., size_y - BAND :].add(from_behind(bottom_slab, -side, tile_size).reshape(thin))
    return result[None]


def solution(mesh):
    sub_size, tile_size = mesh.shape["sub"], mesh.shape["tile"]
    body = two_by_two if tile_size == 4 else any_lattice

    def on_device(seeds, material, decay, coupling):
        return body(seeds, material, decay, coupling, sub_size, tile_size)

    placed = (P("tile", None, "sub", None, None), P("tile", "sub", None, None), P(), P())
    return jax.shard_map(
        on_device,
        mesh=mesh,
        in_specs=placed,
        out_specs=P("tile", None, "sub", None, None),
        check_vma=False,
    )
```

time: 89.3 us -> 51.7 us (0.58)
  local copies, waits for them, and re-layouts: 21.8 us -> 3.67 us
  starting transfers between devices: 23.9 us -> 10.6 us
  other arithmetic: 8.95 us -> 0 us
  Pallas kernels: 0 us -> 7.9 us
  waiting for transfers between devices: 33.8 us -> 29.3 us
    ppermute x8, starting transfers between devices: 23.9 us -> 10.6 us  [the longest x4 5.74 us: swapped(): lax.ppermute(value, 'tile', [(t, t ^ bits) for t in range(tile_size)])]
    scatter-add x2 -> x0, local copies, waits for them, and re-layouts: 12.8 us -> none  [the longest x1 8.83 us: on_device(): result = result.at[..., size_y - BAND:].add(from_above)]
    pallas_call x0 -> x7, Pallas kernels: none -> 7.9 us  [the longest x6 5.26 us: called(): pl.pallas_call(kernel, out_shape=outs, in_specs=in_specs, out_specs=[VMEM...]
    ppermute x8, waiting for transfers between devices: 33.8 us -> 29.3 us  [the longest x4 24.6 us: swapped(): lax.ppermute(value, 'tile', [(t, t ^ bits) for t in range(tile_size)])]
    another operation x2 -> x0, local copies, waits for them, and re-layouts: 4.04 us -> none
    another operation x10 -> x0, other arithmetic: 3.83 us -> none
    unnamed x4 -> x8, local copies, waits for them, and re-layouts: 1.28 us -> 3.67 us
    reshape x2 -> x0, local copies, waits for them, and re-layouts: 2.17 us -> none  [the longest x1 1.79 us: on_device(): bottom_slab = combined[..., :BAND].reshape(6, depth, flat_rows, 128)]
  transfers between devices with their start and end apart: 8 -> 8, of which waited for: 8 -> 3; matrix products, arithmetic and copies ran while one was open for 6% -> 0% of each run, Pallas kernels for 0% -> 8%
where the time goes in v1:
time: 51.7 us; the launch traced here: 51.5 us
  waiting for transfers between devices  29.3 us (57%)
  starting transfers between devices  10.6 us (21%)
  Pallas kernels  7.9 us (15%)
  local copies, waits for them, and re-layouts  3.67 us (7%)
    ppermute x4, waiting for transfers between devices, swapped(): lax.ppermute(value, 'tile', [(t, t ^ bits) for t in range(tile_size)])  24.6 us
    ppermute x4, starting transfers between devices, swapped(): lax.ppermute(value, 'tile', [(t, t ^ bits) for t in range(tile_size)])  5.74 us
    pallas_call x6, Pallas kernels, called(): pl.pallas_call(kernel, out_shape=outs, in_specs=in_specs, out_specs=[VMEM...  5.26 us
    ppermute x2, waiting for transfers between devices, depth_exchange(): far = lax.ppermute(far, ('tile', 'sub'), pairs)  4.7 us
    ppermute x2, starting transfers between devices, depth_exchange(): far = lax.ppermute(far, ('tile', 'sub'), pairs)  4.05 us
    unnamed x8, local copies, waits for them, and re-layouts  3.67 us
    pallas_call x1, Pallas kernels, two_by_two(): pl.pallas_call(last_kernel, grid=(6,), out_shape=jax.ShapeDtypeStruct(see...  2.65 us
  transfers between devices with their start and end apart: 8, of which 3 were waited for; matrix products, arithmetic and copies ran while one was open for 0% of the time, Pallas kernels for 8%

profile of v1, /device:TPU:0, one launch (start us, length us, event | category | flops | bytes accessed | tf_op | source)
XLA Modules:
  0.0 51.5 jit_solution(13384219372246176190)
XLA Ops:
  0.0 0.0 copy-start
  0.0 1.4 %copy-done = f32[1,6,2,256,128]{4,3,2,1,0:T(8,128)S(1)} copy-done((f32[1,6,2,256,128]{4,3,2,1,0:T(8,128)S(1)}, f32[1,6,2,256,128]{4,3,2,1,0:T(8,128)}, u32[]{:S(2)}) %copy-start) | copy-done | bytes 1572888
  1.4 0.0 copy-start.1
  1.4 0.9 %copy-done.1 = s32[1,2,256,128]{3,2,1,0:T(8,128)S(1)} copy-done((s32[1,2,256,128]{3,2,1,0:T(8,128)S(1)}, s32[1,2,256,128]{3,2,1,0:T(8,128)}, u32[]{:S(2)}) %copy-start.1) | copy-done | bytes 262168
  2.4 0.0 copy-start.2
  2.4 0.7 %copy-done.2 = f32[4]{0:T(128)S(1)} copy-done((f32[4]{0:T(128)S(1)}, f32[4]{0:T(128)}, u32[]{:S(2)}) %copy-start.2) | copy-done | bytes 40
  3.0 0.0 copy-start.3
  3.0 0.7 %copy-done.3 = f32[4]{0:T(128)S(1)} copy-done((f32[4]{0:T(128)S(1)}, f32[4]{0:T(128)}, u32[]{:S(2)}) %copy-start.3) | copy-done | bytes 40
  3.7 1.1 %shard_map.50 = (f32[5,208,128]{2,1,0:T(8,128)S(1)}, f32[5,208,128]{2,1,0:T(8,128)S(1)}) custom-call(f32[4]{0:T(128)S(1)} %copy-done.2, f32[4]{0:T(128)S(1)} %copy-done.3, f32[1,6,2,256,128]{4,3,2,1,0:T(8,128)S(1)} %copy-done, s32[1,2,256,128]{3,2,1,0:T(8,128)S(1)} %copy-done.1), custom_call_target="tpu_custom_call" | custom-call | tf_op jit(solution)/shard_map/pallas_call | solution.py:293
  4.8 0.5 %collective-permute-start.5 = (f32[5,208,128]{2,1,0:T(8,128)S(1)}, f32[5,208,128]{2,1,0:T(8,128)S(1)}, u32[]{:S(2)}, u32[]{:S(2)}) collective-permute-start(f32[5,208,128]{2,1,0:T(8,128)S(1)} %get-tuple-element.23), channel_id=1, source_target_pairs={{0,1},{1,0},{2,3},{3,2},{4,5},{5,4},{6,7},{7,6},{8,9},{9,8},{10,11... | collective-permute-start | bytes 1597448 | tf_op jit(solution)/shard_map/ppermute | solution.py:303
  5.3 2.6 %collective-permute-start.6 = (f32[5,208,128]{2,1,0:T(8,128)S(1)}, f32[5,208,128]{2,1,0:T(8,128)S(1)}, u32[]{:S(2)}, u32[]{:S(2)}) collective-permute-start(f32[5,208,128]{2,1,0:T(8,128)S(1)} %get-tuple-element.24), channel_id=1, source_target_pairs={{0,8},{1,2},{2,1},{3,4},{4,3},{5,6},{6,5},{7,15},{8,0},{9,10},{10,... | collective-permute-start | bytes 1597448 | tf_op jit(solution)/shard_map/ppermute | solution.py:313
  7.8 0.8 %shard_map.46 = (f32[5,80,128]{2,1,0:T(8,128)S(1)}, f32[5,80,128]{2,1,0:T(8,128)S(1)}) custom-call(f32[4]{0:T(128)S(1)} %copy-done.2, f32[4]{0:T(128)S(1)} %copy-done.3, f32[1,6,2,256,128]{4,3,2,1,0:T(8,128)S(1)} %copy-done, s32[1,2,256,128]{3,2,1,0:T(8,128)S(1)} %copy-done.1), custom_call_target="tpu_custom_call" | custom-call | tf_op jit(solution)/shard_map/pallas_call | solution.py:293
  8.6 0.3 collective-permute-start
  8.9 1.5 %collective-permute-start.1 = (f32[5,80,128]{2,1,0:T(8,128)S(1)}, f32[5,80,128]{2,1,0:T(8,128)S(1)}, u32[]{:S(2)}, u32[]{:S(2)}) collective-permute-start(f32[5,80,128]{2,1,0:T(8,128)S(1)} %get-tuple-element.17), channel_id=1, source_target_pairs={{0,8},{1,2},{2,1},{3,4},{4,3},{5,6},{6,5},{7,15},{8,0},{9,10},{10,... | collective-permute-start | bytes 614408 | tf_op jit(solution)/shard_map/ppermute | solution.py:313
  10.4 0.0 collective-permute-done.5.near
  10.4 4.7 %collective-permute-done.6.far = f32[5,208,128]{2,1,0:T(8,128)S(1)} collective-permute-done((f32[5,208,128]{2,1,0:T(8,128)S(1)}, f32[5,208,128]{2,1,0:T(8,128)S(1)}, u32[]{:S(2)}, u32[]{:S(2)}) %collective-permute-start.6) | collective-permute-done | bytes 532512 | tf_op jit(solution)/shard_map/ppermute | solution.py:313
  15.1 1.8 %shard_map.51 = (f32[6,2,192,128]{3,2,1,0:T(8,128)S(1)}, f32[6,2,96,128]{3,2,1,0:T(8,128)S(1)}) custom-call(f32[4]{0:T(128)S(1)} %copy-done.2, f32[4]{0:T(128)S(1)} %copy-done.3, f32[1,6,2,256,128]{4,3,2,1,0:T(8,128)S(1)} %copy-done, s32[1,2,256,128]{3,2,1,0:T(8,128)S(1)} %copy-done.1, f32[5,208,128]{2,1,0:T(8,128)S(1)} %collective-permute-done.5.near, ...), custom_call_target="tpu_custom_call" | custom-call | tf_op jit(solution)/shard_map/pallas_call | solution.py:293
  16.9 2.1 %collective-permute-start.7 = (f32[6,2,96,128]{3,2,1,0:T(8,128)S(1)}, f32[6,2,96,128]{3,2,1,0:T(8,128)S(1)}, u32[]{:S(2)}, u32[]{:S(2)}) collective-permute-start(f32[6,2,96,128]{3,2,1,0:T(8,128)S(1)} %get-tuple-element.26), channel_id=1, source_target_pairs={{0,16},{8,24},{16,0},{24,8},{1,17},{9,25},{17,1},{25,9},{2,18},{10... | collective-permute-start | bytes 1769480 | tf_op jit(solution)/shard_map/ppermute | solution.py:318
  19.0 0.0 collective-permute-done.near
  19.0 0.0 collective-permute-done.1.far
  19.0 1.2 %shard_map.47 = (f32[6,2,64,128]{3,2,1,0:T(8,128)S(1)}, f32[6,2,32,128]{3,2,1,0:T(8,128)S(1)}, f32[6,2,16,128]{3,2,1,0:T(8,128)S(1)}) custom-call(f32[4]{0:T(128)S(1)} %copy-done.2, f32[4]{0:T(128)S(1)} %copy-done.3, f32[1,6,2,256,128]{4,3,2,1,0:T(8,128)S(1)} %copy-done, s32[1,2,256,128]{3,2,1,0:T(8,128)S(1)} %copy-done.1, ...), custom_call_target="tpu_custom_call" | custom-call | tf_op jit(solution)/shard_map/pallas_call | solution.py:293
  20.2 0.4 collective-permute-start.2
  20.6 16.3 %collective-permute-done.2.corner = f32[6,2,32,128]{3,2,1,0:T(8,128)S(1)} collective-permute-done((f32[6,2,32,128]{3,2,1,0:T(8,128)S(1)}, f32[6,2,32,128]{3,2,1,0:T(8,128)S(1)}, u32[]{:S(2)}, u32[]{:S(2)}) %collective-permute-start.2) | collective-permute-done | bytes 196640 | tf_op jit(solution)/shard_map/ppermute | solution.py:318
  36.9 0.3 shard_map.48
  37.1 1.8 %collective-permute-start.3 = (f32[6,2,48,128]{3,2,1,0:T(8,128)S(1)}, f32[6,2,48,128]{3,2,1,0:T(8,128)S(1)}, u32[]{:S(2)}, u32[]{:S(2)}) collective-permute-start(f32[6,2,48,128]{3,2,1,0:T(8,128)S(1)} %get-tuple-element.21), channel_id=1, source_target_pairs={{0,8},{8,0},{16,24},{24,16},{1,9},{9,1},{17,25},{25,17},{2,10},{10... | collective-permute-start | bytes 884744 | tf_op jit(solution)/shard_map/ppermute | solution.py:318
  38.9 1.5 %collective-permute-start.4 = (f32[6,2,16,128]{3,2,1,0:T(8,128)S(1)}, f32[6,2,16,128]{3,2,1,0:T(8,128)S(1)}, u32[]{:S(2)}, u32[]{:S(2)}) collective-permute-start(f32[6,2,16,128]{3,2,1,0:T(8,128)S(1)} %get-tuple-element.22), channel_id=1, source_target_pairs={{0,24},{8,16},{16,8},{24,0},{1,25},{9,17},{17,9},{25,1},{2,26},{10... | collective-permute-start | bytes 294920 | tf_op jit(solution)/shard_map/ppermute | solution.py:318
  40.4 8.3 %collective-permute-done.4.strip = f32[6,2,16,128]{3,2,1,0:T(8,128)S(1)} collective-permute-done((f32[6,2,16,128]{3,2,1,0:T(8,128)S(1)}, f32[6,2,16,128]{3,2,1,0:T(8,128)S(1)}, u32[]{:S(2)}, u32[]{:S(2)}) %collective-permute-start.4) | collective-permute-done | bytes 98336 | tf_op jit(solution)/shard_map/ppermute | solution.py:318
  48.7 0.0 collective-permute-done.3.got
  48.7 0.1 shard_map.49.edge
  48.8 0.0 collective-permute-done.7.bands
  48.9 2.6 %shard_map.52 = f32[1,6,2,256,128]{4,3,2,1,0:T(8,128)} custom-call(f32[6,2,64,128]{3,2,1,0:T(8,128)S(1)} %shard_map.49.edge, f32[6,2,192,128]{3,2,1,0:T(8,128)S(1)} %get-tuple-element.25.mid, f32[6,2,96,128]{3,2,1,0:T(8,128)S(1)} %collective-permute-done.7.bands), custom_call_target="tpu_custom_call" | custom-call | tf_op jit(solution)/shard_map/pallas_call | solution.py:364
Async XLA Ops:
  0.0 1.4 %copy-start = (f32[1,6,2,256,128]{4,3,2,1,0:T(8,128)S(1)}, f32[1,6,2,256,128]{4,3,2,1,0:T(8,128)}, u32[]{:S(2)}) copy-start(f32[1,6,2,256,128]{4,3,2,1,0:T(8,128)} %seeds.7) | copy-start | bytes 4718596
  1.4 0.9 %copy-start.1 = (s32[1,2,256,128]{3,2,1,0:T(8,128)S(1)}, s32[1,2,256,128]{3,2,1,0:T(8,128)}, u32[]{:S(2)}) copy-start(s32[1,2,256,128]{3,2,1,0:T(8,128)} %material.7) | copy-start | bytes 786436
  2.4 0.7 %copy-start.2 = (f32[4]{0:T(128)S(1)}, f32[4]{0:T(128)}, u32[]{:S(2)}) copy-start(f32[4]{0:T(128)} %decay.7) | copy-start | bytes 52
  3.0 0.7 %copy-start.3 = (f32[4]{0:T(128)S(1)}, f32[4]{0:T(128)}, u32[]{:S(2)}) copy-start(f32[4]{0:T(128)} %coupling.7) | copy-start | bytes 52
  4.8 5.6 %collective-permute-start.5 = (f32[5,208,128]{2,1,0:T(8,128)S(1)}, f32[5,208,128]{2,1,0:T(8,128)S(1)}, u32[]{:S(2)}, u32[]{:S(2)}) collective-permute-start(f32[5,208,128]{2,1,0:T(8,128)S(1)} %get-tuple-element.23), channel_id=1, source_target_pairs={{0,1},{1,0},{2,3},{3,2},{4,5},{5,4},{6,7},{7,6},{8,9},{9,8},{10,11... | collective-permute-start | bytes 1597448 | tf_op jit(solution)/shard_map/ppermute | solution.py:303
  5.3 9.8 %collective-permute-start.6 = (f32[5,208,128]{2,1,0:T(8,128)S(1)}, f32[5,208,128]{2,1,0:T(8,128)S(1)}, u32[]{:S(2)}, u32[]{:S(2)}) collective-permute-start(f32[5,208,128]{2,1,0:T(8,128)S(1)} %get-tuple-element.24), channel_id=1, source_target_pairs={{0,8},{1,2},{2,1},{3,4},{4,3},{5,6},{6,5},{7,15},{8,0},{9,10},{10,... | collective-permute-start | bytes 1597448 | tf_op jit(solution)/shard_map/ppermute | solution.py:313
  8.6 10.4 %collective-permute-start = (f32[5,80,128]{2,1,0:T(8,128)S(1)}, f32[5,80,128]{2,1,0:T(8,128)S(1)}, u32[]{:S(2)}, u32[]{:S(2)}) collective-permute-start(f32[5,80,128]{2,1,0:T(8,128)S(1)} %get-tuple-element.16), channel_id=1, source_target_pairs={{0,1},{1,0},{2,3},{3,2},{4,5},{5,4},{6,7},{7,6},{8,9},{9,8},{10,11... | collective-permute-start | bytes 614408 | tf_op jit(solution)/shard_map/ppermute | solution.py:303
  8.9 10.1 %collective-permute-start.1 = (f32[5,80,128]{2,1,0:T(8,128)S(1)}, f32[5,80,128]{2,1,0:T(8,128)S(1)}, u32[]{:S(2)}, u32[]{:S(2)}) collective-permute-start(f32[5,80,128]{2,1,0:T(8,128)S(1)} %get-tuple-element.17), channel_id=1, source_target_pairs={{0,8},{1,2},{2,1},{3,4},{4,3},{5,6},{6,5},{7,15},{8,0},{9,10},{10,... | collective-permute-start | bytes 614408 | tf_op jit(solution)/shard_map/ppermute | solution.py:313
  16.9 32.0 %collective-permute-start.7 = (f32[6,2,96,128]{3,2,1,0:T(8,128)S(1)}, f32[6,2,96,128]{3,2,1,0:T(8,128)S(1)}, u32[]{:S(2)}, u32[]{:S(2)}) collective-permute-start(f32[6,2,96,128]{3,2,1,0:T(8,128)S(1)} %get-tuple-element.26), channel_id=1, source_target_pairs={{0,16},{8,24},{16,0},{24,8},{1,17},{9,25},{17,1},{25,9},{2,18},{10... | collective-permute-start | bytes 1769480 | tf_op jit(solution)/shard_map/ppermute | solution.py:318
  20.2 16.7 %collective-permute-start.2 = (f32[6,2,32,128]{3,2,1,0:T(8,128)S(1)}, f32[6,2,32,128]{3,2,1,0:T(8,128)S(1)}, u32[]{:S(2)}, u32[]{:S(2)}) collective-permute-start(f32[6,2,32,128]{3,2,1,0:T(8,128)S(1)} %get-tuple-element.19), channel_id=1, source_target_pairs={{0,16},{8,24},{16,0},{24,8},{1,17},{9,25},{17,1},{25,9},{2,18},{10... | collective-permute-start | bytes 589832 | tf_op jit(solution)/shard_map/ppermute | solution.py:318
  37.1 11.6 %collective-permute-start.3 = (f32[6,2,48,128]{3,2,1,0:T(8,128)S(1)}, f32[6,2,48,128]{3,2,1,0:T(8,128)S(1)}, u32[]{:S(2)}, u32[]{:S(2)}) collective-permute-start(f32[6,2,48,128]{3,2,1,0:T(8,128)S(1)} %get-tuple-element.21), channel_id=1, source_target_pairs={{0,8},{8,0},{16,24},{24,16},{1,9},{9,1},{17,25},{25,17},{2,10},{10... | collective-permute-start | bytes 884744 | tf_op jit(solution)/shard_map/ppermute | solution.py:318
  38.9 9.8 %collective-permute-start.4 = (f32[6,2,16,128]{3,2,1,0:T(8,128)S(1)}, f32[6,2,16,128]{3,2,1,0:T(8,128)S(1)}, u32[]{:S(2)}, u32[]{:S(2)}) collective-permute-start(f32[6,2,16,128]{3,2,1,0:T(8,128)S(1)} %get-tuple-element.22), channel_id=1, source_target_pairs={{0,24},{8,16},{16,8},{24,0},{1,25},{9,17},{17,9},{25,1},{2,26},{10... | collective-permute-start | bytes 294920 | tf_op jit(solution)/shard_map/ppermute | solution.py:318

commit v2 on v1

--- a/solution.py
+++ b/solution.py
@@ -58,10 +58,10 @@
     return v - prev_y(v)
 
 
-def looked_up(labels, table):
-    value = jnp.full(labels.shape, table[0], jnp.float32)
-    for m in range(1, table.shape[0]):
-        value = jnp.where(labels == m, table[m], value)
+def looked_up(labels, entries):
+    value = jnp.broadcast_to(entries[0], labels.shape)
+    for m in range(1, len(entries)):
+        value = jnp.where(labels == m, entries[m], value)
     return value
 
 
@@ -97,35 +97,69 @@
     return [[cb[p] * e[c][p] for p in range(len(cb))] for c in range(3)]
 
 
-def loaded(seeds, material, decay, coupling, lo, hi):
+def joined(ref, index, spans):
+    return jnp.concatenate([ref[*index, lo:hi] for lo, hi in spans], axis=0)
+
+
+def prepared(e, h, labels, tables):
+    ca = [looked_up(m, tables[0]) for m in labels]
+    cb = [looked_up(m, tables[1]) for m in labels]
+    return e, h, ca, cb
+
+
+def loaded(seeds, material, table, spans):
     depth = seeds.shape[2]
-    e = [[seeds[0, c, p, lo:hi] for p in range(depth)] for c in range(3)]
-    h = [[seeds[0, 3 + c, p, lo:hi] for p in range(depth)] for c in range(3)]
-    labels = [material[0, p, lo:hi] for p in range(depth)]
-    ca = [looked_up(m, decay) for m in labels]
-    cb = [looked_up(m, coupling) for m in labels]
-    return e, h, ca, cb
+    count = table.shape[0] // 2
+    e = [[joined(seeds, (0, c, p), spans) for p in range(depth)] for c in range(3)]
+    h = [[joined(seeds, (0, 3 + c, p), spans) for p in range(depth)] for c in range(3)]
+    labels = [joined(material, (0, p), spans) for p in range(depth)]
+    rows = [table[m : m + 1] for m in range(2 * count)]
+    return prepared(e, h, labels, (rows[:count], rows[count:]))
 
 
 NONE = (None, None)
 
 
-def halo_kernel(spans, sub, decay, coupling, seeds, material, near, far):
+def send_halos(sub, fields, near, far):
     odd = lax.rem(lax.axis_index(sub), 2) == 1
+    e, h, ca, cb = fields
+    v1 = scaled(cb, e)
+    h1 = update_h(h, v1, NONE)
+    e1 = update_e(e, ca, h1, NONE)
+    v2 = scaled(cb, e1)
+    h2 = update_h(h1, v2, NONE)
+    up = (h1[0][-1], h1[1][-1], h2[0][-1], h2[1][-1], cb[-1])
+    down = (v1[0][0], v1[1][0], v2[0][0], v2[1][0], cb[0])
+    for k in range(PLANES):
+        near[k] = jnp.where(odd, down[k], up[k])
+        far[k] = jnp.where(odd, up[k], down[k])
+
+
+def halo_kernel(spans, sub, table, seeds, material, near, far):
+    send_halos(sub, loaded(seeds, material, table, spans), near, far)
+
+
+def first_halo_kernel(spans, sub, decay, coupling, seeds, material, near, far, held, labels, tables, sems):
+    copies = [
+        pltpu.make_async_copy(decay, tables.at[0], sems.at[0]),
+        pltpu.make_async_copy(coupling, tables.at[1], sems.at[1]),
+    ]
     at = 0
     for lo, hi in spans:
-        e, h, ca, cb = loaded(seeds, material, decay, coupling, lo, hi)
-        v1 = scaled(cb, e)
-        h1 = update_h(h, v1, NONE)
-        e1 = update_e(e, ca, h1, NONE)
-        v2 = scaled(cb, e1)
-        h2 = update_h(h1, v2, NONE)
-        up = (h1[0][-1], h1[1][-1], h2[0][-1], h2[1][-1], cb[-1])
-        down = (v1[0][0], v1[1][0], v2[0][0], v2[1][0], cb[0])
-        for k in range(PLANES):
-            near[k, at : at + hi - lo] = jnp.where(odd, down[k], up[k])
-            far[k, at : at + hi - lo] = jnp.where(odd, up[k], down[k])
+        rows, here = pl.ds(lo, hi - lo), pl.ds(at, hi - lo)
+        copies.append(pltpu.make_async_copy(seeds.at[0, :, :, rows], held.at[:, :, here], sems.at[len(copies)]))
+        copies.append(pltpu.make_async_copy(material.at[0, :, rows], labels.at[:, here], sems.at[len(copies)]))
         at += hi - lo
+    for copy in copies:
+        copy.start()
+    for copy in copies:
+        copy.wait()
+    depth = held.shape[1]
+    e = [[held[c, p] for p in range(depth)] for c in range(3)]
+    h = [[held[3 + c, p] for p in range(depth)] for c in range(3)]
+    entries = [[tables[k, m] for m in range(tables.shape[1])] for k in range(2)]
+    fields = prepared(e, h, [labels[p] for p in range(depth)], entries)
+    send_halos(sub, fields, near, far)
 
 
 def ramp(position, count):
@@ -137,13 +171,13 @@
     )
 
 
-def final_fields(fields, near, far, at, rows, sub, sub_size):
+def final_fields(fields, near, far, sub, sub_size):
     e, h, ca, cb = fields
     index = lax.axis_index(sub)
     odd = lax.rem(index, 2) == 1
     below, above = index > 0, index < sub_size - 1
-    a = [near[k, at : at + rows] for k in range(PLANES)]
-    b = [far[k, at : at + rows] for k in range(PLANES)]
+    a = [near[k] for k in range(PLANES)]
+    b = [far[k] for k in range(PLANES)]
     from_below = [jnp.where(odd, a[k], b[k]) for k in range(PLANES)]
     from_above = [jnp.where(above, jnp.where(odd, b[k], a[k]), 0.0) for k in range(PLANES)]
     part_h1x, part_h1y, part_h2x, part_h2y, cb_low = from_below
@@ -191,25 +225,24 @@
     return first, second
 
 
-def weighted_planes(seeds, material, decay, coupling, near, far, at, lo, hi, keep, sub, sub_size):
-    fields = loaded(seeds, material, decay, coupling, lo, hi)
-    planes = final_fields(fields, near, far, at, hi - lo, sub, sub_size)
-    start, stop = keep
+def weighted_planes(seeds, material, table, near, far, spans, keeps, sub, sub_size):
+    planes = final_fields(loaded(seeds, material, table, spans), near, far, sub, sub_size)
     size_x, size_y = seeds.shape[3:]
-    shape = (stop - start, size_y)
-    weight = ramp(row_of(shape) + start, size_x) * ramp(lane_of(shape), size_y)
-    return [[plane[start - lo : stop - lo] * weight for plane in part] for part in planes]
-
-
-def edge_kernel(spans, sub, sub_size, tile, decay, coupling, seeds, material, near, far, edge, corner, strip):
-    at = 0
-    parts = []
+    at, results = 0, []
+    for (lo, hi), (start, stop) in zip(spans, keeps):
+        shape = (stop - start, size_y)
+        weight = ramp(row_of(shape) + start, size_x) * ramp(lane_of(shape), size_y)
+        first = at + start - lo
+        results.append([[plane[first : first + stop - start] * weight for plane in part] for part in planes])
+        at += hi - lo
+    return results
+
+
+def edge_kernel(spans, sub, sub_size, tile, table, seeds, material, near, far, edge, corner, strip):
     size_x = seeds.shape[3]
-    for (lo, hi), keep in zip(spans, ((0, BAND), (size_x - BAND, size_x))):
-        parts.append(weighted_planes(seeds, material, decay, coupling, near, far, at, lo, hi, keep, sub, sub_size))
-        at += hi - lo
+    keeps = ((0, BAND), (size_x - BAND, size_x))
+    low, high = weighted_planes(seeds, material, table, near, far, spans, keeps, sub, sub_size)
     odd = lax.rem(lax.axis_index(tile), 2) == 1
-    low, high = parts
     half = BAND // 2
     for c in range(6):
         for p in range(seeds.shape[2]):
@@ -220,11 +253,10 @@
             strip[c, p] = y_packed(middle_out(away[:half]), middle_out(away[half:]))
 
 
-def middle_kernel(spans, sub, sub_size, decay, coupling, seeds, material, near, far, mid, bands):
-    (lo, hi), = spans
+def middle_kernel(spans, sub, sub_size, table, seeds, material, near, far, mid, bands):
     size_x = seeds.shape[3]
     keep = (BAND, size_x - BAND)
-    planes = weighted_planes(seeds, material, decay, coupling, near, far, 0, lo, hi, keep, sub, sub_size)
+    planes, = weighted_planes(seeds, material, table, near, far, spans, (keep,), sub, sub_size)
     half = (keep[1] - keep[0]) // 2
     for c in range(6):
         for p in range(seeds.shape[2]):
@@ -232,9 +264,8 @@
             bands[c, p] = y_packed(planes[c][p][:half], planes[c][p][half:])
 
 
-def whole_kernel(spans, sub, sub_size, decay, coupling, seeds, material, near, far, out):
-    (lo, hi), = spans
-    planes = weighted_planes(seeds, material, decay, coupling, near, far, 0, lo, hi, (lo, hi), sub, sub_size)
+def whole_kernel(spans, sub, sub_size, table, seeds, material, near, far, out):
+    planes, = weighted_planes(seeds, material, table, near, far, spans, spans, sub, sub_size)
     for c in range(6):
         for p in range(seeds.shape[2]):
             out[c, p] = planes[c][p]
@@ -272,31 +303,41 @@
             out[c, p, BAND:] = summed[c, p, BAND:] + jnp.where(odd, away, by)
 
 
-def last_kernel(edge, mid, bands, out):
-    for p in range(mid.shape[1]):
-        half = bands.shape[2]
-        size_x = out.shape[3]
-        first, second = y_unpacked(bands[0, p])
-        out[0, 0, p, :BAND] = edge[0, p, :BAND]
-        out[0, 0, p, BAND : BAND + half] = mid[0, p, :half] + first
-        out[0, 0, p, BAND + half : size_x - BAND] = mid[0, p, half:] + second
-        out[0, 0, p, size_x - BAND :] = edge[0, p, BAND:]
-
-
-SMEM = pl.BlockSpec(memory_space=pltpu.SMEM)
+def last_kernel(edge, mid, bands, out, whole, sems):
+    half = bands.shape[2]
+    size_x = out.shape[3]
+    copies = []
+    for c in range(mid.shape[0]):
+        for p in range(mid.shape[1]):
+            first, second = y_unpacked(bands[c, p])
+            whole[c, p, :BAND] = edge[c, p, :BAND]
+            whole[c, p, BAND : BAND + half] = mid[c, p, :half] + first
+            whole[c, p, BAND + half : size_x - BAND] = mid[c, p, half:] + second
+            whole[c, p, size_x - BAND :] = edge[c, p, BAND:]
+        copies.append(pltpu.make_async_copy(whole.at[c], out.at[0, c], sems.at[c]))
+        copies[-1].start()
+    for copy in copies:
+        copy.wait()
+
+
+HBM = pl.BlockSpec(memory_space=pltpu.HBM)
 VMEM = pl.BlockSpec(memory_space=pltpu.VMEM)
 PARAMS = pltpu.CompilerParams(vmem_limit_bytes=32 * 1024 * 1024)
 
 
-def called(kernel, shapes, in_specs, *operands):
+def called(kernel, shapes, *operands):
     outs = [jax.ShapeDtypeStruct(shape, jnp.float32) for shape in shapes]
     return pl.pallas_call(
         kernel,
         out_shape=outs,
-        in_specs=in_specs,
+        in_specs=[VMEM] * len(operands),
         out_specs=[VMEM] * len(outs),
         compiler_params=PARAMS,
     )(*operands)
+
+
+def after(first, *values):
+    return lax.optimization_barrier((first, *values))
 
 
 def depth_exchange(near, far, sub_size, tile_size):
@@ -322,51 +363,70 @@
     return lax.ppermute(value, "tile", [(t, (t + steps) % count) for t in range(count)])
 
 
+def table_rows(decay, coupling, size_y):
+    entries = jnp.concatenate([decay, coupling])
+    return jnp.broadcast_to(entries[:, None], (entries.shape[0], size_y))
+
+
 def two_by_two(seeds, material, decay, coupling, sub_size, tile_size):
     depth, size_x, size_y = seeds.shape[2:]
     edges = ((0, BAND + HALO), (size_x - BAND - HALO, size_x))
     inner = ((BAND - HALO, size_x - BAND + HALO),)
-    tables = [SMEM, SMEM, VMEM, VMEM]
-
-    def halos(spans):
-        shape = (PLANES, sum(hi - lo for lo, hi in spans), size_y)
-        kernel = functools.partial(halo_kernel, spans, "sub")
-        return called(kernel, [shape, shape], tables, decay, coupling, seeds, material)
-
-    edge_near, edge_far = depth_exchange(*halos(edges), sub_size, tile_size)
-    inner_near, inner_far = depth_exchange(*halos(inner), sub_size, tile_size)
+    rows = size_x - 2 * BAND
+    count = sum(hi - lo for lo, hi in edges)
+
+    shape = jax.ShapeDtypeStruct((PLANES, count, size_y), jnp.float32)
+    near, far = pl.pallas_call(
+        functools.partial(first_halo_kernel, edges, "sub"),
+        out_shape=[shape, shape],
+        in_specs=[HBM] * 4,
+        out_specs=[VMEM] * 2,
+        scratch_shapes=[
+            pltpu.VMEM((6, depth, count, size_y), jnp.float32),
+            pltpu.VMEM((depth, count, size_y), jnp.int32),
+            pltpu.SMEM((2, *decay.shape), jnp.float32),
+            pltpu.SemaphoreType.DMA((2 + 2 * len(edges),)),
+        ],
+        compiler_params=PARAMS,
+    )(*(pltpu.with_memory_space_constraint(x, pltpu.HBM) for x in (decay, coupling, seeds, material)))
+    table = table_rows(decay, coupling, size_y)
+    edge_near, edge_far = depth_exchange(near, far, sub_size, tile_size)
+    edge_near, table = after(edge_near, table)
+
+    shape = (PLANES, rows + 2 * HALO, size_y)
+    near, far = called(functools.partial(halo_kernel, inner, "sub"), [shape, shape], table, seeds, material)
+    edge_far, near, far = after(edge_far, near, far)
+    inner_near, inner_far = depth_exchange(near, far, sub_size, tile_size)
 
     edge, corner, strip = called(
         functools.partial(edge_kernel, edges, "sub", sub_size, "tile"),
         [(6, depth, 2 * BAND, size_y), (6, depth, BAND, size_y), (6, depth, BAND // 2, size_y)],
-        tables + [VMEM, VMEM], decay, coupling, seeds, material, edge_near, edge_far,
+        table, seeds, material, edge_near, edge_far,
     )
     corner = swapped(corner, 2, tile_size)
     strip = swapped(strip, 3, tile_size)
-    rows = size_x - 2 * BAND
     mid, bands = called(
         functools.partial(middle_kernel, inner, "sub", sub_size),
         [(6, depth, rows, size_y), (6, depth, rows // 2, size_y)],
-        tables + [VMEM, VMEM], decay, coupling, seeds, material, inner_near, inner_far,
-    )
+        table, seeds, material, inner_near, inner_far,
+    )
+    corner, bands = after(corner, bands)
     bands = swapped(bands, 2, tile_size)
     summed, send = called(
         functools.partial(corner_kernel, "tile"),
         [(6, depth, 2 * BAND, size_y), (6, depth, BAND + BAND // 2, size_y)],
-        [VMEM, VMEM], edge, corner,
+        edge, corner,
     )
     got = swapped(send, 1, tile_size)
     edge, = called(
-        functools.partial(seam_kernel, "tile"), [(6, depth, 2 * BAND, size_y)],
-        [VMEM, VMEM, VMEM], summed, got, strip,
-    )
-    block = lambda n: pl.BlockSpec((1, depth, n, size_y), lambda c: (c, 0, 0, 0))
+        functools.partial(seam_kernel, "tile"), [(6, depth, 2 * BAND, size_y)], summed, got, strip
+    )
     return pl.pallas_call(
         last_kernel,
-        grid=(6,),
         out_shape=jax.ShapeDtypeStruct(seeds.shape, jnp.float32),
-        in_specs=[block(2 * BAND), block(rows), block(rows // 2)],
-        out_specs=pl.BlockSpec((1, 1, depth, size_x, size_y), lambda c: (0, c, 0, 0, 0)),
+        in_specs=[VMEM] * 3,
+        out_specs=HBM,
+        scratch_shapes=[pltpu.VMEM(seeds.shape[1:], jnp.float32), pltpu.SemaphoreType.DMA((6,))],
         compiler_params=PARAMS,
     )(edge, mid, bands)
 
@@ -374,15 +434,13 @@
 def any_lattice(seeds, material, decay, coupling, sub_size, tile_size):
     depth, size_x, size_y = seeds.shape[2:]
     spans = ((0, size_x),)
-    tables = [SMEM, SMEM, VMEM, VMEM]
+    table = table_rows(decay, coupling, size_y)
     shape = (PLANES, size_x, size_y)
-    near, far = called(
-        functools.partial(halo_kernel, spans, "sub"), [shape, shape], tables, decay, coupling, seeds, material
-    )
+    near, far = called(functools.partial(halo_kernel, spans, "sub"), [shape, shape], table, seeds, material)
     near, far = depth_exchange(near, far, sub_size, tile_size)
     weighted, = called(
         functools.partial(whole_kernel, spans, "sub", sub_size), [(6, depth, size_x, size_y)],
-        tables + [VMEM, VMEM], decay, coupling, seeds, material, near, far,
+        table, seeds, material, near, far,
     )
     side = math.isqrt(tile_size)
     prev_band = from_behind(weighted[:, :, size_x - BAND :, :], 1, tile_size)

time: 51.7 us -> 38.3 us (0.74)
  waiting for transfers between devices: 29.3 us -> 21.8 us
  local copies, waits for them, and re-layouts: 3.67 us -> 0.08 us
  Pallas kernels: 7.9 us -> 5.68 us
    ppermute x4, waiting for transfers between devices: 24.6 us -> 13.7 us  [swapped(): lax.ppermute(value, 'tile', [(t, t ^ bits) for t in range(tile_size)])]
    unnamed x8, local copies, waits for them, and re-layouts: 3.67 us -> 0.01 us
    ppermute x2, waiting for transfers between devices: 4.7 us -> 8.04 us  [depth_exchange(): far = lax.ppermute(far, ('tile', 'sub'), pairs)]
    pallas_call x7, Pallas kernels: 7.9 us -> 5.68 us  [the longest x5 2.87 us: called(): pl.pallas_call(kernel, out_shape=outs, in_specs=[VMEM] * len(operands), o...]
    ppermute x2, starting transfers between devices: 4.05 us -> 4.58 us  [depth_exchange(): far = lax.ppermute(far, ('tile', 'sub'), pairs)]
  transfers between devices with their start and end apart: 8 -> 8, of which waited for: 3 -> 4; matrix products, arithmetic and copies ran while one was open for 0% -> 0% of each run, Pallas kernels for 8% -> 8%
where the time goes in v2:
time: 38.3 us; the launch traced here: 38.2 us
  waiting for transfers between devices  21.8 us (57%)
  starting transfers between devices  10.5 us (27%)
  Pallas kernels  5.68 us (15%)
    ppermute x4, waiting for transfers between devices, swapped(): lax.ppermute(value, 'tile', [(t, t ^ bits) for t in range(tile_size)])  13.7 us
    ppermute x2, waiting for transfers between devices, depth_exchange(): far = lax.ppermute(far, ('tile', 'sub'), pairs)  8.04 us
    ppermute x4, starting transfers between devices, swapped(): lax.ppermute(value, 'tile', [(t, t ^ bits) for t in range(tile_size)])  5.26 us
    ppermute x2, starting transfers between devices, depth_exchange(): far = lax.ppermute(far, ('tile', 'sub'), pairs)  4.58 us
    pallas_call x5, Pallas kernels, called(): pl.pallas_call(kernel, out_shape=outs, in_specs=[VMEM] * len(operands), o...  2.87 us
    pallas_call x1, Pallas kernels, two_by_two(): pl.pallas_call(functools.partial(first_halo_kernel, edges, 'sub'), out_sh...  1.51 us
    pallas_call x1, Pallas kernels, two_by_two(): pl.pallas_call(last_kernel, out_shape=jax.ShapeDtypeStruct(seeds.shape, j...  1.3 us
  transfers between devices with their start and end apart: 8, of which 4 were waited for; matrix products, arithmetic and copies ran while one was open for 0% of the time, Pallas kernels for 8%

profile of v2, /device:TPU:0, one launch (start us, length us, event | category | flops | bytes accessed | tf_op | source)
XLA Modules:
  0.0 38.2 jit_solution(14166551545862178036)
XLA Ops:
  0.0 0.0 copy-start.1
  0.0 0.0 copy-start
  0.0 0.0 copy-start.3
  0.0 1.5 %shard_map.46 = (f32[5,80,128]{2,1,0:T(8,128)S(1)}, f32[5,80,128]{2,1,0:T(8,128)S(1)}) custom-call(f32[4]{0:T(128)} %decay.1, f32[4]{0:T(128)} %coupling.1, f32[1,6,2,256,128]{4,3,2,1,0:T(8,128)} %seeds.7, s32[1,2,256,128]{3,2,1,0:T(8,128)} %material.7), custom_call_target="tpu_custom_call" | custom-call | tf_op jit(solution)/shard_map/pallas_call | solution.py:379
  1.5 0.5 %collective-permute-start = (f32[5,80,128]{2,1,0:T(8,128)S(1)}, f32[5,80,128]{2,1,0:T(8,128)S(1)}, u32[]{:S(2)}, u32[]{:S(2)}) collective-permute-start(f32[5,80,128]{2,1,0:T(8,128)S(1)} %get-tuple-element.23), channel_id=1, source_target_pairs={{0,1},{1,0},{2,3},{3,2},{4,5},{5,4},{6,7},{7,6},{8,9},{9,8},{10,11... | collective-permute-start | bytes 614408 | tf_op jit(solution)/shard_map/ppermute | solution.py:344
  2.1 2.6 %collective-permute-start.1 = (f32[5,80,128]{2,1,0:T(8,128)S(1)}, f32[5,80,128]{2,1,0:T(8,128)S(1)}, u32[]{:S(2)}, u32[]{:S(2)}) collective-permute-start(f32[5,80,128]{2,1,0:T(8,128)S(1)} %get-tuple-element.26), channel_id=1, source_target_pairs={{0,8},{1,2},{2,1},{3,4},{4,3},{5,6},{6,5},{7,15},{8,0},{9,10},{10,... | collective-permute-start | bytes 614408 | tf_op jit(solution)/shard_map/ppermute | solution.py:354
  4.6 0.0 copy-done.2
  4.6 0.0 copy-done.3
  4.6 0.1 pad_maximum_fusion
  4.7 0.0 collective-permute-done.near
  4.7 0.1 broadcast_in_dim.2.table
  4.8 0.0 copy-done.1
  4.8 0.0 copy-done
  4.8 0.5 %shard_map.47 = (f32[5,208,128]{2,1,0:T(8,128)S(1)}, f32[5,208,128]{2,1,0:T(8,128)S(1)}) custom-call(f32[8,128]{1,0:T(8,128)S(1)} %broadcast_in_dim.2.table, f32[1,6,2,256,128]{4,3,2,1,0:T(8,128)S(1)} %copy-done, s32[1,2,256,128]{3,2,1,0:T(8,128)S(1)} %copy-done.1), custom_call_target="tpu_custom_call" | custom-call | tf_op jit(solution)/shard_map/pallas_call | solution.py:330
  5.3 3.0 %collective-permute-done.1.far = f32[5,80,128]{2,1,0:T(8,128)S(1)} collective-permute-done((f32[5,80,128]{2,1,0:T(8,128)S(1)}, f32[5,80,128]{2,1,0:T(8,128)S(1)}, u32[]{:S(2)}, u32[]{:S(2)}) %collective-permute-start.1) | collective-permute-done | bytes 204832 | tf_op jit(solution)/shard_map/ppermute | solution.py:354
  8.4 0.1 collective-permute-start.3
  8.5 2.0 %collective-permute-start.4 = (f32[5,208,128]{2,1,0:T(8,128)S(1)}, f32[5,208,128]{2,1,0:T(8,128)S(1)}, u32[]{:S(2)}, u32[]{:S(2)}) collective-permute-start(f32[5,208,128]{2,1,0:T(8,128)S(1)} %get-tuple-element.33), channel_id=1, source_target_pairs={{0,8},{1,2},{2,1},{3,4},{4,3},{5,6},{6,5},{7,15},{8,0},{9,10},{10,... | collective-permute-start | bytes 1597448 | tf_op jit(solution)/shard_map/ppermute | solution.py:354
  10.5 0.7 %shard_map.48 = (f32[6,2,64,128]{3,2,1,0:T(8,128)S(1)}, f32[6,2,32,128]{3,2,1,0:T(8,128)S(1)}, f32[6,2,16,128]{3,2,1,0:T(8,128)S(1)}) custom-call(f32[8,128]{1,0:T(8,128)S(1)} %broadcast_in_dim.2.table, f32[1,6,2,256,128]{4,3,2,1,0:T(8,128)S(1)} %copy-done, s32[1,2,256,128]{3,2,1,0:T(8,128)S(1)} %copy-done.1, f32[5,80,128]{2,1,0:T(8,128)S(1)} %collective-permute-done.near, ...), custom_call_target="tpu_custom_call" | custom-call | tf_op jit(solution)/shard_map/pallas_call | solution.py:330
  11.1 1.6 %collective-permute-start.2 = (f32[6,2,32,128]{3,2,1,0:T(8,128)S(1)}, f32[6,2,32,128]{3,2,1,0:T(8,128)S(1)}, u32[]{:S(2)}, u32[]{:S(2)}) collective-permute-start(f32[6,2,32,128]{3,2,1,0:T(8,128)S(1)} %get-tuple-element.31), channel_id=1, source_target_pairs={{0,16},{8,24},{16,0},{24,8},{1,17},{9,25},{17,1},{25,9},{2,18},{10... | collective-permute-start | bytes 589832 | tf_op jit(solution)/shard_map/ppermute | solution.py:359
  12.7 0.0 collective-permute-done.3.near
  12.7 5.0 %collective-permute-done.4.far = f32[5,208,128]{2,1,0:T(8,128)S(1)} collective-permute-done((f32[5,208,128]{2,1,0:T(8,128)S(1)}, f32[5,208,128]{2,1,0:T(8,128)S(1)}, u32[]{:S(2)}, u32[]{:S(2)}) %collective-permute-start.4) | collective-permute-done | bytes 532512 | tf_op jit(solution)/shard_map/ppermute | solution.py:354
  17.7 1.3 %shard_map.49 = (f32[6,2,192,128]{3,2,1,0:T(8,128)S(1)}, f32[6,2,96,128]{3,2,1,0:T(8,128)S(1)}) custom-call(f32[8,128]{1,0:T(8,128)S(1)} %broadcast_in_dim.2.table, f32[1,6,2,256,128]{4,3,2,1,0:T(8,128)S(1)} %copy-done, s32[1,2,256,128]{3,2,1,0:T(8,128)S(1)} %copy-done.1, f32[5,208,128]{2,1,0:T(8,128)S(1)} %collective-permute-done.3.near, ...), custom_call_target="tpu_custom_call" | custom-call | tf_op jit(solution)/shard_map/pallas_call | solution.py:330
  19.0 0.0 collective-permute-done.2.corner
  19.0 2.1 %collective-permute-start.7 = (f32[6,2,96,128]{3,2,1,0:T(8,128)S(1)}, f32[6,2,96,128]{3,2,1,0:T(8,128)S(1)}, u32[]{:S(2)}, u32[]{:S(2)}) collective-permute-start(f32[6,2,96,128]{3,2,1,0:T(8,128)S(1)} %get-tuple-element.40), channel_id=1, source_target_pairs={{0,16},{8,24},{16,0},{24,8},{1,17},{9,25},{17,1},{25,9},{2,18},{10... | collective-permute-start | bytes 1769480 | tf_op jit(solution)/shard_map/ppermute | solution.py:359
  21.1 0.3 shard_map.50
  21.4 1.5 %collective-permute-start.5 = (f32[6,2,48,128]{3,2,1,0:T(8,128)S(1)}, f32[6,2,48,128]{3,2,1,0:T(8,128)S(1)}, u32[]{:S(2)}, u32[]{:S(2)}) collective-permute-start(f32[6,2,48,128]{3,2,1,0:T(8,128)S(1)} %get-tuple-element.37), channel_id=1, source_target_pairs={{0,8},{8,0},{16,24},{24,16},{1,9},{9,1},{17,25},{25,17},{2,10},{10... | collective-permute-start | bytes 884744 | tf_op jit(solution)/shard_map/ppermute | solution.py:359
  22.9 0.0 collective-permute-start.6
  23.0 9.2 %collective-permute-done.6.strip = f32[6,2,16,128]{3,2,1,0:T(8,128)S(1)} collective-permute-done((f32[6,2,16,128]{3,2,1,0:T(8,128)S(1)}, f32[6,2,16,128]{3,2,1,0:T(8,128)S(1)}, u32[]{:S(2)}, u32[]{:S(2)}) %collective-permute-start.6) | collective-permute-done | bytes 98336 | tf_op jit(solution)/shard_map/ppermute | solution.py:359
  32.1 0.0 collective-permute-done.5.got
  32.2 0.1 shard_map.51.edge
  32.3 4.6 %collective-permute-done.7.bands = f32[6,2,96,128]{3,2,1,0:T(8,128)S(1)} collective-permute-done((f32[6,2,96,128]{3,2,1,0:T(8,128)S(1)}, f32[6,2,96,128]{3,2,1,0:T(8,128)S(1)}, u32[]{:S(2)}, u32[]{:S(2)}) %collective-permute-start.7) | collective-permute-done | bytes 589856 | tf_op jit(solution)/shard_map/ppermute | solution.py:359
  36.9 1.3 %shard_map.52 = f32[1,6,2,256,128]{4,3,2,1,0:T(8,128)} custom-call(f32[6,2,64,128]{3,2,1,0:T(8,128)S(1)} %shard_map.51.edge, f32[6,2,192,128]{3,2,1,0:T(8,128)S(1)} %get-tuple-element.39.mid, f32[6,2,96,128]{3,2,1,0:T(8,128)S(1)} %collective-permute-done.7.bands), custom_call_target="tpu_custom_call" | custom-call | tf_op jit(solution)/shard_map/pallas_call | solution.py:424
  (1 shorter events, 0.0 us)
Async XLA Ops:
  0.0 4.8 %copy-start.1 = (s32[1,2,256,128]{3,2,1,0:T(8,128)S(1)}, s32[1,2,256,128]{3,2,1,0:T(8,128)}, u32[]{:S(2)}) copy-start(s32[1,2,256,128]{3,2,1,0:T(8,128)} %material.7) | copy-start | bytes 786436
  0.0 4.8 %copy-start = (f32[1,6,2,256,128]{4,3,2,1,0:T(8,128)S(1)}, f32[1,6,2,256,128]{4,3,2,1,0:T(8,128)}, u32[]{:S(2)}) copy-start(f32[1,6,2,256,128]{4,3,2,1,0:T(8,128)} %seeds.7) | copy-start | bytes 4718596
  0.0 4.6 %copy-start.2 = (f32[4]{0:T(128)S(1)}, f32[4]{0:T(128)}, u32[]{:S(2)}) copy-start(f32[4]{0:T(128)} %coupling.1) | copy-start | bytes 52
  0.0 4.6 %copy-start.3 = (f32[4]{0:T(128)S(1)}, f32[4]{0:T(128)}, u32[]{:S(2)}) copy-start(f32[4]{0:T(128)} %decay.1) | copy-start | bytes 52
  1.5 3.2 %collective-permute-start = (f32[5,80,128]{2,1,0:T(8,128)S(1)}, f32[5,80,128]{2,1,0:T(8,128)S(1)}, u32[]{:S(2)}, u32[]{:S(2)}) collective-permute-start(f32[5,80,128]{2,1,0:T(8,128)S(1)} %get-tuple-element.23), channel_id=1, source_target_pairs={{0,1},{1,0},{2,3},{3,2},{4,5},{5,4},{6,7},{7,6},{8,9},{9,8},{10,11... | collective-permute-start | bytes 614408 | tf_op jit(solution)/shard_map/ppermute | solution.py:344
  2.1 6.3 %collective-permute-start.1 = (f32[5,80,128]{2,1,0:T(8,128)S(1)}, f32[5,80,128]{2,1,0:T(8,128)S(1)}, u32[]{:S(2)}, u32[]{:S(2)}) collective-permute-start(f32[5,80,128]{2,1,0:T(8,128)S(1)} %get-tuple-element.26), channel_id=1, source_target_pairs={{0,8},{1,2},{2,1},{3,4},{4,3},{5,6},{6,5},{7,15},{8,0},{9,10},{10,... | collective-permute-start | bytes 614408 | tf_op jit(solution)/shard_map/ppermute | solution.py:354
  8.4 4.4 %collective-permute-start.3 = (f32[5,208,128]{2,1,0:T(8,128)S(1)}, f32[5,208,128]{2,1,0:T(8,128)S(1)}, u32[]{:S(2)}, u32[]{:S(2)}) collective-permute-start(f32[5,208,128]{2,1,0:T(8,128)S(1)} %get-tuple-element.32), channel_id=1, source_target_pairs={{0,1},{1,0},{2,3},{3,2},{4,5},{5,4},{6,7},{7,6},{8,9},{9,8},{10,11... | collective-permute-start | bytes 1597448 | tf_op jit(solution)/shard_map/ppermute | solution.py:344
  8.5 9.3 %collective-permute-start.4 = (f32[5,208,128]{2,1,0:T(8,128)S(1)}, f32[5,208,128]{2,1,0:T(8,128)S(1)}, u32[]{:S(2)}, u32[]{:S(2)}) collective-permute-start(f32[5,208,128]{2,1,0:T(8,128)S(1)} %get-tuple-element.33), channel_id=1, source_target_pairs={{0,8},{1,2},{2,1},{3,4},{4,3},{5,6},{6,5},{7,15},{8,0},{9,10},{10,... | collective-permute-start | bytes 1597448 | tf_op jit(solution)/shard_map/ppermute | solution.py:354
  11.1 7.9 %collective-permute-start.2 = (f32[6,2,32,128]{3,2,1,0:T(8,128)S(1)}, f32[6,2,32,128]{3,2,1,0:T(8,128)S(1)}, u32[]{:S(2)}, u32[]{:S(2)}) collective-permute-start(f32[6,2,32,128]{3,2,1,0:T(8,128)S(1)} %get-tuple-element.31), channel_id=1, source_target_pairs={{0,16},{8,24},{16,0},{24,8},{1,17},{9,25},{17,1},{25,9},{2,18},{10... | collective-permute-start | bytes 589832 | tf_op jit(solution)/shard_map/ppermute | solution.py:359
  19.0 17.8 %collective-permute-start.7 = (f32[6,2,96,128]{3,2,1,0:T(8,128)S(1)}, f32[6,2,96,128]{3,2,1,0:T(8,128)S(1)}, u32[]{:S(2)}, u32[]{:S(2)}) collective-permute-start(f32[6,2,96,128]{3,2,1,0:T(8,128)S(1)} %get-tuple-element.40), channel_id=1, source_target_pairs={{0,16},{8,24},{16,0},{24,8},{1,17},{9,25},{17,1},{25,9},{2,18},{10... | collective-permute-start | bytes 1769480 | tf_op jit(solution)/shard_map/ppermute | solution.py:359
  21.4 10.7 %collective-permute-start.5 = (f32[6,2,48,128]{3,2,1,0:T(8,128)S(1)}, f32[6,2,48,128]{3,2,1,0:T(8,128)S(1)}, u32[]{:S(2)}, u32[]{:S(2)}) collective-permute-start(f32[6,2,48,128]{3,2,1,0:T(8,128)S(1)} %get-tuple-element.37), channel_id=1, source_target_pairs={{0,8},{8,0},{16,24},{24,16},{1,9},{9,1},{17,25},{25,17},{2,10},{10... | collective-permute-start | bytes 884744 | tf_op jit(solution)/shard_map/ppermute | solution.py:359
  22.9 9.2 %collective-permute-start.6 = (f32[6,2,16,128]{3,2,1,0:T(8,128)S(1)}, f32[6,2,16,128]{3,2,1,0:T(8,128)S(1)}, u32[]{:S(2)}, u32[]{:S(2)}) collective-permute-start(f32[6,2,16,128]{3,2,1,0:T(8,128)S(1)} %get-tuple-element.38), channel_id=1, source_target_pairs={{0,24},{8,16},{16,8},{24,0},{1,25},{9,17},{17,9},{25,1},{2,26},{10... | collective-permute-start | bytes 294920 | tf_op jit(solution)/shard_map/ppermute | solution.py:359

commit v3 on v2

--- a/solution.py
+++ b/solution.py
@@ -12,6 +12,7 @@
 STEPS = 2
 HALO = 8
 PLANES = 5
+REACH = 4
 
 magnetic_coeff = 0.5
 
@@ -120,7 +121,7 @@
 NONE = (None, None)
 
 
-def send_halos(sub, fields, near, far):
+def send_halos(sub, fields, near, far, packed=lambda block: block):
     odd = lax.rem(lax.axis_index(sub), 2) == 1
     e, h, ca, cb = fields
     v1 = scaled(cb, e)
@@ -131,8 +132,8 @@
     up = (h1[0][-1], h1[1][-1], h2[0][-1], h2[1][-1], cb[-1])
     down = (v1[0][0], v1[1][0], v2[0][0], v2[1][0], cb[0])
     for k in range(PLANES):
-        near[k] = jnp.where(odd, down[k], up[k])
-        far[k] = jnp.where(odd, up[k], down[k])
+        near[k] = packed(jnp.where(odd, down[k], up[k]))
+        far[k] = packed(jnp.where(odd, up[k], down[k]))
 
 
 def halo_kernel(spans, sub, table, seeds, material, near, far):
@@ -171,13 +172,13 @@
     )
 
 
-def final_fields(fields, near, far, sub, sub_size):
+def final_fields(fields, near, far, sub, sub_size, unpacked=lambda block: block):
     e, h, ca, cb = fields
     index = lax.axis_index(sub)
     odd = lax.rem(index, 2) == 1
     below, above = index > 0, index < sub_size - 1
-    a = [near[k] for k in range(PLANES)]
-    b = [far[k] for k in range(PLANES)]
+    a = [unpacked(near[k]) for k in range(PLANES)]
+    b = [unpacked(far[k]) for k in range(PLANES)]
     from_below = [jnp.where(odd, a[k], b[k]) for k in range(PLANES)]
     from_above = [jnp.where(above, jnp.where(odd, b[k], a[k]), 0.0) for k in range(PLANES)]
     part_h1x, part_h1y, part_h2x, part_h2y, cb_low = from_below
@@ -225,9 +226,67 @@
     return first, second
 
 
+def bands_packed(block):
+    rows, lanes = block.shape
+    half = rows // 2
+    side = jnp.zeros((8, lanes), block.dtype)
+    lane = lane_of(side.shape)
+    for g in range(rows // 8):
+        piece = block[8 * g : 8 * g + 8]
+        at = 2 * REACH * g
+        low = pltpu.roll(piece, (at - BAND) % lanes, 1)
+        high = pltpu.roll(piece, (at + 2 * REACH - lanes + BAND) % lanes, 1)
+        side = jnp.where((lane >= at) & (lane < at + REACH), low, side)
+        side = jnp.where((lane >= at + REACH) & (lane < at + 2 * REACH), high, side)
+    return jnp.concatenate([y_packed(block[:half], block[half:]), side], axis=0)
+
+
+def bands_unpacked(packed):
+    half, lanes = packed.shape[0] - 8, packed.shape[1]
+    main, side = packed[:half], packed[half:]
+    lane = lane_of(main.shape)
+    middle = (lane >= BAND) & (lane < lanes - BAND)
+    block = jnp.concatenate([jnp.where(middle, 0.0, main), jnp.where(middle, 0.0, middle_out(main))], axis=0)
+    lane = lane_of(side.shape)
+    pieces = []
+    for g in range(2 * half // 8):
+        at = 2 * REACH * g
+        low = pltpu.roll(side, (BAND - at) % lanes, 1)
+        high = pltpu.roll(side, (lanes - BAND - 2 * REACH - at) % lanes, 1)
+        piece = block[8 * g : 8 * g + 8]
+        piece = jnp.where((lane >= BAND) & (lane < BAND + REACH), low, piece)
+        pieces.append(jnp.where((lane >= lanes - BAND - REACH) & (lane < lanes - BAND), high, piece))
+    return jnp.concatenate(pieces, axis=0)
+
+
+def share_kernel(spans, seeds, material, shared):
+    depth = seeds.shape[2]
+    for c in range(6):
+        for p in range(depth):
+            shared[depth * c + p] = bands_packed(joined(seeds, (0, c, p), spans))
+    for p in range(depth):
+        shared[6 * depth + p] = bands_packed(joined(material, (0, p), spans).astype(jnp.float32))
+
+
+def shared_fields(table, shared):
+    depth = shared.shape[0] // 7
+    count = table.shape[0] // 2
+    planes = [bands_unpacked(shared[k]) for k in range(7 * depth)]
+    f = [planes[depth * c : depth * (c + 1)] for c in range(7)]
+    rows = [table[m : m + 1] for m in range(2 * count)]
+    return prepared(f[:3], f[3:6], f[6], (rows[:count], rows[count:]))
+
+
+def shared_halo_kernel(sub, table, shared, near, far):
+    send_halos(sub, shared_fields(table, shared), near, far, bands_packed)
+
+
 def weighted_planes(seeds, material, table, near, far, spans, keeps, sub, sub_size):
     planes = final_fields(loaded(seeds, material, table, spans), near, far, sub, sub_size)
-    size_x, size_y = seeds.shape[3:]
+    return weighted(planes, spans, keeps, *seeds.shape[3:])
+
+
+def weighted(planes, spans, keeps, size_x, size_y):
     at, results = 0, []
     for (lo, hi), (start, stop) in zip(spans, keeps):
         shape = (stop - start, size_y)
@@ -238,9 +297,12 @@
     return results
 
 
-def edge_kernel(spans, sub, sub_size, tile, table, seeds, material, near, far, edge, corner, strip):
-    size_x = seeds.shape[3]
-    keeps = ((0, BAND), (size_x - BAND, size_x))
+def edge_keeps(size_x):
+    return ((0, BAND), (size_x - BAND, size_x))
+
+
+def edge_kernel(spans, sub, sub_size, tile, table, seeds, material, near, far, edge, strip):
+    keeps = edge_keeps(seeds.shape[3])
     low, high = weighted_planes(seeds, material, table, near, far, spans, keeps, sub, sub_size)
     odd = lax.rem(lax.axis_index(tile), 2) == 1
     half = BAND // 2
@@ -248,7 +310,6 @@
         for p in range(seeds.shape[2]):
             edge[c, p, :BAND] = low[c][p]
             edge[c, p, BAND:] = high[c][p]
-            corner[c, p] = y_packed(low[c][p], high[c][p])
             away = jnp.where(odd, high[c][p], low[c][p])
             strip[c, p] = y_packed(middle_out(away[:half]), middle_out(away[half:]))
 
@@ -271,14 +332,23 @@
             out[c, p] = planes[c][p]
 
 
-def corner_kernel(tile, edge, corner, summed, send):
+def y_swapped(block):
+    lane = lane_of(block.shape)
+    lanes = block.shape[1]
+    a, b = pltpu.roll(block, BAND, 1), pltpu.roll(block, lanes - BAND, 1)
+    middle = (lane >= BAND) & (lane < lanes - BAND)
+    return jnp.where(middle, 0.0, jnp.where(lane < BAND, a, b))
+
+
+def corner_kernel(spans, size_x, sub, sub_size, tile, table, shared, near, far, edge, summed, send):
+    planes = final_fields(shared_fields(table, shared), near, far, sub, sub_size, bands_unpacked)
+    low_part, high_part = weighted(planes, spans, edge_keeps(size_x), size_x, edge.shape[3])
     odd = lax.rem(lax.axis_index(tile), 2) == 1
     half = BAND // 2
     for c in range(edge.shape[0]):
         for p in range(edge.shape[1]):
-            first, second = y_unpacked(corner[c, p])
-            low = edge[c, p, :BAND] + first
-            high = edge[c, p, BAND:] + second
+            low = edge[c, p, :BAND] + y_swapped(low_part[c][p])
+            high = edge[c, p, BAND:] + y_swapped(high_part[c][p])
             summed[c, p, :BAND] = low
             summed[c, p, BAND:] = high
             by, away = jnp.where(odd, low, high), jnp.where(odd, high, low)
@@ -373,49 +443,57 @@
     edges = ((0, BAND + HALO), (size_x - BAND - HALO, size_x))
     inner = ((BAND - HALO, size_x - BAND + HALO),)
     rows = size_x - 2 * BAND
-    count = sum(hi - lo for lo, hi in edges)
-
-    shape = jax.ShapeDtypeStruct((PLANES, count, size_y), jnp.float32)
+    edge_rows, inner_rows = 2 * (BAND + HALO), rows + 2 * HALO
+    packed_rows = edge_rows // 2 + 8
+
+    shape = jax.ShapeDtypeStruct((PLANES, inner_rows, size_y), jnp.float32)
     near, far = pl.pallas_call(
-        functools.partial(first_halo_kernel, edges, "sub"),
+        functools.partial(first_halo_kernel, inner, "sub"),
         out_shape=[shape, shape],
         in_specs=[HBM] * 4,
         out_specs=[VMEM] * 2,
         scratch_shapes=[
-            pltpu.VMEM((6, depth, count, size_y), jnp.float32),
-            pltpu.VMEM((depth, count, size_y), jnp.int32),
+            pltpu.VMEM((6, depth, inner_rows, size_y), jnp.float32),
+            pltpu.VMEM((depth, inner_rows, size_y), jnp.int32),
             pltpu.SMEM((2, *decay.shape), jnp.float32),
-            pltpu.SemaphoreType.DMA((2 + 2 * len(edges),)),
+            pltpu.SemaphoreType.DMA((2 + 2 * len(inner),)),
         ],
         compiler_params=PARAMS,
     )(*(pltpu.with_memory_space_constraint(x, pltpu.HBM) for x in (decay, coupling, seeds, material)))
-    table = table_rows(decay, coupling, size_y)
+    near, seeds, material = after(near, seeds, material)
+    inner_near, inner_far = depth_exchange(near, far, sub_size, tile_size)
+    shared, = called(
+        functools.partial(share_kernel, edges), [(7 * depth, packed_rows, size_y)], seeds, material
+    )
+    shared = swapped(shared, 2, tile_size)
+
+    inner_near, table = after(inner_near, table_rows(decay, coupling, size_y))
+    shape = (PLANES, edge_rows, size_y)
+    near, far = called(functools.partial(halo_kernel, edges, "sub"), [shape, shape], table, seeds, material)
+    inner_far, near, far = after(inner_far, near, far)
     edge_near, edge_far = depth_exchange(near, far, sub_size, tile_size)
-    edge_near, table = after(edge_near, table)
-
-    shape = (PLANES, rows + 2 * HALO, size_y)
-    near, far = called(functools.partial(halo_kernel, inner, "sub"), [shape, shape], table, seeds, material)
-    edge_far, near, far = after(edge_far, near, far)
-    inner_near, inner_far = depth_exchange(near, far, sub_size, tile_size)
-
-    edge, corner, strip = called(
-        functools.partial(edge_kernel, edges, "sub", sub_size, "tile"),
-        [(6, depth, 2 * BAND, size_y), (6, depth, BAND, size_y), (6, depth, BAND // 2, size_y)],
-        table, seeds, material, edge_near, edge_far,
-    )
-    corner = swapped(corner, 2, tile_size)
-    strip = swapped(strip, 3, tile_size)
+
     mid, bands = called(
         functools.partial(middle_kernel, inner, "sub", sub_size),
         [(6, depth, rows, size_y), (6, depth, rows // 2, size_y)],
         table, seeds, material, inner_near, inner_far,
     )
-    corner, bands = after(corner, bands)
     bands = swapped(bands, 2, tile_size)
+
+    shape = (PLANES, packed_rows, size_y)
+    near, far = called(functools.partial(shared_halo_kernel, "sub"), [shape, shape], table, shared)
+    near, far = depth_exchange(near, far, sub_size, tile_size)
+
+    edge, strip = called(
+        functools.partial(edge_kernel, edges, "sub", sub_size, "tile"),
+        [(6, depth, 2 * BAND, size_y), (6, depth, BAND // 2, size_y)],
+        table, seeds, material, edge_near, edge_far,
+    )
+    strip = swapped(strip, 3, tile_size)
     summed, send = called(
-        functools.partial(corner_kernel, "tile"),
+        functools.partial(corner_kernel, edges, size_x, "sub", sub_size, "tile"),
         [(6, depth, 2 * BAND, size_y), (6, depth, BAND + BAND // 2, size_y)],
-        edge, corner,
+        table, shared, near, far, edge,
     )
     got = swapped(send, 1, tile_size)
     edge, = called(

time: 38.3 us -> 37.7 us (0.984)
  waiting for transfers between devices: 21.8 us -> 16.7 us
  Pallas kernels: 5.68 us -> 8.66 us
  starting transfers between devices: 10.5 us -> 11.9 us
    ppermute x4, waiting for transfers between devices: 13.7 us -> 9.15 us  [swapped(): lax.ppermute(value, 'tile', [(t, t ^ bits) for t in range(tile_size)])]
    pallas_call x5 -> x7, Pallas kernels: 2.87 us -> 5.36 us  [called(): pl.pallas_call(kernel, out_shape=outs, in_specs=[VMEM] * len(operands), o...]
    ppermute x2 -> x3, starting transfers between devices: 4.58 us -> 5.55 us  [depth_exchange(): far = lax.ppermute(far, ('tile', 'sub'), pairs)]
    pallas_call x1, Pallas kernels: 1.51 us -> 1.99 us  [two_by_two(): pl.pallas_call(functools.partial(first_halo_kernel, inner, 'sub'), out_sh...]
    ppermute x4, starting transfers between devices: 5.26 us -> 5.72 us  [swapped(): lax.ppermute(value, 'tile', [(t, t ^ bits) for t in range(tile_size)])]
    ppermute x2 -> x3, waiting for transfers between devices: 8.04 us -> 7.58 us  [depth_exchange(): far = lax.ppermute(far, ('tile', 'sub'), pairs)]
  transfers between devices with their start and end apart: 8 -> 10, of which waited for: 4 -> 4; matrix products, arithmetic and copies ran while one was open for 0% -> 0% of each run, Pallas kernels for 8% -> 14%
where the time goes in v3:
time: 37.7 us; the launch traced here: 37.6 us
  waiting for transfers between devices  16.7 us (44%)
  starting transfers between devices  11.9 us (32%)
  Pallas kernels  8.66 us (23%)
    ppermute x4, waiting for transfers between devices, swapped(): lax.ppermute(value, 'tile', [(t, t ^ bits) for t in range(tile_size)])  9.15 us
    ppermute x3, waiting for transfers between devices, depth_exchange(): far = lax.ppermute(far, ('tile', 'sub'), pairs)  7.58 us
    ppermute x4, starting transfers between devices, swapped(): lax.ppermute(value, 'tile', [(t, t ^ bits) for t in range(tile_size)])  5.72 us
    ppermute x3, starting transfers between devices, depth_exchange(): far = lax.ppermute(far, ('tile', 'sub'), pairs)  5.55 us
    pallas_call x7, Pallas kernels, called(): pl.pallas_call(kernel, out_shape=outs, in_specs=[VMEM] * len(operands), o...  5.36 us
    pallas_call x1, Pallas kernels, two_by_two(): pl.pallas_call(functools.partial(first_halo_kernel, inner, 'sub'), out_sh...  1.99 us
    pallas_call x1, Pallas kernels, two_by_two(): pl.pallas_call(last_kernel, out_shape=jax.ShapeDtypeStruct(seeds.shape, j...  1.31 us
  transfers between devices with their start and end apart: 10, of which 4 were waited for; matrix products, arithmetic and copies ran while one was open for 0% of the time, Pallas kernels for 14%

profile of v3, /device:TPU:0, one launch (start us, length us, event | category | flops | bytes accessed | tf_op | source)
XLA Modules:
  0.0 37.6 jit_solution(6855385522886809603)
XLA Ops:
  0.0 2.0 %shard_map.46 = (f32[5,208,128]{2,1,0:T(8,128)S(1)}, f32[5,208,128]{2,1,0:T(8,128)S(1)}) custom-call(f32[4]{0:T(128)} %decay.1, f32[4]{0:T(128)} %coupling.1, f32[1,6,2,256,128]{4,3,2,1,0:T(8,128)} %seeds.5, s32[1,2,256,128]{3,2,1,0:T(8,128)} %material.5), custom_call_target="tpu_custom_call" | custom-call | tf_op jit(solution)/shard_map/pallas_call | solution.py:450
  2.0 0.5 %collective-permute-start = (f32[5,208,128]{2,1,0:T(8,128)S(1)}, f32[5,208,128]{2,1,0:T(8,128)S(1)}, u32[]{:S(2)}, u32[]{:S(2)}) collective-permute-start(f32[5,208,128]{2,1,0:T(8,128)S(1)} %get-tuple-element.26), channel_id=1, source_target_pairs={{0,1},{1,0},{2,3},{3,2},{4,5},{5,4},{6,7},{7,6},{8,9},{9,8},{10,11... | collective-permute-start | bytes 1597448 | tf_op jit(solution)/shard_map/ppermute | solution.py:414
  2.5 2.6 %collective-permute-start.4 = (f32[5,208,128]{2,1,0:T(8,128)S(1)}, f32[5,208,128]{2,1,0:T(8,128)S(1)}, u32[]{:S(2)}, u32[]{:S(2)}) collective-permute-start(f32[5,208,128]{2,1,0:T(8,128)S(1)} %get-tuple-element.32), channel_id=1, source_target_pairs={{0,8},{1,2},{2,1},{3,4},{4,3},{5,6},{6,5},{7,15},{8,0},{9,10},{10,... | collective-permute-start | bytes 1597448 | tf_op jit(solution)/shard_map/ppermute | solution.py:424
  5.1 0.0 copy-done.1
  5.1 0.4 %shard_map.47 = f32[14,48,128]{2,1,0:T(8,128)S(1)} custom-call(f32[1,6,2,256,128]{4,3,2,1,0:T(8,128)S(1)} %copy-done, s32[1,2,256,128]{3,2,1,0:T(8,128)S(1)} %copy-done.1), custom_call_target="tpu_custom_call" | custom-call | tf_op jit(solution)/shard_map/pallas_call | solution.py:400
  5.5 1.6 %collective-permute-start.1 = (f32[14,48,128]{2,1,0:T(8,128)S(1)}, f32[14,48,128]{2,1,0:T(8,128)S(1)}, u32[]{:S(2)}, u32[]{:S(2)}) collective-permute-start(f32[14,48,128]{2,1,0:T(8,128)S(1)} %shard_map.47), channel_id=1, source_target_pairs={{0,16},{8,24},{16,0},{24,8},{1,17},{9,25},{17,1},{25,9},{2,18},{10... | collective-permute-start | bytes 1032200 | tf_op jit(solution)/shard_map/ppermute | solution.py:429
  7.1 0.1 pad_maximum_fusion
  7.2 0.0 collective-permute-done.near
  7.2 0.1 broadcast_in_dim.2.table
  7.3 0.3 shard_map.49
  7.5 4.8 %collective-permute-done.4.far = f32[5,208,128]{2,1,0:T(8,128)S(1)} collective-permute-done((f32[5,208,128]{2,1,0:T(8,128)S(1)}, f32[5,208,128]{2,1,0:T(8,128)S(1)}, u32[]{:S(2)}, u32[]{:S(2)}) %collective-permute-start.4) | collective-permute-done | bytes 532512 | tf_op jit(solution)/shard_map/ppermute | solution.py:424
  12.4 1.3 %shard_map.53 = (f32[6,2,192,128]{3,2,1,0:T(8,128)S(1)}, f32[6,2,96,128]{3,2,1,0:T(8,128)S(1)}) custom-call(f32[8,128]{1,0:T(8,128)S(1)} %broadcast_in_dim.2.table, f32[1,6,2,256,128]{4,3,2,1,0:T(8,128)S(1)} %copy-done, s32[1,2,256,128]{3,2,1,0:T(8,128)S(1)} %copy-done.1, f32[5,208,128]{2,1,0:T(8,128)S(1)} %collective-permute-done.near, ...), custom_call_target="tpu_custom_call" | custom-call | tf_op jit(solution)/shard_map/pallas_call | solution.py:400
  13.6 2.1 %collective-permute-start.9 = (f32[6,2,96,128]{3,2,1,0:T(8,128)S(1)}, f32[6,2,96,128]{3,2,1,0:T(8,128)S(1)}, u32[]{:S(2)}, u32[]{:S(2)}) collective-permute-start(f32[6,2,96,128]{3,2,1,0:T(8,128)S(1)} %get-tuple-element.44), channel_id=1, source_target_pairs={{0,16},{8,24},{16,0},{24,8},{1,17},{9,25},{17,1},{25,9},{2,18},{10... | collective-permute-start | bytes 1769480 | tf_op jit(solution)/shard_map/ppermute | solution.py:429
  15.8 0.0 collective-permute-start.5
  15.8 1.5 %collective-permute-start.6 = (f32[5,80,128]{2,1,0:T(8,128)S(1)}, f32[5,80,128]{2,1,0:T(8,128)S(1)}, u32[]{:S(2)}, u32[]{:S(2)}) collective-permute-start(f32[5,80,128]{2,1,0:T(8,128)S(1)} %get-tuple-element.36), channel_id=1, source_target_pairs={{0,8},{1,2},{2,1},{3,4},{4,3},{5,6},{6,5},{7,15},{8,0},{9,10},{10,... | collective-permute-start | bytes 614408 | tf_op jit(solution)/shard_map/ppermute | solution.py:424
  17.2 0.0 collective-permute-done.1.shared
  17.2 0.9 %shard_map.48 = (f32[5,48,128]{2,1,0:T(8,128)S(1)}, f32[5,48,128]{2,1,0:T(8,128)S(1)}) custom-call(f32[8,128]{1,0:T(8,128)S(1)} %broadcast_in_dim.2.table, f32[14,48,128]{2,1,0:T(8,128)S(1)} %collective-permute-done.1.shared), custom_call_target="tpu_custom_call" | custom-call | tf_op jit(solution)/shard_map/pallas_call | solution.py:400
  18.1 0.1 collective-permute-start.2
  18.3 1.5 %collective-permute-start.3 = (f32[5,48,128]{2,1,0:T(8,128)S(1)}, f32[5,48,128]{2,1,0:T(8,128)S(1)}, u32[]{:S(2)}, u32[]{:S(2)}) collective-permute-start(f32[5,48,128]{2,1,0:T(8,128)S(1)} %get-tuple-element.31), channel_id=1, source_target_pairs={{0,8},{1,2},{2,1},{3,4},{4,3},{5,6},{6,5},{7,15},{8,0},{9,10},{10,... | collective-permute-start | bytes 368648 | tf_op jit(solution)/shard_map/ppermute | solution.py:424
  19.8 0.0 collective-permute-done.5.near
  19.8 1.7 %collective-permute-done.6.far = f32[5,80,128]{2,1,0:T(8,128)S(1)} collective-permute-done((f32[5,80,128]{2,1,0:T(8,128)S(1)}, f32[5,80,128]{2,1,0:T(8,128)S(1)}, u32[]{:S(2)}, u32[]{:S(2)}) %collective-permute-start.6) | collective-permute-done | bytes 204832 | tf_op jit(solution)/shard_map/ppermute | solution.py:424
  21.5 0.6 %shard_map.50 = (f32[6,2,64,128]{3,2,1,0:T(8,128)S(1)}, f32[6,2,16,128]{3,2,1,0:T(8,128)S(1)}) custom-call(f32[8,128]{1,0:T(8,128)S(1)} %broadcast_in_dim.2.table, f32[1,6,2,256,128]{4,3,2,1,0:T(8,128)S(1)} %copy-done, s32[1,2,256,128]{3,2,1,0:T(8,128)S(1)} %copy-done.1, f32[5,80,128]{2,1,0:T(8,128)S(1)} %collective-permute-done.5.near, ...), custom_call_target="tpu_custom_call" | custom-call | tf_op jit(solution)/shard_map/pallas_call | solution.py:400
  22.1 0.0 collective-permute-done.2.near
  22.1 1.0 %collective-permute-done.3.far = f32[5,48,128]{2,1,0:T(8,128)S(1)} collective-permute-done((f32[5,48,128]{2,1,0:T(8,128)S(1)}, f32[5,48,128]{2,1,0:T(8,128)S(1)}, u32[]{:S(2)}, u32[]{:S(2)}) %collective-permute-start.3) | collective-permute-done | bytes 122912 | tf_op jit(solution)/shard_map/ppermute | solution.py:424
  23.2 1.8 %shard_map.51 = (f32[6,2,64,128]{3,2,1,0:T(8,128)S(1)}, f32[6,2,48,128]{3,2,1,0:T(8,128)S(1)}) custom-call(f32[8,128]{1,0:T(8,128)S(1)} %broadcast_in_dim.2.table, f32[14,48,128]{2,1,0:T(8,128)S(1)} %collective-permute-done.1.shared, f32[5,48,128]{2,1,0:T(8,128)S(1)} %collective-permute-done.2.near, f32[5,48,128]{2,1,0:T(8,128)S(1)} %collective-permute-done.3.far, ...), custom_call_target="tpu_custom_call" | custom-call | tf_op jit(solution)/shard_map/pallas_call | solution.py:400
  24.9 1.5 %collective-permute-start.7 = (f32[6,2,48,128]{3,2,1,0:T(8,128)S(1)}, f32[6,2,48,128]{3,2,1,0:T(8,128)S(1)}, u32[]{:S(2)}, u32[]{:S(2)}) collective-permute-start(f32[6,2,48,128]{3,2,1,0:T(8,128)S(1)} %get-tuple-element.39), channel_id=1, source_target_pairs={{0,8},{8,0},{16,24},{24,16},{1,9},{9,1},{17,25},{25,17},{2,10},{10... | collective-permute-start | bytes 884744 | tf_op jit(solution)/shard_map/ppermute | solution.py:429
  26.5 0.5 %collective-permute-start.8 = (f32[6,2,16,128]{3,2,1,0:T(8,128)S(1)}, f32[6,2,16,128]{3,2,1,0:T(8,128)S(1)}, u32[]{:S(2)}, u32[]{:S(2)}) collective-permute-start(f32[6,2,16,128]{3,2,1,0:T(8,128)S(1)} %get-tuple-element.40), channel_id=1, source_target_pairs={{0,24},{8,16},{16,8},{24,0},{1,25},{9,17},{17,9},{25,1},{2,26},{10... | collective-permute-start | bytes 294920 | tf_op jit(solution)/shard_map/ppermute | solution.py:429
  27.0 9.1 %collective-permute-done.8.strip = f32[6,2,16,128]{3,2,1,0:T(8,128)S(1)} collective-permute-done((f32[6,2,16,128]{3,2,1,0:T(8,128)S(1)}, f32[6,2,16,128]{3,2,1,0:T(8,128)S(1)}, u32[]{:S(2)}, u32[]{:S(2)}) %collective-permute-start.8) | collective-permute-done | bytes 98336 | tf_op jit(solution)/shard_map/ppermute | solution.py:429
  36.1 0.0 collective-permute-done.7.got
  36.1 0.1 shard_map.52.edge
  36.3 0.0 collective-permute-done.9.bands
  36.3 1.3 %shard_map.54 = f32[1,6,2,256,128]{4,3,2,1,0:T(8,128)} custom-call(f32[6,2,64,128]{3,2,1,0:T(8,128)S(1)} %shard_map.52.edge, f32[6,2,192,128]{3,2,1,0:T(8,128)S(1)} %get-tuple-element.43.mid, f32[6,2,96,128]{3,2,1,0:T(8,128)S(1)} %collective-permute-done.9.bands), custom_call_target="tpu_custom_call" | custom-call | tf_op jit(solution)/shard_map/pallas_call | solution.py:502
  (7 shorter events, 0.0 us)
Async XLA Ops:
  0.0 7.1 %copy-start.2 = (f32[4]{0:T(128)S(1)}, f32[4]{0:T(128)}, u32[]{:S(2)}) copy-start(f32[4]{0:T(128)} %coupling.1) | copy-start | bytes 52
  0.0 7.1 %copy-start.3 = (f32[4]{0:T(128)S(1)}, f32[4]{0:T(128)}, u32[]{:S(2)}) copy-start(f32[4]{0:T(128)} %decay.1) | copy-start | bytes 52
  0.0 5.1 %copy-start.1 = (s32[1,2,256,128]{3,2,1,0:T(8,128)S(1)}, s32[1,2,256,128]{3,2,1,0:T(8,128)}, u32[]{:S(2)}) copy-start(s32[1,2,256,128]{3,2,1,0:T(8,128)} %material.5) | copy-start | bytes 786436
  0.0 5.1 %copy-start = (f32[1,6,2,256,128]{4,3,2,1,0:T(8,128)S(1)}, f32[1,6,2,256,128]{4,3,2,1,0:T(8,128)}, u32[]{:S(2)}) copy-start(f32[1,6,2,256,128]{4,3,2,1,0:T(8,128)} %seeds.5) | copy-start | bytes 4718596
  2.0 5.2 %collective-permute-start = (f32[5,208,128]{2,1,0:T(8,128)S(1)}, f32[5,208,128]{2,1,0:T(8,128)S(1)}, u32[]{:S(2)}, u32[]{:S(2)}) collective-permute-start(f32[5,208,128]{2,1,0:T(8,128)S(1)} %get-tuple-element.26), channel_id=1, source_target_pairs={{0,1},{1,0},{2,3},{3,2},{4,5},{5,4},{6,7},{7,6},{8,9},{9,8},{10,11... | collective-permute-start | bytes 1597448 | tf_op jit(solution)/shard_map/ppermute | solution.py:414
  2.5 9.8 %collective-permute-start.4 = (f32[5,208,128]{2,1,0:T(8,128)S(1)}, f32[5,208,128]{2,1,0:T(8,128)S(1)}, u32[]{:S(2)}, u32[]{:S(2)}) collective-permute-start(f32[5,208,128]{2,1,0:T(8,128)S(1)} %get-tuple-element.32), channel_id=1, source_target_pairs={{0,8},{1,2},{2,1},{3,4},{4,3},{5,6},{6,5},{7,15},{8,0},{9,10},{10,... | collective-permute-start | bytes 1597448 | tf_op jit(solution)/shard_map/ppermute | solution.py:424
  5.5 11.7 %collective-permute-start.1 = (f32[14,48,128]{2,1,0:T(8,128)S(1)}, f32[14,48,128]{2,1,0:T(8,128)S(1)}, u32[]{:S(2)}, u32[]{:S(2)}) collective-permute-start(f32[14,48,128]{2,1,0:T(8,128)S(1)} %shard_map.47), channel_id=1, source_target_pairs={{0,16},{8,24},{16,0},{24,8},{1,17},{9,25},{17,1},{25,9},{2,18},{10... | collective-permute-start | bytes 1032200 | tf_op jit(solution)/shard_map/ppermute | solution.py:429
  13.6 22.6 %collective-permute-start.9 = (f32[6,2,96,128]{3,2,1,0:T(8,128)S(1)}, f32[6,2,96,128]{3,2,1,0:T(8,128)S(1)}, u32[]{:S(2)}, u32[]{:S(2)}) collective-permute-start(f32[6,2,96,128]{3,2,1,0:T(8,128)S(1)} %get-tuple-element.44), channel_id=1, source_target_pairs={{0,16},{8,24},{16,0},{24,8},{1,17},{9,25},{17,1},{25,9},{2,18},{10... | collective-permute-start | bytes 1769480 | tf_op jit(solution)/shard_map/ppermute | solution.py:429
  15.8 4.0 %collective-permute-start.5 = (f32[5,80,128]{2,1,0:T(8,128)S(1)}, f32[5,80,128]{2,1,0:T(8,128)S(1)}, u32[]{:S(2)}, u32[]{:S(2)}) collective-permute-start(f32[5,80,128]{2,1,0:T(8,128)S(1)} %get-tuple-element.35), channel_id=1, source_target_pairs={{0,1},{1,0},{2,3},{3,2},{4,5},{5,4},{6,7},{7,6},{8,9},{9,8},{10,11... | collective-permute-start | bytes 614408 | tf_op jit(solution)/shard_map/ppermute | solution.py:414
  15.8 5.8 %collective-permute-start.6 = (f32[5,80,128]{2,1,0:T(8,128)S(1)}, f32[5,80,128]{2,1,0:T(8,128)S(1)}, u32[]{:S(2)}, u32[]{:S(2)}) collective-permute-start(f32[5,80,128]{2,1,0:T(8,128)S(1)} %get-tuple-element.36), channel_id=1, source_target_pairs={{0,8},{1,2},{2,1},{3,4},{4,3},{5,6},{6,5},{7,15},{8,0},{9,10},{10,... | collective-permute-start | bytes 614408 | tf_op jit(solution)/shard_map/ppermute | solution.py:424
  18.1 4.0 %collective-permute-start.2 = (f32[5,48,128]{2,1,0:T(8,128)S(1)}, f32[5,48,128]{2,1,0:T(8,128)S(1)}, u32[]{:S(2)}, u32[]{:S(2)}) collective-permute-start(f32[5,48,128]{2,1,0:T(8,128)S(1)} %get-tuple-element.30), channel_id=1, source_target_pairs={{0,1},{1,0},{2,3},{3,2},{4,5},{5,4},{6,7},{7,6},{8,9},{9,8},{10,11... | collective-permute-start | bytes 368648 | tf_op jit(solution)/shard_map/ppermute | solution.py:414
  18.3 4.9 %collective-permute-start.3 = (f32[5,48,128]{2,1,0:T(8,128)S(1)}, f32[5,48,128]{2,1,0:T(8,128)S(1)}, u32[]{:S(2)}, u32[]{:S(2)}) collective-permute-start(f32[5,48,128]{2,1,0:T(8,128)S(1)} %get-tuple-element.31), channel_id=1, source_target_pairs={{0,8},{1,2},{2,1},{3,4},{4,3},{5,6},{6,5},{7,15},{8,0},{9,10},{10,... | collective-permute-start | bytes 368648 | tf_op jit(solution)/shard_map/ppermute | solution.py:424
  24.9 11.2 %collective-permute-start.7 = (f32[6,2,48,128]{3,2,1,0:T(8,128)S(1)}, f32[6,2,48,128]{3,2,1,0:T(8,128)S(1)}, u32[]{:S(2)}, u32[]{:S(2)}) collective-permute-start(f32[6,2,48,128]{3,2,1,0:T(8,128)S(1)} %get-tuple-element.39), channel_id=1, source_target_pairs={{0,8},{8,0},{16,24},{24,16},{1,9},{9,1},{17,25},{25,17},{2,10},{10... | collective-permute-start | bytes 884744 | tf_op jit(solution)/shard_map/ppermute | solution.py:429
  26.5 9.6 %collective-permute-start.8 = (f32[6,2,16,128]{3,2,1,0:T(8,128)S(1)}, f32[6,2,16,128]{3,2,1,0:T(8,128)S(1)}, u32[]{:S(2)}, u32[]{:S(2)}) collective-permute-start(f32[6,2,16,128]{3,2,1,0:T(8,128)S(1)} %get-tuple-element.40), channel_id=1, source_target_pairs={{0,24},{8,16},{16,8},{24,0},{1,25},{9,17},{17,9},{25,1},{2,26},{10... | collective-permute-start | bytes 294920 | tf_op jit(solution)/shard_map/ppermute | solution.py:429

commit v4 on v2

--- a/solution.py
+++ b/solution.py
@@ -12,6 +12,9 @@
 STEPS = 2
 HALO = 8
 PLANES = 5
+REACH = 4
+SHARED = 64
+LARGE, SMALL = 10**10, 6 * 10**8
 
 magnetic_coeff = 0.5
 
@@ -107,20 +110,27 @@
     return e, h, ca, cb
 
 
-def loaded(seeds, material, table, spans):
+def raw(seeds, material, spans):
     depth = seeds.shape[2]
-    count = table.shape[0] // 2
     e = [[joined(seeds, (0, c, p), spans) for p in range(depth)] for c in range(3)]
     h = [[joined(seeds, (0, 3 + c, p), spans) for p in range(depth)] for c in range(3)]
-    labels = [joined(material, (0, p), spans) for p in range(depth)]
+    return e, h, [joined(material, (0, p), spans) for p in range(depth)]
+
+
+def table_entries(table):
+    count = table.shape[0] // 2
     rows = [table[m : m + 1] for m in range(2 * count)]
-    return prepared(e, h, labels, (rows[:count], rows[count:]))
+    return rows[:count], rows[count:]
+
+
+def loaded(seeds, material, table, spans):
+    return prepared(*raw(seeds, material, spans), table_entries(table))
 
 
 NONE = (None, None)
 
 
-def send_halos(sub, fields, near, far):
+def send_halos(sub, fields, near, far, packed=lambda block: block):
     odd = lax.rem(lax.axis_index(sub), 2) == 1
     e, h, ca, cb = fields
     v1 = scaled(cb, e)
@@ -131,35 +141,12 @@
     up = (h1[0][-1], h1[1][-1], h2[0][-1], h2[1][-1], cb[-1])
     down = (v1[0][0], v1[1][0], v2[0][0], v2[1][0], cb[0])
     for k in range(PLANES):
-        near[k] = jnp.where(odd, down[k], up[k])
-        far[k] = jnp.where(odd, up[k], down[k])
+        near[k] = packed(jnp.where(odd, down[k], up[k]))
+        far[k] = packed(jnp.where(odd, up[k], down[k]))
 
 
 def halo_kernel(spans, sub, table, seeds, material, near, far):
     send_halos(sub, loaded(seeds, material, table, spans), near, far)
-
-
-def first_halo_kernel(spans, sub, decay, coupling, seeds, material, near, far, held, labels, tables, sems):
-    copies = [
-        pltpu.make_async_copy(decay, tables.at[0], sems.at[0]),
-        pltpu.make_async_copy(coupling, tables.at[1], sems.at[1]),
-    ]
-    at = 0
-    for lo, hi in spans:
-        rows, here = pl.ds(lo, hi - lo), pl.ds(at, hi - lo)
-        copies.append(pltpu.make_async_copy(seeds.at[0, :, :, rows], held.at[:, :, here], sems.at[len(copies)]))
-        copies.append(pltpu.make_async_copy(material.at[0, :, rows], labels.at[:, here], sems.at[len(copies)]))
-        at += hi - lo
-    for copy in copies:
-        copy.start()
-    for copy in copies:
-        copy.wait()
-    depth = held.shape[1]
-    e = [[held[c, p] for p in range(depth)] for c in range(3)]
-    h = [[held[3 + c, p] for p in range(depth)] for c in range(3)]
-    entries = [[tables[k, m] for m in range(tables.shape[1])] for k in range(2)]
-    fields = prepared(e, h, [labels[p] for p in range(depth)], entries)
-    send_halos(sub, fields, near, far)
 
 
 def ramp(position, count):
@@ -171,13 +158,13 @@
     )
 
 
-def final_fields(fields, near, far, sub, sub_size):
+def final_fields(fields, near, far, sub, sub_size, unpacked=lambda block: block):
     e, h, ca, cb = fields
     index = lax.axis_index(sub)
     odd = lax.rem(index, 2) == 1
     below, above = index > 0, index < sub_size - 1
-    a = [near[k] for k in range(PLANES)]
-    b = [far[k] for k in range(PLANES)]
+    a = [unpacked(near[k]) for k in range(PLANES)]
+    b = [unpacked(far[k]) for k in range(PLANES)]
     from_below = [jnp.where(odd, a[k], b[k]) for k in range(PLANES)]
     from_above = [jnp.where(above, jnp.where(odd, b[k], a[k]), 0.0) for k in range(PLANES)]
     part_h1x, part_h1y, part_h2x, part_h2y, cb_low = from_below
@@ -225,9 +212,77 @@
     return first, second
 
 
+def bands_packed(block):
+    rows, lanes = block.shape
+    half = rows // 2
+    lane = lane_of((8, lanes))
+    side = jnp.zeros((8, lanes), block.dtype)
+    for g in range(rows // 8):
+        piece = pltpu.roll(block[8 * g : 8 * g + 8], (REACH * g - BAND) % lanes, 1)
+        side = jnp.where(side_lanes(lane, g, lanes), piece, side)
+    return jnp.concatenate([y_packed(block[:half], block[half:]), side], axis=0)
+
+
+def side_lanes(lane, g, lanes):
+    low, high = REACH * g, REACH * g + lanes - 2 * BAND - REACH
+    return ((lane >= low) & (lane < low + REACH)) | ((lane >= high) & (lane < high + REACH))
+
+
+def bands_unpacked(packed):
+    half, lanes = packed.shape[0] - 8, packed.shape[1]
+    main, side = packed[:half], packed[half:]
+    lane = lane_of(main.shape)
+    middle = (lane >= BAND) & (lane < lanes - BAND)
+    block = jnp.concatenate([jnp.where(middle, 0.0, main), jnp.where(middle, 0.0, middle_out(main))], axis=0)
+    lane = lane_of(side.shape)
+    beside = ((lane >= BAND) & (lane < BAND + REACH)) | ((lane >= lanes - BAND - REACH) & (lane < lanes - BAND))
+    pieces = []
+    for g in range(2 * half // 8):
+        moved = pltpu.roll(side, (BAND - REACH * g) % lanes, 1)
+        pieces.append(jnp.where(beside, moved, block[8 * g : 8 * g + 8]))
+    return jnp.concatenate(pieces, axis=0)
+
+
+def first_kernel(edges, inner, span, sub, decay, coupling, seeds, material, *rest):
+    near_edge, far_edge, near, far, shared, held, labels, tables, sems = rest
+    copies = [
+        pltpu.make_async_copy(seeds.at[0], held.at[0], sems.at[0]),
+        pltpu.make_async_copy(material, labels, sems.at[1]),
+        pltpu.make_async_copy(decay, tables.at[0], sems.at[2]),
+        pltpu.make_async_copy(coupling, tables.at[1], sems.at[3]),
+    ]
+    for copy in copies:
+        copy.start()
+    for copy in copies:
+        copy.wait()
+    depth = held.shape[2]
+    for c in range(6):
+        for p in range(depth):
+            shared[depth * c + p] = bands_packed(joined(held, (0, c, p), (span,)))
+    for p in range(depth):
+        shared[6 * depth + p] = bands_packed(joined(labels, (0, p), (span,)).astype(jnp.float32))
+    entries = [[tables[k, m] for m in range(tables.shape[1])] for k in range(2)]
+    send_halos(sub, prepared(*raw(held, labels, edges), entries), near_edge, far_edge)
+    send_halos(sub, prepared(*raw(held, labels, inner), entries), near, far)
+
+
+def shared_fields(table, shared):
+    depth = shared.shape[0] // 7
+    planes = [bands_unpacked(shared[k]) for k in range(7 * depth)]
+    f = [planes[depth * c : depth * (c + 1)] for c in range(7)]
+    return prepared(f[:3], f[3:6], f[6], table_entries(table))
+
+
+def shared_halo_kernel(sub, table, shared, near, far):
+    send_halos(sub, shared_fields(table, shared), near, far, bands_packed)
+
+
 def weighted_planes(seeds, material, table, near, far, spans, keeps, sub, sub_size):
     planes = final_fields(loaded(seeds, material, table, spans), near, far, sub, sub_size)
-    size_x, size_y = seeds.shape[3:]
+    return weighted(planes, spans, keeps, *seeds.shape[3:])
+
+
+def weighted(planes, spans, keeps, size_x, size_y):
     at, results = 0, []
     for (lo, hi), (start, stop) in zip(spans, keeps):
         shape = (stop - start, size_y)
@@ -253,15 +308,15 @@
             strip[c, p] = y_packed(middle_out(away[:half]), middle_out(away[half:]))
 
 
-def middle_kernel(spans, sub, sub_size, table, seeds, material, near, far, mid, bands):
+def middle_kernel(spans, shared, sub, sub_size, table, seeds, material, near, far, mid, bands):
     size_x = seeds.shape[3]
     keep = (BAND, size_x - BAND)
     planes, = weighted_planes(seeds, material, table, near, far, spans, (keep,), sub, sub_size)
-    half = (keep[1] - keep[0]) // 2
+    half = bands.shape[2]
     for c in range(6):
         for p in range(seeds.shape[2]):
             mid[c, p] = planes[c][p]
-            bands[c, p] = y_packed(planes[c][p][:half], planes[c][p][half:])
+            bands[c, p] = y_packed(planes[c][p][:half], planes[c][p][-half:])
 
 
 def whole_kernel(spans, sub, sub_size, table, seeds, material, near, far, out):
@@ -269,6 +324,22 @@
     for c in range(6):
         for p in range(seeds.shape[2]):
             out[c, p] = planes[c][p]
+
+
+def y_swapped(block):
+    lane = lane_of(block.shape)
+    lanes = block.shape[1]
+    a, b = pltpu.roll(block, BAND, 1), pltpu.roll(block, lanes - BAND, 1)
+    middle = (lane >= BAND) & (lane < lanes - BAND)
+    return jnp.where(middle, 0.0, jnp.where(lane < BAND, a, b))
+
+
+def shared_kernel(span, keep, size_x, sub, sub_size, table, shared, near, far, part):
+    planes = final_fields(shared_fields(table, shared), near, far, sub, sub_size, bands_unpacked)
+    found, = weighted(planes, (span,), (keep,), size_x, part.shape[3])
+    for c in range(part.shape[0]):
+        for p in range(part.shape[1]):
+            part[c, p] = y_swapped(found[c][p])
 
 
 def corner_kernel(tile, edge, corner, summed, send):
@@ -303,7 +374,7 @@
             out[c, p, BAND:] = summed[c, p, BAND:] + jnp.where(odd, away, by)
 
 
-def last_kernel(edge, mid, bands, out, whole, sems):
+def last_kernel(edge, mid, bands, part, out, whole, sems):
     half = bands.shape[2]
     size_x = out.shape[3]
     copies = []
@@ -312,7 +383,8 @@
             first, second = y_unpacked(bands[c, p])
             whole[c, p, :BAND] = edge[c, p, :BAND]
             whole[c, p, BAND : BAND + half] = mid[c, p, :half] + first
-            whole[c, p, BAND + half : size_x - BAND] = mid[c, p, half:] + second
+            whole[c, p, BAND + half : size_x - BAND - half] = mid[c, p, half:-half] + part[c, p]
+            whole[c, p, size_x - BAND - half : size_x - BAND] = mid[c, p, -half:] + second
             whole[c, p, size_x - BAND :] = edge[c, p, BAND:]
         copies.append(pltpu.make_async_copy(whole.at[c], out.at[0, c], sems.at[c]))
         copies[-1].start()
@@ -325,7 +397,11 @@
 PARAMS = pltpu.CompilerParams(vmem_limit_bytes=32 * 1024 * 1024)
 
 
-def called(kernel, shapes, *operands):
+def cost(flops):
+    return pl.CostEstimate(flops=flops, bytes_accessed=0, transcendentals=0)
+
+
+def called(kernel, shapes, *operands, flops=0):
     outs = [jax.ShapeDtypeStruct(shape, jnp.float32) for shape in shapes]
     return pl.pallas_call(
         kernel,
@@ -333,6 +409,7 @@
         in_specs=[VMEM] * len(operands),
         out_specs=[VMEM] * len(outs),
         compiler_params=PARAMS,
+        cost_estimate=cost(flops),
     )(*operands)
 
 
@@ -372,31 +449,32 @@
     depth, size_x, size_y = seeds.shape[2:]
     edges = ((0, BAND + HALO), (size_x - BAND - HALO, size_x))
     inner = ((BAND - HALO, size_x - BAND + HALO),)
+    keep = ((size_x - SHARED) // 2, (size_x + SHARED) // 2)
+    span = (keep[0] - HALO, keep[1] + HALO)
     rows = size_x - 2 * BAND
-    count = sum(hi - lo for lo, hi in edges)
-
-    shape = jax.ShapeDtypeStruct((PLANES, count, size_y), jnp.float32)
-    near, far = pl.pallas_call(
-        functools.partial(first_halo_kernel, edges, "sub"),
-        out_shape=[shape, shape],
+    edge_rows, inner_rows, span_rows = 2 * (BAND + HALO), rows + 2 * HALO, SHARED + 2 * HALO
+    packed_rows = span_rows // 2 + 8
+
+    edge_shape = (PLANES, edge_rows, size_y)
+    inner_shape = (PLANES, inner_rows, size_y)
+    shapes = [edge_shape, edge_shape, inner_shape, inner_shape, (7 * depth, packed_rows, size_y)]
+    edge_near, edge_far, near, far, shared = pl.pallas_call(
+        functools.partial(first_kernel, edges, inner, span, "sub"),
+        out_shape=[jax.ShapeDtypeStruct(shape, jnp.float32) for shape in shapes],
         in_specs=[HBM] * 4,
-        out_specs=[VMEM] * 2,
+        out_specs=[VMEM] * 5,
         scratch_shapes=[
-            pltpu.VMEM((6, depth, count, size_y), jnp.float32),
-            pltpu.VMEM((depth, count, size_y), jnp.int32),
+            pltpu.VMEM(seeds.shape, jnp.float32),
+            pltpu.VMEM(material.shape, jnp.int32),
             pltpu.SMEM((2, *decay.shape), jnp.float32),
-            pltpu.SemaphoreType.DMA((2 + 2 * len(edges),)),
+            pltpu.SemaphoreType.DMA((4,)),
         ],
         compiler_params=PARAMS,
     )(*(pltpu.with_memory_space_constraint(x, pltpu.HBM) for x in (decay, coupling, seeds, material)))
+    shared = swapped(shared, 2, tile_size)
+    edge_near, edge_far = depth_exchange(edge_near, edge_far, sub_size, tile_size)
+    inner_near, inner_far = depth_exchange(near, far, sub_size, tile_size)
     table = table_rows(decay, coupling, size_y)
-    edge_near, edge_far = depth_exchange(near, far, sub_size, tile_size)
-    edge_near, table = after(edge_near, table)
-
-    shape = (PLANES, rows + 2 * HALO, size_y)
-    near, far = called(functools.partial(halo_kernel, inner, "sub"), [shape, shape], table, seeds, material)
-    edge_far, near, far = after(edge_far, near, far)
-    inner_near, inner_far = depth_exchange(near, far, sub_size, tile_size)
 
     edge, corner, strip = called(
         functools.partial(edge_kernel, edges, "sub", sub_size, "tile"),
@@ -405,30 +483,43 @@
     )
     corner = swapped(corner, 2, tile_size)
     strip = swapped(strip, 3, tile_size)
+
+    shape = (PLANES, packed_rows, size_y)
+    near, far = called(
+        functools.partial(shared_halo_kernel, "sub"), [shape, shape], table, shared, flops=LARGE
+    )
+    near, inner_far = after(near, inner_far)
+    near, far = depth_exchange(near, far, sub_size, tile_size)
+
     mid, bands = called(
-        functools.partial(middle_kernel, inner, "sub", sub_size),
-        [(6, depth, rows, size_y), (6, depth, rows // 2, size_y)],
+        functools.partial(middle_kernel, inner, keep, "sub", sub_size),
+        [(6, depth, rows, size_y), (6, depth, (rows - SHARED) // 2, size_y)],
         table, seeds, material, inner_near, inner_far,
     )
-    corner, bands = after(corner, bands)
     bands = swapped(bands, 2, tile_size)
+
+    corner, strip = after(corner, strip)
     summed, send = called(
         functools.partial(corner_kernel, "tile"),
         [(6, depth, 2 * BAND, size_y), (6, depth, BAND + BAND // 2, size_y)],
-        edge, corner,
+        edge, corner, flops=SMALL,
     )
     got = swapped(send, 1, tile_size)
+    part, = called(
+        functools.partial(shared_kernel, span, keep, size_x, "sub", sub_size), [(6, depth, SHARED, size_y)],
+        table, shared, near, far,
+    )
     edge, = called(
         functools.partial(seam_kernel, "tile"), [(6, depth, 2 * BAND, size_y)], summed, got, strip
     )
     return pl.pallas_call(
         last_kernel,
         out_shape=jax.ShapeDtypeStruct(seeds.shape, jnp.float32),
-        in_specs=[VMEM] * 3,
+        in_specs=[VMEM] * 4,
         out_specs=HBM,
         scratch_shapes=[pltpu.VMEM(seeds.shape[1:], jnp.float32), pltpu.SemaphoreType.DMA((6,))],
         compiler_params=PARAMS,
-    )(edge, mid, bands)
+    )(edge, mid, bands, part)
 
 
 def any_lattice(seeds, material, decay, coupling, sub_size, tile_size):

time: 38.3 us -> 35.1 us (0.916)
  waiting for transfers between devices: 21.8 us -> 15.5 us
  Pallas kernels: 5.68 us -> 7.85 us
  starting transfers between devices: 10.5 us -> 11.4 us
    ppermute x4 -> x5, waiting for transfers between devices: 13.7 us -> 3.4 us  [swapped(): lax.ppermute(value, 'tile', [(t, t ^ bits) for t in range(tile_size)])]
    ppermute x2 -> x3, waiting for transfers between devices: 8.04 us -> 12.1 us  [depth_exchange(): far = lax.ppermute(far, ('tile', 'sub'), pairs)]
    pallas_call x5 -> x6, Pallas kernels: 2.87 us -> 4.01 us  [called(): pl.pallas_call(kernel, out_shape=outs, in_specs=[VMEM] * len(operands), o...]
    pallas_call x1, Pallas kernels: 1.51 us -> 2.54 us  [two_by_two(): pl.pallas_call(functools.partial(first_kernel, edges, inner, span, 'sub')...]
    ppermute x4 -> x5, starting transfers between devices: 5.26 us -> 6.26 us  [swapped(): lax.ppermute(value, 'tile', [(t, t ^ bits) for t in range(tile_size)])]
    ppermute x2 -> x3, starting transfers between devices: 0.64 us -> 0.21 us  [depth_exchange(): near = lax.ppermute(near, 'sub', [(i, i ^ 1) for i in range(sub_size)])]
    ppermute x2 -> x3, starting transfers between devices: 4.58 us -> 4.92 us  [depth_exchange(): far = lax.ppermute(far, ('tile', 'sub'), pairs)]
  transfers between devices with their start and end apart: 8 -> 11, of which waited for: 4 -> 4; matrix products, arithmetic and copies ran while one was open for 0% -> 0% of each run, Pallas kernels for 8% -> 11%
where the time goes in v4:
time: 35.1 us; the launch traced here: 35 us
  waiting for transfers between devices  15.5 us (44%)
  starting transfers between devices  11.4 us (32%)
  Pallas kernels  7.85 us (22%)
    ppermute x3, waiting for transfers between devices, depth_exchange(): far = lax.ppermute(far, ('tile', 'sub'), pairs)  12.1 us
    ppermute x5, starting transfers between devices, swapped(): lax.ppermute(value, 'tile', [(t, t ^ bits) for t in range(tile_size)])  6.26 us
    ppermute x3, starting transfers between devices, depth_exchange(): far = lax.ppermute(far, ('tile', 'sub'), pairs)  4.92 us
    pallas_call x6, Pallas kernels, called(): pl.pallas_call(kernel, out_shape=outs, in_specs=[VMEM] * len(operands), o...  4.01 us
    ppermute x5, waiting for transfers between devices, swapped(): lax.ppermute(value, 'tile', [(t, t ^ bits) for t in range(tile_size)])  3.4 us
    pallas_call x1, Pallas kernels, two_by_two(): pl.pallas_call(functools.partial(first_kernel, edges, inner, span, 'sub')...  2.54 us
    pallas_call x1, Pallas kernels, two_by_two(): pl.pallas_call(last_kernel, out_shape=jax.ShapeDtypeStruct(seeds.shape, j...  1.3 us
  transfers between devices with their start and end apart: 11, of which 4 were waited for; matrix products, arithmetic and copies ran while one was open for 0% of the time, Pallas kernels for 11%

profile of v4, /device:TPU:0, one launch (start us, length us, event | category | flops | bytes accessed | tf_op | source)
XLA Modules:
  0.0 35.0 jit_solution(9956038023667554459)
XLA Ops:
  0.0 2.5 %shard_map.46 = (f32[5,80,128]{2,1,0:T(8,128)S(1)}, f32[5,80,128]{2,1,0:T(8,128)S(1)}, f32[5,208,128]{2,1,0:T(8,128)S(1)}, f32[5,208,128]{2,1,0:T(8,128)S(1)}, f32[14,48,128]{2,1,0:T(8,128)S(1)}) custom-call(f32[4]{0:T(128)} %decay.1, f32[4]{0:T(128)} %coupling.1, f32[1,6,2,256,128]{4,3,2,1,0:T(8,128)} %seeds.5, s32[1,2,256,128]{3,2,1,0:T(8,128)} %material.5), custom_call_target="tpu_custom_call" | custom-call | tf_op jit(solution)/shard_map/pallas_call | solution.py:461
  2.6 3.0 %collective-permute-start.6 = (f32[14,48,128]{2,1,0:T(8,128)S(1)}, f32[14,48,128]{2,1,0:T(8,128)S(1)}, u32[]{:S(2)}, u32[]{:S(2)}) collective-permute-start(f32[14,48,128]{2,1,0:T(8,128)S(1)} %get-tuple-element.33), channel_id=1, source_target_pairs={{0,16},{8,24},{16,0},{24,8},{1,17},{9,25},{17,1},{25,9},{2,18},{10... | collective-permute-start | bytes 1032200 | tf_op jit(solution)/shard_map/ppermute | solution.py:436
  5.6 0.0 collective-permute-start
  5.6 1.5 %collective-permute-start.1 = (f32[5,80,128]{2,1,0:T(8,128)S(1)}, f32[5,80,128]{2,1,0:T(8,128)S(1)}, u32[]{:S(2)}, u32[]{:S(2)}) collective-permute-start(f32[5,80,128]{2,1,0:T(8,128)S(1)} %get-tuple-element.24), channel_id=1, source_target_pairs={{0,8},{1,2},{2,1},{3,4},{4,3},{5,6},{6,5},{7,15},{8,0},{9,10},{10,... | collective-permute-start | bytes 614408 | tf_op jit(solution)/shard_map/ppermute | solution.py:431
  7.1 0.2 collective-permute-start.5
  7.3 1.5 %collective-permute-start.7 = (f32[5,208,128]{2,1,0:T(8,128)S(1)}, f32[5,208,128]{2,1,0:T(8,128)S(1)}, u32[]{:S(2)}, u32[]{:S(2)}) collective-permute-start(f32[5,208,128]{2,1,0:T(8,128)S(1)} %get-tuple-element.35), channel_id=1, source_target_pairs={{0,8},{1,2},{2,1},{3,4},{4,3},{5,6},{6,5},{7,15},{8,0},{9,10},{10,... | collective-permute-start | bytes 1597448 | tf_op jit(solution)/shard_map/ppermute | solution.py:431
  8.8 0.1 pad_maximum_fusion
  8.9 0.0 collective-permute-done.near
  8.9 2.5 %collective-permute-done.1.far = f32[5,80,128]{2,1,0:T(8,128)S(1)} collective-permute-done((f32[5,80,128]{2,1,0:T(8,128)S(1)}, f32[5,80,128]{2,1,0:T(8,128)S(1)}, u32[]{:S(2)}, u32[]{:S(2)}) %collective-permute-start.1) | collective-permute-done | bytes 204832 | tf_op jit(solution)/shard_map/ppermute | solution.py:431
  11.4 0.1 broadcast_in_dim.2.table
  11.4 0.6 %shard_map.47 = (f32[6,2,64,128]{3,2,1,0:T(8,128)S(1)}, f32[6,2,32,128]{3,2,1,0:T(8,128)S(1)}, f32[6,2,16,128]{3,2,1,0:T(8,128)S(1)}) custom-call(f32[8,128]{1,0:T(8,128)S(1)} %broadcast_in_dim.2.table, f32[1,6,2,256,128]{4,3,2,1,0:T(8,128)S(1)} %copy-done, s32[1,2,256,128]{3,2,1,0:T(8,128)S(1)} %copy-done.1, f32[5,80,128]{2,1,0:T(8,128)S(1)} %collective-permute-done.near, ...), custom_call_target="tpu_custom_call" | custom-call | tf_op jit(solution)/shard_map/pallas_call | solution.py:406
  12.1 1.5 %collective-permute-start.3 = (f32[6,2,16,128]{3,2,1,0:T(8,128)S(1)}, f32[6,2,16,128]{3,2,1,0:T(8,128)S(1)}, u32[]{:S(2)}, u32[]{:S(2)}) collective-permute-start(f32[6,2,16,128]{3,2,1,0:T(8,128)S(1)} %get-tuple-element.27), channel_id=1, source_target_pairs={{0,24},{8,16},{16,8},{24,0},{1,25},{9,17},{17,9},{25,1},{2,26},{10... | collective-permute-start | bytes 294920 | tf_op jit(solution)/shard_map/ppermute | solution.py:436
  13.6 1.5 %collective-permute-start.2 = (f32[6,2,32,128]{3,2,1,0:T(8,128)S(1)}, f32[6,2,32,128]{3,2,1,0:T(8,128)S(1)}, u32[]{:S(2)}, u32[]{:S(2)}) collective-permute-start(f32[6,2,32,128]{3,2,1,0:T(8,128)S(1)} %get-tuple-element.26), channel_id=1, source_target_pairs={{0,16},{8,24},{16,0},{24,8},{1,17},{9,25},{17,1},{25,9},{2,18},{10... | collective-permute-start | bytes 589832 | tf_op jit(solution)/shard_map/ppermute | solution.py:436
  15.1 0.0 collective-permute-done.6.shared
  15.1 0.7 %shard_map.50 = (f32[5,48,128]{2,1,0:T(8,128)S(1)}, f32[5,48,128]{2,1,0:T(8,128)S(1)}) custom-call(f32[8,128]{1,0:T(8,128)S(1)} %broadcast_in_dim.2.table, f32[14,48,128]{2,1,0:T(8,128)S(1)} %collective-permute-done.6.shared), custom_call_target="tpu_custom_call" | custom-call | flops 10000000000 | tf_op jit(solution)/shard_map/pallas_call | solution.py:406
  15.8 2.3 %collective-permute-done.7.far = f32[5,208,128]{2,1,0:T(8,128)S(1)} collective-permute-done((f32[5,208,128]{2,1,0:T(8,128)S(1)}, f32[5,208,128]{2,1,0:T(8,128)S(1)}, u32[]{:S(2)}, u32[]{:S(2)}) %collective-permute-start.7) | collective-permute-done | bytes 532512 | tf_op jit(solution)/shard_map/ppermute | solution.py:431
  18.1 0.0 collective-permute-done.5.near
  18.1 1.2 %shard_map.51 = (f32[6,2,192,128]{3,2,1,0:T(8,128)S(1)}, f32[6,2,64,128]{3,2,1,0:T(8,128)S(1)}) custom-call(f32[8,128]{1,0:T(8,128)S(1)} %broadcast_in_dim.2.table, f32[1,6,2,256,128]{4,3,2,1,0:T(8,128)S(1)} %copy-done, s32[1,2,256,128]{3,2,1,0:T(8,128)S(1)} %copy-done.1, f32[5,208,128]{2,1,0:T(8,128)S(1)} %collective-permute-done.5.near, ...), custom_call_target="tpu_custom_call" | custom-call | tf_op jit(solution)/shard_map/pallas_call | solution.py:406
  19.4 0.1 collective-permute-start.8
  19.5 0.0 collective-permute-done.3.strip
  19.5 3.4 %collective-permute-done.2.corner = f32[6,2,32,128]{3,2,1,0:T(8,128)S(1)} collective-permute-done((f32[6,2,32,128]{3,2,1,0:T(8,128)S(1)}, f32[6,2,32,128]{3,2,1,0:T(8,128)S(1)}, u32[]{:S(2)}, u32[]{:S(2)}) %collective-permute-start.2) | collective-permute-done | bytes 196640 | tf_op jit(solution)/shard_map/ppermute | solution.py:436
  22.9 0.3 shard_map.48
  23.1 0.1 collective-permute-start.4
  23.3 1.9 %collective-permute-start.10 = (f32[5,48,128]{2,1,0:T(8,128)S(1)}, f32[5,48,128]{2,1,0:T(8,128)S(1)}, u32[]{:S(2)}, u32[]{:S(2)}) collective-permute-start(f32[5,48,128]{2,1,0:T(8,128)S(1)} %get-tuple-element.40), channel_id=1, source_target_pairs={{0,8},{1,2},{2,1},{3,4},{4,3},{5,6},{6,5},{7,15},{8,0},{9,10},{10,... | collective-permute-start | bytes 368648 | tf_op jit(solution)/shard_map/ppermute | solution.py:431
  25.2 0.0 collective-permute-start.9
  25.2 7.3 %collective-permute-done.10.far = f32[5,48,128]{2,1,0:T(8,128)S(1)} collective-permute-done((f32[5,48,128]{2,1,0:T(8,128)S(1)}, f32[5,48,128]{2,1,0:T(8,128)S(1)}, u32[]{:S(2)}, u32[]{:S(2)}) %collective-permute-start.10) | collective-permute-done | bytes 122912 | tf_op jit(solution)/shard_map/ppermute | solution.py:431
  32.5 0.0 collective-permute-done.9.near
  32.5 1.0 %shard_map.52.part = f32[6,2,64,128]{3,2,1,0:T(8,128)S(1)} custom-call(f32[8,128]{1,0:T(8,128)S(1)} %broadcast_in_dim.2.table, f32[14,48,128]{2,1,0:T(8,128)S(1)} %collective-permute-done.6.shared, f32[5,48,128]{2,1,0:T(8,128)S(1)} %collective-permute-done.9.near, f32[5,48,128]{2,1,0:T(8,128)S(1)} %collective-permute-done.10.far), custom_call_target="tpu_custom_call" | custom-call | tf_op jit(solution)/shard_map/pallas_call | solution.py:406
  33.5 0.0 collective-permute-done.4.got
  33.5 0.1 shard_map.49.edge
  33.7 0.0 collective-permute-done.8.bands
  33.7 1.3 %shard_map.53 = f32[1,6,2,256,128]{4,3,2,1,0:T(8,128)} custom-call(f32[6,2,64,128]{3,2,1,0:T(8,128)S(1)} %shard_map.49.edge, f32[6,2,192,128]{3,2,1,0:T(8,128)S(1)} %get-tuple-element.37.mid, f32[6,2,64,128]{3,2,1,0:T(8,128)S(1)} %collective-permute-done.8.bands, f32[6,2,64,128]{3,2,1,0:T(8,128)S(1)} %shard_map.52.part), custom_call_target="tpu_custom_call" | custom-call | tf_op jit(solution)/shard_map/pallas_call | solution.py:515
  (8 shorter events, 0.0 us)
Async XLA Ops:
  0.0 11.4 %copy-start.1 = (s32[1,2,256,128]{3,2,1,0:T(8,128)S(1)}, s32[1,2,256,128]{3,2,1,0:T(8,128)}, u32[]{:S(2)}) copy-start(s32[1,2,256,128]{3,2,1,0:T(8,128)} %material.5) | copy-start | bytes 786436
  0.0 11.4 %copy-start = (f32[1,6,2,256,128]{4,3,2,1,0:T(8,128)S(1)}, f32[1,6,2,256,128]{4,3,2,1,0:T(8,128)}, u32[]{:S(2)}) copy-start(f32[1,6,2,256,128]{4,3,2,1,0:T(8,128)} %seeds.5) | copy-start | bytes 4718596
  0.0 8.8 %copy-start.2 = (f32[4]{0:T(128)S(1)}, f32[4]{0:T(128)}, u32[]{:S(2)}) copy-start(f32[4]{0:T(128)} %coupling.1) | copy-start | bytes 52
  0.0 8.8 %copy-start.3 = (f32[4]{0:T(128)S(1)}, f32[4]{0:T(128)}, u32[]{:S(2)}) copy-start(f32[4]{0:T(128)} %decay.1) | copy-start | bytes 52
  2.6 12.5 %collective-permute-start.6 = (f32[14,48,128]{2,1,0:T(8,128)S(1)}, f32[14,48,128]{2,1,0:T(8,128)S(1)}, u32[]{:S(2)}, u32[]{:S(2)}) collective-permute-start(f32[14,48,128]{2,1,0:T(8,128)S(1)} %get-tuple-element.33), channel_id=1, source_target_pairs={{0,16},{8,24},{16,0},{24,8},{1,17},{9,25},{17,1},{25,9},{2,18},{10... | collective-permute-start | bytes 1032200 | tf_op jit(solution)/shard_map/ppermute | solution.py:436
  5.6 3.3 %collective-permute-start = (f32[5,80,128]{2,1,0:T(8,128)S(1)}, f32[5,80,128]{2,1,0:T(8,128)S(1)}, u32[]{:S(2)}, u32[]{:S(2)}) collective-permute-start(f32[5,80,128]{2,1,0:T(8,128)S(1)} %get-tuple-element.23), channel_id=1, source_target_pairs={{0,1},{1,0},{2,3},{3,2},{4,5},{5,4},{6,7},{7,6},{8,9},{9,8},{10,11... | collective-permute-start | bytes 614408 | tf_op jit(solution)/shard_map/ppermute | solution.py:421
  5.6 5.8 %collective-permute-start.1 = (f32[5,80,128]{2,1,0:T(8,128)S(1)}, f32[5,80,128]{2,1,0:T(8,128)S(1)}, u32[]{:S(2)}, u32[]{:S(2)}) collective-permute-start(f32[5,80,128]{2,1,0:T(8,128)S(1)} %get-tuple-element.24), channel_id=1, source_target_pairs={{0,8},{1,2},{2,1},{3,4},{4,3},{5,6},{6,5},{7,15},{8,0},{9,10},{10,... | collective-permute-start | bytes 614408 | tf_op jit(solution)/shard_map/ppermute | solution.py:431
  7.1 11.0 %collective-permute-start.5 = (f32[5,208,128]{2,1,0:T(8,128)S(1)}, f32[5,208,128]{2,1,0:T(8,128)S(1)}, u32[]{:S(2)}, u32[]{:S(2)}) collective-permute-start(f32[5,208,128]{2,1,0:T(8,128)S(1)} %get-tuple-element.32), channel_id=1, source_target_pairs={{0,1},{1,0},{2,3},{3,2},{4,5},{5,4},{6,7},{7,6},{8,9},{9,8},{10,11... | collective-permute-start | bytes 1597448 | tf_op jit(solution)/shard_map/ppermute | solution.py:421
  7.3 10.8 %collective-permute-start.7 = (f32[5,208,128]{2,1,0:T(8,128)S(1)}, f32[5,208,128]{2,1,0:T(8,128)S(1)}, u32[]{:S(2)}, u32[]{:S(2)}) collective-permute-start(f32[5,208,128]{2,1,0:T(8,128)S(1)} %get-tuple-element.35), channel_id=1, source_target_pairs={{0,8},{1,2},{2,1},{3,4},{4,3},{5,6},{6,5},{7,15},{8,0},{9,10},{10,... | collective-permute-start | bytes 1597448 | tf_op jit(solution)/shard_map/ppermute | solution.py:431
  12.1 7.4 %collective-permute-start.3 = (f32[6,2,16,128]{3,2,1,0:T(8,128)S(1)}, f32[6,2,16,128]{3,2,1,0:T(8,128)S(1)}, u32[]{:S(2)}, u32[]{:S(2)}) collective-permute-start(f32[6,2,16,128]{3,2,1,0:T(8,128)S(1)} %get-tuple-element.27), channel_id=1, source_target_pairs={{0,24},{8,16},{16,8},{24,0},{1,25},{9,17},{17,9},{25,1},{2,26},{10... | collective-permute-start | bytes 294920 | tf_op jit(solution)/shard_map/ppermute | solution.py:436
  13.6 9.3 %collective-permute-start.2 = (f32[6,2,32,128]{3,2,1,0:T(8,128)S(1)}, f32[6,2,32,128]{3,2,1,0:T(8,128)S(1)}, u32[]{:S(2)}, u32[]{:S(2)}) collective-permute-start(f32[6,2,32,128]{3,2,1,0:T(8,128)S(1)} %get-tuple-element.26), channel_id=1, source_target_pairs={{0,16},{8,24},{16,0},{24,8},{1,17},{9,25},{17,1},{25,9},{2,18},{10... | collective-permute-start | bytes 589832 | tf_op jit(solution)/shard_map/ppermute | solution.py:436
  19.4 14.3 %collective-permute-start.8 = (f32[6,2,64,128]{3,2,1,0:T(8,128)S(1)}, f32[6,2,64,128]{3,2,1,0:T(8,128)S(1)}, u32[]{:S(2)}, u32[]{:S(2)}) collective-permute-start(f32[6,2,64,128]{3,2,1,0:T(8,128)S(1)} %get-tuple-element.38), channel_id=1, source_target_pairs={{0,16},{8,24},{16,0},{24,8},{1,17},{9,25},{17,1},{25,9},{2,18},{10... | collective-permute-start | bytes 1179656 | tf_op jit(solution)/shard_map/ppermute | solution.py:436
  23.1 10.4 %collective-permute-start.4 = (f32[6,2,48,128]{3,2,1,0:T(8,128)S(1)}, f32[6,2,48,128]{3,2,1,0:T(8,128)S(1)}, u32[]{:S(2)}, u32[]{:S(2)}) collective-permute-start(f32[6,2,48,128]{3,2,1,0:T(8,128)S(1)} %get-tuple-element.30), channel_id=1, source_target_pairs={{0,8},{8,0},{16,24},{24,16},{1,9},{9,1},{17,25},{25,17},{2,10},{10... | collective-permute-start | bytes 884744 | tf_op jit(solution)/shard_map/ppermute | solution.py:436
  23.3 9.2 %collective-permute-start.10 = (f32[5,48,128]{2,1,0:T(8,128)S(1)}, f32[5,48,128]{2,1,0:T(8,128)S(1)}, u32[]{:S(2)}, u32[]{:S(2)}) collective-permute-start(f32[5,48,128]{2,1,0:T(8,128)S(1)} %get-tuple-element.40), channel_id=1, source_target_pairs={{0,8},{1,2},{2,1},{3,4},{4,3},{5,6},{6,5},{7,15},{8,0},{9,10},{10,... | collective-permute-start | bytes 368648 | tf_op jit(solution)/shard_map/ppermute | solution.py:431
  25.2 7.3 %collective-permute-start.9 = (f32[5,48,128]{2,1,0:T(8,128)S(1)}, f32[5,48,128]{2,1,0:T(8,128)S(1)}, u32[]{:S(2)}, u32[]{:S(2)}) collective-permute-start(f32[5,48,128]{2,1,0:T(8,128)S(1)} %get-tuple-element.39), channel_id=1, source_target_pairs={{0,1},{1,0},{2,3},{3,2},{4,5},{5,4},{6,7},{7,6},{8,9},{9,8},{10,11... | collective-permute-start | bytes 368648 | tf_op jit(solution)/shard_map/ppermute | solution.py:421

commit v5 on v4

--- a/solution.py
+++ b/solution.py
@@ -243,27 +243,25 @@
     return jnp.concatenate(pieces, axis=0)
 
 
-def first_kernel(edges, inner, span, sub, decay, coupling, seeds, material, *rest):
-    near_edge, far_edge, near, far, shared, held, labels, tables, sems = rest
-    copies = [
-        pltpu.make_async_copy(seeds.at[0], held.at[0], sems.at[0]),
-        pltpu.make_async_copy(material, labels, sems.at[1]),
-        pltpu.make_async_copy(decay, tables.at[0], sems.at[2]),
-        pltpu.make_async_copy(coupling, tables.at[1], sems.at[3]),
-    ]
+def share_kernel(span, seeds, material, shared, held, labels, sems):
+    rows = pl.ds(span[0], span[1] - span[0])
+    depth = held.shape[1]
+    copies = [pltpu.make_async_copy(material.at[0, :, rows], labels, sems.at[6])]
+    copies += [pltpu.make_async_copy(seeds.at[0, c, :, rows], held.at[c], sems.at[c]) for c in range(6)]
     for copy in copies:
         copy.start()
-    for copy in copies:
-        copy.wait()
-    depth = held.shape[2]
+    copies[0].wait()
+    for p in range(depth):
+        shared[6 * depth + p] = bands_packed(labels[p].astype(jnp.float32))
     for c in range(6):
+        copies[1 + c].wait()
         for p in range(depth):
-            shared[depth * c + p] = bands_packed(joined(held, (0, c, p), (span,)))
-    for p in range(depth):
-        shared[6 * depth + p] = bands_packed(joined(labels, (0, p), (span,)).astype(jnp.float32))
-    entries = [[tables[k, m] for m in range(tables.shape[1])] for k in range(2)]
-    send_halos(sub, prepared(*raw(held, labels, edges), entries), near_edge, far_edge)
-    send_halos(sub, prepared(*raw(held, labels, inner), entries), near, far)
+            shared[depth * c + p] = bands_packed(held[c, p])
+
+
+def halo_pair_kernel(edges, inner, sub, table, seeds, material, near_edge, far_edge, near, far):
+    send_halos(sub, loaded(seeds, material, table, edges), near_edge, far_edge)
+    send_halos(sub, loaded(seeds, material, table, inner), near, far)
 
 
 def shared_fields(table, shared):
@@ -417,19 +415,23 @@
     return lax.optimization_barrier((first, *values))
 
 
-def depth_exchange(near, far, sub_size, tile_size):
-    near = lax.ppermute(near, "sub", [(i, i ^ 1) for i in range(sub_size)])
+def near_exchange(near, sub_size):
+    return lax.ppermute(near, "sub", [(i, i ^ 1) for i in range(sub_size)])
+
+
+def far_exchange(far, sub_size, tile_size, ends_by_tile=True):
     pairs = []
     for t in range(tile_size):
         for i in range(sub_size):
-            other = (i + 1) ^ 1
-            j = other - 1
+            j = ((i + 1) ^ 1) - 1
             if 0 <= j < sub_size:
-                pairs.append((t * sub_size + i, t * sub_size + j))
+                other = (t, j)
+            elif ends_by_tile:
+                other = (t ^ 1, i)
             else:
-                pairs.append((t * sub_size + i, (t ^ 1) * sub_size + i))
-    far = lax.ppermute(far, ("tile", "sub"), pairs)
-    return near, far
+                other = (t, sub_size - 1 - i)
+            pairs.append((t * sub_size + i, other[0] * sub_size + other[1]))
+    return lax.ppermute(far, ("tile", "sub"), pairs)
 
 
 def swapped(value, bits, tile_size):
@@ -455,26 +457,29 @@
     edge_rows, inner_rows, span_rows = 2 * (BAND + HALO), rows + 2 * HALO, SHARED + 2 * HALO
     packed_rows = span_rows // 2 + 8
 
-    edge_shape = (PLANES, edge_rows, size_y)
-    inner_shape = (PLANES, inner_rows, size_y)
-    shapes = [edge_shape, edge_shape, inner_shape, inner_shape, (7 * depth, packed_rows, size_y)]
-    edge_near, edge_far, near, far, shared = pl.pallas_call(
-        functools.partial(first_kernel, edges, inner, span, "sub"),
-        out_shape=[jax.ShapeDtypeStruct(shape, jnp.float32) for shape in shapes],
-        in_specs=[HBM] * 4,
-        out_specs=[VMEM] * 5,
+    shared = pl.pallas_call(
+        functools.partial(share_kernel, span),
+        out_shape=jax.ShapeDtypeStruct((7 * depth, packed_rows, size_y), jnp.float32),
+        in_specs=[HBM] * 2,
+        out_specs=VMEM,
         scratch_shapes=[
-            pltpu.VMEM(seeds.shape, jnp.float32),
-            pltpu.VMEM(material.shape, jnp.int32),
-            pltpu.SMEM((2, *decay.shape), jnp.float32),
-            pltpu.SemaphoreType.DMA((4,)),
+            pltpu.VMEM((6, depth, span_rows, size_y), jnp.float32),
+            pltpu.VMEM((depth, span_rows, size_y), jnp.int32),
+            pltpu.SemaphoreType.DMA((7,)),
         ],
         compiler_params=PARAMS,
-    )(*(pltpu.with_memory_space_constraint(x, pltpu.HBM) for x in (decay, coupling, seeds, material)))
+        cost_estimate=cost(0),
+    )(*(pltpu.with_memory_space_constraint(x, pltpu.HBM) for x in (seeds, material)))
+    table = table_rows(decay, coupling, size_y)
+    shared, table = after(shared, table)
     shared = swapped(shared, 2, tile_size)
-    edge_near, edge_far = depth_exchange(edge_near, edge_far, sub_size, tile_size)
-    inner_near, inner_far = depth_exchange(near, far, sub_size, tile_size)
-    table = table_rows(decay, coupling, size_y)
+    edge_near, edge_far, inner_near, inner_far = called(
+        functools.partial(halo_pair_kernel, edges, inner, "sub"),
+        [(PLANES, edge_rows, size_y)] * 2 + [(PLANES, inner_rows, size_y)] * 2, table, seeds, material,
+    )
+    edge_near, inner_near = near_exchange(edge_near, sub_size), near_exchange(inner_near, sub_size)
+    edge_far = far_exchange(edge_far, sub_size, tile_size)
+    inner_far = far_exchange(inner_far, sub_size, tile_size)
 
     edge, corner, strip = called(
         functools.partial(edge_kernel, edges, "sub", sub_size, "tile"),
@@ -485,11 +490,12 @@
     strip = swapped(strip, 3, tile_size)
 
     shape = (PLANES, packed_rows, size_y)
-    near, far = called(
+    shared_near, shared_far = called(
         functools.partial(shared_halo_kernel, "sub"), [shape, shape], table, shared, flops=LARGE
     )
-    near, inner_far = after(near, inner_far)
-    near, far = depth_exchange(near, far, sub_size, tile_size)
+    shared_near, inner_far = after(shared_near, inner_far)
+    shared_near = near_exchange(shared_near, sub_size)
+    shared_far = far_exchange(shared_far, sub_size, tile_size, ends_by_tile=False)
 
     mid, bands = called(
         functools.partial(middle_kernel, inner, keep, "sub", sub_size),
@@ -507,7 +513,7 @@
     got = swapped(send, 1, tile_size)
     part, = called(
         functools.partial(shared_kernel, span, keep, size_x, "sub", sub_size), [(6, depth, SHARED, size_y)],
-        table, shared, near, far,
+        table, shared, shared_near, shared_far,
     )
     edge, = called(
         functools.partial(seam_kernel, "tile"), [(6, depth, 2 * BAND, size_y)], summed, got, strip
@@ -528,7 +534,8 @@
     table = table_rows(decay, coupling, size_y)
     shape = (PLANES, size_x, size_y)
     near, far = called(functools.partial(halo_kernel, spans, "sub"), [shape, shape], table, seeds, material)
-    near, far = depth_exchange(near, far, sub_size, tile_size)
+    near = near_exchange(near, sub_size)
+    far = far_exchange(far, sub_size, tile_size)
     weighted, = called(
         functools.partial(whole_kernel, spans, "sub", sub_size), [(6, depth, size_x, size_y)],
         table, seeds, material, near, far,

time: 35.1 us -> 33.9 us (0.966)
  waiting for transfers between devices: 15.5 us -> 13.6 us
  other arithmetic: 0.07 us -> 0.88 us
    ppermute x6, waiting for transfers between devices: 12.1 us -> 10.3 us  [the longest x3 10.3 us: far_exchange(): return lax.ppermute(far, ('tile', 'sub'), pairs)]
    pallas_call x1, Pallas kernels: 2.54 us -> 1.63 us  [two_by_two(): pl.pallas_call(functools.partial(share_kernel, span), out_shape=jax.Shape...]
    concatenate x1, other arithmetic: 0.07 us -> 0.88 us  [table_rows(): entries = jnp.concatenate([decay, coupling])]
    pallas_call x6 -> x7, Pallas kernels: 4.01 us -> 4.77 us  [called(): pl.pallas_call(kernel, out_shape=outs, in_specs=[VMEM] * len(operands), o...]
  transfers between devices with their start and end apart: 11 -> 11, of which waited for: 4 -> 4; matrix products, arithmetic and copies ran while one was open for 0% -> 0% of each run, Pallas kernels for 11% -> 14%
where the time goes in v5:
time: 33.9 us; the launch traced here: 33.7 us
  waiting for transfers between devices  13.6 us (40%)
  starting transfers between devices  11.3 us (33%)
  Pallas kernels  7.69 us (23%)
  other arithmetic  0.88 us (3%)
    ppermute x3, waiting for transfers between devices, far_exchange(): return lax.ppermute(far, ('tile', 'sub'), pairs)  10.3 us
    ppermute x5, starting transfers between devices, swapped(): lax.ppermute(value, 'tile', [(t, t ^ bits) for t in range(tile_size)])  6.11 us
    pallas_call x7, Pallas kernels, called(): pl.pallas_call(kernel, out_shape=outs, in_specs=[VMEM] * len(operands), o...  4.77 us
    ppermute x3, starting transfers between devices, far_exchange(): return lax.ppermute(far, ('tile', 'sub'), pairs)  4.52 us
    ppermute x5, waiting for transfers between devices, swapped(): lax.ppermute(value, 'tile', [(t, t ^ bits) for t in range(tile_size)])  3.31 us
    pallas_call x1, Pallas kernels, two_by_two(): pl.pallas_call(functools.partial(share_kernel, span), out_shape=jax.Shape...  1.63 us
    pallas_call x1, Pallas kernels, two_by_two(): pl.pallas_call(last_kernel, out_shape=jax.ShapeDtypeStruct(seeds.shape, j...  1.3 us
    concatenate x1, other arithmetic, table_rows(): entries = jnp.concatenate([decay, coupling])  0.88 us
  transfers between devices with their start and end apart: 11, of which 4 were waited for; matrix products, arithmetic and copies ran while one was open for 0% of the time, Pallas kernels for 14%

profile of v5, /device:TPU:0, one launch (start us, length us, event | category | flops | bytes accessed | tf_op | source)
XLA Modules:
  0.0 33.7 jit_solution(13521315355098129916)
XLA Ops:
  0.0 0.9 %pad_maximum_fusion = f32[8]{0:T(128)S(1)} fusion(f32[4]{0:T(128)} %param.7, f32[4]{0:T(128)} %param.6), kind=kLoop, calls=%fused_computation | loop fusion | flops 8 | bytes 64 | tf_op jit(solution)/shard_map/concatenate | solution.py:446
  0.9 1.6 %shard_map.46 = f32[14,48,128]{2,1,0:T(8,128)S(1)} custom-call(f32[1,6,2,256,128]{4,3,2,1,0:T(8,128)} %seeds.7, s32[1,2,256,128]{3,2,1,0:T(8,128)} %material.7), custom_call_target="tpu_custom_call" | custom-call | tf_op jit(solution)/shard_map/pallas_call | solution.py:460
  2.5 0.1 broadcast_in_dim.2.table
  2.6 3.0 %collective-permute-start.6 = (f32[14,48,128]{2,1,0:T(8,128)S(1)}, f32[14,48,128]{2,1,0:T(8,128)S(1)}, u32[]{:S(2)}, u32[]{:S(2)}) collective-permute-start(f32[14,48,128]{2,1,0:T(8,128)S(1)} %shard_map.46), channel_id=1, source_target_pairs={{0,16},{8,24},{16,0},{24,8},{1,17},{9,25},{17,1},{25,9},{2,18},{10... | collective-permute-start | bytes 1032200 | tf_op jit(solution)/shard_map/ppermute | solution.py:438
  5.6 0.8 %shard_map.47 = (f32[5,80,128]{2,1,0:T(8,128)S(1)}, f32[5,80,128]{2,1,0:T(8,128)S(1)}, f32[5,208,128]{2,1,0:T(8,128)S(1)}, f32[5,208,128]{2,1,0:T(8,128)S(1)}) custom-call(f32[8,128]{1,0:T(8,128)S(1)} %broadcast_in_dim.2.table, f32[1,6,2,256,128]{4,3,2,1,0:T(8,128)S(1)} %copy-done, s32[1,2,256,128]{3,2,1,0:T(8,128)S(1)} %copy-done.1), custom_call_target="tpu_custom_call" | custom-call | tf_op jit(solution)/shard_map/pallas_call | solution.py:404
  6.3 0.1 collective-permute-start
  6.4 1.6 %collective-permute-start.1 = (f32[5,80,128]{2,1,0:T(8,128)S(1)}, f32[5,80,128]{2,1,0:T(8,128)S(1)}, u32[]{:S(2)}, u32[]{:S(2)}) collective-permute-start(f32[5,80,128]{2,1,0:T(8,128)S(1)} %get-tuple-element.26), channel_id=1, source_target_pairs={{0,8},{1,2},{2,1},{3,4},{4,3},{5,6},{6,5},{7,15},{8,0},{9,10},{10,... | collective-permute-start | bytes 614408 | tf_op jit(solution)/shard_map/ppermute | solution.py:434
  8.0 0.2 collective-permute-start.5
  8.2 1.5 %collective-permute-start.7 = (f32[5,208,128]{2,1,0:T(8,128)S(1)}, f32[5,208,128]{2,1,0:T(8,128)S(1)}, u32[]{:S(2)}, u32[]{:S(2)}) collective-permute-start(f32[5,208,128]{2,1,0:T(8,128)S(1)} %get-tuple-element.37), channel_id=1, source_target_pairs={{0,8},{1,2},{2,1},{3,4},{4,3},{5,6},{6,5},{7,15},{8,0},{9,10},{10,... | collective-permute-start | bytes 1597448 | tf_op jit(solution)/shard_map/ppermute | solution.py:434
  9.7 0.0 collective-permute-done.near
  9.7 2.6 %collective-permute-done.1.far = f32[5,80,128]{2,1,0:T(8,128)S(1)} collective-permute-done((f32[5,80,128]{2,1,0:T(8,128)S(1)}, f32[5,80,128]{2,1,0:T(8,128)S(1)}, u32[]{:S(2)}, u32[]{:S(2)}) %collective-permute-start.1) | collective-permute-done | bytes 204832 | tf_op jit(solution)/shard_map/ppermute | solution.py:434
  12.2 0.7 %shard_map.48 = (f32[6,2,64,128]{3,2,1,0:T(8,128)S(1)}, f32[6,2,32,128]{3,2,1,0:T(8,128)S(1)}, f32[6,2,16,128]{3,2,1,0:T(8,128)S(1)}) custom-call(f32[8,128]{1,0:T(8,128)S(1)} %broadcast_in_dim.2.table, f32[1,6,2,256,128]{4,3,2,1,0:T(8,128)S(1)} %copy-done, s32[1,2,256,128]{3,2,1,0:T(8,128)S(1)} %copy-done.1, f32[5,80,128]{2,1,0:T(8,128)S(1)} %collective-permute-done.near, ...), custom_call_target="tpu_custom_call" | custom-call | tf_op jit(solution)/shard_map/pallas_call | solution.py:404
  12.9 1.5 %collective-permute-start.3 = (f32[6,2,16,128]{3,2,1,0:T(8,128)S(1)}, f32[6,2,16,128]{3,2,1,0:T(8,128)S(1)}, u32[]{:S(2)}, u32[]{:S(2)}) collective-permute-start(f32[6,2,16,128]{3,2,1,0:T(8,128)S(1)} %get-tuple-element.29), channel_id=1, source_target_pairs={{0,24},{8,16},{16,8},{24,0},{1,25},{9,17},{17,9},{25,1},{2,26},{10... | collective-permute-start | bytes 294920 | tf_op jit(solution)/shard_map/ppermute | solution.py:438
  14.4 1.5 %collective-permute-start.2 = (f32[6,2,32,128]{3,2,1,0:T(8,128)S(1)}, f32[6,2,32,128]{3,2,1,0:T(8,128)S(1)}, u32[]{:S(2)}, u32[]{:S(2)}) collective-permute-start(f32[6,2,32,128]{3,2,1,0:T(8,128)S(1)} %get-tuple-element.28), channel_id=1, source_target_pairs={{0,16},{8,24},{16,0},{24,8},{1,17},{9,25},{17,1},{25,9},{2,18},{10... | collective-permute-start | bytes 589832 | tf_op jit(solution)/shard_map/ppermute | solution.py:438
  15.9 0.0 collective-permute-done.6.shared
  15.9 0.7 %shard_map.51 = (f32[5,48,128]{2,1,0:T(8,128)S(1)}, f32[5,48,128]{2,1,0:T(8,128)S(1)}) custom-call(f32[8,128]{1,0:T(8,128)S(1)} %broadcast_in_dim.2.table, f32[14,48,128]{2,1,0:T(8,128)S(1)} %collective-permute-done.6.shared), custom_call_target="tpu_custom_call" | custom-call | flops 10000000000 | tf_op jit(solution)/shard_map/pallas_call | solution.py:404
  16.6 2.4 %collective-permute-done.7.far = f32[5,208,128]{2,1,0:T(8,128)S(1)} collective-permute-done((f32[5,208,128]{2,1,0:T(8,128)S(1)}, f32[5,208,128]{2,1,0:T(8,128)S(1)}, u32[]{:S(2)}, u32[]{:S(2)}) %collective-permute-start.7) | collective-permute-done | bytes 532512 | tf_op jit(solution)/shard_map/ppermute | solution.py:434
  19.0 0.0 collective-permute-done.5.near
  19.0 1.2 %shard_map.52 = (f32[6,2,192,128]{3,2,1,0:T(8,128)S(1)}, f32[6,2,64,128]{3,2,1,0:T(8,128)S(1)}) custom-call(f32[8,128]{1,0:T(8,128)S(1)} %broadcast_in_dim.2.table, f32[1,6,2,256,128]{4,3,2,1,0:T(8,128)S(1)} %copy-done, s32[1,2,256,128]{3,2,1,0:T(8,128)S(1)} %copy-done.1, f32[5,208,128]{2,1,0:T(8,128)S(1)} %collective-permute-done.5.near, ...), custom_call_target="tpu_custom_call" | custom-call | tf_op jit(solution)/shard_map/pallas_call | solution.py:404
  20.2 0.1 collective-permute-start.8
  20.3 3.3 %collective-permute-done.2.corner = f32[6,2,32,128]{3,2,1,0:T(8,128)S(1)} collective-permute-done((f32[6,2,32,128]{3,2,1,0:T(8,128)S(1)}, f32[6,2,32,128]{3,2,1,0:T(8,128)S(1)}, u32[]{:S(2)}, u32[]{:S(2)}) %collective-permute-start.2) | collective-permute-done | bytes 196640 | tf_op jit(solution)/shard_map/ppermute | solution.py:438
  23.6 0.3 shard_map.49
  23.9 0.1 collective-permute-start.4
  24.0 1.5 %collective-permute-start.10 = (f32[5,48,128]{2,1,0:T(8,128)S(1)}, f32[5,48,128]{2,1,0:T(8,128)S(1)}, u32[]{:S(2)}, u32[]{:S(2)}) collective-permute-start(f32[5,48,128]{2,1,0:T(8,128)S(1)} %get-tuple-element.42), channel_id=1, source_target_pairs={{0,7},{1,2},{2,1},{3,4},{4,3},{5,6},{6,5},{7,0},{8,15},{9,10},{10,... | collective-permute-start | bytes 368648 | tf_op jit(solution)/shard_map/ppermute | solution.py:434
  25.4 0.4 %collective-permute-start.9 = (f32[5,48,128]{2,1,0:T(8,128)S(1)}, f32[5,48,128]{2,1,0:T(8,128)S(1)}, u32[]{:S(2)}, u32[]{:S(2)}) collective-permute-start(f32[5,48,128]{2,1,0:T(8,128)S(1)} %get-tuple-element.41), channel_id=1, source_target_pairs={{0,1},{1,0},{2,3},{3,2},{4,5},{5,4},{6,7},{7,6},{8,9},{9,8},{10,11... | collective-permute-start | bytes 368648 | tf_op jit(solution)/shard_map/ppermute | solution.py:419
  25.9 5.4 %collective-permute-done.10.far = f32[5,48,128]{2,1,0:T(8,128)S(1)} collective-permute-done((f32[5,48,128]{2,1,0:T(8,128)S(1)}, f32[5,48,128]{2,1,0:T(8,128)S(1)}, u32[]{:S(2)}, u32[]{:S(2)}) %collective-permute-start.10) | collective-permute-done | bytes 122912 | tf_op jit(solution)/shard_map/ppermute | solution.py:434
  31.2 0.0 collective-permute-done.9.near
  31.2 1.0 %shard_map.53.part = f32[6,2,64,128]{3,2,1,0:T(8,128)S(1)} custom-call(f32[8,128]{1,0:T(8,128)S(1)} %broadcast_in_dim.2.table, f32[14,48,128]{2,1,0:T(8,128)S(1)} %collective-permute-done.6.shared, f32[5,48,128]{2,1,0:T(8,128)S(1)} %collective-permute-done.9.near, f32[5,48,128]{2,1,0:T(8,128)S(1)} %collective-permute-done.10.far), custom_call_target="tpu_custom_call" | custom-call | tf_op jit(solution)/shard_map/pallas_call | solution.py:404
  32.2 0.0 collective-permute-done.4.got
  32.3 0.1 shard_map.50.edge
  32.4 0.0 collective-permute-done.8.bands
  32.4 1.3 %shard_map.54 = f32[1,6,2,256,128]{4,3,2,1,0:T(8,128)} custom-call(f32[6,2,64,128]{3,2,1,0:T(8,128)S(1)} %shard_map.50.edge, f32[6,2,192,128]{3,2,1,0:T(8,128)S(1)} %get-tuple-element.39.mid, f32[6,2,64,128]{3,2,1,0:T(8,128)S(1)} %collective-permute-done.8.bands, f32[6,2,64,128]{3,2,1,0:T(8,128)S(1)} %shard_map.53.part), custom_call_target="tpu_custom_call" | custom-call | tf_op jit(solution)/shard_map/pallas_call | solution.py:521
  (5 shorter events, 0.0 us)
Async XLA Ops:
  0.0 5.6 %copy-start.1 = (s32[1,2,256,128]{3,2,1,0:T(8,128)S(1)}, s32[1,2,256,128]{3,2,1,0:T(8,128)}, u32[]{:S(2)}) copy-start(s32[1,2,256,128]{3,2,1,0:T(8,128)} %material.7) | copy-start | bytes 786436
  0.0 5.6 %copy-start = (f32[1,6,2,256,128]{4,3,2,1,0:T(8,128)S(1)}, f32[1,6,2,256,128]{4,3,2,1,0:T(8,128)}, u32[]{:S(2)}) copy-start(f32[1,6,2,256,128]{4,3,2,1,0:T(8,128)} %seeds.7) | copy-start | bytes 4718596
  2.6 13.3 %collective-permute-start.6 = (f32[14,48,128]{2,1,0:T(8,128)S(1)}, f32[14,48,128]{2,1,0:T(8,128)S(1)}, u32[]{:S(2)}, u32[]{:S(2)}) collective-permute-start(f32[14,48,128]{2,1,0:T(8,128)S(1)} %shard_map.46), channel_id=1, source_target_pairs={{0,16},{8,24},{16,0},{24,8},{1,17},{9,25},{17,1},{25,9},{2,18},{10... | collective-permute-start | bytes 1032200 | tf_op jit(solution)/shard_map/ppermute | solution.py:438
  6.3 3.3 %collective-permute-start = (f32[5,80,128]{2,1,0:T(8,128)S(1)}, f32[5,80,128]{2,1,0:T(8,128)S(1)}, u32[]{:S(2)}, u32[]{:S(2)}) collective-permute-start(f32[5,80,128]{2,1,0:T(8,128)S(1)} %get-tuple-element.25), channel_id=1, source_target_pairs={{0,1},{1,0},{2,3},{3,2},{4,5},{5,4},{6,7},{7,6},{8,9},{9,8},{10,11... | collective-permute-start | bytes 614408 | tf_op jit(solution)/shard_map/ppermute | solution.py:419
  6.4 5.8 %collective-permute-start.1 = (f32[5,80,128]{2,1,0:T(8,128)S(1)}, f32[5,80,128]{2,1,0:T(8,128)S(1)}, u32[]{:S(2)}, u32[]{:S(2)}) collective-permute-start(f32[5,80,128]{2,1,0:T(8,128)S(1)} %get-tuple-element.26), channel_id=1, source_target_pairs={{0,8},{1,2},{2,1},{3,4},{4,3},{5,6},{6,5},{7,15},{8,0},{9,10},{10,... | collective-permute-start | bytes 614408 | tf_op jit(solution)/shard_map/ppermute | solution.py:434
  8.0 11.0 %collective-permute-start.5 = (f32[5,208,128]{2,1,0:T(8,128)S(1)}, f32[5,208,128]{2,1,0:T(8,128)S(1)}, u32[]{:S(2)}, u32[]{:S(2)}) collective-permute-start(f32[5,208,128]{2,1,0:T(8,128)S(1)} %get-tuple-element.34), channel_id=1, source_target_pairs={{0,1},{1,0},{2,3},{3,2},{4,5},{5,4},{6,7},{7,6},{8,9},{9,8},{10,11... | collective-permute-start | bytes 1597448 | tf_op jit(solution)/shard_map/ppermute | solution.py:419
  8.2 10.8 %collective-permute-start.7 = (f32[5,208,128]{2,1,0:T(8,128)S(1)}, f32[5,208,128]{2,1,0:T(8,128)S(1)}, u32[]{:S(2)}, u32[]{:S(2)}) collective-permute-start(f32[5,208,128]{2,1,0:T(8,128)S(1)} %get-tuple-element.37), channel_id=1, source_target_pairs={{0,8},{1,2},{2,1},{3,4},{4,3},{5,6},{6,5},{7,15},{8,0},{9,10},{10,... | collective-permute-start | bytes 1597448 | tf_op jit(solution)/shard_map/ppermute | solution.py:434
  12.9 7.4 %collective-permute-start.3 = (f32[6,2,16,128]{3,2,1,0:T(8,128)S(1)}, f32[6,2,16,128]{3,2,1,0:T(8,128)S(1)}, u32[]{:S(2)}, u32[]{:S(2)}) collective-permute-start(f32[6,2,16,128]{3,2,1,0:T(8,128)S(1)} %get-tuple-element.29), channel_id=1, source_target_pairs={{0,24},{8,16},{16,8},{24,0},{1,25},{9,17},{17,9},{25,1},{2,26},{10... | collective-permute-start | bytes 294920 | tf_op jit(solution)/shard_map/ppermute | solution.py:438
  14.4 9.3 %collective-permute-start.2 = (f32[6,2,32,128]{3,2,1,0:T(8,128)S(1)}, f32[6,2,32,128]{3,2,1,0:T(8,128)S(1)}, u32[]{:S(2)}, u32[]{:S(2)}) collective-permute-start(f32[6,2,32,128]{3,2,1,0:T(8,128)S(1)} %get-tuple-element.28), channel_id=1, source_target_pairs={{0,16},{8,24},{16,0},{24,8},{1,17},{9,25},{17,1},{25,9},{2,18},{10... | collective-permute-start | bytes 589832 | tf_op jit(solution)/shard_map/ppermute | solution.py:438
  20.2 12.2 %collective-permute-start.8 = (f32[6,2,64,128]{3,2,1,0:T(8,128)S(1)}, f32[6,2,64,128]{3,2,1,0:T(8,128)S(1)}, u32[]{:S(2)}, u32[]{:S(2)}) collective-permute-start(f32[6,2,64,128]{3,2,1,0:T(8,128)S(1)} %get-tuple-element.40), channel_id=1, source_target_pairs={{0,16},{8,24},{16,0},{24,8},{1,17},{9,25},{17,1},{25,9},{2,18},{10... | collective-permute-start | bytes 1179656 | tf_op jit(solution)/shard_map/ppermute | solution.py:438
  23.9 8.3 %collective-permute-start.4 = (f32[6,2,48,128]{3,2,1,0:T(8,128)S(1)}, f32[6,2,48,128]{3,2,1,0:T(8,128)S(1)}, u32[]{:S(2)}, u32[]{:S(2)}) collective-permute-start(f32[6,2,48,128]{3,2,1,0:T(8,128)S(1)} %get-tuple-element.32), channel_id=1, source_target_pairs={{0,8},{8,0},{16,24},{24,16},{1,9},{9,1},{17,25},{25,17},{2,10},{10... | collective-permute-start | bytes 884744 | tf_op jit(solution)/shard_map/ppermute | solution.py:438
  24.0 7.3 %collective-permute-start.10 = (f32[5,48,128]{2,1,0:T(8,128)S(1)}, f32[5,48,128]{2,1,0:T(8,128)S(1)}, u32[]{:S(2)}, u32[]{:S(2)}) collective-permute-start(f32[5,48,128]{2,1,0:T(8,128)S(1)} %get-tuple-element.42), channel_id=1, source_target_pairs={{0,7},{1,2},{2,1},{3,4},{4,3},{5,6},{6,5},{7,0},{8,15},{9,10},{10,... | collective-permute-start | bytes 368648 | tf_op jit(solution)/shard_map/ppermute | solution.py:434
  25.4 5.8 %collective-permute-start.9 = (f32[5,48,128]{2,1,0:T(8,128)S(1)}, f32[5,48,128]{2,1,0:T(8,128)S(1)}, u32[]{:S(2)}, u32[]{:S(2)}) collective-permute-start(f32[5,48,128]{2,1,0:T(8,128)S(1)} %get-tuple-element.41), channel_id=1, source_target_pairs={{0,1},{1,0},{2,3},{3,2},{4,5},{5,4},{6,7},{7,6},{8,9},{9,8},{10,11... | collective-permute-start | bytes 368648 | tf_op jit(solution)/shard_map/ppermute | solution.py:419

commit v6 on v5

--- a/solution.py
+++ b/solution.py
@@ -12,8 +12,8 @@
 STEPS = 2
 HALO = 8
 PLANES = 5
-REACH = 4
-SHARED = 64
+REACH = 2
+SHARED = 80
 LARGE, SMALL = 10**10, 6 * 10**8
 
 magnetic_coeff = 0.5
@@ -212,51 +212,56 @@
     return first, second
 
 
+def side_lanes(shape, groups, apart):
+    lane = lane_of(shape)
+    width = REACH * groups
+    return (lane < width) | ((lane >= apart) & (lane < apart + width))
+
+
 def bands_packed(block):
     rows, lanes = block.shape
-    half = rows // 2
-    lane = lane_of((8, lanes))
+    half, groups, apart = rows // 2, rows // 8, lanes - 2 * BAND - REACH
     side = jnp.zeros((8, lanes), block.dtype)
-    for g in range(rows // 8):
+    for g in range(groups):
         piece = pltpu.roll(block[8 * g : 8 * g + 8], (REACH * g - BAND) % lanes, 1)
-        side = jnp.where(side_lanes(lane, g, lanes), piece, side)
+        side = jnp.where(side_lanes(side.shape, g, apart), side, piece)
+    upper, lower = side[:4], pltpu.roll(side[4:], REACH * groups, 1)
+    side = jnp.where(side_lanes(upper.shape, groups, apart), upper, lower)
     return jnp.concatenate([y_packed(block[:half], block[half:]), side], axis=0)
 
 
-def side_lanes(lane, g, lanes):
-    low, high = REACH * g, REACH * g + lanes - 2 * BAND - REACH
-    return ((lane >= low) & (lane < low + REACH)) | ((lane >= high) & (lane < high + REACH))
-
-
 def bands_unpacked(packed):
-    half, lanes = packed.shape[0] - 8, packed.shape[1]
+    half, lanes = packed.shape[0] - 4, packed.shape[1]
+    groups = half // 4
     main, side = packed[:half], packed[half:]
     lane = lane_of(main.shape)
     middle = (lane >= BAND) & (lane < lanes - BAND)
     block = jnp.concatenate([jnp.where(middle, 0.0, main), jnp.where(middle, 0.0, middle_out(main))], axis=0)
+    side = jnp.concatenate([side, pltpu.roll(side, lanes - REACH * groups, 1)], axis=0)
     lane = lane_of(side.shape)
     beside = ((lane >= BAND) & (lane < BAND + REACH)) | ((lane >= lanes - BAND - REACH) & (lane < lanes - BAND))
     pieces = []
-    for g in range(2 * half // 8):
+    for g in range(groups):
         moved = pltpu.roll(side, (BAND - REACH * g) % lanes, 1)
         pieces.append(jnp.where(beside, moved, block[8 * g : 8 * g + 8]))
     return jnp.concatenate(pieces, axis=0)
 
 
-def share_kernel(span, seeds, material, shared, held, labels, sems):
+def share_kernel(span, skip, seeds, material, shared, held, labels, sems):
     rows = pl.ds(span[0], span[1] - span[0])
     depth = held.shape[1]
+    stop = span[1] - span[0] - skip
     copies = [pltpu.make_async_copy(material.at[0, :, rows], labels, sems.at[6])]
     copies += [pltpu.make_async_copy(seeds.at[0, c, :, rows], held.at[c], sems.at[c]) for c in range(6)]
     for copy in copies:
         copy.start()
     copies[0].wait()
     for p in range(depth):
-        shared[6 * depth + p] = bands_packed(labels[p].astype(jnp.float32))
+        shared[6 * depth + p] = bands_packed(labels[p, skip:stop].astype(jnp.float32))
     for c in range(6):
         copies[1 + c].wait()
         for p in range(depth):
-            shared[depth * c + p] = bands_packed(held[c, p])
+            shared[depth * c + p] = bands_packed(held[c, p, skip:stop])
 
 
 def halo_pair_kernel(edges, inner, sub, table, seeds, material, near_edge, far_edge, near, far):
@@ -372,20 +377,37 @@
             out[c, p, BAND:] = summed[c, p, BAND:] + jnp.where(odd, away, by)
 
 
-def last_kernel(edge, mid, bands, part, out, whole, sems):
+def early_kernel(edge, mid, part, out, whole, sems):
+    size_x = out.shape[3]
+    start = (size_x - part.shape[2]) // 2
+    rows = pl.ds(start, part.shape[2])
+    low, high = pl.ds(0, BAND), pl.ds(size_x - BAND, BAND)
+    for c in range(mid.shape[0]):
+        for p in range(mid.shape[1]):
+            whole[c, p] = mid[c, p, start - BAND : start - BAND + part.shape[2]] + part[c, p]
+    copies = [
+        pltpu.make_async_copy(whole, out.at[0, :, :, rows], sems.at[0]),
+        pltpu.make_async_copy(edge.at[:, :, pl.ds(0, BAND)], out.at[0, :, :, low], sems.at[1]),
+        pltpu.make_async_copy(edge.at[:, :, pl.ds(BAND, BAND)], out.at[0, :, :, high], sems.at[2]),
+    ]
+    for copy in copies:
+        copy.start()
+    for copy in copies:
+        copy.wait()
+
+
+def last_kernel(mid, bands, _, out, low, high, sems):
     half = bands.shape[2]
     size_x = out.shape[3]
     copies = []
     for c in range(mid.shape[0]):
         for p in range(mid.shape[1]):
             first, second = y_unpacked(bands[c, p])
-            whole[c, p, :BAND] = edge[c, p, :BAND]
-            whole[c, p, BAND : BAND + half] = mid[c, p, :half] + first
-            whole[c, p, BAND + half : size_x - BAND - half] = mid[c, p, half:-half] + part[c, p]
-            whole[c, p, size_x - BAND - half : size_x - BAND] = mid[c, p, -half:] + second
-            whole[c, p, size_x - BAND :] = edge[c, p, BAND:]
-        copies.append(pltpu.make_async_copy(whole.at[c], out.at[0, c], sems.at[c]))
-        copies[-1].start()
+            low[c, p] = mid[c, p, :half] + first
+            high[c, p] = mid[c, p, -half:] + second
+        for k, (rows, start) in enumerate(((low, BAND), (high, size_x - BAND - half))):
+            copies.append(pltpu.make_async_copy(rows.at[c], out.at[0, c, :, pl.ds(start, half)], sems.at[2 * c + k]))
+            copies[-1].start()
     for copy in copies:
         copy.wait()
 
@@ -452,13 +474,14 @@
     edges = ((0, BAND + HALO), (size_x - BAND - HALO, size_x))
     inner = ((BAND - HALO, size_x - BAND + HALO),)
     keep = ((size_x - SHARED) // 2, (size_x + SHARED) // 2)
-    span = (keep[0] - HALO, keep[1] + HALO)
+    span = (keep[0] - HALO // 2, keep[1] + HALO // 2)
+    fetched = (keep[0] - HALO, keep[1] + HALO)
     rows = size_x - 2 * BAND
     edge_rows, inner_rows, span_rows = 2 * (BAND + HALO), rows + 2 * HALO, SHARED + 2 * HALO
-    packed_rows = span_rows // 2 + 8
+    packed_rows = (SHARED + HALO) // 2 + 4
 
     shared = pl.pallas_call(
-        functools.partial(share_kernel, span),
+        functools.partial(share_kernel, fetched, HALO // 2),
         out_shape=jax.ShapeDtypeStruct((7 * depth, packed_rows, size_y), jnp.float32),
         in_specs=[HBM] * 2,
         out_specs=VMEM,
@@ -470,8 +493,8 @@
         compiler_params=PARAMS,
         cost_estimate=cost(0),
     )(*(pltpu.with_memory_space_constraint(x, pltpu.HBM) for x in (seeds, material)))
+    shared, decay, coupling = after(shared, decay, coupling)
     table = table_rows(decay, coupling, size_y)
-    shared, table = after(shared, table)
     shared = swapped(shared, 2, tile_size)
     edge_near, edge_far, inner_near, inner_far = called(
         functools.partial(halo_pair_kernel, edges, inner, "sub"),
@@ -481,10 +504,11 @@
     edge_far = far_exchange(edge_far, sub_size, tile_size)
     inner_far = far_exchange(inner_far, sub_size, tile_size)
 
+    edge_far, decay, coupling = after(edge_far, decay, coupling)
     edge, corner, strip = called(
         functools.partial(edge_kernel, edges, "sub", sub_size, "tile"),
         [(6, depth, 2 * BAND, size_y), (6, depth, BAND, size_y), (6, depth, BAND // 2, size_y)],
-        table, seeds, material, edge_near, edge_far,
+        table_rows(decay, coupling, size_y), seeds, material, edge_near, edge_far,
     )
     corner = swapped(corner, 2, tile_size)
     strip = swapped(strip, 3, tile_size)
@@ -504,7 +528,7 @@
     )
     bands = swapped(bands, 2, tile_size)
 
-    corner, strip = after(corner, strip)
+    corner, strip, shared_near, shared_far = after(corner, strip, shared_near, shared_far)
     summed, send = called(
         functools.partial(corner_kernel, "tile"),
         [(6, depth, 2 * BAND, size_y), (6, depth, BAND + BAND // 2, size_y)],
@@ -518,14 +542,27 @@
     edge, = called(
         functools.partial(seam_kernel, "tile"), [(6, depth, 2 * BAND, size_y)], summed, got, strip
     )
+    half = (rows - SHARED) // 2
+    whole = jax.ShapeDtypeStruct(seeds.shape, jnp.float32)
+    early = pl.pallas_call(
+        early_kernel,
+        out_shape=whole,
+        in_specs=[VMEM] * 3,
+        out_specs=HBM,
+        scratch_shapes=[pltpu.VMEM((6, depth, SHARED, size_y), jnp.float32), pltpu.SemaphoreType.DMA((3,))],
+        compiler_params=PARAMS,
+        cost_estimate=cost(0),
+    )(edge, mid, part)
     return pl.pallas_call(
         last_kernel,
-        out_shape=jax.ShapeDtypeStruct(seeds.shape, jnp.float32),
-        in_specs=[VMEM] * 4,
+        out_shape=whole,
+        in_specs=[VMEM, VMEM, HBM],
         out_specs=HBM,
-        scratch_shapes=[pltpu.VMEM(seeds.shape[1:], jnp.float32), pltpu.SemaphoreType.DMA((6,))],
+        scratch_shapes=[pltpu.VMEM((6, depth, half, size_y), jnp.float32)] * 2 + [pltpu.SemaphoreType.DMA((12,))],
+        input_output_aliases={2: 0},
         compiler_params=PARAMS,
-    )(edge, mid, bands, part)
+        cost_estimate=cost(0),
+    )(mid, bands, early)
 
 
 def any_lattice(seeds, material, decay, coupling, sub_size, tile_size):

time: 33.9 us -> 35.2 us (1.038)
  waiting for transfers between devices: 13.6 us -> 9.34 us
  Pallas kernels: 7.69 us -> 11.9 us
  starting transfers between devices: 11.3 us -> 13.4 us
  other arithmetic: 0.88 us -> 0.15 us
    ppermute x3, waiting for transfers between devices: 10.3 us -> 2.58 us  [far_exchange(): return lax.ppermute(far, ('tile', 'sub'), pairs)]
    ppermute x5, waiting for transfers between devices: 3.31 us -> 6.76 us  [swapped(): lax.ppermute(value, 'tile', [(t, t ^ bits) for t in range(tile_size)])]
    pallas_call x7, Pallas kernels: 4.77 us -> 7.63 us  [called(): pl.pallas_call(kernel, out_shape=outs, in_specs=[VMEM] * len(operands), o...]
    ppermute x5, starting transfers between devices: 6.11 us -> 7.74 us  [swapped(): lax.ppermute(value, 'tile', [(t, t ^ bits) for t in range(tile_size)])]
    pallas_call x2 -> x3, Pallas kernels: 2.92 us -> 4.26 us  [the longest x1 2.22 us: two_by_two(): pl.pallas_call(functools.partial(share_kernel, fetched, HALO // 2), out_s...]
    concatenate x1 -> x2, other arithmetic: 0.88 us -> 0.15 us  [table_rows(): entries = jnp.concatenate([decay, coupling])]
    ppermute x3, starting transfers between devices: 4.52 us -> 5.2 us  [far_exchange(): return lax.ppermute(far, ('tile', 'sub'), pairs)]
  transfers between devices with their start and end apart: 11 -> 11, of which waited for: 4 -> 4; matrix products, arithmetic and copies ran while one was open for 0% -> 1% of each run, Pallas kernels for 14% -> 25%
where the time goes in v6:
time: 35.2 us; the launch traced here: 35.1 us
  starting transfers between devices  13.4 us (38%)
  Pallas kernels  11.9 us (34%)
  waiting for transfers between devices  9.34 us (27%)
    ppermute x5, starting transfers between devices, swapped(): lax.ppermute(value, 'tile', [(t, t ^ bits) for t in range(tile_size)])  7.74 us
    pallas_call x7, Pallas kernels, called(): pl.pallas_call(kernel, out_shape=outs, in_specs=[VMEM] * len(operands), o...  7.63 us
    ppermute x5, waiting for transfers between devices, swapped(): lax.ppermute(value, 'tile', [(t, t ^ bits) for t in range(tile_size)])  6.76 us
    ppermute x3, starting transfers between devices, far_exchange(): return lax.ppermute(far, ('tile', 'sub'), pairs)  5.2 us
    ppermute x3, waiting for transfers between devices, far_exchange(): return lax.ppermute(far, ('tile', 'sub'), pairs)  2.58 us
    pallas_call x1, Pallas kernels, two_by_two(): pl.pallas_call(functools.partial(share_kernel, fetched, HALO // 2), out_s...  2.22 us
    pallas_call x1, Pallas kernels, two_by_two(): pl.pallas_call(last_kernel, out_shape=whole, in_specs=[VMEM, VMEM, HBM],...  1.04 us
    pallas_call x1, Pallas kernels, two_by_two(): pl.pallas_call(early_kernel, out_shape=whole, in_specs=[VMEM] * 3, out_sp...  1 us
  transfers between devices with their start and end apart: 11, of which 4 were waited for; matrix products, arithmetic and copies ran while one was open for 1% of the time, Pallas kernels for 25%

profile of v6, /device:TPU:0, one launch (start us, length us, event | category | flops | bytes accessed | tf_op | source)
XLA Modules:
  0.0 35.1 jit_solution(7668738345720117576)
XLA Ops:
  0.0 2.2 %shard_map.46 = f32[14,48,128]{2,1,0:T(8,128)S(1)} custom-call(f32[1,6,2,256,128]{4,3,2,1,0:T(8,128)} %seeds.7, s32[1,2,256,128]{3,2,1,0:T(8,128)} %material.7), custom_call_target="tpu_custom_call" | custom-call | tf_op jit(solution)/shard_map/pallas_call | solution.py:483
  2.2 3.0 %collective-permute-start.1 = (f32[14,48,128]{2,1,0:T(8,128)S(1)}, f32[14,48,128]{2,1,0:T(8,128)S(1)}, u32[]{:S(2)}, u32[]{:S(2)}) collective-permute-start(f32[14,48,128]{2,1,0:T(8,128)S(1)} %shard_map.46), channel_id=1, source_target_pairs={{0,16},{8,24},{16,0},{24,8},{1,17},{9,25},{17,1},{25,9},{2,18},{10... | collective-permute-start | bytes 1032200 | tf_op jit(solution)/shard_map/ppermute | solution.py:460
  5.3 0.1 pad_maximum_fusion
  5.4 0.1 broadcast_in_dim.4.table
  5.4 0.8 %shard_map.47 = (f32[5,80,128]{2,1,0:T(8,128)S(1)}, f32[5,80,128]{2,1,0:T(8,128)S(1)}, f32[5,208,128]{2,1,0:T(8,128)S(1)}, f32[5,208,128]{2,1,0:T(8,128)S(1)}) custom-call(f32[8,128]{1,0:T(8,128)S(1)} %broadcast_in_dim.4.table, f32[1,6,2,256,128]{4,3,2,1,0:T(8,128)S(1)} %copy-done, s32[1,2,256,128]{3,2,1,0:T(8,128)S(1)} %copy-done.1), custom_call_target="tpu_custom_call" | custom-call | tf_op jit(solution)/shard_map/pallas_call | solution.py:426
  6.2 1.6 %collective-permute-start.4 = (f32[5,80,128]{2,1,0:T(8,128)S(1)}, f32[5,80,128]{2,1,0:T(8,128)S(1)}, u32[]{:S(2)}, u32[]{:S(2)}) collective-permute-start(f32[5,80,128]{2,1,0:T(8,128)S(1)} %get-tuple-element.39), channel_id=1, source_target_pairs={{0,8},{1,2},{2,1},{3,4},{4,3},{5,6},{6,5},{7,15},{8,0},{9,10},{10,... | collective-permute-start | bytes 614408 | tf_op jit(solution)/shard_map/ppermute | solution.py:456
  7.8 0.2 collective-permute-start.5
  8.0 0.3 collective-permute-start
  8.3 1.2 %collective-permute-start.2 = (f32[5,208,128]{2,1,0:T(8,128)S(1)}, f32[5,208,128]{2,1,0:T(8,128)S(1)}, u32[]{:S(2)}, u32[]{:S(2)}) collective-permute-start(f32[5,208,128]{2,1,0:T(8,128)S(1)} %get-tuple-element.35), channel_id=1, source_target_pairs={{0,8},{1,2},{2,1},{3,4},{4,3},{5,6},{6,5},{7,15},{8,0},{9,10},{10,... | collective-permute-start | bytes 1597448 | tf_op jit(solution)/shard_map/ppermute | solution.py:456
  9.5 2.6 %collective-permute-done.4.far = f32[5,80,128]{2,1,0:T(8,128)S(1)} collective-permute-done((f32[5,80,128]{2,1,0:T(8,128)S(1)}, f32[5,80,128]{2,1,0:T(8,128)S(1)}, u32[]{:S(2)}, u32[]{:S(2)}) %collective-permute-start.4) | collective-permute-done | bytes 204832 | tf_op jit(solution)/shard_map/ppermute | solution.py:456
  12.0 0.1 pad_maximum_fusion.1
  12.1 0.1 broadcast_in_dim.5.table
  12.2 0.7 %shard_map.50 = (f32[6,2,64,128]{3,2,1,0:T(8,128)S(1)}, f32[6,2,32,128]{3,2,1,0:T(8,128)S(1)}, f32[6,2,16,128]{3,2,1,0:T(8,128)S(1)}) custom-call(f32[8,128]{1,0:T(8,128)S(1)} %broadcast_in_dim.5.table, f32[1,6,2,256,128]{4,3,2,1,0:T(8,128)S(1)} %copy-done, s32[1,2,256,128]{3,2,1,0:T(8,128)S(1)} %copy-done.1, f32[5,80,128]{2,1,0:T(8,128)S(1)} %collective-permute-done.5.near, ...), custom_call_target="tpu_custom_call" | custom-call | tf_op jit(solution)/shard_map/pallas_call | solution.py:426
  12.8 0.1 collective-permute-start.6
  12.9 0.4 %collective-permute-done.1.shared = f32[14,48,128]{2,1,0:T(8,128)S(1)} collective-permute-done((f32[14,48,128]{2,1,0:T(8,128)S(1)}, f32[14,48,128]{2,1,0:T(8,128)S(1)}, u32[]{:S(2)}, u32[]{:S(2)}) %collective-permute-start.1) | collective-permute-done | bytes 344096 | tf_op jit(solution)/shard_map/ppermute | solution.py:460
  13.3 2.0 %shard_map.48 = (f32[5,48,128]{2,1,0:T(8,128)S(1)}, f32[5,48,128]{2,1,0:T(8,128)S(1)}) custom-call(f32[8,128]{1,0:T(8,128)S(1)} %broadcast_in_dim.4.table, f32[14,48,128]{2,1,0:T(8,128)S(1)} %collective-permute-done.1.shared), custom_call_target="tpu_custom_call" | custom-call | flops 10000000000 | tf_op jit(solution)/shard_map/pallas_call | solution.py:426
  15.3 2.5 %collective-permute-start.9 = (f32[5,48,128]{2,1,0:T(8,128)S(1)}, f32[5,48,128]{2,1,0:T(8,128)S(1)}, u32[]{:S(2)}, u32[]{:S(2)}) collective-permute-start(f32[5,48,128]{2,1,0:T(8,128)S(1)} %get-tuple-element.48), channel_id=1, source_target_pairs={{0,7},{1,2},{2,1},{3,4},{4,3},{5,6},{6,5},{7,0},{8,15},{9,10},{10,... | collective-permute-start | bytes 368648 | tf_op jit(solution)/shard_map/ppermute | solution.py:456
  17.8 0.0 collective-permute-done.2.far
  17.8 0.0 collective-permute-start.8
  17.8 2.4 %collective-permute-start.7 = (f32[6,2,16,128]{3,2,1,0:T(8,128)S(1)}, f32[6,2,16,128]{3,2,1,0:T(8,128)S(1)}, u32[]{:S(2)}, u32[]{:S(2)}) collective-permute-start(f32[6,2,16,128]{3,2,1,0:T(8,128)S(1)} %get-tuple-element.46), channel_id=1, source_target_pairs={{0,24},{8,16},{16,8},{24,0},{1,25},{9,17},{17,9},{25,1},{2,26},{10... | collective-permute-start | bytes 294920 | tf_op jit(solution)/shard_map/ppermute | solution.py:460
  20.2 0.0 collective-permute-done.near
  20.2 1.2 %shard_map.49 = (f32[6,2,192,128]{3,2,1,0:T(8,128)S(1)}, f32[6,2,56,128]{3,2,1,0:T(8,128)S(1)}) custom-call(f32[8,128]{1,0:T(8,128)S(1)} %broadcast_in_dim.4.table, f32[1,6,2,256,128]{4,3,2,1,0:T(8,128)S(1)} %copy-done, s32[1,2,256,128]{3,2,1,0:T(8,128)S(1)} %copy-done.1, f32[5,208,128]{2,1,0:T(8,128)S(1)} %collective-permute-done.near, ...), custom_call_target="tpu_custom_call" | custom-call | tf_op jit(solution)/shard_map/pallas_call | solution.py:426
  21.5 0.6 %collective-permute-start.3 = (f32[6,2,56,128]{3,2,1,0:T(8,128)S(1)}, f32[6,2,56,128]{3,2,1,0:T(8,128)S(1)}, u32[]{:S(2)}, u32[]{:S(2)}) collective-permute-start(f32[6,2,56,128]{3,2,1,0:T(8,128)S(1)} %get-tuple-element.38), channel_id=1, source_target_pairs={{0,16},{8,24},{16,0},{24,8},{1,17},{9,25},{17,1},{25,9},{2,18},{10... | collective-permute-start | bytes 1032200 | tf_op jit(solution)/shard_map/ppermute | solution.py:460
  22.1 1.8 %collective-permute-done.7.strip = f32[6,2,16,128]{3,2,1,0:T(8,128)S(1)} collective-permute-done((f32[6,2,16,128]{3,2,1,0:T(8,128)S(1)}, f32[6,2,16,128]{3,2,1,0:T(8,128)S(1)}, u32[]{:S(2)}, u32[]{:S(2)}) %collective-permute-start.7) | collective-permute-done | bytes 98336 | tf_op jit(solution)/shard_map/ppermute | solution.py:460
  23.9 0.0 collective-permute-done.6.corner
  23.9 0.3 shard_map.51
  24.2 1.6 %collective-permute-start.10 = (f32[6,2,48,128]{3,2,1,0:T(8,128)S(1)}, f32[6,2,48,128]{3,2,1,0:T(8,128)S(1)}, u32[]{:S(2)}, u32[]{:S(2)}) collective-permute-start(f32[6,2,48,128]{3,2,1,0:T(8,128)S(1)} %get-tuple-element.51), channel_id=1, source_target_pairs={{0,8},{8,0},{16,24},{24,16},{1,9},{9,1},{17,25},{25,17},{2,10},{10... | collective-permute-start | bytes 884744 | tf_op jit(solution)/shard_map/ppermute | solution.py:460
  25.7 2.6 %shard_map.53.part = f32[6,2,80,128]{3,2,1,0:T(8,128)S(1)} custom-call(f32[8,128]{1,0:T(8,128)S(1)} %broadcast_in_dim.4.table, f32[14,48,128]{2,1,0:T(8,128)S(1)} %collective-permute-done.1.shared, f32[5,48,128]{2,1,0:T(8,128)S(1)} %collective-permute-done.8.near, f32[5,48,128]{2,1,0:T(8,128)S(1)} %collective-permute-done.9.far), custom_call_target="tpu_custom_call" | custom-call | tf_op jit(solution)/shard_map/pallas_call | solution.py:426
  28.4 4.5 %collective-permute-done.10.got = f32[6,2,48,128]{3,2,1,0:T(8,128)S(1)} collective-permute-done((f32[6,2,48,128]{3,2,1,0:T(8,128)S(1)}, f32[6,2,48,128]{3,2,1,0:T(8,128)S(1)}, u32[]{:S(2)}, u32[]{:S(2)}) %collective-permute-start.10) | collective-permute-done | bytes 294944 | tf_op jit(solution)/shard_map/ppermute | solution.py:460
  32.8 0.1 shard_map.52.edge
  33.0 1.0 %shard_map.54._ = f32[1,6,2,256,128]{4,3,2,1,0:T(8,128)} custom-call(f32[6,2,64,128]{3,2,1,0:T(8,128)S(1)} %shard_map.52.edge, f32[6,2,192,128]{3,2,1,0:T(8,128)S(1)} %get-tuple-element.37.mid, f32[6,2,80,128]{3,2,1,0:T(8,128)S(1)} %shard_map.53.part), custom_call_target="tpu_custom_call" | custom-call | tf_op jit(solution)/shard_map/pallas_call | solution.py:547
  34.0 1.0 %shard_map.55 = f32[1,6,2,256,128]{4,3,2,1,0:T(8,128)} custom-call(f32[6,2,192,128]{3,2,1,0:T(8,128)S(1)} %get-tuple-element.37.mid, f32[6,2,56,128]{3,2,1,0:T(8,128)S(1)} %collective-permute-done.3.bands, f32[1,6,2,256,128]{4,3,2,1,0:T(8,128)} %shard_map.54._), custom_call_target="tpu_custom_call", output_to_operand_aliasing={{}: (2, {})} | custom-call | tf_op jit(solution)/shard_map/pallas_call | solution.py:556
  (12 shorter events, 0.0 us)
Async XLA Ops:
  0.0 5.4 %copy-start.1 = (s32[1,2,256,128]{3,2,1,0:T(8,128)S(1)}, s32[1,2,256,128]{3,2,1,0:T(8,128)}, u32[]{:S(2)}) copy-start(s32[1,2,256,128]{3,2,1,0:T(8,128)} %material.7) | copy-start | bytes 786436
  0.0 5.4 %copy-start = (f32[1,6,2,256,128]{4,3,2,1,0:T(8,128)S(1)}, f32[1,6,2,256,128]{4,3,2,1,0:T(8,128)}, u32[]{:S(2)}) copy-start(f32[1,6,2,256,128]{4,3,2,1,0:T(8,128)} %seeds.7) | copy-start | bytes 4718596
  0.0 5.3 %copy-start.2 = (f32[4]{0:T(128)S(1)}, f32[4]{0:T(128)}, u32[]{:S(2)}) copy-start(f32[4]{0:T(128)} %param.7) | copy-start | bytes 52
  0.0 5.3 %copy-start.3 = (f32[4]{0:T(128)S(1)}, f32[4]{0:T(128)}, u32[]{:S(2)}) copy-start(f32[4]{0:T(128)} %param.6) | copy-start | bytes 52
  2.2 11.1 %collective-permute-start.1 = (f32[14,48,128]{2,1,0:T(8,128)S(1)}, f32[14,48,128]{2,1,0:T(8,128)S(1)}, u32[]{:S(2)}, u32[]{:S(2)}) collective-permute-start(f32[14,48,128]{2,1,0:T(8,128)S(1)} %shard_map.46), channel_id=1, source_target_pairs={{0,16},{8,24},{16,0},{24,8},{1,17},{9,25},{17,1},{25,9},{2,18},{10... | collective-permute-start | bytes 1032200 | tf_op jit(solution)/shard_map/ppermute | solution.py:460
  6.2 5.8 %collective-permute-start.4 = (f32[5,80,128]{2,1,0:T(8,128)S(1)}, f32[5,80,128]{2,1,0:T(8,128)S(1)}, u32[]{:S(2)}, u32[]{:S(2)}) collective-permute-start(f32[5,80,128]{2,1,0:T(8,128)S(1)} %get-tuple-element.39), channel_id=1, source_target_pairs={{0,8},{1,2},{2,1},{3,4},{4,3},{5,6},{6,5},{7,15},{8,0},{9,10},{10,... | collective-permute-start | bytes 614408 | tf_op jit(solution)/shard_map/ppermute | solution.py:456
  7.8 4.3 %collective-permute-start.5 = (f32[5,80,128]{2,1,0:T(8,128)S(1)}, f32[5,80,128]{2,1,0:T(8,128)S(1)}, u32[]{:S(2)}, u32[]{:S(2)}) collective-permute-start(f32[5,80,128]{2,1,0:T(8,128)S(1)} %get-tuple-element.42), channel_id=1, source_target_pairs={{0,1},{1,0},{2,3},{3,2},{4,5},{5,4},{6,7},{7,6},{8,9},{9,8},{10,11... | collective-permute-start | bytes 614408 | tf_op jit(solution)/shard_map/ppermute | solution.py:441
  8.0 12.3 %collective-permute-start = (f32[5,208,128]{2,1,0:T(8,128)S(1)}, f32[5,208,128]{2,1,0:T(8,128)S(1)}, u32[]{:S(2)}, u32[]{:S(2)}) collective-permute-start(f32[5,208,128]{2,1,0:T(8,128)S(1)} %get-tuple-element.32), channel_id=1, source_target_pairs={{0,1},{1,0},{2,3},{3,2},{4,5},{5,4},{6,7},{7,6},{8,9},{9,8},{10,11... | collective-permute-start | bytes 1597448 | tf_op jit(solution)/shard_map/ppermute | solution.py:441
  8.3 9.5 %collective-permute-start.2 = (f32[5,208,128]{2,1,0:T(8,128)S(1)}, f32[5,208,128]{2,1,0:T(8,128)S(1)}, u32[]{:S(2)}, u32[]{:S(2)}) collective-permute-start(f32[5,208,128]{2,1,0:T(8,128)S(1)} %get-tuple-element.35), channel_id=1, source_target_pairs={{0,8},{1,2},{2,1},{3,4},{4,3},{5,6},{6,5},{7,15},{8,0},{9,10},{10,... | collective-permute-start | bytes 1597448 | tf_op jit(solution)/shard_map/ppermute | solution.py:456
  12.8 11.1 %collective-permute-start.6 = (f32[6,2,32,128]{3,2,1,0:T(8,128)S(1)}, f32[6,2,32,128]{3,2,1,0:T(8,128)S(1)}, u32[]{:S(2)}, u32[]{:S(2)}) collective-permute-start(f32[6,2,32,128]{3,2,1,0:T(8,128)S(1)} %get-tuple-element.45), channel_id=1, source_target_pairs={{0,16},{8,24},{16,0},{24,8},{1,17},{9,25},{17,1},{25,9},{2,18},{10... | collective-permute-start | bytes 589832 | tf_op jit(solution)/shard_map/ppermute | solution.py:460
  15.3 8.6 %collective-permute-start.9 = (f32[5,48,128]{2,1,0:T(8,128)S(1)}, f32[5,48,128]{2,1,0:T(8,128)S(1)}, u32[]{:S(2)}, u32[]{:S(2)}) collective-permute-start(f32[5,48,128]{2,1,0:T(8,128)S(1)} %get-tuple-element.48), channel_id=1, source_target_pairs={{0,7},{1,2},{2,1},{3,4},{4,3},{5,6},{6,5},{7,0},{8,15},{9,10},{10,... | collective-permute-start | bytes 368648 | tf_op jit(solution)/shard_map/ppermute | solution.py:456
  17.8 6.1 %collective-permute-start.8 = (f32[5,48,128]{2,1,0:T(8,128)S(1)}, f32[5,48,128]{2,1,0:T(8,128)S(1)}, u32[]{:S(2)}, u32[]{:S(2)}) collective-permute-start(f32[5,48,128]{2,1,0:T(8,128)S(1)} %get-tuple-element.47), channel_id=1, source_target_pairs={{0,1},{1,0},{2,3},{3,2},{4,5},{5,4},{6,7},{7,6},{8,9},{9,8},{10,11... | collective-permute-start | bytes 368648 | tf_op jit(solution)/shard_map/ppermute | solution.py:441
  17.8 6.1 %collective-permute-start.7 = (f32[6,2,16,128]{3,2,1,0:T(8,128)S(1)}, f32[6,2,16,128]{3,2,1,0:T(8,128)S(1)}, u32[]{:S(2)}, u32[]{:S(2)}) collective-permute-start(f32[6,2,16,128]{3,2,1,0:T(8,128)S(1)} %get-tuple-element.46), channel_id=1, source_target_pairs={{0,24},{8,16},{16,8},{24,0},{1,25},{9,17},{17,9},{25,1},{2,26},{10... | collective-permute-start | bytes 294920 | tf_op jit(solution)/shard_map/ppermute | solution.py:460
  21.5 12.5 %collective-permute-start.3 = (f32[6,2,56,128]{3,2,1,0:T(8,128)S(1)}, f32[6,2,56,128]{3,2,1,0:T(8,128)S(1)}, u32[]{:S(2)}, u32[]{:S(2)}) collective-permute-start(f32[6,2,56,128]{3,2,1,0:T(8,128)S(1)} %get-tuple-element.38), channel_id=1, source_target_pairs={{0,16},{8,24},{16,0},{24,8},{1,17},{9,25},{17,1},{25,9},{2,18},{10... | collective-permute-start | bytes 1032200 | tf_op jit(solution)/shard_map/ppermute | solution.py:460
  24.2 8.7 %collective-permute-start.10 = (f32[6,2,48,128]{3,2,1,0:T(8,128)S(1)}, f32[6,2,48,128]{3,2,1,0:T(8,128)S(1)}, u32[]{:S(2)}, u32[]{:S(2)}) collective-permute-start(f32[6,2,48,128]{3,2,1,0:T(8,128)S(1)} %get-tuple-element.51), channel_id=1, source_target_pairs={{0,8},{8,0},{16,24},{24,16},{1,9},{9,1},{17,25},{25,17},{2,10},{10... | collective-permute-start | bytes 884744 | tf_op jit(solution)/shard_map/ppermute | solution.py:460

commit v7 on v6

--- a/solution.py
+++ b/solution.py
@@ -14,7 +14,7 @@
 PLANES = 5
 REACH = 2
 SHARED = 80
-LARGE, SMALL = 10**10, 6 * 10**8
+LARGE, MEDIUM, SMALL = 10**10, 3 * 10**9, 2 * 10**8
 
 magnetic_coeff = 0.5
 
@@ -212,39 +212,54 @@
     return first, second
 
 
-def side_lanes(shape, groups, apart):
-    lane = lane_of(shape)
-    width = REACH * groups
-    return (lane < width) | ((lane >= apart) & (lane < apart + width))
+def low_rows(shape):
+    return row_of(shape) < 4
 
 
 def bands_packed(block):
     rows, lanes = block.shape
-    half, groups, apart = rows // 2, rows // 8, lanes - 2 * BAND - REACH
+    count = rows // 2 + 4
+    width = REACH * (rows // 8)
     side = jnp.zeros((8, lanes), block.dtype)
-    for g in range(groups):
-        piece = pltpu.roll(block[8 * g : 8 * g + 8], (REACH * g - BAND) % lanes, 1)
-        side = jnp.where(side_lanes(side.shape, g, apart), side, piece)
-    upper, lower = side[:4], pltpu.roll(side[4:], REACH * groups, 1)
-    side = jnp.where(side_lanes(upper.shape, groups, apart), upper, lower)
-    return jnp.concatenate([y_packed(block[:half], block[half:]), side], axis=0)
+    lane = lane_of(side.shape)
+    high = lanes - BAND
+    for g in range(rows // 8):
+        at = BAND + REACH * (g + 1)
+        piece = pltpu.roll(block[8 * g : 8 * g + 8], REACH * (g + 1), 1)
+        here = ((lane >= at) & (lane < at + REACH)) | (
+            (lane >= at + high - BAND - REACH) & (lane < at + high - BAND)
+        )
+        side = jnp.where(here, piece, side)
+    other = pltpu.roll(pltpu.roll(side, 4, 0), width + REACH, 1)
+    own = ((lane >= BAND) & (lane < BAND + REACH + width)) | ((lane >= high) & (lane < high + width))
+    side = jnp.where(own, side, other)
+    middle = (lane >= BAND) & (lane < high)
+    packed = y_packed(block[:count], block[rows - count :])
+    first = jnp.where(low_rows(side.shape) & middle, side, packed[:8])
+    last = jnp.where(low_rows(side.shape) | middle, packed[count - 8 :], side)
+    return jnp.concatenate([first, packed[8 : count - 8], last], axis=0)
 
 
 def bands_unpacked(packed):
-    half, lanes = packed.shape[0] - 4, packed.shape[1]
-    groups = half // 4
-    main, side = packed[:half], packed[half:]
-    lane = lane_of(main.shape)
-    middle = (lane >= BAND) & (lane < lanes - BAND)
-    block = jnp.concatenate([jnp.where(middle, 0.0, main), jnp.where(middle, 0.0, middle_out(main))], axis=0)
-    side = jnp.concatenate([side, pltpu.roll(side, lanes - REACH * groups, 1)], axis=0)
-    lane = lane_of(side.shape)
-    beside = ((lane >= BAND) & (lane < BAND + REACH)) | ((lane >= lanes - BAND - REACH) & (lane < lanes - BAND))
-    pieces = []
-    for g in range(groups):
-        moved = pltpu.roll(side, (BAND - REACH * g) % lanes, 1)
-        pieces.append(jnp.where(beside, moved, block[8 * g : 8 * g + 8]))
-    return jnp.concatenate(pieces, axis=0)
+    count, lanes = packed.shape
+    rows = 2 * count - 8
+    width = REACH * (rows // 8)
+    high = lanes - BAND
+    first, last = packed[:8], packed[count - 8 :]
+    low = low_rows(first.shape)
+    lane = lane_of(first.shape)
+    middle = (lane >= BAND) & (lane < high)
+    side = jnp.where(low, first, last)
+    other = pltpu.roll(pltpu.roll(side, 4, 0), lanes - width - REACH, 1)
+    side = jnp.where(low == middle, side, other)
+    beside = ((lane >= BAND) & (lane < BAND + REACH)) | ((lane >= high - REACH) & (lane < high))
+    moved = [pltpu.roll(packed[at : at + 8], lanes // 2, 1) for at in range(0, count, 8)]
+    pieces = [packed[at : at + 8] for at in range(0, count - 8, 8)] + [jnp.where(low, last, moved[0])] + moved[1:]
+    result = []
+    for g, piece in enumerate(pieces):
+        near_by = pltpu.roll(side, lanes - REACH * (g + 1), 1)
+        result.append(jnp.where(middle, jnp.where(beside, near_by, 0.0), piece))
+    return jnp.concatenate(result, axis=0)
 
 
 def share_kernel(span, skip, seeds, material, shared, held, labels, sems):
@@ -337,9 +352,9 @@
     return jnp.where(middle, 0.0, jnp.where(lane < BAND, a, b))
 
 
-def shared_kernel(span, keep, size_x, sub, sub_size, table, shared, near, far, part):
+def shared_kernel(span, size_x, sub, sub_size, table, shared, near, far, part):
     planes = final_fields(shared_fields(table, shared), near, far, sub, sub_size, bands_unpacked)
-    found, = weighted(planes, (span,), (keep,), size_x, part.shape[3])
+    found, = weighted(planes, (span,), (span,), size_x, part.shape[3])
     for c in range(part.shape[0]):
         for p in range(part.shape[1]):
             part[c, p] = y_swapped(found[c][p])
@@ -379,12 +394,14 @@
 
 def early_kernel(edge, mid, part, out, whole, sems):
     size_x = out.shape[3]
-    start = (size_x - part.shape[2]) // 2
-    rows = pl.ds(start, part.shape[2])
+    skip = HALO // 2
+    count = part.shape[2] - 2 * skip
+    start = (size_x - count) // 2
+    rows = pl.ds(start, count)
     low, high = pl.ds(0, BAND), pl.ds(size_x - BAND, BAND)
     for c in range(mid.shape[0]):
         for p in range(mid.shape[1]):
-            whole[c, p] = mid[c, p, start - BAND : start - BAND + part.shape[2]] + part[c, p]
+            whole[c, p] = mid[c, p, start - BAND : start - BAND + count] + part[c, p, skip : skip + count]
     copies = [
         pltpu.make_async_copy(whole, out.at[0, :, :, rows], sems.at[0]),
         pltpu.make_async_copy(edge.at[:, :, pl.ds(0, BAND)], out.at[0, :, :, low], sems.at[1]),
@@ -528,7 +545,7 @@
     )
     bands = swapped(bands, 2, tile_size)
 
-    corner, strip, shared_near, shared_far = after(corner, strip, shared_near, shared_far)
+    corner, strip, mid = after(corner, strip, mid)
     summed, send = called(
         functools.partial(corner_kernel, "tile"),
         [(6, depth, 2 * BAND, size_y), (6, depth, BAND + BAND // 2, size_y)],
@@ -536,8 +553,8 @@
     )
     got = swapped(send, 1, tile_size)
     part, = called(
-        functools.partial(shared_kernel, span, keep, size_x, "sub", sub_size), [(6, depth, SHARED, size_y)],
-        table, shared, shared_near, shared_far,
+        functools.partial(shared_kernel, span, size_x, "sub", sub_size),
+        [(6, depth, SHARED + HALO, size_y)], table, shared, shared_near, shared_far, flops=MEDIUM,
     )
     edge, = called(
         functools.partial(seam_kernel, "tile"), [(6, depth, 2 * BAND, size_y)], summed, got, strip

time: 35.2 us -> 33.4 us (0.949)
  starting transfers between devices: 13.4 us -> 12 us
    ppermute x5, waiting for transfers between devices: 6.76 us -> 5.1 us  [swapped(): lax.ppermute(value, 'tile', [(t, t ^ bits) for t in range(tile_size)])]
    ppermute x3, waiting for transfers between devices: 2.58 us -> 4.11 us  [far_exchange(): return lax.ppermute(far, ('tile', 'sub'), pairs)]
    ppermute x3, starting transfers between devices: 5.2 us -> 4.15 us  [far_exchange(): return lax.ppermute(far, ('tile', 'sub'), pairs)]
    ppermute x5, starting transfers between devices: 7.74 us -> 7.31 us  [swapped(): lax.ppermute(value, 'tile', [(t, t ^ bits) for t in range(tile_size)])]
where the time goes in v7:
time: 33.4 us; the launch traced here: 33.2 us
  starting transfers between devices  12 us (36%)
  Pallas kernels  11.6 us (35%)
  waiting for transfers between devices  9.21 us (28%)
    pallas_call x7, Pallas kernels, called(): pl.pallas_call(kernel, out_shape=outs, in_specs=[VMEM] * len(operands), o...  7.39 us
    ppermute x5, starting transfers between devices, swapped(): lax.ppermute(value, 'tile', [(t, t ^ bits) for t in range(tile_size)])  7.31 us
    ppermute x5, waiting for transfers between devices, swapped(): lax.ppermute(value, 'tile', [(t, t ^ bits) for t in range(tile_size)])  5.1 us
    ppermute x3, starting transfers between devices, far_exchange(): return lax.ppermute(far, ('tile', 'sub'), pairs)  4.15 us
    ppermute x3, waiting for transfers between devices, far_exchange(): return lax.ppermute(far, ('tile', 'sub'), pairs)  4.11 us
    pallas_call x1, Pallas kernels, two_by_two(): pl.pallas_call(functools.partial(share_kernel, fetched, HALO // 2), out_s...  2.22 us
    pallas_call x1, Pallas kernels, two_by_two(): pl.pallas_call(last_kernel, out_shape=whole, in_specs=[VMEM, VMEM, HBM],...  1.04 us
    pallas_call x1, Pallas kernels, two_by_two(): pl.pallas_call(early_kernel, out_shape=whole, in_specs=[VMEM] * 3, out_sp...  1 us
  transfers between devices with their start and end apart: 11, of which 4 were waited for; matrix products, arithmetic and copies ran while one was open for 1% of the time, Pallas kernels for 25%

profile of v7, /device:TPU:0, one launch (start us, length us, event | category | flops | bytes accessed | tf_op | source)
XLA Modules:
  0.0 33.2 jit_solution(5582437960344596756)
XLA Ops:
  0.0 2.2 %shard_map.46 = f32[14,48,128]{2,1,0:T(8,128)S(1)} custom-call(f32[1,6,2,256,128]{4,3,2,1,0:T(8,128)} %seeds.7, s32[1,2,256,128]{3,2,1,0:T(8,128)} %material.7), custom_call_target="tpu_custom_call" | custom-call | tf_op jit(solution)/shard_map/pallas_call | solution.py:500
  2.2 3.0 %collective-permute-start.5 = (f32[14,48,128]{2,1,0:T(8,128)S(1)}, f32[14,48,128]{2,1,0:T(8,128)S(1)}, u32[]{:S(2)}, u32[]{:S(2)}) collective-permute-start(f32[14,48,128]{2,1,0:T(8,128)S(1)} %shard_map.46), channel_id=1, source_target_pairs={{0,16},{8,24},{16,0},{24,8},{1,17},{9,25},{17,1},{25,9},{2,18},{10... | collective-permute-start | bytes 1032200 | tf_op jit(solution)/shard_map/ppermute | solution.py:477
  5.3 0.1 pad_maximum_fusion
  5.4 0.1 broadcast_in_dim.4.table
  5.4 0.8 %shard_map.47 = (f32[5,80,128]{2,1,0:T(8,128)S(1)}, f32[5,80,128]{2,1,0:T(8,128)S(1)}, f32[5,208,128]{2,1,0:T(8,128)S(1)}, f32[5,208,128]{2,1,0:T(8,128)S(1)}) custom-call(f32[8,128]{1,0:T(8,128)S(1)} %broadcast_in_dim.4.table, f32[1,6,2,256,128]{4,3,2,1,0:T(8,128)S(1)} %copy-done, s32[1,2,256,128]{3,2,1,0:T(8,128)S(1)} %copy-done.1), custom_call_target="tpu_custom_call" | custom-call | tf_op jit(solution)/shard_map/pallas_call | solution.py:443
  6.2 1.6 %collective-permute-start = (f32[5,80,128]{2,1,0:T(8,128)S(1)}, f32[5,80,128]{2,1,0:T(8,128)S(1)}, u32[]{:S(2)}, u32[]{:S(2)}) collective-permute-start(f32[5,80,128]{2,1,0:T(8,128)S(1)} %get-tuple-element.31), channel_id=1, source_target_pairs={{0,8},{1,2},{2,1},{3,4},{4,3},{5,6},{6,5},{7,15},{8,0},{9,10},{10,... | collective-permute-start | bytes 614408 | tf_op jit(solution)/shard_map/ppermute | solution.py:473
  7.8 0.2 collective-permute-start.1
  8.0 0.3 collective-permute-start.4
  8.3 1.2 %collective-permute-start.6 = (f32[5,208,128]{2,1,0:T(8,128)S(1)}, f32[5,208,128]{2,1,0:T(8,128)S(1)}, u32[]{:S(2)}, u32[]{:S(2)}) collective-permute-start(f32[5,208,128]{2,1,0:T(8,128)S(1)} %get-tuple-element.41), channel_id=1, source_target_pairs={{0,8},{1,2},{2,1},{3,4},{4,3},{5,6},{6,5},{7,15},{8,0},{9,10},{10,... | collective-permute-start | bytes 1597448 | tf_op jit(solution)/shard_map/ppermute | solution.py:473
  9.5 2.6 %collective-permute-done.far = f32[5,80,128]{2,1,0:T(8,128)S(1)} collective-permute-done((f32[5,80,128]{2,1,0:T(8,128)S(1)}, f32[5,80,128]{2,1,0:T(8,128)S(1)}, u32[]{:S(2)}, u32[]{:S(2)}) %collective-permute-start) | collective-permute-done | bytes 204832 | tf_op jit(solution)/shard_map/ppermute | solution.py:473
  12.0 0.1 pad_maximum_fusion.1
  12.1 0.0 collective-permute-done.1.near
  12.1 0.1 broadcast_in_dim.5.table
  12.2 0.6 %shard_map.48 = (f32[6,2,64,128]{3,2,1,0:T(8,128)S(1)}, f32[6,2,32,128]{3,2,1,0:T(8,128)S(1)}, f32[6,2,16,128]{3,2,1,0:T(8,128)S(1)}) custom-call(f32[8,128]{1,0:T(8,128)S(1)} %broadcast_in_dim.5.table, f32[1,6,2,256,128]{4,3,2,1,0:T(8,128)S(1)} %copy-done, s32[1,2,256,128]{3,2,1,0:T(8,128)S(1)} %copy-done.1, f32[5,80,128]{2,1,0:T(8,128)S(1)} %collective-permute-done.1.near, ...), custom_call_target="tpu_custom_call" | custom-call | tf_op jit(solution)/shard_map/pallas_call | solution.py:443
  12.8 1.5 %collective-permute-start.3 = (f32[6,2,16,128]{3,2,1,0:T(8,128)S(1)}, f32[6,2,16,128]{3,2,1,0:T(8,128)S(1)}, u32[]{:S(2)}, u32[]{:S(2)}) collective-permute-start(f32[6,2,16,128]{3,2,1,0:T(8,128)S(1)} %get-tuple-element.37), channel_id=1, source_target_pairs={{0,24},{8,16},{16,8},{24,0},{1,25},{9,17},{17,9},{25,1},{2,26},{10... | collective-permute-start | bytes 294920 | tf_op jit(solution)/shard_map/ppermute | solution.py:477
  14.3 1.5 %collective-permute-start.2 = (f32[6,2,32,128]{3,2,1,0:T(8,128)S(1)}, f32[6,2,32,128]{3,2,1,0:T(8,128)S(1)}, u32[]{:S(2)}, u32[]{:S(2)}) collective-permute-start(f32[6,2,32,128]{3,2,1,0:T(8,128)S(1)} %get-tuple-element.36), channel_id=1, source_target_pairs={{0,16},{8,24},{16,0},{24,8},{1,17},{9,25},{17,1},{25,9},{2,18},{10... | collective-permute-start | bytes 589832 | tf_op jit(solution)/shard_map/ppermute | solution.py:477
  15.8 1.9 %shard_map.49 = (f32[5,48,128]{2,1,0:T(8,128)S(1)}, f32[5,48,128]{2,1,0:T(8,128)S(1)}) custom-call(f32[8,128]{1,0:T(8,128)S(1)} %broadcast_in_dim.4.table, f32[14,48,128]{2,1,0:T(8,128)S(1)} %collective-permute-done.5.shared), custom_call_target="tpu_custom_call" | custom-call | flops 10000000000 | tf_op jit(solution)/shard_map/pallas_call | solution.py:443
  17.7 1.4 %collective-permute-start.10 = (f32[5,48,128]{2,1,0:T(8,128)S(1)}, f32[5,48,128]{2,1,0:T(8,128)S(1)}, u32[]{:S(2)}, u32[]{:S(2)}) collective-permute-start(f32[5,48,128]{2,1,0:T(8,128)S(1)} %get-tuple-element.52), channel_id=1, source_target_pairs={{0,7},{1,2},{2,1},{3,4},{4,3},{5,6},{6,5},{7,0},{8,15},{9,10},{10,... | collective-permute-start | bytes 368648 | tf_op jit(solution)/shard_map/ppermute | solution.py:473
  19.1 0.0 collective-permute-done.6.far
  19.2 0.0 collective-permute-start.9
  19.2 1.2 %shard_map.50 = (f32[6,2,192,128]{3,2,1,0:T(8,128)S(1)}, f32[6,2,56,128]{3,2,1,0:T(8,128)S(1)}) custom-call(f32[8,128]{1,0:T(8,128)S(1)} %broadcast_in_dim.4.table, f32[1,6,2,256,128]{4,3,2,1,0:T(8,128)S(1)} %copy-done, s32[1,2,256,128]{3,2,1,0:T(8,128)S(1)} %copy-done.1, f32[5,208,128]{2,1,0:T(8,128)S(1)} %collective-permute-done.4.near, ...), custom_call_target="tpu_custom_call" | custom-call | tf_op jit(solution)/shard_map/pallas_call | solution.py:443
  20.4 0.6 %collective-permute-start.7 = (f32[6,2,56,128]{3,2,1,0:T(8,128)S(1)}, f32[6,2,56,128]{3,2,1,0:T(8,128)S(1)}, u32[]{:S(2)}, u32[]{:S(2)}) collective-permute-start(f32[6,2,56,128]{3,2,1,0:T(8,128)S(1)} %get-tuple-element.45), channel_id=1, source_target_pairs={{0,16},{8,24},{16,0},{24,8},{1,17},{9,25},{17,1},{25,9},{2,18},{10... | collective-permute-start | bytes 1032200 | tf_op jit(solution)/shard_map/ppermute | solution.py:477
  21.0 0.0 collective-permute-done.3.strip
  21.0 1.5 %collective-permute-done.2.corner = f32[6,2,32,128]{3,2,1,0:T(8,128)S(1)} collective-permute-done((f32[6,2,32,128]{3,2,1,0:T(8,128)S(1)}, f32[6,2,32,128]{3,2,1,0:T(8,128)S(1)}, u32[]{:S(2)}, u32[]{:S(2)}) %collective-permute-start.2) | collective-permute-done | bytes 196640 | tf_op jit(solution)/shard_map/ppermute | solution.py:477
  22.5 0.3 shard_map.51
  22.8 0.7 %collective-permute-start.8 = (f32[6,2,48,128]{3,2,1,0:T(8,128)S(1)}, f32[6,2,48,128]{3,2,1,0:T(8,128)S(1)}, u32[]{:S(2)}, u32[]{:S(2)}) collective-permute-start(f32[6,2,48,128]{3,2,1,0:T(8,128)S(1)} %get-tuple-element.49), channel_id=1, source_target_pairs={{0,8},{8,0},{16,24},{24,16},{1,9},{9,1},{17,25},{25,17},{2,10},{10... | collective-permute-start | bytes 884744 | tf_op jit(solution)/shard_map/ppermute | solution.py:477
  23.5 1.5 %collective-permute-done.10.far = f32[5,48,128]{2,1,0:T(8,128)S(1)} collective-permute-done((f32[5,48,128]{2,1,0:T(8,128)S(1)}, f32[5,48,128]{2,1,0:T(8,128)S(1)}, u32[]{:S(2)}, u32[]{:S(2)}) %collective-permute-start.10) | collective-permute-done | bytes 122912 | tf_op jit(solution)/shard_map/ppermute | solution.py:473
  25.0 2.5 %shard_map.53.part = f32[6,2,88,128]{3,2,1,0:T(8,128)S(1)} custom-call(f32[8,128]{1,0:T(8,128)S(1)} %broadcast_in_dim.4.table, f32[14,48,128]{2,1,0:T(8,128)S(1)} %collective-permute-done.5.shared, f32[5,48,128]{2,1,0:T(8,128)S(1)} %collective-permute-done.9.near, f32[5,48,128]{2,1,0:T(8,128)S(1)} %collective-permute-done.10.far), custom_call_target="tpu_custom_call" | custom-call | flops 3000000000 | tf_op jit(solution)/shard_map/pallas_call | solution.py:443
  27.5 3.5 %collective-permute-done.8.got = f32[6,2,48,128]{3,2,1,0:T(8,128)S(1)} collective-permute-done((f32[6,2,48,128]{3,2,1,0:T(8,128)S(1)}, f32[6,2,48,128]{3,2,1,0:T(8,128)S(1)}, u32[]{:S(2)}, u32[]{:S(2)}) %collective-permute-start.8) | collective-permute-done | bytes 294944 | tf_op jit(solution)/shard_map/ppermute | solution.py:477
  31.0 0.1 shard_map.52.edge
  31.2 1.0 %shard_map.54._ = f32[1,6,2,256,128]{4,3,2,1,0:T(8,128)} custom-call(f32[6,2,64,128]{3,2,1,0:T(8,128)S(1)} %shard_map.52.edge, f32[6,2,192,128]{3,2,1,0:T(8,128)S(1)} %get-tuple-element.44.mid, f32[6,2,88,128]{3,2,1,0:T(8,128)S(1)} %shard_map.53.part), custom_call_target="tpu_custom_call" | custom-call | tf_op jit(solution)/shard_map/pallas_call | solution.py:564
  32.2 1.0 %shard_map.55 = f32[1,6,2,256,128]{4,3,2,1,0:T(8,128)} custom-call(f32[6,2,192,128]{3,2,1,0:T(8,128)S(1)} %get-tuple-element.44.mid, f32[6,2,56,128]{3,2,1,0:T(8,128)S(1)} %collective-permute-done.7.bands, f32[1,6,2,256,128]{4,3,2,1,0:T(8,128)} %shard_map.54._), custom_call_target="tpu_custom_call", output_to_operand_aliasing={{}: (2, {})} | custom-call | tf_op jit(solution)/shard_map/pallas_call | solution.py:573
  (12 shorter events, 0.0 us)
Async XLA Ops:
  0.0 5.4 %copy-start.1 = (s32[1,2,256,128]{3,2,1,0:T(8,128)S(1)}, s32[1,2,256,128]{3,2,1,0:T(8,128)}, u32[]{:S(2)}) copy-start(s32[1,2,256,128]{3,2,1,0:T(8,128)} %material.7) | copy-start | bytes 786436
  0.0 5.4 %copy-start = (f32[1,6,2,256,128]{4,3,2,1,0:T(8,128)S(1)}, f32[1,6,2,256,128]{4,3,2,1,0:T(8,128)}, u32[]{:S(2)}) copy-start(f32[1,6,2,256,128]{4,3,2,1,0:T(8,128)} %seeds.7) | copy-start | bytes 4718596
  0.0 5.3 %copy-start.2 = (f32[4]{0:T(128)S(1)}, f32[4]{0:T(128)}, u32[]{:S(2)}) copy-start(f32[4]{0:T(128)} %param.7) | copy-start | bytes 52
  0.0 5.3 %copy-start.3 = (f32[4]{0:T(128)S(1)}, f32[4]{0:T(128)}, u32[]{:S(2)}) copy-start(f32[4]{0:T(128)} %param.6) | copy-start | bytes 52
  2.2 13.6 %collective-permute-start.5 = (f32[14,48,128]{2,1,0:T(8,128)S(1)}, f32[14,48,128]{2,1,0:T(8,128)S(1)}, u32[]{:S(2)}, u32[]{:S(2)}) collective-permute-start(f32[14,48,128]{2,1,0:T(8,128)S(1)} %shard_map.46), channel_id=1, source_target_pairs={{0,16},{8,24},{16,0},{24,8},{1,17},{9,25},{17,1},{25,9},{2,18},{10... | collective-permute-start | bytes 1032200 | tf_op jit(solution)/shard_map/ppermute | solution.py:477
  6.2 5.8 %collective-permute-start = (f32[5,80,128]{2,1,0:T(8,128)S(1)}, f32[5,80,128]{2,1,0:T(8,128)S(1)}, u32[]{:S(2)}, u32[]{:S(2)}) collective-permute-start(f32[5,80,128]{2,1,0:T(8,128)S(1)} %get-tuple-element.31), channel_id=1, source_target_pairs={{0,8},{1,2},{2,1},{3,4},{4,3},{5,6},{6,5},{7,15},{8,0},{9,10},{10,... | collective-permute-start | bytes 614408 | tf_op jit(solution)/shard_map/ppermute | solution.py:473
  7.8 4.3 %collective-permute-start.1 = (f32[5,80,128]{2,1,0:T(8,128)S(1)}, f32[5,80,128]{2,1,0:T(8,128)S(1)}, u32[]{:S(2)}, u32[]{:S(2)}) collective-permute-start(f32[5,80,128]{2,1,0:T(8,128)S(1)} %get-tuple-element.34), channel_id=1, source_target_pairs={{0,1},{1,0},{2,3},{3,2},{4,5},{5,4},{6,7},{7,6},{8,9},{9,8},{10,11... | collective-permute-start | bytes 614408 | tf_op jit(solution)/shard_map/ppermute | solution.py:458
  8.0 11.2 %collective-permute-start.4 = (f32[5,208,128]{2,1,0:T(8,128)S(1)}, f32[5,208,128]{2,1,0:T(8,128)S(1)}, u32[]{:S(2)}, u32[]{:S(2)}) collective-permute-start(f32[5,208,128]{2,1,0:T(8,128)S(1)} %get-tuple-element.38), channel_id=1, source_target_pairs={{0,1},{1,0},{2,3},{3,2},{4,5},{5,4},{6,7},{7,6},{8,9},{9,8},{10,11... | collective-permute-start | bytes 1597448 | tf_op jit(solution)/shard_map/ppermute | solution.py:458
  8.3 10.9 %collective-permute-start.6 = (f32[5,208,128]{2,1,0:T(8,128)S(1)}, f32[5,208,128]{2,1,0:T(8,128)S(1)}, u32[]{:S(2)}, u32[]{:S(2)}) collective-permute-start(f32[5,208,128]{2,1,0:T(8,128)S(1)} %get-tuple-element.41), channel_id=1, source_target_pairs={{0,8},{1,2},{2,1},{3,4},{4,3},{5,6},{6,5},{7,15},{8,0},{9,10},{10,... | collective-permute-start | bytes 1597448 | tf_op jit(solution)/shard_map/ppermute | solution.py:473
  12.8 8.2 %collective-permute-start.3 = (f32[6,2,16,128]{3,2,1,0:T(8,128)S(1)}, f32[6,2,16,128]{3,2,1,0:T(8,128)S(1)}, u32[]{:S(2)}, u32[]{:S(2)}) collective-permute-start(f32[6,2,16,128]{3,2,1,0:T(8,128)S(1)} %get-tuple-element.37), channel_id=1, source_target_pairs={{0,24},{8,16},{16,8},{24,0},{1,25},{9,17},{17,9},{25,1},{2,26},{10... | collective-permute-start | bytes 294920 | tf_op jit(solution)/shard_map/ppermute | solution.py:477
  14.3 8.2 %collective-permute-start.2 = (f32[6,2,32,128]{3,2,1,0:T(8,128)S(1)}, f32[6,2,32,128]{3,2,1,0:T(8,128)S(1)}, u32[]{:S(2)}, u32[]{:S(2)}) collective-permute-start(f32[6,2,32,128]{3,2,1,0:T(8,128)S(1)} %get-tuple-element.36), channel_id=1, source_target_pairs={{0,16},{8,24},{16,0},{24,8},{1,17},{9,25},{17,1},{25,9},{2,18},{10... | collective-permute-start | bytes 589832 | tf_op jit(solution)/shard_map/ppermute | solution.py:477
  17.7 7.3 %collective-permute-start.10 = (f32[5,48,128]{2,1,0:T(8,128)S(1)}, f32[5,48,128]{2,1,0:T(8,128)S(1)}, u32[]{:S(2)}, u32[]{:S(2)}) collective-permute-start(f32[5,48,128]{2,1,0:T(8,128)S(1)} %get-tuple-element.52), channel_id=1, source_target_pairs={{0,7},{1,2},{2,1},{3,4},{4,3},{5,6},{6,5},{7,0},{8,15},{9,10},{10,... | collective-permute-start | bytes 368648 | tf_op jit(solution)/shard_map/ppermute | solution.py:473
  19.2 5.9 %collective-permute-start.9 = (f32[5,48,128]{2,1,0:T(8,128)S(1)}, f32[5,48,128]{2,1,0:T(8,128)S(1)}, u32[]{:S(2)}, u32[]{:S(2)}) collective-permute-start(f32[5,48,128]{2,1,0:T(8,128)S(1)} %get-tuple-element.51), channel_id=1, source_target_pairs={{0,1},{1,0},{2,3},{3,2},{4,5},{5,4},{6,7},{7,6},{8,9},{9,8},{10,11... | collective-permute-start | bytes 368648 | tf_op jit(solution)/shard_map/ppermute | solution.py:458
  20.4 11.8 %collective-permute-start.7 = (f32[6,2,56,128]{3,2,1,0:T(8,128)S(1)}, f32[6,2,56,128]{3,2,1,0:T(8,128)S(1)}, u32[]{:S(2)}, u32[]{:S(2)}) collective-permute-start(f32[6,2,56,128]{3,2,1,0:T(8,128)S(1)} %get-tuple-element.45), channel_id=1, source_target_pairs={{0,16},{8,24},{16,0},{24,8},{1,17},{9,25},{17,1},{25,9},{2,18},{10... | collective-permute-start | bytes 1032200 | tf_op jit(solution)/shard_map/ppermute | solution.py:477
  22.8 8.2 %collective-permute-start.8 = (f32[6,2,48,128]{3,2,1,0:T(8,128)S(1)}, f32[6,2,48,128]{3,2,1,0:T(8,128)S(1)}, u32[]{:S(2)}, u32[]{:S(2)}) collective-permute-start(f32[6,2,48,128]{3,2,1,0:T(8,128)S(1)} %get-tuple-element.49), channel_id=1, source_target_pairs={{0,8},{8,0},{16,24},{24,16},{1,9},{9,1},{17,25},{25,17},{2,10},{10... | collective-permute-start | bytes 884744 | tf_op jit(solution)/shard_map/ppermute | solution.py:477

commit v8 on v7

--- a/solution.py
+++ b/solution.py
@@ -20,11 +20,15 @@
 
 
 def lane_of(shape):
-    return lax.broadcasted_iota(jnp.int32, shape, 1)
+    return lax.broadcasted_iota(jnp.int32, shape, len(shape) - 1)
 
 
 def row_of(shape):
-    return lax.broadcasted_iota(jnp.int32, shape, 0)
+    return lax.broadcasted_iota(jnp.int32, shape, len(shape) - 2)
+
+
+def rolled(v, shift):
+    return pltpu.roll(v, shift % v.shape[-1], v.ndim - 1)
 
 
 def next_x(v):
@@ -130,7 +134,7 @@
 NONE = (None, None)
 
 
-def send_halos(sub, fields, near, far, packed=lambda block: block):
+def send_halos(sub, fields, near, far, packed=lambda planes: planes):
     odd = lax.rem(lax.axis_index(sub), 2) == 1
     e, h, ca, cb = fields
     v1 = scaled(cb, e)
@@ -140,9 +144,9 @@
     h2 = update_h(h1, v2, NONE)
     up = (h1[0][-1], h1[1][-1], h2[0][-1], h2[1][-1], cb[-1])
     down = (v1[0][0], v1[1][0], v2[0][0], v2[1][0], cb[0])
-    for k in range(PLANES):
-        near[k] = packed(jnp.where(odd, down[k], up[k]))
-        far[k] = packed(jnp.where(odd, up[k], down[k]))
+    up, down = packed(jnp.stack(up)), packed(jnp.stack(down))
+    near[...] = jnp.where(odd, down, up)
+    far[...] = jnp.where(odd, up, down)
 
 
 def halo_kernel(spans, sub, table, seeds, material, near, far):
@@ -158,15 +162,14 @@
     )
 
 
-def final_fields(fields, near, far, sub, sub_size, unpacked=lambda block: block):
+def final_fields(fields, near, far, sub, sub_size, unpacked=lambda planes: planes):
     e, h, ca, cb = fields
     index = lax.axis_index(sub)
     odd = lax.rem(index, 2) == 1
     below, above = index > 0, index < sub_size - 1
-    a = [unpacked(near[k]) for k in range(PLANES)]
-    b = [unpacked(far[k]) for k in range(PLANES)]
-    from_below = [jnp.where(odd, a[k], b[k]) for k in range(PLANES)]
-    from_above = [jnp.where(above, jnp.where(odd, b[k], a[k]), 0.0) for k in range(PLANES)]
+    a, b = near[...], far[...]
+    from_below = unpacked(jnp.where(odd, a, b))
+    from_above = unpacked(jnp.where(above, jnp.where(odd, b, a), 0.0))
     part_h1x, part_h1y, part_h2x, part_h2y, cb_low = from_below
     v1x_up, v1y_up, part_v2x, part_v2y, cb_up = from_above
 
@@ -192,14 +195,13 @@
 
 
 def middle_out(block):
-    return pltpu.roll(block, block.shape[1] // 2, 1)
+    return rolled(block, block.shape[-1] // 2)
 
 
 def y_packed(first, second):
     lane = lane_of(first.shape)
-    lanes = first.shape[1]
-    middle = (lane >= BAND) & (lane < lanes - BAND)
-    return jnp.where(middle, pltpu.roll(second, lanes // 2, 1), first)
+    middle = (lane >= BAND) & (lane < first.shape[-1] - BAND)
+    return jnp.where(middle, middle_out(second), first)
 
 
 def y_unpacked(block):
@@ -217,49 +219,48 @@
 
 
 def bands_packed(block):
-    rows, lanes = block.shape
-    count = rows // 2 + 4
-    width = REACH * (rows // 8)
-    side = jnp.zeros((8, lanes), block.dtype)
-    lane = lane_of(side.shape)
-    high = lanes - BAND
+    rows, lanes = block.shape[1:]
+    count, width, high = rows // 2 + 4, REACH * (rows // 8), lanes - BAND
+    shape = (block.shape[0], 8, lanes)
+    lane = lane_of(shape)
+    low = low_rows(shape)
+    side = jnp.zeros(shape, block.dtype)
     for g in range(rows // 8):
         at = BAND + REACH * (g + 1)
-        piece = pltpu.roll(block[8 * g : 8 * g + 8], REACH * (g + 1), 1)
+        piece = rolled(block[:, 8 * g : 8 * g + 8], REACH * (g + 1))
         here = ((lane >= at) & (lane < at + REACH)) | (
             (lane >= at + high - BAND - REACH) & (lane < at + high - BAND)
         )
         side = jnp.where(here, piece, side)
-    other = pltpu.roll(pltpu.roll(side, 4, 0), width + REACH, 1)
+    other = rolled(pltpu.roll(side, 4, 1), width + REACH)
     own = ((lane >= BAND) & (lane < BAND + REACH + width)) | ((lane >= high) & (lane < high + width))
     side = jnp.where(own, side, other)
     middle = (lane >= BAND) & (lane < high)
-    packed = y_packed(block[:count], block[rows - count :])
-    first = jnp.where(low_rows(side.shape) & middle, side, packed[:8])
-    last = jnp.where(low_rows(side.shape) | middle, packed[count - 8 :], side)
-    return jnp.concatenate([first, packed[8 : count - 8], last], axis=0)
+    packed = y_packed(block[:, :count], block[:, rows - count :])
+    first = jnp.where(low & middle, side, packed[:, :8])
+    last = jnp.where(low | middle, packed[:, count - 8 :], side)
+    return jnp.concatenate([first, packed[:, 8 : count - 8], last], axis=1)
 
 
 def bands_unpacked(packed):
-    count, lanes = packed.shape
+    count, lanes = packed.shape[1:]
     rows = 2 * count - 8
-    width = REACH * (rows // 8)
-    high = lanes - BAND
-    first, last = packed[:8], packed[count - 8 :]
+    width, high = REACH * (rows // 8), lanes - BAND
+    first, last = packed[:, :8], packed[:, count - 8 :]
     low = low_rows(first.shape)
     lane = lane_of(first.shape)
     middle = (lane >= BAND) & (lane < high)
     side = jnp.where(low, first, last)
-    other = pltpu.roll(pltpu.roll(side, 4, 0), lanes - width - REACH, 1)
+    other = rolled(pltpu.roll(side, 4, 1), -width - REACH)
     side = jnp.where(low == middle, side, other)
     beside = ((lane >= BAND) & (lane < BAND + REACH)) | ((lane >= high - REACH) & (lane < high))
-    moved = [pltpu.roll(packed[at : at + 8], lanes // 2, 1) for at in range(0, count, 8)]
-    pieces = [packed[at : at + 8] for at in range(0, count - 8, 8)] + [jnp.where(low, last, moved[0])] + moved[1:]
+    moved = [rolled(packed[:, at : at + 8], lanes // 2) for at in range(0, count, 8)]
+    pieces = [packed[:, at : at + 8] for at in range(0, count - 8, 8)]
+    pieces += [jnp.where(low, last, moved[0])] + moved[1:]
     result = []
     for g, piece in enumerate(pieces):
-        near_by = pltpu.roll(side, lanes - REACH * (g + 1), 1)
-        result.append(jnp.where(middle, jnp.where(beside, near_by, 0.0), piece))
-    return jnp.concatenate(result, axis=0)
+        result.append(jnp.where(middle, jnp.where(beside, rolled(side, -REACH * (g + 1)), 0.0), piece))
+    return jnp.concatenate(result, axis=1)
 
 
 def share_kernel(span, skip, seeds, material, shared, held, labels, sems):
@@ -271,12 +272,10 @@
     for copy in copies:
         copy.start()
     copies[0].wait()
-    for p in range(depth):
-        shared[6 * depth + p] = bands_packed(labels[p, skip:stop].astype(jnp.float32))
+    shared[6 * depth :] = bands_packed(labels[:, skip:stop].astype(jnp.float32))
     for c in range(6):
         copies[1 + c].wait()
-        for p in range(depth):
-            shared[depth * c + p] = bands_packed(held[c, p, skip:stop])
+    shared[: 6 * depth] = bands_packed(jnp.concatenate([held[c, :, skip:stop] for c in range(6)], axis=0))
 
 
 def halo_pair_kernel(edges, inner, sub, table, seeds, material, near_edge, far_edge, near, far):
@@ -286,7 +285,7 @@
 
 def shared_fields(table, shared):
     depth = shared.shape[0] // 7
-    planes = [bands_unpacked(shared[k]) for k in range(7 * depth)]
+    planes = bands_unpacked(shared[...])
     f = [planes[depth * c : depth * (c + 1)] for c in range(7)]
     return prepared(f[:3], f[3:6], f[6], table_entries(table))
 

time: 33.4 us -> 32.9 us (0.985)
  Pallas kernels: 11.6 us -> 9.07 us
  waiting for transfers between devices: 9.21 us -> 11.5 us
    ppermute x5, waiting for transfers between devices: 5.1 us -> 7.73 us  [swapped(): lax.ppermute(value, 'tile', [(t, t ^ bits) for t in range(tile_size)])]
    pallas_call x7, Pallas kernels: 7.39 us -> 5.31 us  [called(): pl.pallas_call(kernel, out_shape=outs, in_specs=[VMEM] * len(operands), o...]
    pallas_call x1, Pallas kernels: 2.22 us -> 1.72 us  [two_by_two(): pl.pallas_call(functools.partial(share_kernel, fetched, HALO // 2), out_s...]
    ppermute x3, waiting for transfers between devices: 4.11 us -> 3.74 us  [far_exchange(): return lax.ppermute(far, ('tile', 'sub'), pairs)]
  transfers between devices with their start and end apart: 11 -> 11, of which waited for: 4 -> 5; matrix products, arithmetic and copies ran while one was open for 1% -> 1% of each run, Pallas kernels for 25% -> 19%
where the time goes in v8:
time: 32.9 us; the launch traced here: 32.7 us
  starting transfers between devices  11.8 us (36%)
  waiting for transfers between devices  11.5 us (35%)
  Pallas kernels  9.07 us (28%)
    ppermute x5, waiting for transfers between devices, swapped(): lax.ppermute(value, 'tile', [(t, t ^ bits) for t in range(tile_size)])  7.73 us
    ppermute x5, starting transfers between devices, swapped(): lax.ppermute(value, 'tile', [(t, t ^ bits) for t in range(tile_size)])  7.12 us
    pallas_call x7, Pallas kernels, called(): pl.pallas_call(kernel, out_shape=outs, in_specs=[VMEM] * len(operands), o...  5.31 us
    ppermute x3, starting transfers between devices, far_exchange(): return lax.ppermute(far, ('tile', 'sub'), pairs)  4.15 us
    ppermute x3, waiting for transfers between devices, far_exchange(): return lax.ppermute(far, ('tile', 'sub'), pairs)  3.74 us
    pallas_call x1, Pallas kernels, two_by_two(): pl.pallas_call(functools.partial(share_kernel, fetched, HALO // 2), out_s...  1.72 us
    pallas_call x1, Pallas kernels, two_by_two(): pl.pallas_call(last_kernel, out_shape=whole, in_specs=[VMEM, VMEM, HBM],...  1.04 us
    pallas_call x1, Pallas kernels, two_by_two(): pl.pallas_call(early_kernel, out_shape=whole, in_specs=[VMEM] * 3, out_sp...  1 us
  transfers between devices with their start and end apart: 11, of which 5 were waited for; matrix products, arithmetic and copies ran while one was open for 1% of the time, Pallas kernels for 19%

profile of v8, /device:TPU:0, one launch (start us, length us, event | category | flops | bytes accessed | tf_op | source)
XLA Modules:
  0.0 32.7 jit_solution(804197838804239988)
XLA Ops:
  0.0 1.7 %shard_map.46 = f32[14,48,128]{2,1,0:T(8,128)S(1)} custom-call(f32[1,6,2,256,128]{4,3,2,1,0:T(8,128)} %seeds.7, s32[1,2,256,128]{3,2,1,0:T(8,128)} %material.7), custom_call_target="tpu_custom_call" | custom-call | tf_op jit(solution)/shard_map/pallas_call | solution.py:499
  1.7 3.0 %collective-permute-start.5 = (f32[14,48,128]{2,1,0:T(8,128)S(1)}, f32[14,48,128]{2,1,0:T(8,128)S(1)}, u32[]{:S(2)}, u32[]{:S(2)}) collective-permute-start(f32[14,48,128]{2,1,0:T(8,128)S(1)} %shard_map.46), channel_id=1, source_target_pairs={{0,16},{8,24},{16,0},{24,8},{1,17},{9,25},{17,1},{25,9},{2,18},{10... | collective-permute-start | bytes 1032200 | tf_op jit(solution)/shard_map/ppermute | solution.py:476
  4.8 0.1 pad_maximum_fusion
  4.9 0.1 broadcast_in_dim.4.table
  4.9 0.8 %shard_map.47 = (f32[5,80,128]{2,1,0:T(8,128)S(1)}, f32[5,80,128]{2,1,0:T(8,128)S(1)}, f32[5,208,128]{2,1,0:T(8,128)S(1)}, f32[5,208,128]{2,1,0:T(8,128)S(1)}) custom-call(f32[8,128]{1,0:T(8,128)S(1)} %broadcast_in_dim.4.table, f32[1,6,2,256,128]{4,3,2,1,0:T(8,128)S(1)} %copy-done, s32[1,2,256,128]{3,2,1,0:T(8,128)S(1)} %copy-done.1), custom_call_target="tpu_custom_call" | custom-call | tf_op jit(solution)/shard_map/pallas_call | solution.py:442
  5.7 1.6 %collective-permute-start = (f32[5,80,128]{2,1,0:T(8,128)S(1)}, f32[5,80,128]{2,1,0:T(8,128)S(1)}, u32[]{:S(2)}, u32[]{:S(2)}) collective-permute-start(f32[5,80,128]{2,1,0:T(8,128)S(1)} %get-tuple-element.31), channel_id=1, source_target_pairs={{0,8},{1,2},{2,1},{3,4},{4,3},{5,6},{6,5},{7,15},{8,0},{9,10},{10,... | collective-permute-start | bytes 614408 | tf_op jit(solution)/shard_map/ppermute | solution.py:472
  7.3 0.2 collective-permute-start.1
  7.5 0.3 collective-permute-start.4
  7.8 1.2 %collective-permute-start.6 = (f32[5,208,128]{2,1,0:T(8,128)S(1)}, f32[5,208,128]{2,1,0:T(8,128)S(1)}, u32[]{:S(2)}, u32[]{:S(2)}) collective-permute-start(f32[5,208,128]{2,1,0:T(8,128)S(1)} %get-tuple-element.41), channel_id=1, source_target_pairs={{0,8},{1,2},{2,1},{3,4},{4,3},{5,6},{6,5},{7,15},{8,0},{9,10},{10,... | collective-permute-start | bytes 1597448 | tf_op jit(solution)/shard_map/ppermute | solution.py:472
  9.0 2.6 %collective-permute-done.far = f32[5,80,128]{2,1,0:T(8,128)S(1)} collective-permute-done((f32[5,80,128]{2,1,0:T(8,128)S(1)}, f32[5,80,128]{2,1,0:T(8,128)S(1)}, u32[]{:S(2)}, u32[]{:S(2)}) %collective-permute-start) | collective-permute-done | bytes 204832 | tf_op jit(solution)/shard_map/ppermute | solution.py:472
  11.5 0.1 pad_maximum_fusion.1
  11.6 0.0 collective-permute-done.1.near
  11.6 0.1 broadcast_in_dim.5.table
  11.7 0.6 %shard_map.48 = (f32[6,2,64,128]{3,2,1,0:T(8,128)S(1)}, f32[6,2,32,128]{3,2,1,0:T(8,128)S(1)}, f32[6,2,16,128]{3,2,1,0:T(8,128)S(1)}) custom-call(f32[8,128]{1,0:T(8,128)S(1)} %broadcast_in_dim.5.table, f32[1,6,2,256,128]{4,3,2,1,0:T(8,128)S(1)} %copy-done, s32[1,2,256,128]{3,2,1,0:T(8,128)S(1)} %copy-done.1, f32[5,80,128]{2,1,0:T(8,128)S(1)} %collective-permute-done.1.near, ...), custom_call_target="tpu_custom_call" | custom-call | tf_op jit(solution)/shard_map/pallas_call | solution.py:442
  12.3 1.5 %collective-permute-start.3 = (f32[6,2,16,128]{3,2,1,0:T(8,128)S(1)}, f32[6,2,16,128]{3,2,1,0:T(8,128)S(1)}, u32[]{:S(2)}, u32[]{:S(2)}) collective-permute-start(f32[6,2,16,128]{3,2,1,0:T(8,128)S(1)} %get-tuple-element.37), channel_id=1, source_target_pairs={{0,24},{8,16},{16,8},{24,0},{1,25},{9,17},{17,9},{25,1},{2,26},{10... | collective-permute-start | bytes 294920 | tf_op jit(solution)/shard_map/ppermute | solution.py:476
  13.8 1.5 %collective-permute-start.2 = (f32[6,2,32,128]{3,2,1,0:T(8,128)S(1)}, f32[6,2,32,128]{3,2,1,0:T(8,128)S(1)}, u32[]{:S(2)}, u32[]{:S(2)}) collective-permute-start(f32[6,2,32,128]{3,2,1,0:T(8,128)S(1)} %get-tuple-element.36), channel_id=1, source_target_pairs={{0,16},{8,24},{16,0},{24,8},{1,17},{9,25},{17,1},{25,9},{2,18},{10... | collective-permute-start | bytes 589832 | tf_op jit(solution)/shard_map/ppermute | solution.py:476
  15.3 0.0 collective-permute-done.5.shared
  15.3 1.0 %shard_map.49 = (f32[5,48,128]{2,1,0:T(8,128)S(1)}, f32[5,48,128]{2,1,0:T(8,128)S(1)}) custom-call(f32[8,128]{1,0:T(8,128)S(1)} %broadcast_in_dim.4.table, f32[14,48,128]{2,1,0:T(8,128)S(1)} %collective-permute-done.5.shared), custom_call_target="tpu_custom_call" | custom-call | flops 10000000000 | tf_op jit(solution)/shard_map/pallas_call | solution.py:442
  16.3 1.4 %collective-permute-start.10 = (f32[5,48,128]{2,1,0:T(8,128)S(1)}, f32[5,48,128]{2,1,0:T(8,128)S(1)}, u32[]{:S(2)}, u32[]{:S(2)}) collective-permute-start(f32[5,48,128]{2,1,0:T(8,128)S(1)} %get-tuple-element.52), channel_id=1, source_target_pairs={{0,7},{1,2},{2,1},{3,4},{4,3},{5,6},{6,5},{7,0},{8,15},{9,10},{10,... | collective-permute-start | bytes 368648 | tf_op jit(solution)/shard_map/ppermute | solution.py:472
  17.7 0.5 %collective-permute-done.6.far = f32[5,208,128]{2,1,0:T(8,128)S(1)} collective-permute-done((f32[5,208,128]{2,1,0:T(8,128)S(1)}, f32[5,208,128]{2,1,0:T(8,128)S(1)}, u32[]{:S(2)}, u32[]{:S(2)}) %collective-permute-start.6) | collective-permute-done | bytes 532512 | tf_op jit(solution)/shard_map/ppermute | solution.py:472
  18.3 1.2 %shard_map.50 = (f32[6,2,192,128]{3,2,1,0:T(8,128)S(1)}, f32[6,2,56,128]{3,2,1,0:T(8,128)S(1)}) custom-call(f32[8,128]{1,0:T(8,128)S(1)} %broadcast_in_dim.4.table, f32[1,6,2,256,128]{4,3,2,1,0:T(8,128)S(1)} %copy-done, s32[1,2,256,128]{3,2,1,0:T(8,128)S(1)} %copy-done.1, f32[5,208,128]{2,1,0:T(8,128)S(1)} %collective-permute-done.4.near, ...), custom_call_target="tpu_custom_call" | custom-call | tf_op jit(solution)/shard_map/pallas_call | solution.py:442
  19.5 0.4 %collective-permute-start.7 = (f32[6,2,56,128]{3,2,1,0:T(8,128)S(1)}, f32[6,2,56,128]{3,2,1,0:T(8,128)S(1)}, u32[]{:S(2)}, u32[]{:S(2)}) collective-permute-start(f32[6,2,56,128]{3,2,1,0:T(8,128)S(1)} %get-tuple-element.45), channel_id=1, source_target_pairs={{0,16},{8,24},{16,0},{24,8},{1,17},{9,25},{17,1},{25,9},{2,18},{10... | collective-permute-start | bytes 1032200 | tf_op jit(solution)/shard_map/ppermute | solution.py:476
  19.9 0.0 collective-permute-done.3.strip
  19.9 2.1 %collective-permute-done.2.corner = f32[6,2,32,128]{3,2,1,0:T(8,128)S(1)} collective-permute-done((f32[6,2,32,128]{3,2,1,0:T(8,128)S(1)}, f32[6,2,32,128]{3,2,1,0:T(8,128)S(1)}, u32[]{:S(2)}, u32[]{:S(2)}) %collective-permute-start.2) | collective-permute-done | bytes 196640 | tf_op jit(solution)/shard_map/ppermute | solution.py:476
  22.0 0.3 shard_map.51
  22.3 0.7 %collective-permute-start.8 = (f32[6,2,48,128]{3,2,1,0:T(8,128)S(1)}, f32[6,2,48,128]{3,2,1,0:T(8,128)S(1)}, u32[]{:S(2)}, u32[]{:S(2)}) collective-permute-start(f32[6,2,48,128]{3,2,1,0:T(8,128)S(1)} %get-tuple-element.49), channel_id=1, source_target_pairs={{0,8},{8,0},{16,24},{24,16},{1,9},{9,1},{17,25},{25,17},{2,10},{10... | collective-permute-start | bytes 884744 | tf_op jit(solution)/shard_map/ppermute | solution.py:476
  23.0 0.6 %collective-permute-done.10.far = f32[5,48,128]{2,1,0:T(8,128)S(1)} collective-permute-done((f32[5,48,128]{2,1,0:T(8,128)S(1)}, f32[5,48,128]{2,1,0:T(8,128)S(1)}, u32[]{:S(2)}, u32[]{:S(2)}) %collective-permute-start.10) | collective-permute-done | bytes 122912 | tf_op jit(solution)/shard_map/ppermute | solution.py:472
  23.6 1.3 %shard_map.53.part = f32[6,2,88,128]{3,2,1,0:T(8,128)S(1)} custom-call(f32[8,128]{1,0:T(8,128)S(1)} %broadcast_in_dim.4.table, f32[14,48,128]{2,1,0:T(8,128)S(1)} %collective-permute-done.5.shared, f32[5,48,128]{2,1,0:T(8,128)S(1)} %collective-permute-done.9.near, f32[5,48,128]{2,1,0:T(8,128)S(1)} %collective-permute-done.10.far), custom_call_target="tpu_custom_call" | custom-call | flops 3000000000 | tf_op jit(solution)/shard_map/pallas_call | solution.py:442
  24.9 5.6 %collective-permute-done.8.got = f32[6,2,48,128]{3,2,1,0:T(8,128)S(1)} collective-permute-done((f32[6,2,48,128]{3,2,1,0:T(8,128)S(1)}, f32[6,2,48,128]{3,2,1,0:T(8,128)S(1)}, u32[]{:S(2)}, u32[]{:S(2)}) %collective-permute-start.8) | collective-permute-done | bytes 294944 | tf_op jit(solution)/shard_map/ppermute | solution.py:476
  30.5 0.1 shard_map.52.edge
  30.7 1.0 %shard_map.54._ = f32[1,6,2,256,128]{4,3,2,1,0:T(8,128)} custom-call(f32[6,2,64,128]{3,2,1,0:T(8,128)S(1)} %shard_map.52.edge, f32[6,2,192,128]{3,2,1,0:T(8,128)S(1)} %get-tuple-element.44.mid, f32[6,2,88,128]{3,2,1,0:T(8,128)S(1)} %shard_map.53.part), custom_call_target="tpu_custom_call" | custom-call | tf_op jit(solution)/shard_map/pallas_call | solution.py:563
  31.7 1.0 %shard_map.55 = f32[1,6,2,256,128]{4,3,2,1,0:T(8,128)} custom-call(f32[6,2,192,128]{3,2,1,0:T(8,128)S(1)} %get-tuple-element.44.mid, f32[6,2,56,128]{3,2,1,0:T(8,128)S(1)} %collective-permute-done.7.bands, f32[1,6,2,256,128]{4,3,2,1,0:T(8,128)} %shard_map.54._), custom_call_target="tpu_custom_call", output_to_operand_aliasing={{}: (2, {})} | custom-call | tf_op jit(solution)/shard_map/pallas_call | solution.py:572
  (12 shorter events, 0.0 us)
Async XLA Ops:
  0.0 4.9 %copy-start.1 = (s32[1,2,256,128]{3,2,1,0:T(8,128)S(1)}, s32[1,2,256,128]{3,2,1,0:T(8,128)}, u32[]{:S(2)}) copy-start(s32[1,2,256,128]{3,2,1,0:T(8,128)} %material.7) | copy-start | bytes 786436
  0.0 4.9 %copy-start = (f32[1,6,2,256,128]{4,3,2,1,0:T(8,128)S(1)}, f32[1,6,2,256,128]{4,3,2,1,0:T(8,128)}, u32[]{:S(2)}) copy-start(f32[1,6,2,256,128]{4,3,2,1,0:T(8,128)} %seeds.7) | copy-start | bytes 4718596
  0.0 4.8 %copy-start.2 = (f32[4]{0:T(128)S(1)}, f32[4]{0:T(128)}, u32[]{:S(2)}) copy-start(f32[4]{0:T(128)} %param.7) | copy-start | bytes 52
  0.0 4.8 %copy-start.3 = (f32[4]{0:T(128)S(1)}, f32[4]{0:T(128)}, u32[]{:S(2)}) copy-start(f32[4]{0:T(128)} %param.6) | copy-start | bytes 52
  1.7 13.6 %collective-permute-start.5 = (f32[14,48,128]{2,1,0:T(8,128)S(1)}, f32[14,48,128]{2,1,0:T(8,128)S(1)}, u32[]{:S(2)}, u32[]{:S(2)}) collective-permute-start(f32[14,48,128]{2,1,0:T(8,128)S(1)} %shard_map.46), channel_id=1, source_target_pairs={{0,16},{8,24},{16,0},{24,8},{1,17},{9,25},{17,1},{25,9},{2,18},{10... | collective-permute-start | bytes 1032200 | tf_op jit(solution)/shard_map/ppermute | solution.py:476
  5.7 5.8 %collective-permute-start = (f32[5,80,128]{2,1,0:T(8,128)S(1)}, f32[5,80,128]{2,1,0:T(8,128)S(1)}, u32[]{:S(2)}, u32[]{:S(2)}) collective-permute-start(f32[5,80,128]{2,1,0:T(8,128)S(1)} %get-tuple-element.31), channel_id=1, source_target_pairs={{0,8},{1,2},{2,1},{3,4},{4,3},{5,6},{6,5},{7,15},{8,0},{9,10},{10,... | collective-permute-start | bytes 614408 | tf_op jit(solution)/shard_map/ppermute | solution.py:472
  7.3 4.3 %collective-permute-start.1 = (f32[5,80,128]{2,1,0:T(8,128)S(1)}, f32[5,80,128]{2,1,0:T(8,128)S(1)}, u32[]{:S(2)}, u32[]{:S(2)}) collective-permute-start(f32[5,80,128]{2,1,0:T(8,128)S(1)} %get-tuple-element.34), channel_id=1, source_target_pairs={{0,1},{1,0},{2,3},{3,2},{4,5},{5,4},{6,7},{7,6},{8,9},{9,8},{10,11... | collective-permute-start | bytes 614408 | tf_op jit(solution)/shard_map/ppermute | solution.py:457
  7.5 10.8 %collective-permute-start.4 = (f32[5,208,128]{2,1,0:T(8,128)S(1)}, f32[5,208,128]{2,1,0:T(8,128)S(1)}, u32[]{:S(2)}, u32[]{:S(2)}) collective-permute-start(f32[5,208,128]{2,1,0:T(8,128)S(1)} %get-tuple-element.38), channel_id=1, source_target_pairs={{0,1},{1,0},{2,3},{3,2},{4,5},{5,4},{6,7},{7,6},{8,9},{9,8},{10,11... | collective-permute-start | bytes 1597448 | tf_op jit(solution)/shard_map/ppermute | solution.py:457
  7.8 10.5 %collective-permute-start.6 = (f32[5,208,128]{2,1,0:T(8,128)S(1)}, f32[5,208,128]{2,1,0:T(8,128)S(1)}, u32[]{:S(2)}, u32[]{:S(2)}) collective-permute-start(f32[5,208,128]{2,1,0:T(8,128)S(1)} %get-tuple-element.41), channel_id=1, source_target_pairs={{0,8},{1,2},{2,1},{3,4},{4,3},{5,6},{6,5},{7,15},{8,0},{9,10},{10,... | collective-permute-start | bytes 1597448 | tf_op jit(solution)/shard_map/ppermute | solution.py:472
  12.3 7.6 %collective-permute-start.3 = (f32[6,2,16,128]{3,2,1,0:T(8,128)S(1)}, f32[6,2,16,128]{3,2,1,0:T(8,128)S(1)}, u32[]{:S(2)}, u32[]{:S(2)}) collective-permute-start(f32[6,2,16,128]{3,2,1,0:T(8,128)S(1)} %get-tuple-element.37), channel_id=1, source_target_pairs={{0,24},{8,16},{16,8},{24,0},{1,25},{9,17},{17,9},{25,1},{2,26},{10... | collective-permute-start | bytes 294920 | tf_op jit(solution)/shard_map/ppermute | solution.py:476
  13.8 8.2 %collective-permute-start.2 = (f32[6,2,32,128]{3,2,1,0:T(8,128)S(1)}, f32[6,2,32,128]{3,2,1,0:T(8,128)S(1)}, u32[]{:S(2)}, u32[]{:S(2)}) collective-permute-start(f32[6,2,32,128]{3,2,1,0:T(8,128)S(1)} %get-tuple-element.36), channel_id=1, source_target_pairs={{0,16},{8,24},{16,0},{24,8},{1,17},{9,25},{17,1},{25,9},{2,18},{10... | collective-permute-start | bytes 589832 | tf_op jit(solution)/shard_map/ppermute | solution.py:476
  16.3 7.3 %collective-permute-start.10 = (f32[5,48,128]{2,1,0:T(8,128)S(1)}, f32[5,48,128]{2,1,0:T(8,128)S(1)}, u32[]{:S(2)}, u32[]{:S(2)}) collective-permute-start(f32[5,48,128]{2,1,0:T(8,128)S(1)} %get-tuple-element.52), channel_id=1, source_target_pairs={{0,7},{1,2},{2,1},{3,4},{4,3},{5,6},{6,5},{7,0},{8,15},{9,10},{10,... | collective-permute-start | bytes 368648 | tf_op jit(solution)/shard_map/ppermute | solution.py:472
  18.3 5.3 %collective-permute-start.9 = (f32[5,48,128]{2,1,0:T(8,128)S(1)}, f32[5,48,128]{2,1,0:T(8,128)S(1)}, u32[]{:S(2)}, u32[]{:S(2)}) collective-permute-start(f32[5,48,128]{2,1,0:T(8,128)S(1)} %get-tuple-element.51), channel_id=1, source_target_pairs={{0,1},{1,0},{2,3},{3,2},{4,5},{5,4},{6,7},{7,6},{8,9},{9,8},{10,11... | collective-permute-start | bytes 368648 | tf_op jit(solution)/shard_map/ppermute | solution.py:457
  19.5 12.1 %collective-permute-start.7 = (f32[6,2,56,128]{3,2,1,0:T(8,128)S(1)}, f32[6,2,56,128]{3,2,1,0:T(8,128)S(1)}, u32[]{:S(2)}, u32[]{:S(2)}) collective-permute-start(f32[6,2,56,128]{3,2,1,0:T(8,128)S(1)} %get-tuple-element.45), channel_id=1, source_target_pairs={{0,16},{8,24},{16,0},{24,8},{1,17},{9,25},{17,1},{25,9},{2,18},{10... | collective-permute-start | bytes 1032200 | tf_op jit(solution)/shard_map/ppermute | solution.py:476
  22.3 8.2 %collective-permute-start.8 = (f32[6,2,48,128]{3,2,1,0:T(8,128)S(1)}, f32[6,2,48,128]{3,2,1,0:T(8,128)S(1)}, u32[]{:S(2)}, u32[]{:S(2)}) collective-permute-start(f32[6,2,48,128]{3,2,1,0:T(8,128)S(1)} %get-tuple-element.49), channel_id=1, source_target_pairs={{0,8},{8,0},{16,24},{24,16},{1,9},{9,1},{17,25},{25,17},{2,10},{10... | collective-permute-start | bytes 884744 | tf_op jit(solution)/shard_map/ppermute | solution.py:476

commit v9 on v8

--- a/solution.py
+++ b/solution.py
@@ -14,7 +14,7 @@
 PLANES = 5
 REACH = 2
 SHARED = 80
-LARGE, MEDIUM, SMALL = 10**10, 3 * 10**9, 2 * 10**8
+LARGE, MEDIUM, SMALL = 10**10, 3 * 10**9, 0
 
 magnetic_coeff = 0.5
 

time: 32.9 us -> 34.6 us (1.052)
  starting transfers between devices: 11.8 us -> 13.5 us
    ppermute x3, starting transfers between devices: 4.15 us -> 5.2 us  [far_exchange(): return lax.ppermute(far, ('tile', 'sub'), pairs)]
    ppermute x5, starting transfers between devices: 7.12 us -> 7.75 us  [swapped(): lax.ppermute(value, 'tile', [(t, t ^ bits) for t in range(tile_size)])]
  transfers between devices with their start and end apart: 11 -> 11, of which waited for: 5 -> 5; matrix products, arithmetic and copies ran while one was open for 1% -> 1% of each run, Pallas kernels for 19% -> 18%
where the time goes in v9:
time: 34.6 us; the launch traced here: 34.5 us
  starting transfers between devices  13.5 us (39%)
  waiting for transfers between devices  11.6 us (34%)
  Pallas kernels  9.07 us (26%)
    ppermute x5, waiting for transfers between devices, swapped(): lax.ppermute(value, 'tile', [(t, t ^ bits) for t in range(tile_size)])  8.06 us
    ppermute x5, starting transfers between devices, swapped(): lax.ppermute(value, 'tile', [(t, t ^ bits) for t in range(tile_size)])  7.75 us
    pallas_call x7, Pallas kernels, called(): pl.pallas_call(kernel, out_shape=outs, in_specs=[VMEM] * len(operands), o...  5.32 us
    ppermute x3, starting transfers between devices, far_exchange(): return lax.ppermute(far, ('tile', 'sub'), pairs)  5.2 us
    ppermute x3, waiting for transfers between devices, far_exchange(): return lax.ppermute(far, ('tile', 'sub'), pairs)  3.52 us
    pallas_call x1, Pallas kernels, two_by_two(): pl.pallas_call(functools.partial(share_kernel, fetched, HALO // 2), out_s...  1.72 us
    pallas_call x1, Pallas kernels, two_by_two(): pl.pallas_call(last_kernel, out_shape=whole, in_specs=[VMEM, VMEM, HBM],...  1.03 us
    pallas_call x1, Pallas kernels, two_by_two(): pl.pallas_call(early_kernel, out_shape=whole, in_specs=[VMEM] * 3, out_sp...  1 us
  transfers between devices with their start and end apart: 11, of which 5 were waited for; matrix products, arithmetic and copies ran while one was open for 1% of the time, Pallas kernels for 18%

profile of v9, /device:TPU:0, one launch (start us, length us, event | category | flops | bytes accessed | tf_op | source)
XLA Modules:
  0.0 34.5 jit_solution(7261340810102562031)
XLA Ops:
  0.0 1.7 %shard_map.46 = f32[14,48,128]{2,1,0:T(8,128)S(1)} custom-call(f32[1,6,2,256,128]{4,3,2,1,0:T(8,128)} %seeds.7, s32[1,2,256,128]{3,2,1,0:T(8,128)} %material.7), custom_call_target="tpu_custom_call" | custom-call | tf_op jit(solution)/shard_map/pallas_call | solution.py:499
  1.7 3.0 %collective-permute-start.5 = (f32[14,48,128]{2,1,0:T(8,128)S(1)}, f32[14,48,128]{2,1,0:T(8,128)S(1)}, u32[]{:S(2)}, u32[]{:S(2)}) collective-permute-start(f32[14,48,128]{2,1,0:T(8,128)S(1)} %shard_map.46), channel_id=1, source_target_pairs={{0,16},{8,24},{16,0},{24,8},{1,17},{9,25},{17,1},{25,9},{2,18},{10... | collective-permute-start | bytes 1032200 | tf_op jit(solution)/shard_map/ppermute | solution.py:476
  4.8 0.1 pad_maximum_fusion
  4.9 0.1 broadcast_in_dim.4.table
  4.9 0.8 %shard_map.47 = (f32[5,80,128]{2,1,0:T(8,128)S(1)}, f32[5,80,128]{2,1,0:T(8,128)S(1)}, f32[5,208,128]{2,1,0:T(8,128)S(1)}, f32[5,208,128]{2,1,0:T(8,128)S(1)}) custom-call(f32[8,128]{1,0:T(8,128)S(1)} %broadcast_in_dim.4.table, f32[1,6,2,256,128]{4,3,2,1,0:T(8,128)S(1)} %copy-done, s32[1,2,256,128]{3,2,1,0:T(8,128)S(1)} %copy-done.1), custom_call_target="tpu_custom_call" | custom-call | tf_op jit(solution)/shard_map/pallas_call | solution.py:442
  5.7 1.6 %collective-permute-start = (f32[5,80,128]{2,1,0:T(8,128)S(1)}, f32[5,80,128]{2,1,0:T(8,128)S(1)}, u32[]{:S(2)}, u32[]{:S(2)}) collective-permute-start(f32[5,80,128]{2,1,0:T(8,128)S(1)} %get-tuple-element.31), channel_id=1, source_target_pairs={{0,8},{1,2},{2,1},{3,4},{4,3},{5,6},{6,5},{7,15},{8,0},{9,10},{10,... | collective-permute-start | bytes 614408 | tf_op jit(solution)/shard_map/ppermute | solution.py:472
  7.3 0.2 collective-permute-start.1
  7.5 0.3 collective-permute-start.4
  7.8 1.2 %collective-permute-start.6 = (f32[5,208,128]{2,1,0:T(8,128)S(1)}, f32[5,208,128]{2,1,0:T(8,128)S(1)}, u32[]{:S(2)}, u32[]{:S(2)}) collective-permute-start(f32[5,208,128]{2,1,0:T(8,128)S(1)} %get-tuple-element.41), channel_id=1, source_target_pairs={{0,8},{1,2},{2,1},{3,4},{4,3},{5,6},{6,5},{7,15},{8,0},{9,10},{10,... | collective-permute-start | bytes 1597448 | tf_op jit(solution)/shard_map/ppermute | solution.py:472
  9.0 2.6 %collective-permute-done.far = f32[5,80,128]{2,1,0:T(8,128)S(1)} collective-permute-done((f32[5,80,128]{2,1,0:T(8,128)S(1)}, f32[5,80,128]{2,1,0:T(8,128)S(1)}, u32[]{:S(2)}, u32[]{:S(2)}) %collective-permute-start) | collective-permute-done | bytes 204832 | tf_op jit(solution)/shard_map/ppermute | solution.py:472
  11.5 0.1 pad_maximum_fusion.1
  11.6 0.1 broadcast_in_dim.5.table
  11.7 0.7 %shard_map.48 = (f32[6,2,64,128]{3,2,1,0:T(8,128)S(1)}, f32[6,2,32,128]{3,2,1,0:T(8,128)S(1)}, f32[6,2,16,128]{3,2,1,0:T(8,128)S(1)}) custom-call(f32[8,128]{1,0:T(8,128)S(1)} %broadcast_in_dim.5.table, f32[1,6,2,256,128]{4,3,2,1,0:T(8,128)S(1)} %copy-done, s32[1,2,256,128]{3,2,1,0:T(8,128)S(1)} %copy-done.1, f32[5,80,128]{2,1,0:T(8,128)S(1)} %collective-permute-done.1.near, ...), custom_call_target="tpu_custom_call" | custom-call | tf_op jit(solution)/shard_map/pallas_call | solution.py:442
  12.3 0.1 collective-permute-start.2
  12.4 0.4 %collective-permute-done.5.shared = f32[14,48,128]{2,1,0:T(8,128)S(1)} collective-permute-done((f32[14,48,128]{2,1,0:T(8,128)S(1)}, f32[14,48,128]{2,1,0:T(8,128)S(1)}, u32[]{:S(2)}, u32[]{:S(2)}) %collective-permute-start.5) | collective-permute-done | bytes 344096 | tf_op jit(solution)/shard_map/ppermute | solution.py:476
  12.8 1.0 %shard_map.49 = (f32[5,48,128]{2,1,0:T(8,128)S(1)}, f32[5,48,128]{2,1,0:T(8,128)S(1)}) custom-call(f32[8,128]{1,0:T(8,128)S(1)} %broadcast_in_dim.4.table, f32[14,48,128]{2,1,0:T(8,128)S(1)} %collective-permute-done.5.shared), custom_call_target="tpu_custom_call" | custom-call | flops 10000000000 | tf_op jit(solution)/shard_map/pallas_call | solution.py:442
  13.8 2.5 %collective-permute-start.10 = (f32[5,48,128]{2,1,0:T(8,128)S(1)}, f32[5,48,128]{2,1,0:T(8,128)S(1)}, u32[]{:S(2)}, u32[]{:S(2)}) collective-permute-start(f32[5,48,128]{2,1,0:T(8,128)S(1)} %get-tuple-element.52), channel_id=1, source_target_pairs={{0,7},{1,2},{2,1},{3,4},{4,3},{5,6},{6,5},{7,0},{8,15},{9,10},{10,... | collective-permute-start | bytes 368648 | tf_op jit(solution)/shard_map/ppermute | solution.py:472
  16.3 0.9 %collective-permute-done.6.far = f32[5,208,128]{2,1,0:T(8,128)S(1)} collective-permute-done((f32[5,208,128]{2,1,0:T(8,128)S(1)}, f32[5,208,128]{2,1,0:T(8,128)S(1)}, u32[]{:S(2)}, u32[]{:S(2)}) %collective-permute-start.6) | collective-permute-done | bytes 532512 | tf_op jit(solution)/shard_map/ppermute | solution.py:472
  17.2 1.5 %collective-permute-start.3 = (f32[6,2,16,128]{3,2,1,0:T(8,128)S(1)}, f32[6,2,16,128]{3,2,1,0:T(8,128)S(1)}, u32[]{:S(2)}, u32[]{:S(2)}) collective-permute-start(f32[6,2,16,128]{3,2,1,0:T(8,128)S(1)} %get-tuple-element.37), channel_id=1, source_target_pairs={{0,24},{8,16},{16,8},{24,0},{1,25},{9,17},{17,9},{25,1},{2,26},{10... | collective-permute-start | bytes 294920 | tf_op jit(solution)/shard_map/ppermute | solution.py:476
  18.7 0.0 collective-permute-done.4.near
  18.7 1.2 %shard_map.50 = (f32[6,2,192,128]{3,2,1,0:T(8,128)S(1)}, f32[6,2,56,128]{3,2,1,0:T(8,128)S(1)}) custom-call(f32[8,128]{1,0:T(8,128)S(1)} %broadcast_in_dim.4.table, f32[1,6,2,256,128]{4,3,2,1,0:T(8,128)S(1)} %copy-done, s32[1,2,256,128]{3,2,1,0:T(8,128)S(1)} %copy-done.1, f32[5,208,128]{2,1,0:T(8,128)S(1)} %collective-permute-done.4.near, ...), custom_call_target="tpu_custom_call" | custom-call | tf_op jit(solution)/shard_map/pallas_call | solution.py:442
  20.0 1.5 %collective-permute-start.7 = (f32[6,2,56,128]{3,2,1,0:T(8,128)S(1)}, f32[6,2,56,128]{3,2,1,0:T(8,128)S(1)}, u32[]{:S(2)}, u32[]{:S(2)}) collective-permute-start(f32[6,2,56,128]{3,2,1,0:T(8,128)S(1)} %get-tuple-element.45), channel_id=1, source_target_pairs={{0,16},{8,24},{16,0},{24,8},{1,17},{9,25},{17,1},{25,9},{2,18},{10... | collective-permute-start | bytes 1032200 | tf_op jit(solution)/shard_map/ppermute | solution.py:476
  21.5 1.9 %collective-permute-done.3.strip = f32[6,2,16,128]{3,2,1,0:T(8,128)S(1)} collective-permute-done((f32[6,2,16,128]{3,2,1,0:T(8,128)S(1)}, f32[6,2,16,128]{3,2,1,0:T(8,128)S(1)}, u32[]{:S(2)}, u32[]{:S(2)}) %collective-permute-start.3) | collective-permute-done | bytes 98336 | tf_op jit(solution)/shard_map/ppermute | solution.py:476
  23.4 0.0 collective-permute-done.2.corner
  23.4 0.3 shard_map.51
  23.7 1.6 %collective-permute-start.8 = (f32[6,2,48,128]{3,2,1,0:T(8,128)S(1)}, f32[6,2,48,128]{3,2,1,0:T(8,128)S(1)}, u32[]{:S(2)}, u32[]{:S(2)}) collective-permute-start(f32[6,2,48,128]{3,2,1,0:T(8,128)S(1)} %get-tuple-element.49), channel_id=1, source_target_pairs={{0,8},{8,0},{16,24},{24,16},{1,9},{9,1},{17,25},{25,17},{2,10},{10... | collective-permute-start | bytes 884744 | tf_op jit(solution)/shard_map/ppermute | solution.py:476
  25.2 1.3 %shard_map.53.part = f32[6,2,88,128]{3,2,1,0:T(8,128)S(1)} custom-call(f32[8,128]{1,0:T(8,128)S(1)} %broadcast_in_dim.4.table, f32[14,48,128]{2,1,0:T(8,128)S(1)} %collective-permute-done.5.shared, f32[5,48,128]{2,1,0:T(8,128)S(1)} %collective-permute-done.9.near, f32[5,48,128]{2,1,0:T(8,128)S(1)} %collective-permute-done.10.far), custom_call_target="tpu_custom_call" | custom-call | flops 3000000000 | tf_op jit(solution)/shard_map/pallas_call | solution.py:442
  26.5 5.7 %collective-permute-done.8.got = f32[6,2,48,128]{3,2,1,0:T(8,128)S(1)} collective-permute-done((f32[6,2,48,128]{3,2,1,0:T(8,128)S(1)}, f32[6,2,48,128]{3,2,1,0:T(8,128)S(1)}, u32[]{:S(2)}, u32[]{:S(2)}) %collective-permute-start.8) | collective-permute-done | bytes 294944 | tf_op jit(solution)/shard_map/ppermute | solution.py:476
  32.3 0.1 shard_map.52.edge
  32.4 1.0 %shard_map.54._ = f32[1,6,2,256,128]{4,3,2,1,0:T(8,128)} custom-call(f32[6,2,64,128]{3,2,1,0:T(8,128)S(1)} %shard_map.52.edge, f32[6,2,192,128]{3,2,1,0:T(8,128)S(1)} %get-tuple-element.44.mid, f32[6,2,88,128]{3,2,1,0:T(8,128)S(1)} %shard_map.53.part), custom_call_target="tpu_custom_call" | custom-call | tf_op jit(solution)/shard_map/pallas_call | solution.py:563
  33.4 0.0 collective-permute-done.7.bands
  33.5 1.0 %shard_map.55 = f32[1,6,2,256,128]{4,3,2,1,0:T(8,128)} custom-call(f32[6,2,192,128]{3,2,1,0:T(8,128)S(1)} %get-tuple-element.44.mid, f32[6,2,56,128]{3,2,1,0:T(8,128)S(1)} %collective-permute-done.7.bands, f32[1,6,2,256,128]{4,3,2,1,0:T(8,128)} %shard_map.54._), custom_call_target="tpu_custom_call", output_to_operand_aliasing={{}: (2, {})} | custom-call | tf_op jit(solution)/shard_map/pallas_call | solution.py:572
  (12 shorter events, 0.0 us)
Async XLA Ops:
  0.0 4.9 %copy-start.1 = (s32[1,2,256,128]{3,2,1,0:T(8,128)S(1)}, s32[1,2,256,128]{3,2,1,0:T(8,128)}, u32[]{:S(2)}) copy-start(s32[1,2,256,128]{3,2,1,0:T(8,128)} %material.7) | copy-start | bytes 786436
  0.0 4.9 %copy-start = (f32[1,6,2,256,128]{4,3,2,1,0:T(8,128)S(1)}, f32[1,6,2,256,128]{4,3,2,1,0:T(8,128)}, u32[]{:S(2)}) copy-start(f32[1,6,2,256,128]{4,3,2,1,0:T(8,128)} %seeds.7) | copy-start | bytes 4718596
  0.0 4.8 %copy-start.2 = (f32[4]{0:T(128)S(1)}, f32[4]{0:T(128)}, u32[]{:S(2)}) copy-start(f32[4]{0:T(128)} %param.7) | copy-start | bytes 52
  0.0 4.8 %copy-start.3 = (f32[4]{0:T(128)S(1)}, f32[4]{0:T(128)}, u32[]{:S(2)}) copy-start(f32[4]{0:T(128)} %param.6) | copy-start | bytes 52
  1.7 11.1 %collective-permute-start.5 = (f32[14,48,128]{2,1,0:T(8,128)S(1)}, f32[14,48,128]{2,1,0:T(8,128)S(1)}, u32[]{:S(2)}, u32[]{:S(2)}) collective-permute-start(f32[14,48,128]{2,1,0:T(8,128)S(1)} %shard_map.46), channel_id=1, source_target_pairs={{0,16},{8,24},{16,0},{24,8},{1,17},{9,25},{17,1},{25,9},{2,18},{10... | collective-permute-start | bytes 1032200 | tf_op jit(solution)/shard_map/ppermute | solution.py:476
  5.7 5.8 %collective-permute-start = (f32[5,80,128]{2,1,0:T(8,128)S(1)}, f32[5,80,128]{2,1,0:T(8,128)S(1)}, u32[]{:S(2)}, u32[]{:S(2)}) collective-permute-start(f32[5,80,128]{2,1,0:T(8,128)S(1)} %get-tuple-element.31), channel_id=1, source_target_pairs={{0,8},{1,2},{2,1},{3,4},{4,3},{5,6},{6,5},{7,15},{8,0},{9,10},{10,... | collective-permute-start | bytes 614408 | tf_op jit(solution)/shard_map/ppermute | solution.py:472
  7.3 4.3 %collective-permute-start.1 = (f32[5,80,128]{2,1,0:T(8,128)S(1)}, f32[5,80,128]{2,1,0:T(8,128)S(1)}, u32[]{:S(2)}, u32[]{:S(2)}) collective-permute-start(f32[5,80,128]{2,1,0:T(8,128)S(1)} %get-tuple-element.34), channel_id=1, source_target_pairs={{0,1},{1,0},{2,3},{3,2},{4,5},{5,4},{6,7},{7,6},{8,9},{9,8},{10,11... | collective-permute-start | bytes 614408 | tf_op jit(solution)/shard_map/ppermute | solution.py:457
  7.5 11.3 %collective-permute-start.4 = (f32[5,208,128]{2,1,0:T(8,128)S(1)}, f32[5,208,128]{2,1,0:T(8,128)S(1)}, u32[]{:S(2)}, u32[]{:S(2)}) collective-permute-start(f32[5,208,128]{2,1,0:T(8,128)S(1)} %get-tuple-element.38), channel_id=1, source_target_pairs={{0,1},{1,0},{2,3},{3,2},{4,5},{5,4},{6,7},{7,6},{8,9},{9,8},{10,11... | collective-permute-start | bytes 1597448 | tf_op jit(solution)/shard_map/ppermute | solution.py:457
  7.8 9.5 %collective-permute-start.6 = (f32[5,208,128]{2,1,0:T(8,128)S(1)}, f32[5,208,128]{2,1,0:T(8,128)S(1)}, u32[]{:S(2)}, u32[]{:S(2)}) collective-permute-start(f32[5,208,128]{2,1,0:T(8,128)S(1)} %get-tuple-element.41), channel_id=1, source_target_pairs={{0,8},{1,2},{2,1},{3,4},{4,3},{5,6},{6,5},{7,15},{8,0},{9,10},{10,... | collective-permute-start | bytes 1597448 | tf_op jit(solution)/shard_map/ppermute | solution.py:472
  12.3 11.1 %collective-permute-start.2 = (f32[6,2,32,128]{3,2,1,0:T(8,128)S(1)}, f32[6,2,32,128]{3,2,1,0:T(8,128)S(1)}, u32[]{:S(2)}, u32[]{:S(2)}) collective-permute-start(f32[6,2,32,128]{3,2,1,0:T(8,128)S(1)} %get-tuple-element.36), channel_id=1, source_target_pairs={{0,16},{8,24},{16,0},{24,8},{1,17},{9,25},{17,1},{25,9},{2,18},{10... | collective-permute-start | bytes 589832 | tf_op jit(solution)/shard_map/ppermute | solution.py:476
  13.8 11.4 %collective-permute-start.10 = (f32[5,48,128]{2,1,0:T(8,128)S(1)}, f32[5,48,128]{2,1,0:T(8,128)S(1)}, u32[]{:S(2)}, u32[]{:S(2)}) collective-permute-start(f32[5,48,128]{2,1,0:T(8,128)S(1)} %get-tuple-element.52), channel_id=1, source_target_pairs={{0,7},{1,2},{2,1},{3,4},{4,3},{5,6},{6,5},{7,0},{8,15},{9,10},{10,... | collective-permute-start | bytes 368648 | tf_op jit(solution)/shard_map/ppermute | solution.py:472
  17.2 8.0 %collective-permute-start.9 = (f32[5,48,128]{2,1,0:T(8,128)S(1)}, f32[5,48,128]{2,1,0:T(8,128)S(1)}, u32[]{:S(2)}, u32[]{:S(2)}) collective-permute-start(f32[5,48,128]{2,1,0:T(8,128)S(1)} %get-tuple-element.51), channel_id=1, source_target_pairs={{0,1},{1,0},{2,3},{3,2},{4,5},{5,4},{6,7},{7,6},{8,9},{9,8},{10,11... | collective-permute-start | bytes 368648 | tf_op jit(solution)/shard_map/ppermute | solution.py:457
  17.2 6.2 %collective-permute-start.3 = (f32[6,2,16,128]{3,2,1,0:T(8,128)S(1)}, f32[6,2,16,128]{3,2,1,0:T(8,128)S(1)}, u32[]{:S(2)}, u32[]{:S(2)}) collective-permute-start(f32[6,2,16,128]{3,2,1,0:T(8,128)S(1)} %get-tuple-element.37), channel_id=1, source_target_pairs={{0,24},{8,16},{16,8},{24,0},{1,25},{9,17},{17,9},{25,1},{2,26},{10... | collective-permute-start | bytes 294920 | tf_op jit(solution)/shard_map/ppermute | solution.py:476
  20.0 13.5 %collective-permute-start.7 = (f32[6,2,56,128]{3,2,1,0:T(8,128)S(1)}, f32[6,2,56,128]{3,2,1,0:T(8,128)S(1)}, u32[]{:S(2)}, u32[]{:S(2)}) collective-permute-start(f32[6,2,56,128]{3,2,1,0:T(8,128)S(1)} %get-tuple-element.45), channel_id=1, source_target_pairs={{0,16},{8,24},{16,0},{24,8},{1,17},{9,25},{17,1},{25,9},{2,18},{10... | collective-permute-start | bytes 1032200 | tf_op jit(solution)/shard_map/ppermute | solution.py:476
  23.7 8.6 %collective-permute-start.8 = (f32[6,2,48,128]{3,2,1,0:T(8,128)S(1)}, f32[6,2,48,128]{3,2,1,0:T(8,128)S(1)}, u32[]{:S(2)}, u32[]{:S(2)}) collective-permute-start(f32[6,2,48,128]{3,2,1,0:T(8,128)S(1)} %get-tuple-element.49), channel_id=1, source_target_pairs={{0,8},{8,0},{16,24},{24,16},{1,9},{9,1},{17,25},{25,17},{2,10},{10... | collective-permute-start | bytes 884744 | tf_op jit(solution)/shard_map/ppermute | solution.py:476

commit v10 on v9

--- a/solution.py
+++ b/solution.py
@@ -14,7 +14,7 @@
 PLANES = 5
 REACH = 2
 SHARED = 80
-LARGE, MEDIUM, SMALL = 10**10, 3 * 10**9, 0
+LARGE, MEDIUM, SMALL = 10**10, 25 * 10**8, 0
 
 magnetic_coeff = 0.5
 
@@ -290,7 +290,8 @@
     return prepared(f[:3], f[3:6], f[6], table_entries(table))
 
 
-def shared_halo_kernel(sub, table, shared, near, far):
+def shared_halo_kernel(sub, table, shared, near, far, done):
+    done[...] = jnp.zeros(done.shape, done.dtype)
     send_halos(sub, shared_fields(table, shared), near, far, bands_packed)
 
 
@@ -325,15 +326,20 @@
             strip[c, p] = y_packed(middle_out(away[:half]), middle_out(away[half:]))
 
 
-def middle_kernel(spans, shared, sub, sub_size, table, seeds, material, near, far, mid, bands):
+def middle_kernel(
+    spans, sub, sub_size, tile, table, seeds, material, near, far, edge, _, mid, bands, beside
+):
     size_x = seeds.shape[3]
     keep = (BAND, size_x - BAND)
     planes, = weighted_planes(seeds, material, table, near, far, spans, (keep,), sub, sub_size)
-    half = bands.shape[2]
+    odd = lax.rem(lax.axis_index(tile), 2) == 1
+    half, quarter = bands.shape[2], BAND // 2
     for c in range(6):
         for p in range(seeds.shape[2]):
             mid[c, p] = planes[c][p]
             bands[c, p] = y_packed(planes[c][p][:half], planes[c][p][-half:])
+            by = jnp.where(odd, edge[c, p, :BAND], edge[c, p, BAND:])
+            beside[c, p] = y_packed(middle_out(by[:quarter]), middle_out(by[quarter:]))
 
 
 def whole_kernel(spans, sub, sub_size, table, seeds, material, near, far, out):
@@ -370,59 +376,49 @@
             summed[c, p, :BAND] = low
             summed[c, p, BAND:] = high
             by, away = jnp.where(odd, low, high), jnp.where(odd, high, low)
-            send[c, p, :BAND] = by
-            send[c, p, BAND:] = y_packed(away[:half], away[half:])
-
-
-def seam_kernel(tile, summed, got, strip, out):
-    odd = lax.rem(lax.axis_index(tile), 2) == 1
-    half = BAND // 2
-    for c in range(summed.shape[0]):
-        for p in range(summed.shape[1]):
-            by = got[c, p, :BAND]
-            corners = y_unpacked(got[c, p, BAND:])
-            block = strip[c, p]
-            lane = lane_of(block.shape)
-            middle = (lane >= BAND) & (lane < block.shape[1] - BAND)
-            first = jnp.where(middle, middle_out(block), corners[0])
-            second = jnp.where(middle, block, corners[1])
-            away = jnp.concatenate([first, second], axis=0)
-            out[c, p, :BAND] = summed[c, p, :BAND] + jnp.where(odd, by, away)
-            out[c, p, BAND:] = summed[c, p, BAND:] + jnp.where(odd, away, by)
-
-
-def early_kernel(edge, mid, part, out, whole, sems):
+            send[c, p, :half] = y_packed(by[:half], by[half:])
+            send[c, p, half:] = y_packed(away[:half], away[half:])
+
+
+def strip_of(corners, block):
+    lane = lane_of(block.shape)
+    middle = (lane >= BAND) & (lane < block.shape[-1] - BAND)
+    first = jnp.where(middle, middle_out(block), corners[0])
+    second = jnp.where(middle, block, corners[1])
+    return jnp.concatenate([first, second], axis=0)
+
+
+def early_kernel(mid, part, out, whole, sem):
     size_x = out.shape[3]
     skip = HALO // 2
     count = part.shape[2] - 2 * skip
     start = (size_x - count) // 2
-    rows = pl.ds(start, count)
-    low, high = pl.ds(0, BAND), pl.ds(size_x - BAND, BAND)
     for c in range(mid.shape[0]):
         for p in range(mid.shape[1]):
             whole[c, p] = mid[c, p, start - BAND : start - BAND + count] + part[c, p, skip : skip + count]
-    copies = [
-        pltpu.make_async_copy(whole, out.at[0, :, :, rows], sems.at[0]),
-        pltpu.make_async_copy(edge.at[:, :, pl.ds(0, BAND)], out.at[0, :, :, low], sems.at[1]),
-        pltpu.make_async_copy(edge.at[:, :, pl.ds(BAND, BAND)], out.at[0, :, :, high], sems.at[2]),
-    ]
-    for copy in copies:
-        copy.start()
-    for copy in copies:
-        copy.wait()
-
-
-def last_kernel(mid, bands, _, out, low, high, sems):
-    half = bands.shape[2]
+    copy = pltpu.make_async_copy(whole, out.at[0, :, :, pl.ds(start, count)], sem)
+    copy.start()
+    copy.wait()
+
+
+def last_kernel(tile, mid, bands, summed, got, strip, beside, _, out, low, high, sems):
+    odd = lax.rem(lax.axis_index(tile), 2) == 1
+    half, count = bands.shape[2], low.shape[2]
+    quarter = BAND // 2
     size_x = out.shape[3]
     copies = []
     for c in range(mid.shape[0]):
         for p in range(mid.shape[1]):
             first, second = y_unpacked(bands[c, p])
-            low[c, p] = mid[c, p, :half] + first
-            high[c, p] = mid[c, p, -half:] + second
-        for k, (rows, start) in enumerate(((low, BAND), (high, size_x - BAND - half))):
-            copies.append(pltpu.make_async_copy(rows.at[c], out.at[0, c, :, pl.ds(start, half)], sems.at[2 * c + k]))
+            low[c, p, BAND:] = mid[c, p, :half] + first
+            high[c, p, :half] = mid[c, p, -half:] + second
+            straight = got[c, p, :quarter]
+            by = strip_of((straight, middle_out(straight)), beside[c, p])
+            away = strip_of(y_unpacked(got[c, p, quarter:]), strip[c, p])
+            low[c, p, :BAND] = summed[c, p, :BAND] + jnp.where(odd, by, away)
+            high[c, p, half:] = summed[c, p, BAND:] + jnp.where(odd, away, by)
+        for k, (rows, start) in enumerate(((low, 0), (high, size_x - count))):
+            copies.append(pltpu.make_async_copy(rows.at[c], out.at[0, c, :, pl.ds(start, count)], sems.at[2 * c + k]))
             copies[-1].start()
     for copy in copies:
         copy.wait()
@@ -530,55 +526,53 @@
     strip = swapped(strip, 3, tile_size)
 
     shape = (PLANES, packed_rows, size_y)
-    shared_near, shared_far = called(
-        functools.partial(shared_halo_kernel, "sub"), [shape, shape], table, shared, flops=LARGE
-    )
-    shared_near, inner_far = after(shared_near, inner_far)
+    shared_near, shared_far, done = called(
+        functools.partial(shared_halo_kernel, "sub"), [shape, shape, (8, size_y)], table, shared, flops=LARGE
+    )
     shared_near = near_exchange(shared_near, sub_size)
     shared_far = far_exchange(shared_far, sub_size, tile_size, ends_by_tile=False)
 
-    mid, bands = called(
-        functools.partial(middle_kernel, inner, keep, "sub", sub_size),
-        [(6, depth, rows, size_y), (6, depth, (rows - SHARED) // 2, size_y)],
-        table, seeds, material, inner_near, inner_far,
+    mid, bands, beside = called(
+        functools.partial(middle_kernel, inner, "sub", sub_size, "tile"),
+        [(6, depth, rows, size_y), (6, depth, (rows - SHARED) // 2, size_y), (6, depth, BAND // 2, size_y)],
+        table, seeds, material, inner_near, inner_far, edge, done,
     )
     bands = swapped(bands, 2, tile_size)
+    beside = swapped(beside, 1, tile_size)
 
     corner, strip, mid = after(corner, strip, mid)
     summed, send = called(
         functools.partial(corner_kernel, "tile"),
-        [(6, depth, 2 * BAND, size_y), (6, depth, BAND + BAND // 2, size_y)],
+        [(6, depth, 2 * BAND, size_y), (6, depth, BAND, size_y)],
         edge, corner, flops=SMALL,
     )
     got = swapped(send, 1, tile_size)
+    beside, shared_near = after(beside, shared_near)
     part, = called(
         functools.partial(shared_kernel, span, size_x, "sub", sub_size),
         [(6, depth, SHARED + HALO, size_y)], table, shared, shared_near, shared_far, flops=MEDIUM,
     )
-    edge, = called(
-        functools.partial(seam_kernel, "tile"), [(6, depth, 2 * BAND, size_y)], summed, got, strip
-    )
-    half = (rows - SHARED) // 2
     whole = jax.ShapeDtypeStruct(seeds.shape, jnp.float32)
     early = pl.pallas_call(
         early_kernel,
         out_shape=whole,
-        in_specs=[VMEM] * 3,
+        in_specs=[VMEM] * 2,
         out_specs=HBM,
-        scratch_shapes=[pltpu.VMEM((6, depth, SHARED, size_y), jnp.float32), pltpu.SemaphoreType.DMA((3,))],
+        scratch_shapes=[pltpu.VMEM((6, depth, SHARED, size_y), jnp.float32), pltpu.SemaphoreType.DMA],
         compiler_params=PARAMS,
         cost_estimate=cost(0),
-    )(edge, mid, part)
+    )(mid, part)
     return pl.pallas_call(
-        last_kernel,
+        functools.partial(last_kernel, "tile"),
         out_shape=whole,
-        in_specs=[VMEM, VMEM, HBM],
+        in_specs=[VMEM] * 6 + [HBM],
         out_specs=HBM,
-        scratch_shapes=[pltpu.VMEM((6, depth, half, size_y), jnp.float32)] * 2 + [pltpu.SemaphoreType.DMA((12,))],
-        input_output_aliases={2: 0},
+        scratch_shapes=[pltpu.VMEM((6, depth, (size_x - SHARED) // 2, size_y), jnp.float32)] * 2
+        + [pltpu.SemaphoreType.DMA((12,))],
+        input_output_aliases={6: 0},
         compiler_params=PARAMS,
         cost_estimate=cost(0),
-    )(mid, bands, early)
+    )(mid, bands, summed, got, strip, beside, early)
 
 
 def any_lattice(seeds, material, decay, coupling, sub_size, tile_size):

time: 34.6 us -> 31 us (0.90)
  waiting for transfers between devices: 11.6 us -> 5.76 us
  starting transfers between devices: 13.5 us -> 15.2 us
  Pallas kernels: 9.07 us -> 9.47 us
    ppermute x5 -> x6, waiting for transfers between devices: 8.06 us -> 3.18 us  [swapped(): lax.ppermute(value, 'tile', [(t, t ^ bits) for t in range(tile_size)])]
    ppermute x5 -> x6, starting transfers between devices: 7.75 us -> 8.72 us  [swapped(): lax.ppermute(value, 'tile', [(t, t ^ bits) for t in range(tile_size)])]
    ppermute x3, waiting for transfers between devices: 3.52 us -> 2.58 us  [far_exchange(): return lax.ppermute(far, ('tile', 'sub'), pairs)]
    ppermute x3, starting transfers between devices: 5.2 us -> 5.86 us  [far_exchange(): return lax.ppermute(far, ('tile', 'sub'), pairs)]
    pallas_call x7 -> x6, Pallas kernels: 5.32 us -> 5.7 us  [called(): pl.pallas_call(kernel, out_shape=outs, in_specs=[VMEM] * len(operands), o...]
  transfers between devices with their start and end apart: 11 -> 12, of which waited for: 5 -> 2; matrix products, arithmetic and copies ran while one was open for 1% -> 1% of each run, Pallas kernels for 18% -> 21%
where the time goes in v10:
time: 31 us; the launch traced here: 30.8 us
  starting transfers between devices  15.2 us (49%)
  Pallas kernels  9.47 us (31%)
  waiting for transfers between devices  5.76 us (19%)
    ppermute x6, starting transfers between devices, swapped(): lax.ppermute(value, 'tile', [(t, t ^ bits) for t in range(tile_size)])  8.72 us
    ppermute x3, starting transfers between devices, far_exchange(): return lax.ppermute(far, ('tile', 'sub'), pairs)  5.86 us
    pallas_call x6, Pallas kernels, called(): pl.pallas_call(kernel, out_shape=outs, in_specs=[VMEM] * len(operands), o...  5.7 us
    ppermute x6, waiting for transfers between devices, swapped(): lax.ppermute(value, 'tile', [(t, t ^ bits) for t in range(tile_size)])  3.18 us
    ppermute x3, waiting for transfers between devices, far_exchange(): return lax.ppermute(far, ('tile', 'sub'), pairs)  2.58 us
    pallas_call x1, Pallas kernels, two_by_two(): pl.pallas_call(functools.partial(share_kernel, fetched, HALO // 2), out_s...  1.72 us
    pallas_call x1, Pallas kernels, two_by_two(): pl.pallas_call(functools.partial(last_kernel, 'tile'), out_shape=whole, i...  1.2 us
    pallas_call x1, Pallas kernels, two_by_two(): pl.pallas_call(early_kernel, out_shape=whole, in_specs=[VMEM] * 2, out_sp...  0.86 us
  transfers between devices with their start and end apart: 12, of which 2 were waited for; matrix products, arithmetic and copies ran while one was open for 1% of the time, Pallas kernels for 21%

profile of v10, /device:TPU:0, one launch (start us, length us, event | category | flops | bytes accessed | tf_op | source)
XLA Modules:
  0.0 30.8 jit_solution(17654513028858113846)
XLA Ops:
  0.0 1.7 %shard_map.46 = f32[14,48,128]{2,1,0:T(8,128)S(1)} custom-call(f32[1,6,2,256,128]{4,3,2,1,0:T(8,128)} %seeds.7, s32[1,2,256,128]{3,2,1,0:T(8,128)} %material.7), custom_call_target="tpu_custom_call" | custom-call | tf_op jit(solution)/shard_map/pallas_call | solution.py:495
  1.7 3.0 %collective-permute-start.6 = (f32[14,48,128]{2,1,0:T(8,128)S(1)}, f32[14,48,128]{2,1,0:T(8,128)S(1)}, u32[]{:S(2)}, u32[]{:S(2)}) collective-permute-start(f32[14,48,128]{2,1,0:T(8,128)S(1)} %shard_map.46), channel_id=1, source_target_pairs={{0,16},{8,24},{16,0},{24,8},{1,17},{9,25},{17,1},{25,9},{2,18},{10... | collective-permute-start | bytes 1032200 | tf_op jit(solution)/shard_map/ppermute | solution.py:472
  4.8 0.1 pad_maximum_fusion
  4.9 0.1 broadcast_in_dim.4.table
  4.9 0.8 %shard_map.47 = (f32[5,80,128]{2,1,0:T(8,128)S(1)}, f32[5,80,128]{2,1,0:T(8,128)S(1)}, f32[5,208,128]{2,1,0:T(8,128)S(1)}, f32[5,208,128]{2,1,0:T(8,128)S(1)}) custom-call(f32[8,128]{1,0:T(8,128)S(1)} %broadcast_in_dim.4.table, f32[1,6,2,256,128]{4,3,2,1,0:T(8,128)S(1)} %copy-done, s32[1,2,256,128]{3,2,1,0:T(8,128)S(1)} %copy-done.1), custom_call_target="tpu_custom_call" | custom-call | tf_op jit(solution)/shard_map/pallas_call | solution.py:438
  5.7 1.6 %collective-permute-start = (f32[5,80,128]{2,1,0:T(8,128)S(1)}, f32[5,80,128]{2,1,0:T(8,128)S(1)}, u32[]{:S(2)}, u32[]{:S(2)}) collective-permute-start(f32[5,80,128]{2,1,0:T(8,128)S(1)} %get-tuple-element.33), channel_id=1, source_target_pairs={{0,8},{1,2},{2,1},{3,4},{4,3},{5,6},{6,5},{7,15},{8,0},{9,10},{10,... | collective-permute-start | bytes 614408 | tf_op jit(solution)/shard_map/ppermute | solution.py:468
  7.3 0.2 collective-permute-start.1
  7.5 0.3 %collective-permute-start.4 = (f32[5,208,128]{2,1,0:T(8,128)S(1)}, f32[5,208,128]{2,1,0:T(8,128)S(1)}, u32[]{:S(2)}, u32[]{:S(2)}) collective-permute-start(f32[5,208,128]{2,1,0:T(8,128)S(1)} %get-tuple-element.40), channel_id=1, source_target_pairs={{0,1},{1,0},{2,3},{3,2},{4,5},{5,4},{6,7},{7,6},{8,9},{9,8},{10,11... | collective-permute-start | bytes 1597448 | tf_op jit(solution)/shard_map/ppermute | solution.py:453
  7.8 1.2 %collective-permute-start.5 = (f32[5,208,128]{2,1,0:T(8,128)S(1)}, f32[5,208,128]{2,1,0:T(8,128)S(1)}, u32[]{:S(2)}, u32[]{:S(2)}) collective-permute-start(f32[5,208,128]{2,1,0:T(8,128)S(1)} %get-tuple-element.41), channel_id=1, source_target_pairs={{0,8},{1,2},{2,1},{3,4},{4,3},{5,6},{6,5},{7,15},{8,0},{9,10},{10,... | collective-permute-start | bytes 1597448 | tf_op jit(solution)/shard_map/ppermute | solution.py:468
  9.0 2.6 %collective-permute-done.far = f32[5,80,128]{2,1,0:T(8,128)S(1)} collective-permute-done((f32[5,80,128]{2,1,0:T(8,128)S(1)}, f32[5,80,128]{2,1,0:T(8,128)S(1)}, u32[]{:S(2)}, u32[]{:S(2)}) %collective-permute-start) | collective-permute-done | bytes 204832 | tf_op jit(solution)/shard_map/ppermute | solution.py:468
  11.5 0.1 pad_maximum_fusion.1
  11.6 0.0 collective-permute-done.1.near
  11.6 0.1 broadcast_in_dim.5.table
  11.7 0.6 %shard_map.48 = (f32[6,2,64,128]{3,2,1,0:T(8,128)S(1)}, f32[6,2,32,128]{3,2,1,0:T(8,128)S(1)}, f32[6,2,16,128]{3,2,1,0:T(8,128)S(1)}) custom-call(f32[8,128]{1,0:T(8,128)S(1)} %broadcast_in_dim.5.table, f32[1,6,2,256,128]{4,3,2,1,0:T(8,128)S(1)} %copy-done, s32[1,2,256,128]{3,2,1,0:T(8,128)S(1)} %copy-done.1, f32[5,80,128]{2,1,0:T(8,128)S(1)} %collective-permute-done.1.near, ...), custom_call_target="tpu_custom_call" | custom-call | tf_op jit(solution)/shard_map/pallas_call | solution.py:438
  12.3 1.5 %collective-permute-start.3 = (f32[6,2,16,128]{3,2,1,0:T(8,128)S(1)}, f32[6,2,16,128]{3,2,1,0:T(8,128)S(1)}, u32[]{:S(2)}, u32[]{:S(2)}) collective-permute-start(f32[6,2,16,128]{3,2,1,0:T(8,128)S(1)} %get-tuple-element.39), channel_id=1, source_target_pairs={{0,24},{8,16},{16,8},{24,0},{1,25},{9,17},{17,9},{25,1},{2,26},{10... | collective-permute-start | bytes 294920 | tf_op jit(solution)/shard_map/ppermute | solution.py:472
  13.8 1.5 %collective-permute-start.2 = (f32[6,2,32,128]{3,2,1,0:T(8,128)S(1)}, f32[6,2,32,128]{3,2,1,0:T(8,128)S(1)}, u32[]{:S(2)}, u32[]{:S(2)}) collective-permute-start(f32[6,2,32,128]{3,2,1,0:T(8,128)S(1)} %get-tuple-element.38), channel_id=1, source_target_pairs={{0,16},{8,24},{16,0},{24,8},{1,17},{9,25},{17,1},{25,9},{2,18},{10... | collective-permute-start | bytes 589832 | tf_op jit(solution)/shard_map/ppermute | solution.py:472
  15.3 1.0 %shard_map.49 = (f32[5,48,128]{2,1,0:T(8,128)S(1)}, f32[5,48,128]{2,1,0:T(8,128)S(1)}, f32[8,128]{1,0:T(8,128)S(1)}) custom-call(f32[8,128]{1,0:T(8,128)S(1)} %broadcast_in_dim.4.table, f32[14,48,128]{2,1,0:T(8,128)S(1)} %collective-permute-done.6.shared), custom_call_target="tpu_custom_call" | custom-call | flops 10000000000 | tf_op jit(solution)/shard_map/pallas_call | solution.py:438
  16.3 0.1 collective-permute-start.10
  16.4 0.0 collective-permute-done.4.near
  16.4 3.1 %collective-permute-start.11 = (f32[5,48,128]{2,1,0:T(8,128)S(1)}, f32[5,48,128]{2,1,0:T(8,128)S(1)}, u32[]{:S(2)}, u32[]{:S(2)}) collective-permute-start(f32[5,48,128]{2,1,0:T(8,128)S(1)} %get-tuple-element.56), channel_id=1, source_target_pairs={{0,7},{1,2},{2,1},{3,4},{4,3},{5,6},{6,5},{7,0},{8,15},{9,10},{10,... | collective-permute-start | bytes 368648 | tf_op jit(solution)/shard_map/ppermute | solution.py:468
  19.5 1.7 %shard_map.50 = (f32[6,2,192,128]{3,2,1,0:T(8,128)S(1)}, f32[6,2,56,128]{3,2,1,0:T(8,128)S(1)}, f32[6,2,16,128]{3,2,1,0:T(8,128)S(1)}) custom-call(f32[8,128]{1,0:T(8,128)S(1)} %broadcast_in_dim.4.table, f32[1,6,2,256,128]{4,3,2,1,0:T(8,128)S(1)} %copy-done, s32[1,2,256,128]{3,2,1,0:T(8,128)S(1)} %copy-done.1, ...), custom_call_target="tpu_custom_call" | custom-call | tf_op jit(solution)/shard_map/pallas_call | solution.py:438
  21.3 0.6 %collective-permute-start.7 = (f32[6,2,56,128]{3,2,1,0:T(8,128)S(1)}, f32[6,2,56,128]{3,2,1,0:T(8,128)S(1)}, u32[]{:S(2)}, u32[]{:S(2)}) collective-permute-start(f32[6,2,56,128]{3,2,1,0:T(8,128)S(1)} %get-tuple-element.47), channel_id=1, source_target_pairs={{0,16},{8,24},{16,0},{24,8},{1,17},{9,25},{17,1},{25,9},{2,18},{10... | collective-permute-start | bytes 1032200 | tf_op jit(solution)/shard_map/ppermute | solution.py:472
  21.8 0.8 %collective-permute-start.9 = (f32[6,2,16,128]{3,2,1,0:T(8,128)S(1)}, f32[6,2,16,128]{3,2,1,0:T(8,128)S(1)}, u32[]{:S(2)}, u32[]{:S(2)}) collective-permute-start(f32[6,2,16,128]{3,2,1,0:T(8,128)S(1)} %get-tuple-element.52), channel_id=1, source_target_pairs={{0,8},{8,0},{16,24},{24,16},{1,9},{9,1},{17,25},{25,17},{2,10},{10... | collective-permute-start | bytes 294920 | tf_op jit(solution)/shard_map/ppermute | solution.py:472
  22.6 0.0 collective-permute-done.2.corner
  22.6 0.3 shard_map.51
  23.0 1.3 %collective-permute-start.8 = (f32[6,2,32,128]{3,2,1,0:T(8,128)S(1)}, f32[6,2,32,128]{3,2,1,0:T(8,128)S(1)}, u32[]{:S(2)}, u32[]{:S(2)}) collective-permute-start(f32[6,2,32,128]{3,2,1,0:T(8,128)S(1)} %get-tuple-element.50), channel_id=1, source_target_pairs={{0,8},{8,0},{16,24},{24,16},{1,9},{9,1},{17,25},{25,17},{2,10},{10... | collective-permute-start | bytes 589832 | tf_op jit(solution)/shard_map/ppermute | solution.py:472
  24.3 3.2 %collective-permute-done.9.beside = f32[6,2,16,128]{3,2,1,0:T(8,128)S(1)} collective-permute-done((f32[6,2,16,128]{3,2,1,0:T(8,128)S(1)}, f32[6,2,16,128]{3,2,1,0:T(8,128)S(1)}, u32[]{:S(2)}, u32[]{:S(2)}) %collective-permute-start.9) | collective-permute-done | bytes 98336 | tf_op jit(solution)/shard_map/ppermute | solution.py:472
  27.4 0.0 collective-permute-done.11.far
  27.4 1.3 %shard_map.52.part = f32[6,2,88,128]{3,2,1,0:T(8,128)S(1)} custom-call(f32[8,128]{1,0:T(8,128)S(1)} %broadcast_in_dim.4.table, f32[14,48,128]{2,1,0:T(8,128)S(1)} %collective-permute-done.6.shared, f32[5,48,128]{2,1,0:T(8,128)S(1)} %collective-permute-done.10.near, f32[5,48,128]{2,1,0:T(8,128)S(1)} %collective-permute-done.11.far), custom_call_target="tpu_custom_call" | custom-call | flops 2500000000 | tf_op jit(solution)/shard_map/pallas_call | solution.py:438
  28.7 0.9 %shard_map.53._ = f32[1,6,2,256,128]{4,3,2,1,0:T(8,128)} custom-call(f32[6,2,192,128]{3,2,1,0:T(8,128)S(1)} %get-tuple-element.46.mid, f32[6,2,88,128]{3,2,1,0:T(8,128)S(1)} %shard_map.52.part), custom_call_target="tpu_custom_call" | custom-call | tf_op jit(solution)/shard_map/pallas_call | solution.py:556
  29.6 0.0 collective-permute-done.8.got
  29.6 1.2 %shard_map.54 = f32[1,6,2,256,128]{4,3,2,1,0:T(8,128)} custom-call(f32[6,2,192,128]{3,2,1,0:T(8,128)S(1)} %get-tuple-element.46.mid, f32[6,2,56,128]{3,2,1,0:T(8,128)S(1)} %collective-permute-done.7.bands, f32[6,2,64,128]{3,2,1,0:T(8,128)S(1)} %get-tuple-element.49.summed, ...), custom_call_target="tpu_custom_call", output_to_operand_aliasing={{}: (6, {})} | custom-call | tf_op jit(solution)/shard_map/pallas_call | solution.py:565
  (13 shorter events, 0.0 us)
Async XLA Ops:
  0.0 4.9 %copy-start.1 = (s32[1,2,256,128]{3,2,1,0:T(8,128)S(1)}, s32[1,2,256,128]{3,2,1,0:T(8,128)}, u32[]{:S(2)}) copy-start(s32[1,2,256,128]{3,2,1,0:T(8,128)} %material.7) | copy-start | bytes 786436
  0.0 4.9 %copy-start = (f32[1,6,2,256,128]{4,3,2,1,0:T(8,128)S(1)}, f32[1,6,2,256,128]{4,3,2,1,0:T(8,128)}, u32[]{:S(2)}) copy-start(f32[1,6,2,256,128]{4,3,2,1,0:T(8,128)} %seeds.7) | copy-start | bytes 4718596
  0.0 4.8 %copy-start.2 = (f32[4]{0:T(128)S(1)}, f32[4]{0:T(128)}, u32[]{:S(2)}) copy-start(f32[4]{0:T(128)} %param.7) | copy-start | bytes 52
  0.0 4.8 %copy-start.3 = (f32[4]{0:T(128)S(1)}, f32[4]{0:T(128)}, u32[]{:S(2)}) copy-start(f32[4]{0:T(128)} %param.6) | copy-start | bytes 52
  1.7 13.6 %collective-permute-start.6 = (f32[14,48,128]{2,1,0:T(8,128)S(1)}, f32[14,48,128]{2,1,0:T(8,128)S(1)}, u32[]{:S(2)}, u32[]{:S(2)}) collective-permute-start(f32[14,48,128]{2,1,0:T(8,128)S(1)} %shard_map.46), channel_id=1, source_target_pairs={{0,16},{8,24},{16,0},{24,8},{1,17},{9,25},{17,1},{25,9},{2,18},{10... | collective-permute-start | bytes 1032200 | tf_op jit(solution)/shard_map/ppermute | solution.py:472
  5.7 5.8 %collective-permute-start = (f32[5,80,128]{2,1,0:T(8,128)S(1)}, f32[5,80,128]{2,1,0:T(8,128)S(1)}, u32[]{:S(2)}, u32[]{:S(2)}) collective-permute-start(f32[5,80,128]{2,1,0:T(8,128)S(1)} %get-tuple-element.33), channel_id=1, source_target_pairs={{0,8},{1,2},{2,1},{3,4},{4,3},{5,6},{6,5},{7,15},{8,0},{9,10},{10,... | collective-permute-start | bytes 614408 | tf_op jit(solution)/shard_map/ppermute | solution.py:468
  7.3 4.3 %collective-permute-start.1 = (f32[5,80,128]{2,1,0:T(8,128)S(1)}, f32[5,80,128]{2,1,0:T(8,128)S(1)}, u32[]{:S(2)}, u32[]{:S(2)}) collective-permute-start(f32[5,80,128]{2,1,0:T(8,128)S(1)} %get-tuple-element.36), channel_id=1, source_target_pairs={{0,1},{1,0},{2,3},{3,2},{4,5},{5,4},{6,7},{7,6},{8,9},{9,8},{10,11... | collective-permute-start | bytes 614408 | tf_op jit(solution)/shard_map/ppermute | solution.py:453
  7.5 9.0 %collective-permute-start.4 = (f32[5,208,128]{2,1,0:T(8,128)S(1)}, f32[5,208,128]{2,1,0:T(8,128)S(1)}, u32[]{:S(2)}, u32[]{:S(2)}) collective-permute-start(f32[5,208,128]{2,1,0:T(8,128)S(1)} %get-tuple-element.40), channel_id=1, source_target_pairs={{0,1},{1,0},{2,3},{3,2},{4,5},{5,4},{6,7},{7,6},{8,9},{9,8},{10,11... | collective-permute-start | bytes 1597448 | tf_op jit(solution)/shard_map/ppermute | solution.py:453
  7.8 11.8 %collective-permute-start.5 = (f32[5,208,128]{2,1,0:T(8,128)S(1)}, f32[5,208,128]{2,1,0:T(8,128)S(1)}, u32[]{:S(2)}, u32[]{:S(2)}) collective-permute-start(f32[5,208,128]{2,1,0:T(8,128)S(1)} %get-tuple-element.41), channel_id=1, source_target_pairs={{0,8},{1,2},{2,1},{3,4},{4,3},{5,6},{6,5},{7,15},{8,0},{9,10},{10,... | collective-permute-start | bytes 1597448 | tf_op jit(solution)/shard_map/ppermute | solution.py:468
  12.3 9.5 %collective-permute-start.3 = (f32[6,2,16,128]{3,2,1,0:T(8,128)S(1)}, f32[6,2,16,128]{3,2,1,0:T(8,128)S(1)}, u32[]{:S(2)}, u32[]{:S(2)}) collective-permute-start(f32[6,2,16,128]{3,2,1,0:T(8,128)S(1)} %get-tuple-element.39), channel_id=1, source_target_pairs={{0,24},{8,16},{16,8},{24,0},{1,25},{9,17},{17,9},{25,1},{2,26},{10... | collective-permute-start | bytes 294920 | tf_op jit(solution)/shard_map/ppermute | solution.py:472
  13.8 8.8 %collective-permute-start.2 = (f32[6,2,32,128]{3,2,1,0:T(8,128)S(1)}, f32[6,2,32,128]{3,2,1,0:T(8,128)S(1)}, u32[]{:S(2)}, u32[]{:S(2)}) collective-permute-start(f32[6,2,32,128]{3,2,1,0:T(8,128)S(1)} %get-tuple-element.38), channel_id=1, source_target_pairs={{0,16},{8,24},{16,0},{24,8},{1,17},{9,25},{17,1},{25,9},{2,18},{10... | collective-permute-start | bytes 589832 | tf_op jit(solution)/shard_map/ppermute | solution.py:472
  16.3 7.9 %collective-permute-start.10 = (f32[5,48,128]{2,1,0:T(8,128)S(1)}, f32[5,48,128]{2,1,0:T(8,128)S(1)}, u32[]{:S(2)}, u32[]{:S(2)}) collective-permute-start(f32[5,48,128]{2,1,0:T(8,128)S(1)} %get-tuple-element.53), channel_id=1, source_target_pairs={{0,1},{1,0},{2,3},{3,2},{4,5},{5,4},{6,7},{7,6},{8,9},{9,8},{10,11... | collective-permute-start | bytes 368648 | tf_op jit(solution)/shard_map/ppermute | solution.py:453
  16.4 11.0 %collective-permute-start.11 = (f32[5,48,128]{2,1,0:T(8,128)S(1)}, f32[5,48,128]{2,1,0:T(8,128)S(1)}, u32[]{:S(2)}, u32[]{:S(2)}) collective-permute-start(f32[5,48,128]{2,1,0:T(8,128)S(1)} %get-tuple-element.56), channel_id=1, source_target_pairs={{0,7},{1,2},{2,1},{3,4},{4,3},{5,6},{6,5},{7,0},{8,15},{9,10},{10,... | collective-permute-start | bytes 368648 | tf_op jit(solution)/shard_map/ppermute | solution.py:468
  21.3 8.3 %collective-permute-start.7 = (f32[6,2,56,128]{3,2,1,0:T(8,128)S(1)}, f32[6,2,56,128]{3,2,1,0:T(8,128)S(1)}, u32[]{:S(2)}, u32[]{:S(2)}) collective-permute-start(f32[6,2,56,128]{3,2,1,0:T(8,128)S(1)} %get-tuple-element.47), channel_id=1, source_target_pairs={{0,16},{8,24},{16,0},{24,8},{1,17},{9,25},{17,1},{25,9},{2,18},{10... | collective-permute-start | bytes 1032200 | tf_op jit(solution)/shard_map/ppermute | solution.py:472
  21.8 5.6 %collective-permute-start.9 = (f32[6,2,16,128]{3,2,1,0:T(8,128)S(1)}, f32[6,2,16,128]{3,2,1,0:T(8,128)S(1)}, u32[]{:S(2)}, u32[]{:S(2)}) collective-permute-start(f32[6,2,16,128]{3,2,1,0:T(8,128)S(1)} %get-tuple-element.52), channel_id=1, source_target_pairs={{0,8},{8,0},{16,24},{24,16},{1,9},{9,1},{17,25},{25,17},{2,10},{10... | collective-permute-start | bytes 294920 | tf_op jit(solution)/shard_map/ppermute | solution.py:472
  23.0 6.6 %collective-permute-start.8 = (f32[6,2,32,128]{3,2,1,0:T(8,128)S(1)}, f32[6,2,32,128]{3,2,1,0:T(8,128)S(1)}, u32[]{:S(2)}, u32[]{:S(2)}) collective-permute-start(f32[6,2,32,128]{3,2,1,0:T(8,128)S(1)} %get-tuple-element.50), channel_id=1, source_target_pairs={{0,8},{8,0},{16,24},{24,16},{1,9},{9,1},{17,25},{25,17},{2,10},{10... | collective-permute-start | bytes 589832 | tf_op jit(solution)/shard_map/ppermute | solution.py:472

commit v11 on v10

--- a/solution.py
+++ b/solution.py
@@ -13,8 +13,8 @@
 HALO = 8
 PLANES = 5
 REACH = 2
-SHARED = 80
-LARGE, MEDIUM, SMALL = 10**10, 25 * 10**8, 0
+SHARED = 96
+LARGE, MEDIUM, SMALL = 10**10, 2 * 10**9, 0
 
 magnetic_coeff = 0.5
 
@@ -453,17 +453,12 @@
     return lax.ppermute(near, "sub", [(i, i ^ 1) for i in range(sub_size)])
 
 
-def far_exchange(far, sub_size, tile_size, ends_by_tile=True):
+def far_exchange(far, sub_size, tile_size):
     pairs = []
     for t in range(tile_size):
         for i in range(sub_size):
             j = ((i + 1) ^ 1) - 1
-            if 0 <= j < sub_size:
-                other = (t, j)
-            elif ends_by_tile:
-                other = (t ^ 1, i)
-            else:
-                other = (t, sub_size - 1 - i)
+            other = (t, j) if 0 <= j < sub_size else (t ^ 1, i)
             pairs.append((t * sub_size + i, other[0] * sub_size + other[1]))
     return lax.ppermute(far, ("tile", "sub"), pairs)
 
@@ -530,7 +525,7 @@
         functools.partial(shared_halo_kernel, "sub"), [shape, shape, (8, size_y)], table, shared, flops=LARGE
     )
     shared_near = near_exchange(shared_near, sub_size)
-    shared_far = far_exchange(shared_far, sub_size, tile_size, ends_by_tile=False)
+    shared_far = far_exchange(shared_far, sub_size, tile_size)
 
     mid, bands, beside = called(
         functools.partial(middle_kernel, inner, "sub", sub_size, "tile"),

time: 31 us -> 30.5 us (0.984)
  starting transfers between devices: 15.2 us -> 12.7 us
  waiting for transfers between devices: 5.76 us -> 7.5 us
    ppermute x3, starting transfers between devices: 5.86 us -> 3.34 us  [far_exchange(): return lax.ppermute(far, ('tile', 'sub'), pairs)]
    ppermute x3, waiting for transfers between devices: 2.58 us -> 3.74 us  [far_exchange(): return lax.ppermute(far, ('tile', 'sub'), pairs)]
    ppermute x6, waiting for transfers between devices: 3.18 us -> 3.75 us  [swapped(): lax.ppermute(value, 'tile', [(t, t ^ bits) for t in range(tile_size)])]
  transfers between devices with their start and end apart: 12 -> 12, of which waited for: 2 -> 4; matrix products, arithmetic and copies ran while one was open for 1% -> 1% of each run, Pallas kernels for 21% -> 22%
where the time goes in v11:
time: 30.5 us; the launch traced here: 30.4 us
  starting transfers between devices  12.7 us (42%)
  Pallas kernels  9.75 us (32%)
  waiting for transfers between devices  7.5 us (25%)
    ppermute x6, starting transfers between devices, swapped(): lax.ppermute(value, 'tile', [(t, t ^ bits) for t in range(tile_size)])  8.82 us
    pallas_call x6, Pallas kernels, called(): pl.pallas_call(kernel, out_shape=outs, in_specs=[VMEM] * len(operands), o...  5.89 us
    ppermute x6, waiting for transfers between devices, swapped(): lax.ppermute(value, 'tile', [(t, t ^ bits) for t in range(tile_size)])  3.75 us
    ppermute x3, waiting for transfers between devices, far_exchange(): return lax.ppermute(far, ('tile', 'sub'), pairs)  3.74 us
    ppermute x3, starting transfers between devices, far_exchange(): return lax.ppermute(far, ('tile', 'sub'), pairs)  3.34 us
    pallas_call x1, Pallas kernels, two_by_two(): pl.pallas_call(functools.partial(share_kernel, fetched, HALO // 2), out_s...  1.79 us
    pallas_call x1, Pallas kernels, two_by_two(): pl.pallas_call(functools.partial(last_kernel, 'tile'), out_shape=whole, i...  1.15 us
    pallas_call x1, Pallas kernels, two_by_two(): pl.pallas_call(early_kernel, out_shape=whole, in_specs=[VMEM] * 2, out_sp...  0.91 us
  transfers between devices with their start and end apart: 12, of which 4 were waited for; matrix products, arithmetic and copies ran while one was open for 1% of the time, Pallas kernels for 22%

profile of v11, /device:TPU:0, one launch (start us, length us, event | category | flops | bytes accessed | tf_op | source)
XLA Modules:
  0.0 30.4 jit_solution(2797556263760902317)
XLA Ops:
  0.0 1.8 %shard_map.46 = f32[14,56,128]{2,1,0:T(8,128)S(1)} custom-call(f32[1,6,2,256,128]{4,3,2,1,0:T(8,128)} %seeds.7, s32[1,2,256,128]{3,2,1,0:T(8,128)} %material.7), custom_call_target="tpu_custom_call" | custom-call | tf_op jit(solution)/shard_map/pallas_call | solution.py:490
  1.8 3.0 %collective-permute-start.6 = (f32[14,56,128]{2,1,0:T(8,128)S(1)}, f32[14,56,128]{2,1,0:T(8,128)S(1)}, u32[]{:S(2)}, u32[]{:S(2)}) collective-permute-start(f32[14,56,128]{2,1,0:T(8,128)S(1)} %shard_map.46), channel_id=1, source_target_pairs={{0,16},{8,24},{16,0},{24,8},{1,17},{9,25},{17,1},{25,9},{2,18},{10... | collective-permute-start | bytes 1204232 | tf_op jit(solution)/shard_map/ppermute | solution.py:467
  4.9 0.1 pad_maximum_fusion
  4.9 0.1 broadcast_in_dim.4.table
  5.0 0.8 %shard_map.47 = (f32[5,80,128]{2,1,0:T(8,128)S(1)}, f32[5,80,128]{2,1,0:T(8,128)S(1)}, f32[5,208,128]{2,1,0:T(8,128)S(1)}, f32[5,208,128]{2,1,0:T(8,128)S(1)}) custom-call(f32[8,128]{1,0:T(8,128)S(1)} %broadcast_in_dim.4.table, f32[1,6,2,256,128]{4,3,2,1,0:T(8,128)S(1)} %copy-done, s32[1,2,256,128]{3,2,1,0:T(8,128)S(1)} %copy-done.1), custom_call_target="tpu_custom_call" | custom-call | tf_op jit(solution)/shard_map/pallas_call | solution.py:438
  5.8 1.6 %collective-permute-start = (f32[5,80,128]{2,1,0:T(8,128)S(1)}, f32[5,80,128]{2,1,0:T(8,128)S(1)}, u32[]{:S(2)}, u32[]{:S(2)}) collective-permute-start(f32[5,80,128]{2,1,0:T(8,128)S(1)} %get-tuple-element.33), channel_id=1, source_target_pairs={{0,8},{1,2},{2,1},{3,4},{4,3},{5,6},{6,5},{7,15},{8,0},{9,10},{10,... | collective-permute-start | bytes 614408 | tf_op jit(solution)/shard_map/ppermute | solution.py:463
  7.3 0.2 collective-permute-start.1
  7.5 0.3 %collective-permute-start.4 = (f32[5,208,128]{2,1,0:T(8,128)S(1)}, f32[5,208,128]{2,1,0:T(8,128)S(1)}, u32[]{:S(2)}, u32[]{:S(2)}) collective-permute-start(f32[5,208,128]{2,1,0:T(8,128)S(1)} %get-tuple-element.40), channel_id=1, source_target_pairs={{0,1},{1,0},{2,3},{3,2},{4,5},{5,4},{6,7},{7,6},{8,9},{9,8},{10,11... | collective-permute-start | bytes 1597448 | tf_op jit(solution)/shard_map/ppermute | solution.py:453
  7.8 1.2 %collective-permute-start.5 = (f32[5,208,128]{2,1,0:T(8,128)S(1)}, f32[5,208,128]{2,1,0:T(8,128)S(1)}, u32[]{:S(2)}, u32[]{:S(2)}) collective-permute-start(f32[5,208,128]{2,1,0:T(8,128)S(1)} %get-tuple-element.41), channel_id=1, source_target_pairs={{0,8},{1,2},{2,1},{3,4},{4,3},{5,6},{6,5},{7,15},{8,0},{9,10},{10,... | collective-permute-start | bytes 1597448 | tf_op jit(solution)/shard_map/ppermute | solution.py:463
  9.0 2.6 %collective-permute-done.far = f32[5,80,128]{2,1,0:T(8,128)S(1)} collective-permute-done((f32[5,80,128]{2,1,0:T(8,128)S(1)}, f32[5,80,128]{2,1,0:T(8,128)S(1)}, u32[]{:S(2)}, u32[]{:S(2)}) %collective-permute-start) | collective-permute-done | bytes 204832 | tf_op jit(solution)/shard_map/ppermute | solution.py:463
  11.6 0.1 pad_maximum_fusion.1
  11.7 0.0 collective-permute-done.1.near
  11.7 0.1 broadcast_in_dim.5.table
  11.7 0.6 %shard_map.48 = (f32[6,2,64,128]{3,2,1,0:T(8,128)S(1)}, f32[6,2,32,128]{3,2,1,0:T(8,128)S(1)}, f32[6,2,16,128]{3,2,1,0:T(8,128)S(1)}) custom-call(f32[8,128]{1,0:T(8,128)S(1)} %broadcast_in_dim.5.table, f32[1,6,2,256,128]{4,3,2,1,0:T(8,128)S(1)} %copy-done, s32[1,2,256,128]{3,2,1,0:T(8,128)S(1)} %copy-done.1, f32[5,80,128]{2,1,0:T(8,128)S(1)} %collective-permute-done.1.near, ...), custom_call_target="tpu_custom_call" | custom-call | tf_op jit(solution)/shard_map/pallas_call | solution.py:438
  12.4 1.5 %collective-permute-start.3 = (f32[6,2,16,128]{3,2,1,0:T(8,128)S(1)}, f32[6,2,16,128]{3,2,1,0:T(8,128)S(1)}, u32[]{:S(2)}, u32[]{:S(2)}) collective-permute-start(f32[6,2,16,128]{3,2,1,0:T(8,128)S(1)} %get-tuple-element.39), channel_id=1, source_target_pairs={{0,24},{8,16},{16,8},{24,0},{1,25},{9,17},{17,9},{25,1},{2,26},{10... | collective-permute-start | bytes 294920 | tf_op jit(solution)/shard_map/ppermute | solution.py:467
  13.9 1.5 %collective-permute-start.2 = (f32[6,2,32,128]{3,2,1,0:T(8,128)S(1)}, f32[6,2,32,128]{3,2,1,0:T(8,128)S(1)}, u32[]{:S(2)}, u32[]{:S(2)}) collective-permute-start(f32[6,2,32,128]{3,2,1,0:T(8,128)S(1)} %get-tuple-element.38), channel_id=1, source_target_pairs={{0,16},{8,24},{16,0},{24,8},{1,17},{9,25},{17,1},{25,9},{2,18},{10... | collective-permute-start | bytes 589832 | tf_op jit(solution)/shard_map/ppermute | solution.py:467
  15.4 0.0 collective-permute-done.6.shared
  15.4 1.1 %shard_map.49 = (f32[5,56,128]{2,1,0:T(8,128)S(1)}, f32[5,56,128]{2,1,0:T(8,128)S(1)}, f32[8,128]{1,0:T(8,128)S(1)}) custom-call(f32[8,128]{1,0:T(8,128)S(1)} %broadcast_in_dim.4.table, f32[14,56,128]{2,1,0:T(8,128)S(1)} %collective-permute-done.6.shared), custom_call_target="tpu_custom_call" | custom-call | flops 10000000000 | tf_op jit(solution)/shard_map/pallas_call | solution.py:438
  16.5 0.1 collective-permute-start.10
  16.6 0.6 %collective-permute-start.11 = (f32[5,56,128]{2,1,0:T(8,128)S(1)}, f32[5,56,128]{2,1,0:T(8,128)S(1)}, u32[]{:S(2)}, u32[]{:S(2)}) collective-permute-start(f32[5,56,128]{2,1,0:T(8,128)S(1)} %get-tuple-element.56), channel_id=1, source_target_pairs={{0,8},{1,2},{2,1},{3,4},{4,3},{5,6},{6,5},{7,15},{8,0},{9,10},{10,... | collective-permute-start | bytes 430088 | tf_op jit(solution)/shard_map/ppermute | solution.py:463
  17.2 1.2 %collective-permute-done.5.far = f32[5,208,128]{2,1,0:T(8,128)S(1)} collective-permute-done((f32[5,208,128]{2,1,0:T(8,128)S(1)}, f32[5,208,128]{2,1,0:T(8,128)S(1)}, u32[]{:S(2)}, u32[]{:S(2)}) %collective-permute-start.5) | collective-permute-done | bytes 532512 | tf_op jit(solution)/shard_map/ppermute | solution.py:463
  18.4 1.7 %shard_map.50 = (f32[6,2,192,128]{3,2,1,0:T(8,128)S(1)}, f32[6,2,48,128]{3,2,1,0:T(8,128)S(1)}, f32[6,2,16,128]{3,2,1,0:T(8,128)S(1)}) custom-call(f32[8,128]{1,0:T(8,128)S(1)} %broadcast_in_dim.4.table, f32[1,6,2,256,128]{4,3,2,1,0:T(8,128)S(1)} %copy-done, s32[1,2,256,128]{3,2,1,0:T(8,128)S(1)} %copy-done.1, ...), custom_call_target="tpu_custom_call" | custom-call | tf_op jit(solution)/shard_map/pallas_call | solution.py:438
  20.0 0.4 %collective-permute-start.7 = (f32[6,2,48,128]{3,2,1,0:T(8,128)S(1)}, f32[6,2,48,128]{3,2,1,0:T(8,128)S(1)}, u32[]{:S(2)}, u32[]{:S(2)}) collective-permute-start(f32[6,2,48,128]{3,2,1,0:T(8,128)S(1)} %get-tuple-element.47), channel_id=1, source_target_pairs={{0,16},{8,24},{16,0},{24,8},{1,17},{9,25},{17,1},{25,9},{2,18},{10... | collective-permute-start | bytes 884744 | tf_op jit(solution)/shard_map/ppermute | solution.py:467
  20.4 1.7 %collective-permute-start.9 = (f32[6,2,16,128]{3,2,1,0:T(8,128)S(1)}, f32[6,2,16,128]{3,2,1,0:T(8,128)S(1)}, u32[]{:S(2)}, u32[]{:S(2)}) collective-permute-start(f32[6,2,16,128]{3,2,1,0:T(8,128)S(1)} %get-tuple-element.52), channel_id=1, source_target_pairs={{0,8},{8,0},{16,24},{24,16},{1,9},{9,1},{17,25},{25,17},{2,10},{10... | collective-permute-start | bytes 294920 | tf_op jit(solution)/shard_map/ppermute | solution.py:467
  22.1 0.0 collective-permute-done.2.corner
  22.1 0.3 %shard_map.51 = (f32[6,2,64,128]{3,2,1,0:T(8,128)S(1)}, f32[6,2,32,128]{3,2,1,0:T(8,128)S(1)}) custom-call(f32[6,2,64,128]{3,2,1,0:T(8,128)S(1)} %get-tuple-element.42.edge, f32[6,2,32,128]{3,2,1,0:T(8,128)S(1)} %collective-permute-done.2.corner), custom_call_target="tpu_custom_call" | custom-call | tf_op jit(solution)/shard_map/pallas_call | solution.py:438
  22.4 0.7 %collective-permute-start.8 = (f32[6,2,32,128]{3,2,1,0:T(8,128)S(1)}, f32[6,2,32,128]{3,2,1,0:T(8,128)S(1)}, u32[]{:S(2)}, u32[]{:S(2)}) collective-permute-start(f32[6,2,32,128]{3,2,1,0:T(8,128)S(1)} %get-tuple-element.50), channel_id=1, source_target_pairs={{0,8},{8,0},{16,24},{24,16},{1,9},{9,1},{17,25},{25,17},{2,10},{10... | collective-permute-start | bytes 589832 | tf_op jit(solution)/shard_map/ppermute | solution.py:467
  23.1 2.5 %collective-permute-done.9.beside = f32[6,2,16,128]{3,2,1,0:T(8,128)S(1)} collective-permute-done((f32[6,2,16,128]{3,2,1,0:T(8,128)S(1)}, f32[6,2,16,128]{3,2,1,0:T(8,128)S(1)}, u32[]{:S(2)}, u32[]{:S(2)}) %collective-permute-start.9) | collective-permute-done | bytes 98336 | tf_op jit(solution)/shard_map/ppermute | solution.py:467
  25.7 1.5 %shard_map.52.part = f32[6,2,104,128]{3,2,1,0:T(8,128)S(1)} custom-call(f32[8,128]{1,0:T(8,128)S(1)} %broadcast_in_dim.4.table, f32[14,56,128]{2,1,0:T(8,128)S(1)} %collective-permute-done.6.shared, f32[5,56,128]{2,1,0:T(8,128)S(1)} %collective-permute-done.10.near, f32[5,56,128]{2,1,0:T(8,128)S(1)} %collective-permute-done.11.far), custom_call_target="tpu_custom_call" | custom-call | flops 2000000000 | tf_op jit(solution)/shard_map/pallas_call | solution.py:438
  27.1 0.9 %shard_map.53._ = f32[1,6,2,256,128]{4,3,2,1,0:T(8,128)} custom-call(f32[6,2,192,128]{3,2,1,0:T(8,128)S(1)} %get-tuple-element.46.mid, f32[6,2,104,128]{3,2,1,0:T(8,128)S(1)} %shard_map.52.part), custom_call_target="tpu_custom_call" | custom-call | tf_op jit(solution)/shard_map/pallas_call | solution.py:551
  28.0 1.2 %collective-permute-done.8.got = f32[6,2,32,128]{3,2,1,0:T(8,128)S(1)} collective-permute-done((f32[6,2,32,128]{3,2,1,0:T(8,128)S(1)}, f32[6,2,32,128]{3,2,1,0:T(8,128)S(1)}, u32[]{:S(2)}, u32[]{:S(2)}) %collective-permute-start.8) | collective-permute-done | bytes 196640 | tf_op jit(solution)/shard_map/ppermute | solution.py:467
  29.2 1.2 %shard_map.54 = f32[1,6,2,256,128]{4,3,2,1,0:T(8,128)} custom-call(f32[6,2,192,128]{3,2,1,0:T(8,128)S(1)} %get-tuple-element.46.mid, f32[6,2,48,128]{3,2,1,0:T(8,128)S(1)} %collective-permute-done.7.bands, f32[6,2,64,128]{3,2,1,0:T(8,128)S(1)} %get-tuple-element.49.summed, ...), custom_call_target="tpu_custom_call", output_to_operand_aliasing={{}: (6, {})} | custom-call | tf_op jit(solution)/shard_map/pallas_call | solution.py:560
  (13 shorter events, 0.0 us)
Async XLA Ops:
  0.0 5.0 %copy-start.1 = (s32[1,2,256,128]{3,2,1,0:T(8,128)S(1)}, s32[1,2,256,128]{3,2,1,0:T(8,128)}, u32[]{:S(2)}) copy-start(s32[1,2,256,128]{3,2,1,0:T(8,128)} %material.7) | copy-start | bytes 786436
  0.0 5.0 %copy-start = (f32[1,6,2,256,128]{4,3,2,1,0:T(8,128)S(1)}, f32[1,6,2,256,128]{4,3,2,1,0:T(8,128)}, u32[]{:S(2)}) copy-start(f32[1,6,2,256,128]{4,3,2,1,0:T(8,128)} %seeds.7) | copy-start | bytes 4718596
  0.0 4.8 %copy-start.2 = (f32[4]{0:T(128)S(1)}, f32[4]{0:T(128)}, u32[]{:S(2)}) copy-start(f32[4]{0:T(128)} %param.7) | copy-start | bytes 52
  0.0 4.8 %copy-start.3 = (f32[4]{0:T(128)S(1)}, f32[4]{0:T(128)}, u32[]{:S(2)}) copy-start(f32[4]{0:T(128)} %param.6) | copy-start | bytes 52
  1.8 13.6 %collective-permute-start.6 = (f32[14,56,128]{2,1,0:T(8,128)S(1)}, f32[14,56,128]{2,1,0:T(8,128)S(1)}, u32[]{:S(2)}, u32[]{:S(2)}) collective-permute-start(f32[14,56,128]{2,1,0:T(8,128)S(1)} %shard_map.46), channel_id=1, source_target_pairs={{0,16},{8,24},{16,0},{24,8},{1,17},{9,25},{17,1},{25,9},{2,18},{10... | collective-permute-start | bytes 1204232 | tf_op jit(solution)/shard_map/ppermute | solution.py:467
  5.8 5.8 %collective-permute-start = (f32[5,80,128]{2,1,0:T(8,128)S(1)}, f32[5,80,128]{2,1,0:T(8,128)S(1)}, u32[]{:S(2)}, u32[]{:S(2)}) collective-permute-start(f32[5,80,128]{2,1,0:T(8,128)S(1)} %get-tuple-element.33), channel_id=1, source_target_pairs={{0,8},{1,2},{2,1},{3,4},{4,3},{5,6},{6,5},{7,15},{8,0},{9,10},{10,... | collective-permute-start | bytes 614408 | tf_op jit(solution)/shard_map/ppermute | solution.py:463
  7.3 4.3 %collective-permute-start.1 = (f32[5,80,128]{2,1,0:T(8,128)S(1)}, f32[5,80,128]{2,1,0:T(8,128)S(1)}, u32[]{:S(2)}, u32[]{:S(2)}) collective-permute-start(f32[5,80,128]{2,1,0:T(8,128)S(1)} %get-tuple-element.36), channel_id=1, source_target_pairs={{0,1},{1,0},{2,3},{3,2},{4,5},{5,4},{6,7},{7,6},{8,9},{9,8},{10,11... | collective-permute-start | bytes 614408 | tf_op jit(solution)/shard_map/ppermute | solution.py:453
  7.5 9.0 %collective-permute-start.4 = (f32[5,208,128]{2,1,0:T(8,128)S(1)}, f32[5,208,128]{2,1,0:T(8,128)S(1)}, u32[]{:S(2)}, u32[]{:S(2)}) collective-permute-start(f32[5,208,128]{2,1,0:T(8,128)S(1)} %get-tuple-element.40), channel_id=1, source_target_pairs={{0,1},{1,0},{2,3},{3,2},{4,5},{5,4},{6,7},{7,6},{8,9},{9,8},{10,11... | collective-permute-start | bytes 1597448 | tf_op jit(solution)/shard_map/ppermute | solution.py:453
  7.8 10.5 %collective-permute-start.5 = (f32[5,208,128]{2,1,0:T(8,128)S(1)}, f32[5,208,128]{2,1,0:T(8,128)S(1)}, u32[]{:S(2)}, u32[]{:S(2)}) collective-permute-start(f32[5,208,128]{2,1,0:T(8,128)S(1)} %get-tuple-element.41), channel_id=1, source_target_pairs={{0,8},{1,2},{2,1},{3,4},{4,3},{5,6},{6,5},{7,15},{8,0},{9,10},{10,... | collective-permute-start | bytes 1597448 | tf_op jit(solution)/shard_map/ppermute | solution.py:463
  12.4 8.0 %collective-permute-start.3 = (f32[6,2,16,128]{3,2,1,0:T(8,128)S(1)}, f32[6,2,16,128]{3,2,1,0:T(8,128)S(1)}, u32[]{:S(2)}, u32[]{:S(2)}) collective-permute-start(f32[6,2,16,128]{3,2,1,0:T(8,128)S(1)} %get-tuple-element.39), channel_id=1, source_target_pairs={{0,24},{8,16},{16,8},{24,0},{1,25},{9,17},{17,9},{25,1},{2,26},{10... | collective-permute-start | bytes 294920 | tf_op jit(solution)/shard_map/ppermute | solution.py:467
  13.9 8.2 %collective-permute-start.2 = (f32[6,2,32,128]{3,2,1,0:T(8,128)S(1)}, f32[6,2,32,128]{3,2,1,0:T(8,128)S(1)}, u32[]{:S(2)}, u32[]{:S(2)}) collective-permute-start(f32[6,2,32,128]{3,2,1,0:T(8,128)S(1)} %get-tuple-element.38), channel_id=1, source_target_pairs={{0,16},{8,24},{16,0},{24,8},{1,17},{9,25},{17,1},{25,9},{2,18},{10... | collective-permute-start | bytes 589832 | tf_op jit(solution)/shard_map/ppermute | solution.py:467
  16.5 6.6 %collective-permute-start.10 = (f32[5,56,128]{2,1,0:T(8,128)S(1)}, f32[5,56,128]{2,1,0:T(8,128)S(1)}, u32[]{:S(2)}, u32[]{:S(2)}) collective-permute-start(f32[5,56,128]{2,1,0:T(8,128)S(1)} %get-tuple-element.53), channel_id=1, source_target_pairs={{0,1},{1,0},{2,3},{3,2},{4,5},{5,4},{6,7},{7,6},{8,9},{9,8},{10,11... | collective-permute-start | bytes 430088 | tf_op jit(solution)/shard_map/ppermute | solution.py:453
  16.6 9.1 %collective-permute-start.11 = (f32[5,56,128]{2,1,0:T(8,128)S(1)}, f32[5,56,128]{2,1,0:T(8,128)S(1)}, u32[]{:S(2)}, u32[]{:S(2)}) collective-permute-start(f32[5,56,128]{2,1,0:T(8,128)S(1)} %get-tuple-element.56), channel_id=1, source_target_pairs={{0,8},{1,2},{2,1},{3,4},{4,3},{5,6},{6,5},{7,15},{8,0},{9,10},{10,... | collective-permute-start | bytes 430088 | tf_op jit(solution)/shard_map/ppermute | solution.py:463
  20.0 9.2 %collective-permute-start.7 = (f32[6,2,48,128]{3,2,1,0:T(8,128)S(1)}, f32[6,2,48,128]{3,2,1,0:T(8,128)S(1)}, u32[]{:S(2)}, u32[]{:S(2)}) collective-permute-start(f32[6,2,48,128]{3,2,1,0:T(8,128)S(1)} %get-tuple-element.47), channel_id=1, source_target_pairs={{0,16},{8,24},{16,0},{24,8},{1,17},{9,25},{17,1},{25,9},{2,18},{10... | collective-permute-start | bytes 884744 | tf_op jit(solution)/shard_map/ppermute | solution.py:467
  20.4 5.3 %collective-permute-start.9 = (f32[6,2,16,128]{3,2,1,0:T(8,128)S(1)}, f32[6,2,16,128]{3,2,1,0:T(8,128)S(1)}, u32[]{:S(2)}, u32[]{:S(2)}) collective-permute-start(f32[6,2,16,128]{3,2,1,0:T(8,128)S(1)} %get-tuple-element.52), channel_id=1, source_target_pairs={{0,8},{8,0},{16,24},{24,16},{1,9},{9,1},{17,25},{25,17},{2,10},{10... | collective-permute-start | bytes 294920 | tf_op jit(solution)/shard_map/ppermute | solution.py:467
  22.4 6.8 %collective-permute-start.8 = (f32[6,2,32,128]{3,2,1,0:T(8,128)S(1)}, f32[6,2,32,128]{3,2,1,0:T(8,128)S(1)}, u32[]{:S(2)}, u32[]{:S(2)}) collective-permute-start(f32[6,2,32,128]{3,2,1,0:T(8,128)S(1)} %get-tuple-element.50), channel_id=1, source_target_pairs={{0,8},{8,0},{16,24},{24,16},{1,9},{9,1},{17,25},{25,17},{2,10},{10... | collective-permute-start | bytes 589832 | tf_op jit(solution)/shard_map/ppermute | solution.py:467

commit v12 on v11

--- a/solution.py
+++ b/solution.py
@@ -9,7 +9,6 @@
 from jax.sharding import PartitionSpec as P
 
 BAND = 32
-STEPS = 2
 HALO = 8
 PLANES = 5
 REACH = 2
@@ -115,10 +114,10 @@
 
 
 def raw(seeds, material, spans):
-    depth = seeds.shape[2]
-    e = [[joined(seeds, (0, c, p), spans) for p in range(depth)] for c in range(3)]
-    h = [[joined(seeds, (0, 3 + c, p), spans) for p in range(depth)] for c in range(3)]
-    return e, h, [joined(material, (0, p), spans) for p in range(depth)]
+    depth = seeds.shape[1]
+    e = [[joined(seeds, (c, p), spans) for p in range(depth)] for c in range(3)]
+    h = [[joined(seeds, (3 + c, p), spans) for p in range(depth)] for c in range(3)]
+    return e, h, [joined(material, (p,), spans) for p in range(depth)]
 
 
 def table_entries(table):
@@ -204,14 +203,31 @@
     return jnp.where(middle, middle_out(second), first)
 
 
+def inner_lanes(shape):
+    lane = lane_of(shape)
+    return (lane >= BAND) & (lane < shape[-1] - BAND)
+
+
 def y_unpacked(block):
-    lane = lane_of(block.shape)
-    lanes = block.shape[1]
-    a, b = pltpu.roll(block, BAND, 1), pltpu.roll(block, lanes - BAND, 1)
-    middle = (lane >= BAND) & (lane < lanes - BAND)
-    first = jnp.where(middle, 0.0, jnp.where(lane < BAND, a, b))
-    second = jnp.where(middle, 0.0, jnp.where(lane < BAND, b, a))
+    a, b = rolled(block, BAND), rolled(block, -BAND)
+    middle = inner_lanes(block.shape)
+    below = lane_of(block.shape) < BAND
+    first = jnp.where(middle, 0.0, jnp.where(below, a, b))
+    second = jnp.where(middle, 0.0, jnp.where(below, b, a))
     return first, second
+
+
+def strip_packed(strip):
+    half = strip.shape[1] // 2
+    first, second = strip[:, :half], strip[:, half:]
+    return jnp.where(inner_lanes(first.shape), second, middle_out(first))
+
+
+def strip_of(corners, block):
+    middle = inner_lanes(block.shape)
+    first = jnp.where(middle, middle_out(block), corners[0])
+    second = jnp.where(middle, block, corners[1])
+    return jnp.concatenate([first, second], axis=1)
 
 
 def low_rows(shape):
@@ -263,19 +279,38 @@
     return jnp.concatenate(result, axis=1)
 
 
-def share_kernel(span, skip, seeds, material, shared, held, labels, sems):
-    rows = pl.ds(span[0], span[1] - span[0])
-    depth = held.shape[1]
-    stop = span[1] - span[0] - skip
-    copies = [pltpu.make_async_copy(material.at[0, :, rows], labels, sems.at[6])]
-    copies += [pltpu.make_async_copy(seeds.at[0, c, :, rows], held.at[c], sems.at[c]) for c in range(6)]
-    for copy in copies:
-        copy.start()
-    copies[0].wait()
-    shared[6 * depth :] = bands_packed(labels[:, skip:stop].astype(jnp.float32))
-    for c in range(6):
-        copies[1 + c].wait()
-    shared[: 6 * depth] = bands_packed(jnp.concatenate([held[c, :, skip:stop] for c in range(6)], axis=0))
+def first_kernel(span, skip, decay, coupling, seeds, material, shared, held, labels, table, entries, sems):
+    size_x = held.shape[2]
+    copies = []
+
+    def fetch(source, target):
+        copies.append(pltpu.make_async_copy(source, target, sems.at[len(copies)]))
+        copies[-1].start()
+
+    def fetch_rows(lo, hi):
+        rows = pl.ds(lo, hi - lo)
+        fetch(material.at[0, :, rows], labels.at[:, rows])
+        for c in range(0, 6, 2):
+            some = pl.ds(c, 2)
+            fetch(seeds.at[0, some, :, rows], held.at[some, :, rows])
+
+    fetch_rows(*span)
+    early = len(copies)
+    fetch(decay, entries.at[0])
+    fetch(coupling, entries.at[1])
+    fetch_rows(0, span[0])
+    fetch_rows(span[1], size_x)
+    rows = slice(span[0] + skip, span[1] - skip)
+    for copy in copies[:early]:
+        copy.wait()
+    planes = [held[c, :, rows] for c in range(6)] + [labels[:, rows].astype(jnp.float32)]
+    shared[...] = bands_packed(jnp.concatenate(planes, axis=0))
+    for copy in copies[early:]:
+        copy.wait()
+    count = entries.shape[1]
+    for k in range(2):
+        for m in range(count):
+            table[k * count + m : k * count + m + 1] = jnp.full((1, table.shape[1]), entries[k, m], jnp.float32)
 
 
 def halo_pair_kernel(edges, inner, sub, table, seeds, material, near_edge, far_edge, near, far):
@@ -297,7 +332,7 @@
 
 def weighted_planes(seeds, material, table, near, far, spans, keeps, sub, sub_size):
     planes = final_fields(loaded(seeds, material, table, spans), near, far, sub, sub_size)
-    return weighted(planes, spans, keeps, *seeds.shape[3:])
+    return weighted(planes, spans, keeps, *seeds.shape[2:])
 
 
 def weighted(planes, spans, keeps, size_x, size_y):
@@ -306,96 +341,69 @@
         shape = (stop - start, size_y)
         weight = ramp(row_of(shape) + start, size_x) * ramp(lane_of(shape), size_y)
         first = at + start - lo
-        results.append([[plane[first : first + stop - start] * weight for plane in part] for part in planes])
+        results.append(jnp.stack([plane[first : first + stop - start] * weight for part in planes for plane in part]))
         at += hi - lo
     return results
 
 
 def edge_kernel(spans, sub, sub_size, tile, table, seeds, material, near, far, edge, corner, strip):
-    size_x = seeds.shape[3]
+    size_x = seeds.shape[2]
     keeps = ((0, BAND), (size_x - BAND, size_x))
     low, high = weighted_planes(seeds, material, table, near, far, spans, keeps, sub, sub_size)
     odd = lax.rem(lax.axis_index(tile), 2) == 1
-    half = BAND // 2
-    for c in range(6):
-        for p in range(seeds.shape[2]):
-            edge[c, p, :BAND] = low[c][p]
-            edge[c, p, BAND:] = high[c][p]
-            corner[c, p] = y_packed(low[c][p], high[c][p])
-            away = jnp.where(odd, high[c][p], low[c][p])
-            strip[c, p] = y_packed(middle_out(away[:half]), middle_out(away[half:]))
-
-
-def middle_kernel(
-    spans, sub, sub_size, tile, table, seeds, material, near, far, edge, _, mid, bands, beside
-):
-    size_x = seeds.shape[3]
+    edge[:, :BAND] = low
+    edge[:, BAND:] = high
+    corner[...] = y_packed(low, high)
+    strip[...] = strip_packed(jnp.where(odd, high, low))
+
+
+def middle_kernel(spans, sub, sub_size, tile, table, seeds, material, near, far, edge, _, mid, bands, beside):
+    size_x = seeds.shape[2]
     keep = (BAND, size_x - BAND)
+    odd = lax.rem(lax.axis_index(tile), 2) == 1
+    beside[...] = strip_packed(jnp.where(odd, edge[:, :BAND], edge[:, BAND:]))
     planes, = weighted_planes(seeds, material, table, near, far, spans, (keep,), sub, sub_size)
-    odd = lax.rem(lax.axis_index(tile), 2) == 1
-    half, quarter = bands.shape[2], BAND // 2
-    for c in range(6):
-        for p in range(seeds.shape[2]):
-            mid[c, p] = planes[c][p]
-            bands[c, p] = y_packed(planes[c][p][:half], planes[c][p][-half:])
-            by = jnp.where(odd, edge[c, p, :BAND], edge[c, p, BAND:])
-            beside[c, p] = y_packed(middle_out(by[:quarter]), middle_out(by[quarter:]))
+    half = bands.shape[1]
+    mid[...] = planes
+    bands[...] = y_packed(planes[:, :half], planes[:, -half:])
 
 
 def whole_kernel(spans, sub, sub_size, table, seeds, material, near, far, out):
     planes, = weighted_planes(seeds, material, table, near, far, spans, spans, sub, sub_size)
-    for c in range(6):
-        for p in range(seeds.shape[2]):
-            out[c, p] = planes[c][p]
+    out[...] = planes
 
 
 def y_swapped(block):
-    lane = lane_of(block.shape)
-    lanes = block.shape[1]
-    a, b = pltpu.roll(block, BAND, 1), pltpu.roll(block, lanes - BAND, 1)
-    middle = (lane >= BAND) & (lane < lanes - BAND)
-    return jnp.where(middle, 0.0, jnp.where(lane < BAND, a, b))
+    below = lane_of(block.shape) < BAND
+    return jnp.where(inner_lanes(block.shape), 0.0, jnp.where(below, rolled(block, BAND), rolled(block, -BAND)))
 
 
 def shared_kernel(span, size_x, sub, sub_size, table, shared, near, far, part):
     planes = final_fields(shared_fields(table, shared), near, far, sub, sub_size, bands_unpacked)
-    found, = weighted(planes, (span,), (span,), size_x, part.shape[3])
-    for c in range(part.shape[0]):
-        for p in range(part.shape[1]):
-            part[c, p] = y_swapped(found[c][p])
+    found, = weighted(planes, (span,), (span,), size_x, part.shape[2])
+    part[...] = y_swapped(found)
 
 
 def corner_kernel(tile, edge, corner, summed, send):
     odd = lax.rem(lax.axis_index(tile), 2) == 1
     half = BAND // 2
-    for c in range(edge.shape[0]):
-        for p in range(edge.shape[1]):
-            first, second = y_unpacked(corner[c, p])
-            low = edge[c, p, :BAND] + first
-            high = edge[c, p, BAND:] + second
-            summed[c, p, :BAND] = low
-            summed[c, p, BAND:] = high
-            by, away = jnp.where(odd, low, high), jnp.where(odd, high, low)
-            send[c, p, :half] = y_packed(by[:half], by[half:])
-            send[c, p, half:] = y_packed(away[:half], away[half:])
-
-
-def strip_of(corners, block):
-    lane = lane_of(block.shape)
-    middle = (lane >= BAND) & (lane < block.shape[-1] - BAND)
-    first = jnp.where(middle, middle_out(block), corners[0])
-    second = jnp.where(middle, block, corners[1])
-    return jnp.concatenate([first, second], axis=0)
+    first, second = y_unpacked(corner[...])
+    low = edge[:, :BAND] + first
+    high = edge[:, BAND:] + second
+    summed[:, :BAND] = low
+    summed[:, BAND:] = high
+    by, away = jnp.where(odd, low, high), jnp.where(odd, high, low)
+    send[:, :half] = y_packed(by[:, :half], by[:, half:])
+    send[:, half:] = y_packed(away[:, :half], away[:, half:])
 
 
 def early_kernel(mid, part, out, whole, sem):
     size_x = out.shape[3]
     skip = HALO // 2
-    count = part.shape[2] - 2 * skip
+    count = part.shape[1] - 2 * skip
     start = (size_x - count) // 2
-    for c in range(mid.shape[0]):
-        for p in range(mid.shape[1]):
-            whole[c, p] = mid[c, p, start - BAND : start - BAND + count] + part[c, p, skip : skip + count]
+    found = mid[:, start - BAND : start - BAND + count] + part[:, skip : skip + count]
+    whole[...] = found.reshape(whole.shape)
     copy = pltpu.make_async_copy(whole, out.at[0, :, :, pl.ds(start, count)], sem)
     copy.start()
     copy.wait()
@@ -403,20 +411,20 @@
 
 def last_kernel(tile, mid, bands, summed, got, strip, beside, _, out, low, high, sems):
     odd = lax.rem(lax.axis_index(tile), 2) == 1
-    half, count = bands.shape[2], low.shape[2]
+    half, count = bands.shape[1], low.shape[2]
     quarter = BAND // 2
-    size_x = out.shape[3]
+    depth, size_x = out.shape[2:4]
     copies = []
-    for c in range(mid.shape[0]):
-        for p in range(mid.shape[1]):
-            first, second = y_unpacked(bands[c, p])
-            low[c, p, BAND:] = mid[c, p, :half] + first
-            high[c, p, :half] = mid[c, p, -half:] + second
-            straight = got[c, p, :quarter]
-            by = strip_of((straight, middle_out(straight)), beside[c, p])
-            away = strip_of(y_unpacked(got[c, p, quarter:]), strip[c, p])
-            low[c, p, :BAND] = summed[c, p, :BAND] + jnp.where(odd, by, away)
-            high[c, p, half:] = summed[c, p, BAND:] + jnp.where(odd, away, by)
+    for c in range(6):
+        at = slice(depth * c, depth * (c + 1))
+        first, second = y_unpacked(bands[at])
+        low[c, :, BAND:] = mid[at, :half] + first
+        high[c, :, :half] = mid[at, -half:] + second
+        straight = got[at, :quarter]
+        by = strip_of((straight, middle_out(straight)), beside[at])
+        away = strip_of(y_unpacked(got[at, quarter:]), strip[at])
+        low[c, :, :BAND] = summed[at, :BAND] + jnp.where(odd, by, away)
+        high[c, :, half:] = summed[at, BAND:] + jnp.where(odd, away, by)
         for k, (rows, start) in enumerate(((low, 0), (high, size_x - count))):
             copies.append(pltpu.make_async_copy(rows.at[c], out.at[0, c, :, pl.ds(start, count)], sems.at[2 * c + k]))
             copies[-1].start()
@@ -478,30 +486,31 @@
 
 def two_by_two(seeds, material, decay, coupling, sub_size, tile_size):
     depth, size_x, size_y = seeds.shape[2:]
+    planes = 6 * depth
     edges = ((0, BAND + HALO), (size_x - BAND - HALO, size_x))
     inner = ((BAND - HALO, size_x - BAND + HALO),)
     keep = ((size_x - SHARED) // 2, (size_x + SHARED) // 2)
     span = (keep[0] - HALO // 2, keep[1] + HALO // 2)
     fetched = (keep[0] - HALO, keep[1] + HALO)
     rows = size_x - 2 * BAND
-    edge_rows, inner_rows, span_rows = 2 * (BAND + HALO), rows + 2 * HALO, SHARED + 2 * HALO
+    edge_rows, inner_rows = 2 * (BAND + HALO), rows + 2 * HALO
     packed_rows = (SHARED + HALO) // 2 + 4
-
-    shared = pl.pallas_call(
-        functools.partial(share_kernel, fetched, HALO // 2),
-        out_shape=jax.ShapeDtypeStruct((7 * depth, packed_rows, size_y), jnp.float32),
-        in_specs=[HBM] * 2,
-        out_specs=VMEM,
-        scratch_shapes=[
-            pltpu.VMEM((6, depth, span_rows, size_y), jnp.float32),
-            pltpu.VMEM((depth, span_rows, size_y), jnp.int32),
-            pltpu.SemaphoreType.DMA((7,)),
+    whole = jax.ShapeDtypeStruct(seeds.shape, jnp.float32)
+
+    shared, seeds, material, table = pl.pallas_call(
+        functools.partial(first_kernel, fetched, HALO // 2),
+        out_shape=[
+            jax.ShapeDtypeStruct((7 * depth, packed_rows, size_y), jnp.float32),
+            jax.ShapeDtypeStruct(seeds.shape[1:], jnp.float32),
+            jax.ShapeDtypeStruct(material.shape[1:], jnp.int32),
+            jax.ShapeDtypeStruct((2 * decay.shape[0], size_y), jnp.float32),
         ],
+        in_specs=[HBM] * 4,
+        out_specs=[VMEM] * 4,
+        scratch_shapes=[pltpu.SMEM((2, *decay.shape), jnp.float32), pltpu.SemaphoreType.DMA((14,))],
         compiler_params=PARAMS,
         cost_estimate=cost(0),
-    )(*(pltpu.with_memory_space_constraint(x, pltpu.HBM) for x in (seeds, material)))
-    shared, decay, coupling = after(shared, decay, coupling)
-    table = table_rows(decay, coupling, size_y)
+    )(*(pltpu.with_memory_space_constraint(x, pltpu.HBM) for x in (decay, coupling, seeds, material)))
     shared = swapped(shared, 2, tile_size)
     edge_near, edge_far, inner_near, inner_far = called(
         functools.partial(halo_pair_kernel, edges, inner, "sub"),
@@ -511,11 +520,10 @@
     edge_far = far_exchange(edge_far, sub_size, tile_size)
     inner_far = far_exchange(inner_far, sub_size, tile_size)
 
-    edge_far, decay, coupling = after(edge_far, decay, coupling)
     edge, corner, strip = called(
         functools.partial(edge_kernel, edges, "sub", sub_size, "tile"),
-        [(6, depth, 2 * BAND, size_y), (6, depth, BAND, size_y), (6, depth, BAND // 2, size_y)],
-        table_rows(decay, coupling, size_y), seeds, material, edge_near, edge_far,
+        [(planes, 2 * BAND, size_y), (planes, BAND, size_y), (planes, BAND // 2, size_y)],
+        table, seeds, material, edge_near, edge_far,
     )
     corner = swapped(corner, 2, tile_size)
     strip = swapped(strip, 3, tile_size)
@@ -529,7 +537,7 @@
 
     mid, bands, beside = called(
         functools.partial(middle_kernel, inner, "sub", sub_size, "tile"),
-        [(6, depth, rows, size_y), (6, depth, (rows - SHARED) // 2, size_y), (6, depth, BAND // 2, size_y)],
+        [(planes, rows, size_y), (planes, (rows - SHARED) // 2, size_y), (planes, BAND // 2, size_y)],
         table, seeds, material, inner_near, inner_far, edge, done,
     )
     bands = swapped(bands, 2, tile_size)
@@ -537,17 +545,15 @@
 
     corner, strip, mid = after(corner, strip, mid)
     summed, send = called(
-        functools.partial(corner_kernel, "tile"),
-        [(6, depth, 2 * BAND, size_y), (6, depth, BAND, size_y)],
+        functools.partial(corner_kernel, "tile"), [(planes, 2 * BAND, size_y), (planes, BAND, size_y)],
         edge, corner, flops=SMALL,
     )
     got = swapped(send, 1, tile_size)
     beside, shared_near = after(beside, shared_near)
     part, = called(
         functools.partial(shared_kernel, span, size_x, "sub", sub_size),
-        [(6, depth, SHARED + HALO, size_y)], table, shared, shared_near, shared_far, flops=MEDIUM,
-    )
-    whole = jax.ShapeDtypeStruct(seeds.shape, jnp.float32)
+        [(planes, SHARED + HALO, size_y)], table, shared, shared_near, shared_far, flops=MEDIUM,
+    )
     early = pl.pallas_call(
         early_kernel,
         out_shape=whole,
@@ -572,6 +578,7 @@
 
 def any_lattice(seeds, material, decay, coupling, sub_size, tile_size):
     depth, size_x, size_y = seeds.shape[2:]
+    seeds, material = seeds[0], material[0]
     spans = ((0, size_x),)
     table = table_rows(decay, coupling, size_y)
     shape = (PLANES, size_x, size_y)
@@ -579,9 +586,10 @@
     near = near_exchange(near, sub_size)
     far = far_exchange(far, sub_size, tile_size)
     weighted, = called(
-        functools.partial(whole_kernel, spans, "sub", sub_size), [(6, depth, size_x, size_y)],
+        functools.partial(whole_kernel, spans, "sub", sub_size), [(6 * depth, size_x, size_y)],
         table, seeds, material, near, far,
     )
+    weighted = weighted.reshape(6, depth, size_x, size_y)
     side = math.isqrt(tile_size)
     prev_band = from_behind(weighted[:, :, size_x - BAND :, :], 1, tile_size)
     next_band = from_behind(weighted[:, :, :BAND, :], -1, tile_size)

time: 30.5 us -> 30.2 us (level)
  waiting for transfers between devices: 7.5 us -> 8.36 us
  Pallas kernels: 9.75 us -> 9.22 us
    ppermute x6, waiting for transfers between devices: 3.75 us -> 4.59 us  [swapped(): lax.ppermute(value, 'tile', [(t, t ^ bits) for t in range(tile_size)])]
    ppermute x6, starting transfers between devices: 8.82 us -> 8.18 us  [swapped(): lax.ppermute(value, 'tile', [(t, t ^ bits) for t in range(tile_size)])]
    pallas_call x6, Pallas kernels: 5.89 us -> 5.34 us  [called(): pl.pallas_call(kernel, out_shape=outs, in_specs=[VMEM] * len(operands), o...]
    ppermute x3, starting transfers between devices: 3.34 us -> 3.89 us  [far_exchange(): return lax.ppermute(far, ('tile', 'sub'), pairs)]
  transfers between devices with their start and end apart: 12 -> 12, of which waited for: 4 -> 5; matrix products, arithmetic and copies ran while one was open for 1% -> 0% of each run, Pallas kernels for 22% -> 21%
where the time goes in v12:
time: 30.2 us; the launch traced here: 30.1 us
  starting transfers between devices  12.4 us (41%)
  Pallas kernels  9.22 us (31%)
  waiting for transfers between devices  8.36 us (28%)
    ppermute x6, starting transfers between devices, swapped(): lax.ppermute(value, 'tile', [(t, t ^ bits) for t in range(tile_size)])  8.18 us
    pallas_call x6, Pallas kernels, called(): pl.pallas_call(kernel, out_shape=outs, in_specs=[VMEM] * len(operands), o...  5.34 us
    ppermute x6, waiting for transfers between devices, swapped(): lax.ppermute(value, 'tile', [(t, t ^ bits) for t in range(tile_size)])  4.59 us
    ppermute x3, starting transfers between devices, far_exchange(): return lax.ppermute(far, ('tile', 'sub'), pairs)  3.89 us
    ppermute x3, waiting for transfers between devices, far_exchange(): return lax.ppermute(far, ('tile', 'sub'), pairs)  3.76 us
    pallas_call x1, Pallas kernels, two_by_two(): pl.pallas_call(functools.partial(first_kernel, fetched, HALO // 2), out_s...  1.81 us
    pallas_call x1, Pallas kernels, two_by_two(): pl.pallas_call(functools.partial(last_kernel, 'tile'), out_shape=whole, i...  1.16 us
    pallas_call x1, Pallas kernels, two_by_two(): pl.pallas_call(early_kernel, out_shape=whole, in_specs=[VMEM] * 2, out_sp...  0.91 us
  transfers between devices with their start and end apart: 12, of which 5 were waited for; matrix products, arithmetic and copies ran while one was open for 0% of the time, Pallas kernels for 21%

profile of v12, /device:TPU:0, one launch (start us, length us, event | category | flops | bytes accessed | tf_op | source)
XLA Modules:
  0.0 30.1 jit_solution(11398431662043634165)
XLA Ops:
  0.0 1.8 %shard_map.46 = (f32[14,56,128]{2,1,0:T(8,128)S(1)}, f32[6,2,256,128]{3,2,1,0:T(8,128)S(1)}, s32[2,256,128]{2,1,0:T(8,128)S(1)}, f32[8,128]{1,0:T(8,128)S(1)}) custom-call(f32[4]{0:T(128)} %decay.1, f32[4]{0:T(128)} %coupling.1, f32[1,6,2,256,128]{4,3,2,1,0:T(8,128)} %seeds.1, s32[1,2,256,128]{3,2,1,0:T(8,128)} %material.1), custom_call_target="tpu_custom_call" | custom-call | tf_op jit(solution)/shard_map/pallas_call | solution.py:500
  1.8 3.0 %collective-permute-start.6 = (f32[14,56,128]{2,1,0:T(8,128)S(1)}, f32[14,56,128]{2,1,0:T(8,128)S(1)}, u32[]{:S(2)}, u32[]{:S(2)}) collective-permute-start(f32[14,56,128]{2,1,0:T(8,128)S(1)} %get-tuple-element.39), channel_id=1, source_target_pairs={{0,16},{8,24},{16,0},{24,8},{1,17},{9,25},{17,1},{25,9},{2,18},{10... | collective-permute-start | bytes 1204232 | tf_op jit(solution)/shard_map/ppermute | solution.py:475
  4.9 0.8 %shard_map.47 = (f32[5,80,128]{2,1,0:T(8,128)S(1)}, f32[5,80,128]{2,1,0:T(8,128)S(1)}, f32[5,208,128]{2,1,0:T(8,128)S(1)}, f32[5,208,128]{2,1,0:T(8,128)S(1)}) custom-call(f32[8,128]{1,0:T(8,128)S(1)} %get-tuple-element.29.table, f32[6,2,256,128]{3,2,1,0:T(8,128)S(1)} %get-tuple-element.30.seeds, s32[2,256,128]{2,1,0:T(8,128)S(1)} %get-tuple-element.31.material), custom_call_target="tpu_custom_call" | custom-call | tf_op jit(solution)/shard_map/pallas_call | solution.py:446
  5.6 0.1 collective-permute-start
  5.7 1.6 %collective-permute-start.1 = (f32[5,80,128]{2,1,0:T(8,128)S(1)}, f32[5,80,128]{2,1,0:T(8,128)S(1)}, u32[]{:S(2)}, u32[]{:S(2)}) collective-permute-start(f32[5,80,128]{2,1,0:T(8,128)S(1)} %get-tuple-element.33), channel_id=1, source_target_pairs={{0,8},{1,2},{2,1},{3,4},{4,3},{5,6},{6,5},{7,15},{8,0},{9,10},{10,... | collective-permute-start | bytes 614408 | tf_op jit(solution)/shard_map/ppermute | solution.py:471
  7.2 0.2 collective-permute-start.4
  7.4 1.5 %collective-permute-start.5 = (f32[5,208,128]{2,1,0:T(8,128)S(1)}, f32[5,208,128]{2,1,0:T(8,128)S(1)}, u32[]{:S(2)}, u32[]{:S(2)}) collective-permute-start(f32[5,208,128]{2,1,0:T(8,128)S(1)} %get-tuple-element.37), channel_id=1, source_target_pairs={{0,8},{1,2},{2,1},{3,4},{4,3},{5,6},{6,5},{7,15},{8,0},{9,10},{10,... | collective-permute-start | bytes 1597448 | tf_op jit(solution)/shard_map/ppermute | solution.py:471
  8.9 0.0 collective-permute-done.near
  8.9 2.6 %collective-permute-done.1.far = f32[5,80,128]{2,1,0:T(8,128)S(1)} collective-permute-done((f32[5,80,128]{2,1,0:T(8,128)S(1)}, f32[5,80,128]{2,1,0:T(8,128)S(1)}, u32[]{:S(2)}, u32[]{:S(2)}) %collective-permute-start.1) | collective-permute-done | bytes 204832 | tf_op jit(solution)/shard_map/ppermute | solution.py:471
  11.5 0.5 %shard_map.48 = (f32[12,64,128]{2,1,0:T(8,128)S(1)}, f32[12,32,128]{2,1,0:T(8,128)S(1)}, f32[12,16,128]{2,1,0:T(8,128)S(1)}) custom-call(f32[8,128]{1,0:T(8,128)S(1)} %get-tuple-element.29.table, f32[6,2,256,128]{3,2,1,0:T(8,128)S(1)} %get-tuple-element.30.seeds, s32[2,256,128]{2,1,0:T(8,128)S(1)} %get-tuple-element.31.material, ...), custom_call_target="tpu_custom_call" | custom-call | tf_op jit(solution)/shard_map/pallas_call | solution.py:446
  12.1 1.5 %collective-permute-start.3 = (f32[12,16,128]{2,1,0:T(8,128)S(1)}, f32[12,16,128]{2,1,0:T(8,128)S(1)}, u32[]{:S(2)}, u32[]{:S(2)}) collective-permute-start(f32[12,16,128]{2,1,0:T(8,128)S(1)} %get-tuple-element.35), channel_id=1, source_target_pairs={{0,24},{8,16},{16,8},{24,0},{1,25},{9,17},{17,9},{25,1},{2,26},{10... | collective-permute-start | bytes 294920 | tf_op jit(solution)/shard_map/ppermute | solution.py:475
  13.6 1.5 %collective-permute-start.2 = (f32[12,32,128]{2,1,0:T(8,128)S(1)}, f32[12,32,128]{2,1,0:T(8,128)S(1)}, u32[]{:S(2)}, u32[]{:S(2)}) collective-permute-start(f32[12,32,128]{2,1,0:T(8,128)S(1)} %get-tuple-element.34), channel_id=1, source_target_pairs={{0,16},{8,24},{16,0},{24,8},{1,17},{9,25},{17,1},{25,9},{2,18},{10... | collective-permute-start | bytes 589832 | tf_op jit(solution)/shard_map/ppermute | solution.py:475
  15.1 0.0 collective-permute-done.6.shared
  15.1 1.1 %shard_map.49 = (f32[5,56,128]{2,1,0:T(8,128)S(1)}, f32[5,56,128]{2,1,0:T(8,128)S(1)}, f32[8,128]{1,0:T(8,128)S(1)}) custom-call(f32[8,128]{1,0:T(8,128)S(1)} %get-tuple-element.29.table, f32[14,56,128]{2,1,0:T(8,128)S(1)} %collective-permute-done.6.shared), custom_call_target="tpu_custom_call" | custom-call | flops 10000000000 | tf_op jit(solution)/shard_map/pallas_call | solution.py:446
  16.2 0.1 collective-permute-start.10
  16.2 0.0 collective-permute-done.4.near
  16.2 0.8 %collective-permute-start.11 = (f32[5,56,128]{2,1,0:T(8,128)S(1)}, f32[5,56,128]{2,1,0:T(8,128)S(1)}, u32[]{:S(2)}, u32[]{:S(2)}) collective-permute-start(f32[5,56,128]{2,1,0:T(8,128)S(1)} %get-tuple-element.52), channel_id=1, source_target_pairs={{0,8},{1,2},{2,1},{3,4},{4,3},{5,6},{6,5},{7,15},{8,0},{9,10},{10,... | collective-permute-start | bytes 430088 | tf_op jit(solution)/shard_map/ppermute | solution.py:471
  17.1 1.2 %collective-permute-done.5.far = f32[5,208,128]{2,1,0:T(8,128)S(1)} collective-permute-done((f32[5,208,128]{2,1,0:T(8,128)S(1)}, f32[5,208,128]{2,1,0:T(8,128)S(1)}, u32[]{:S(2)}, u32[]{:S(2)}) %collective-permute-start.5) | collective-permute-done | bytes 532512 | tf_op jit(solution)/shard_map/ppermute | solution.py:471
  18.3 1.3 %shard_map.50 = (f32[12,192,128]{2,1,0:T(8,128)S(1)}, f32[12,48,128]{2,1,0:T(8,128)S(1)}, f32[12,16,128]{2,1,0:T(8,128)S(1)}) custom-call(f32[8,128]{1,0:T(8,128)S(1)} %get-tuple-element.29.table, f32[6,2,256,128]{3,2,1,0:T(8,128)S(1)} %get-tuple-element.30.seeds, s32[2,256,128]{2,1,0:T(8,128)S(1)} %get-tuple-element.31.material, ...), custom_call_target="tpu_custom_call" | custom-call | tf_op jit(solution)/shard_map/pallas_call | solution.py:446
  19.5 0.4 %collective-permute-start.7 = (f32[12,48,128]{2,1,0:T(8,128)S(1)}, f32[12,48,128]{2,1,0:T(8,128)S(1)}, u32[]{:S(2)}, u32[]{:S(2)}) collective-permute-start(f32[12,48,128]{2,1,0:T(8,128)S(1)} %get-tuple-element.43), channel_id=1, source_target_pairs={{0,16},{8,24},{16,0},{24,8},{1,17},{9,25},{17,1},{25,9},{2,18},{10... | collective-permute-start | bytes 884744 | tf_op jit(solution)/shard_map/ppermute | solution.py:475
  19.9 0.0 collective-permute-done.3.strip
  19.9 1.7 %collective-permute-start.9 = (f32[12,16,128]{2,1,0:T(8,128)S(1)}, f32[12,16,128]{2,1,0:T(8,128)S(1)}, u32[]{:S(2)}, u32[]{:S(2)}) collective-permute-start(f32[12,16,128]{2,1,0:T(8,128)S(1)} %get-tuple-element.48), channel_id=1, source_target_pairs={{0,8},{8,0},{16,24},{24,16},{1,9},{9,1},{17,25},{25,17},{2,10},{10... | collective-permute-start | bytes 294920 | tf_op jit(solution)/shard_map/ppermute | solution.py:475
  21.6 1.2 %collective-permute-done.2.corner = f32[12,32,128]{2,1,0:T(8,128)S(1)} collective-permute-done((f32[12,32,128]{2,1,0:T(8,128)S(1)}, f32[12,32,128]{2,1,0:T(8,128)S(1)}, u32[]{:S(2)}, u32[]{:S(2)}) %collective-permute-start.2) | collective-permute-done | bytes 196640 | tf_op jit(solution)/shard_map/ppermute | solution.py:475
  22.8 0.3 shard_map.51
  23.1 0.1 collective-permute-start.8
  23.1 0.0 collective-permute-done.10.near
  23.2 1.6 %collective-permute-done.9.beside = f32[12,16,128]{2,1,0:T(8,128)S(1)} collective-permute-done((f32[12,16,128]{2,1,0:T(8,128)S(1)}, f32[12,16,128]{2,1,0:T(8,128)S(1)}, u32[]{:S(2)}, u32[]{:S(2)}) %collective-permute-start.9) | collective-permute-done | bytes 98336 | tf_op jit(solution)/shard_map/ppermute | solution.py:475
  24.8 0.0 collective-permute-done.11.far
  24.8 1.5 %shard_map.52.part = f32[12,104,128]{2,1,0:T(8,128)S(1)} custom-call(f32[8,128]{1,0:T(8,128)S(1)} %get-tuple-element.29.table, f32[14,56,128]{2,1,0:T(8,128)S(1)} %collective-permute-done.6.shared, f32[5,56,128]{2,1,0:T(8,128)S(1)} %collective-permute-done.10.near, f32[5,56,128]{2,1,0:T(8,128)S(1)} %collective-permute-done.11.far), custom_call_target="tpu_custom_call" | custom-call | flops 2000000000 | tf_op jit(solution)/shard_map/pallas_call | solution.py:446
  26.3 0.9 %shard_map.53._ = f32[1,6,2,256,128]{4,3,2,1,0:T(8,128)} custom-call(f32[12,192,128]{2,1,0:T(8,128)S(1)} %get-tuple-element.42.mid, f32[12,104,128]{2,1,0:T(8,128)S(1)} %shard_map.52.part), custom_call_target="tpu_custom_call" | custom-call | tf_op jit(solution)/shard_map/pallas_call | solution.py:557
  27.2 1.7 %collective-permute-done.8.got = f32[12,32,128]{2,1,0:T(8,128)S(1)} collective-permute-done((f32[12,32,128]{2,1,0:T(8,128)S(1)}, f32[12,32,128]{2,1,0:T(8,128)S(1)}, u32[]{:S(2)}, u32[]{:S(2)}) %collective-permute-start.8) | collective-permute-done | bytes 196640 | tf_op jit(solution)/shard_map/ppermute | solution.py:475
  28.9 1.2 %shard_map.54 = f32[1,6,2,256,128]{4,3,2,1,0:T(8,128)} custom-call(f32[12,192,128]{2,1,0:T(8,128)S(1)} %get-tuple-element.42.mid, f32[12,48,128]{2,1,0:T(8,128)S(1)} %collective-permute-done.7.bands, f32[12,64,128]{2,1,0:T(8,128)S(1)} %get-tuple-element.45.summed, f32[12,32,128]{2,1,0:T(8,128)S(1)} %collective-permute-done.8.got, ...), custom_call_target="tpu_custom_call", output_to_operand_aliasing={{}: (6, {})} | custom-call | tf_op jit(solution)/shard_map/pallas_call | solution.py:566
  (1 shorter events, 0.0 us)
Async XLA Ops:
  1.8 13.3 %collective-permute-start.6 = (f32[14,56,128]{2,1,0:T(8,128)S(1)}, f32[14,56,128]{2,1,0:T(8,128)S(1)}, u32[]{:S(2)}, u32[]{:S(2)}) collective-permute-start(f32[14,56,128]{2,1,0:T(8,128)S(1)} %get-tuple-element.39), channel_id=1, source_target_pairs={{0,16},{8,24},{16,0},{24,8},{1,17},{9,25},{17,1},{25,9},{2,18},{10... | collective-permute-start | bytes 1204232 | tf_op jit(solution)/shard_map/ppermute | solution.py:475
  5.6 3.3 %collective-permute-start = (f32[5,80,128]{2,1,0:T(8,128)S(1)}, f32[5,80,128]{2,1,0:T(8,128)S(1)}, u32[]{:S(2)}, u32[]{:S(2)}) collective-permute-start(f32[5,80,128]{2,1,0:T(8,128)S(1)} %get-tuple-element.32), channel_id=1, source_target_pairs={{0,1},{1,0},{2,3},{3,2},{4,5},{5,4},{6,7},{7,6},{8,9},{9,8},{10,11... | collective-permute-start | bytes 614408 | tf_op jit(solution)/shard_map/ppermute | solution.py:461
  5.7 5.8 %collective-permute-start.1 = (f32[5,80,128]{2,1,0:T(8,128)S(1)}, f32[5,80,128]{2,1,0:T(8,128)S(1)}, u32[]{:S(2)}, u32[]{:S(2)}) collective-permute-start(f32[5,80,128]{2,1,0:T(8,128)S(1)} %get-tuple-element.33), channel_id=1, source_target_pairs={{0,8},{1,2},{2,1},{3,4},{4,3},{5,6},{6,5},{7,15},{8,0},{9,10},{10,... | collective-permute-start | bytes 614408 | tf_op jit(solution)/shard_map/ppermute | solution.py:471
  7.2 9.0 %collective-permute-start.4 = (f32[5,208,128]{2,1,0:T(8,128)S(1)}, f32[5,208,128]{2,1,0:T(8,128)S(1)}, u32[]{:S(2)}, u32[]{:S(2)}) collective-permute-start(f32[5,208,128]{2,1,0:T(8,128)S(1)} %get-tuple-element.36), channel_id=1, source_target_pairs={{0,1},{1,0},{2,3},{3,2},{4,5},{5,4},{6,7},{7,6},{8,9},{9,8},{10,11... | collective-permute-start | bytes 1597448 | tf_op jit(solution)/shard_map/ppermute | solution.py:461
  7.4 10.8 %collective-permute-start.5 = (f32[5,208,128]{2,1,0:T(8,128)S(1)}, f32[5,208,128]{2,1,0:T(8,128)S(1)}, u32[]{:S(2)}, u32[]{:S(2)}) collective-permute-start(f32[5,208,128]{2,1,0:T(8,128)S(1)} %get-tuple-element.37), channel_id=1, source_target_pairs={{0,8},{1,2},{2,1},{3,4},{4,3},{5,6},{6,5},{7,15},{8,0},{9,10},{10,... | collective-permute-start | bytes 1597448 | tf_op jit(solution)/shard_map/ppermute | solution.py:471
  12.1 7.9 %collective-permute-start.3 = (f32[12,16,128]{2,1,0:T(8,128)S(1)}, f32[12,16,128]{2,1,0:T(8,128)S(1)}, u32[]{:S(2)}, u32[]{:S(2)}) collective-permute-start(f32[12,16,128]{2,1,0:T(8,128)S(1)} %get-tuple-element.35), channel_id=1, source_target_pairs={{0,24},{8,16},{16,8},{24,0},{1,25},{9,17},{17,9},{25,1},{2,26},{10... | collective-permute-start | bytes 294920 | tf_op jit(solution)/shard_map/ppermute | solution.py:475
  13.6 9.3 %collective-permute-start.2 = (f32[12,32,128]{2,1,0:T(8,128)S(1)}, f32[12,32,128]{2,1,0:T(8,128)S(1)}, u32[]{:S(2)}, u32[]{:S(2)}) collective-permute-start(f32[12,32,128]{2,1,0:T(8,128)S(1)} %get-tuple-element.34), channel_id=1, source_target_pairs={{0,16},{8,24},{16,0},{24,8},{1,17},{9,25},{17,1},{25,9},{2,18},{10... | collective-permute-start | bytes 589832 | tf_op jit(solution)/shard_map/ppermute | solution.py:475
  16.2 7.0 %collective-permute-start.10 = (f32[5,56,128]{2,1,0:T(8,128)S(1)}, f32[5,56,128]{2,1,0:T(8,128)S(1)}, u32[]{:S(2)}, u32[]{:S(2)}) collective-permute-start(f32[5,56,128]{2,1,0:T(8,128)S(1)} %get-tuple-element.49), channel_id=1, source_target_pairs={{0,1},{1,0},{2,3},{3,2},{4,5},{5,4},{6,7},{7,6},{8,9},{9,8},{10,11... | collective-permute-start | bytes 430088 | tf_op jit(solution)/shard_map/ppermute | solution.py:461
  16.2 8.5 %collective-permute-start.11 = (f32[5,56,128]{2,1,0:T(8,128)S(1)}, f32[5,56,128]{2,1,0:T(8,128)S(1)}, u32[]{:S(2)}, u32[]{:S(2)}) collective-permute-start(f32[5,56,128]{2,1,0:T(8,128)S(1)} %get-tuple-element.52), channel_id=1, source_target_pairs={{0,8},{1,2},{2,1},{3,4},{4,3},{5,6},{6,5},{7,15},{8,0},{9,10},{10,... | collective-permute-start | bytes 430088 | tf_op jit(solution)/shard_map/ppermute | solution.py:471
  19.5 9.4 %collective-permute-start.7 = (f32[12,48,128]{2,1,0:T(8,128)S(1)}, f32[12,48,128]{2,1,0:T(8,128)S(1)}, u32[]{:S(2)}, u32[]{:S(2)}) collective-permute-start(f32[12,48,128]{2,1,0:T(8,128)S(1)} %get-tuple-element.43), channel_id=1, source_target_pairs={{0,16},{8,24},{16,0},{24,8},{1,17},{9,25},{17,1},{25,9},{2,18},{10... | collective-permute-start | bytes 884744 | tf_op jit(solution)/shard_map/ppermute | solution.py:475
  19.9 4.8 %collective-permute-start.9 = (f32[12,16,128]{2,1,0:T(8,128)S(1)}, f32[12,16,128]{2,1,0:T(8,128)S(1)}, u32[]{:S(2)}, u32[]{:S(2)}) collective-permute-start(f32[12,16,128]{2,1,0:T(8,128)S(1)} %get-tuple-element.48), channel_id=1, source_target_pairs={{0,8},{8,0},{16,24},{24,16},{1,9},{9,1},{17,25},{25,17},{2,10},{10... | collective-permute-start | bytes 294920 | tf_op jit(solution)/shard_map/ppermute | solution.py:475
  23.1 5.9 %collective-permute-start.8 = (f32[12,32,128]{2,1,0:T(8,128)S(1)}, f32[12,32,128]{2,1,0:T(8,128)S(1)}, u32[]{:S(2)}, u32[]{:S(2)}) collective-permute-start(f32[12,32,128]{2,1,0:T(8,128)S(1)} %get-tuple-element.46), channel_id=1, source_target_pairs={{0,8},{8,0},{16,24},{24,16},{1,9},{9,1},{17,25},{25,17},{2,10},{10... | collective-permute-start | bytes 589832 | tf_op jit(solution)/shard_map/ppermute | solution.py:475

commit v13 on v12

--- a/solution.py
+++ b/solution.py
@@ -13,7 +13,7 @@
 PLANES = 5
 REACH = 2
 SHARED = 96
-LARGE, MEDIUM, SMALL = 10**10, 2 * 10**9, 0
+CORNER, SHARE = 5 * 10**9, 15 * 10**8
 
 magnetic_coeff = 0.5
 
@@ -325,9 +325,12 @@
     return prepared(f[:3], f[3:6], f[6], table_entries(table))
 
 
-def shared_halo_kernel(sub, table, shared, near, far, done):
-    done[...] = jnp.zeros(done.shape, done.dtype)
-    send_halos(sub, shared_fields(table, shared), near, far, bands_packed)
+def shared_halo_kernel(spans, sub, table, seeds, material, shared, _, near, far):
+    other = shared.shape[1]
+    own = pl.ds(other, near.shape[1] - other)
+    send_halos(sub, loaded(seeds, material, table, spans), near.at[:, own], far.at[:, own])
+    both = pl.ds(0, other)
+    send_halos(sub, shared_fields(table, shared), near.at[:, both], far.at[:, both], bands_packed)
 
 
 def weighted_planes(seeds, material, table, near, far, spans, keeps, sub, sub_size):
@@ -346,7 +349,7 @@
     return results
 
 
-def edge_kernel(spans, sub, sub_size, tile, table, seeds, material, near, far, edge, corner, strip):
+def edge_kernel(spans, sub, sub_size, tile, table, seeds, material, near, far, edge, corner, beside):
     size_x = seeds.shape[2]
     keeps = ((0, BAND), (size_x - BAND, size_x))
     low, high = weighted_planes(seeds, material, table, near, far, spans, keeps, sub, sub_size)
@@ -354,18 +357,17 @@
     edge[:, :BAND] = low
     edge[:, BAND:] = high
     corner[...] = y_packed(low, high)
-    strip[...] = strip_packed(jnp.where(odd, high, low))
-
-
-def middle_kernel(spans, sub, sub_size, tile, table, seeds, material, near, far, edge, _, mid, bands, beside):
-    size_x = seeds.shape[2]
-    keep = (BAND, size_x - BAND)
+    beside[...] = strip_packed(jnp.where(odd, low, high))
+
+
+def late_kernel(spans, keeps, sub, sub_size, tile, table, seeds, material, near, far, edge, late, bands, strip):
     odd = lax.rem(lax.axis_index(tile), 2) == 1
-    beside[...] = strip_packed(jnp.where(odd, edge[:, :BAND], edge[:, BAND:]))
-    planes, = weighted_planes(seeds, material, table, near, far, spans, (keep,), sub, sub_size)
+    strip[...] = strip_packed(jnp.where(odd, edge[:, BAND:], edge[:, :BAND]))
+    low, high = weighted_planes(seeds, material, table, near, far, spans, keeps, sub, sub_size)
     half = bands.shape[1]
-    mid[...] = planes
-    bands[...] = y_packed(planes[:, :half], planes[:, -half:])
+    late[:, :half] = low
+    late[:, half:] = high
+    bands[...] = y_packed(low, high)
 
 
 def whole_kernel(spans, sub, sub_size, table, seeds, material, near, far, out):
@@ -378,13 +380,26 @@
     return jnp.where(inner_lanes(block.shape), 0.0, jnp.where(below, rolled(block, BAND), rolled(block, -BAND)))
 
 
-def shared_kernel(span, size_x, sub, sub_size, table, shared, near, far, part):
-    planes = final_fields(shared_fields(table, shared), near, far, sub, sub_size, bands_unpacked)
-    found, = weighted(planes, (span,), (span,), size_x, part.shape[2])
-    part[...] = y_swapped(found)
-
-
-def corner_kernel(tile, edge, corner, summed, send):
+def shared_kernel(spans, span, keep, sub, sub_size, table, seeds, material, shared, near, far, out, whole, sem):
+    other = shared.shape[1]
+    own = pl.ds(other, near.shape[1] - other)
+    size_x, size_y = seeds.shape[2:]
+    mine, = weighted_planes(seeds, material, table, near.at[:, own], far.at[:, own], spans, (keep,), sub, sub_size)
+    both = pl.ds(0, other)
+    planes = final_fields(
+        shared_fields(table, shared), near.at[:, both], far.at[:, both], sub, sub_size, bands_unpacked
+    )
+    found, = weighted(planes, (span,), (span,), size_x, size_y)
+    found = y_swapped(found)
+    start, stop = keep
+    skip = start - span[0]
+    whole[...] = (mine + found[:, skip : skip + stop - start]).reshape(whole.shape)
+    copy = pltpu.make_async_copy(whole, out.at[0, :, :, pl.ds(start, stop - start)], sem)
+    copy.start()
+    copy.wait()
+
+
+def corner_kernel(tile, edge, corner, _, summed, send):
     odd = lax.rem(lax.axis_index(tile), 2) == 1
     half = BAND // 2
     first, second = y_unpacked(corner[...])
@@ -397,19 +412,7 @@
     send[:, half:] = y_packed(away[:, :half], away[:, half:])
 
 
-def early_kernel(mid, part, out, whole, sem):
-    size_x = out.shape[3]
-    skip = HALO // 2
-    count = part.shape[1] - 2 * skip
-    start = (size_x - count) // 2
-    found = mid[:, start - BAND : start - BAND + count] + part[:, skip : skip + count]
-    whole[...] = found.reshape(whole.shape)
-    copy = pltpu.make_async_copy(whole, out.at[0, :, :, pl.ds(start, count)], sem)
-    copy.start()
-    copy.wait()
-
-
-def last_kernel(tile, mid, bands, summed, got, strip, beside, _, out, low, high, sems):
+def last_kernel(tile, late, bands, summed, got, strip, beside, _, out, low, high, sems):
     odd = lax.rem(lax.axis_index(tile), 2) == 1
     half, count = bands.shape[1], low.shape[2]
     quarter = BAND // 2
@@ -418,8 +421,8 @@
     for c in range(6):
         at = slice(depth * c, depth * (c + 1))
         first, second = y_unpacked(bands[at])
-        low[c, :, BAND:] = mid[at, :half] + first
-        high[c, :, :half] = mid[at, -half:] + second
+        low[c, :, BAND:] = late[at, :half] + first
+        high[c, :, :half] = late[at, half:] + second
         straight = got[at, :quarter]
         by = strip_of((straight, middle_out(straight)), beside[at])
         away = strip_of(y_unpacked(got[at, quarter:]), strip[at])
@@ -487,18 +490,19 @@
 def two_by_two(seeds, material, decay, coupling, sub_size, tile_size):
     depth, size_x, size_y = seeds.shape[2:]
     planes = 6 * depth
-    edges = ((0, BAND + HALO), (size_x - BAND - HALO, size_x))
-    inner = ((BAND - HALO, size_x - BAND + HALO),)
     keep = ((size_x - SHARED) // 2, (size_x + SHARED) // 2)
     span = (keep[0] - HALO // 2, keep[1] + HALO // 2)
-    fetched = (keep[0] - HALO, keep[1] + HALO)
-    rows = size_x - 2 * BAND
-    edge_rows, inner_rows = 2 * (BAND + HALO), rows + 2 * HALO
+    own = (keep[0] - HALO, keep[1] + HALO)
+    late_keeps = ((BAND, keep[0]), (keep[1], size_x - BAND))
+    late_spans = ((BAND - HALO, own[0] + 2 * HALO), (own[1] - 2 * HALO, size_x - BAND + HALO))
+    edges = ((0, BAND + HALO), (size_x - BAND - HALO, size_x))
+    edge_rows, late_rows = (sum(hi - lo for lo, hi in spans) for spans in (edges, late_spans))
+    late = late_keeps[0][1] - late_keeps[0][0]
     packed_rows = (SHARED + HALO) // 2 + 4
     whole = jax.ShapeDtypeStruct(seeds.shape, jnp.float32)
 
     shared, seeds, material, table = pl.pallas_call(
-        functools.partial(first_kernel, fetched, HALO // 2),
+        functools.partial(first_kernel, own, HALO // 2),
         out_shape=[
             jax.ShapeDtypeStruct((7 * depth, packed_rows, size_y), jnp.float32),
             jax.ShapeDtypeStruct(seeds.shape[1:], jnp.float32),
@@ -512,57 +516,52 @@
         cost_estimate=cost(0),
     )(*(pltpu.with_memory_space_constraint(x, pltpu.HBM) for x in (decay, coupling, seeds, material)))
     shared = swapped(shared, 2, tile_size)
-    edge_near, edge_far, inner_near, inner_far = called(
-        functools.partial(halo_pair_kernel, edges, inner, "sub"),
-        [(PLANES, edge_rows, size_y)] * 2 + [(PLANES, inner_rows, size_y)] * 2, table, seeds, material,
-    )
-    edge_near, inner_near = near_exchange(edge_near, sub_size), near_exchange(inner_near, sub_size)
+    edge_near, edge_far, late_near, late_far = called(
+        functools.partial(halo_pair_kernel, edges, late_spans, "sub"),
+        [(PLANES, edge_rows, size_y)] * 2 + [(PLANES, late_rows, size_y)] * 2, table, seeds, material,
+    )
+    edge_near, late_near = near_exchange(edge_near, sub_size), near_exchange(late_near, sub_size)
     edge_far = far_exchange(edge_far, sub_size, tile_size)
-    inner_far = far_exchange(inner_far, sub_size, tile_size)
-
-    edge, corner, strip = called(
+    late_far = far_exchange(late_far, sub_size, tile_size)
+
+    edge, corner, beside = called(
         functools.partial(edge_kernel, edges, "sub", sub_size, "tile"),
         [(planes, 2 * BAND, size_y), (planes, BAND, size_y), (planes, BAND // 2, size_y)],
         table, seeds, material, edge_near, edge_far,
     )
     corner = swapped(corner, 2, tile_size)
+    beside = swapped(beside, 1, tile_size)
+
+    late, bands, strip = called(
+        functools.partial(late_kernel, late_spans, late_keeps, "sub", sub_size, "tile"),
+        [(planes, 2 * late, size_y), (planes, late, size_y), (planes, BAND // 2, size_y)],
+        table, seeds, material, late_near, late_far, edge,
+    )
+    bands = swapped(bands, 2, tile_size)
     strip = swapped(strip, 3, tile_size)
 
-    shape = (PLANES, packed_rows, size_y)
-    shared_near, shared_far, done = called(
-        functools.partial(shared_halo_kernel, "sub"), [shape, shape, (8, size_y)], table, shared, flops=LARGE
+    shape = (PLANES, packed_rows + SHARED + 2 * HALO, size_y)
+    shared_near, shared_far = called(
+        functools.partial(shared_halo_kernel, (own,), "sub"), [shape, shape],
+        table, seeds, material, shared, late,
     )
     shared_near = near_exchange(shared_near, sub_size)
     shared_far = far_exchange(shared_far, sub_size, tile_size)
 
-    mid, bands, beside = called(
-        functools.partial(middle_kernel, inner, "sub", sub_size, "tile"),
-        [(planes, rows, size_y), (planes, (rows - SHARED) // 2, size_y), (planes, BAND // 2, size_y)],
-        table, seeds, material, inner_near, inner_far, edge, done,
-    )
-    bands = swapped(bands, 2, tile_size)
-    beside = swapped(beside, 1, tile_size)
-
-    corner, strip, mid = after(corner, strip, mid)
     summed, send = called(
         functools.partial(corner_kernel, "tile"), [(planes, 2 * BAND, size_y), (planes, BAND, size_y)],
-        edge, corner, flops=SMALL,
+        edge, corner, beside, flops=CORNER,
     )
     got = swapped(send, 1, tile_size)
-    beside, shared_near = after(beside, shared_near)
-    part, = called(
-        functools.partial(shared_kernel, span, size_x, "sub", sub_size),
-        [(planes, SHARED + HALO, size_y)], table, shared, shared_near, shared_far, flops=MEDIUM,
-    )
     early = pl.pallas_call(
-        early_kernel,
+        functools.partial(shared_kernel, (own,), span, keep, "sub", sub_size),
         out_shape=whole,
-        in_specs=[VMEM] * 2,
+        in_specs=[VMEM] * 6,
         out_specs=HBM,
         scratch_shapes=[pltpu.VMEM((6, depth, SHARED, size_y), jnp.float32), pltpu.SemaphoreType.DMA],
         compiler_params=PARAMS,
-        cost_estimate=cost(0),
-    )(mid, part)
+        cost_estimate=cost(SHARE),
+    )(table, seeds, material, shared, shared_near, shared_far)
     return pl.pallas_call(
         functools.partial(last_kernel, "tile"),
         out_shape=whole,
@@ -573,7 +572,7 @@
         input_output_aliases={6: 0},
         compiler_params=PARAMS,
         cost_estimate=cost(0),
-    )(mid, bands, summed, got, strip, beside, early)
+    )(late, bands, summed, got, strip, beside, early)
 
 
 def any_lattice(seeds, material, decay, coupling, sub_size, tile_size):

time: 30.2 us -> 34.4 us (1.14)
  waiting for transfers between devices: 8.36 us -> 11.2 us
  starting transfers between devices: 12.4 us -> 13.8 us
    ppermute x3, waiting for transfers between devices: 3.76 us -> 9.84 us  [far_exchange(): return lax.ppermute(far, ('tile', 'sub'), pairs)]
    ppermute x6, waiting for transfers between devices: 4.59 us -> 1.31 us  [swapped(): lax.ppermute(value, 'tile', [(t, t ^ bits) for t in range(tile_size)])]
    pallas_call x2, Pallas kernels: 2.72 us -> 4.63 us  [the longest x1 2.82 us: two_by_two(): pl.pallas_call(functools.partial(shared_kernel, (own,), span, keep, 'sub'...]
    pallas_call x6 -> x5, Pallas kernels: 5.34 us -> 3.46 us  [called(): pl.pallas_call(kernel, out_shape=outs, in_specs=[VMEM] * len(operands), o...]
    ppermute x6, starting transfers between devices: 8.18 us -> 8.98 us  [swapped(): lax.ppermute(value, 'tile', [(t, t ^ bits) for t in range(tile_size)])]
    ppermute x3, starting transfers between devices: 3.89 us -> 4.48 us  [far_exchange(): return lax.ppermute(far, ('tile', 'sub'), pairs)]
  transfers between devices with their start and end apart: 12 -> 12, of which waited for: 5 -> 5; matrix products, arithmetic and copies ran while one was open for 0% -> 0% of each run, Pallas kernels for 21% -> 18%
where the time goes in v13:
time: 34.4 us; the launch traced here: 34.3 us
  starting transfers between devices  13.8 us (40%)
  waiting for transfers between devices  11.2 us (33%)
  Pallas kernels  9.24 us (27%)
    ppermute x3, waiting for transfers between devices, far_exchange(): return lax.ppermute(far, ('tile', 'sub'), pairs)  9.84 us
    ppermute x6, starting transfers between devices, swapped(): lax.ppermute(value, 'tile', [(t, t ^ bits) for t in range(tile_size)])  8.98 us
    ppermute x3, starting transfers between devices, far_exchange(): return lax.ppermute(far, ('tile', 'sub'), pairs)  4.48 us
    pallas_call x5, Pallas kernels, called(): pl.pallas_call(kernel, out_shape=outs, in_specs=[VMEM] * len(operands), o...  3.46 us
    pallas_call x1, Pallas kernels, two_by_two(): pl.pallas_call(functools.partial(shared_kernel, (own,), span, keep, 'sub'...  2.82 us
    pallas_call x1, Pallas kernels, two_by_two(): pl.pallas_call(functools.partial(first_kernel, own, HALO // 2), out_shape...  1.81 us
    ppermute x6, waiting for transfers between devices, swapped(): lax.ppermute(value, 'tile', [(t, t ^ bits) for t in range(tile_size)])  1.31 us
    pallas_call x1, Pallas kernels, two_by_two(): pl.pallas_call(functools.partial(last_kernel, 'tile'), out_shape=whole, i...  1.16 us
  transfers between devices with their start and end apart: 12, of which 5 were waited for; matrix products, arithmetic and copies ran while one was open for 0% of the time, Pallas kernels for 18%

profile of v13, /device:TPU:0, one launch (start us, length us, event | category | flops | bytes accessed | tf_op | source)
XLA Modules:
  0.0 34.3 jit_solution(14414918949796051771)
XLA Ops:
  0.0 1.8 %shard_map.46 = (f32[14,56,128]{2,1,0:T(8,128)S(1)}, f32[6,2,256,128]{3,2,1,0:T(8,128)S(1)}, s32[2,256,128]{2,1,0:T(8,128)S(1)}, f32[8,128]{1,0:T(8,128)S(1)}) custom-call(f32[4]{0:T(128)} %decay.1, f32[4]{0:T(128)} %coupling.1, f32[1,6,2,256,128]{4,3,2,1,0:T(8,128)} %seeds.1, s32[1,2,256,128]{3,2,1,0:T(8,128)} %material.1), custom_call_target="tpu_custom_call" | custom-call | tf_op jit(solution)/shard_map/pallas_call | solution.py:504
  1.8 3.0 %collective-permute-start.9 = (f32[14,56,128]{2,1,0:T(8,128)S(1)}, f32[14,56,128]{2,1,0:T(8,128)S(1)}, u32[]{:S(2)}, u32[]{:S(2)}) collective-permute-start(f32[14,56,128]{2,1,0:T(8,128)S(1)} %get-tuple-element.38), channel_id=1, source_target_pairs={{0,16},{8,24},{16,0},{24,8},{1,17},{9,25},{17,1},{25,9},{2,18},{10... | collective-permute-start | bytes 1204232 | tf_op jit(solution)/shard_map/ppermute | solution.py:478
  4.9 0.5 %shard_map.47 = (f32[5,80,128]{2,1,0:T(8,128)S(1)}, f32[5,80,128]{2,1,0:T(8,128)S(1)}, f32[5,128,128]{2,1,0:T(8,128)S(1)}, f32[5,128,128]{2,1,0:T(8,128)S(1)}) custom-call(f32[8,128]{1,0:T(8,128)S(1)} %get-tuple-element.23.table, f32[6,2,256,128]{3,2,1,0:T(8,128)S(1)} %get-tuple-element.24.seeds, s32[2,256,128]{2,1,0:T(8,128)S(1)} %get-tuple-element.25.material), custom_call_target="tpu_custom_call" | custom-call | tf_op jit(solution)/shard_map/pallas_call | solution.py:449
  5.4 0.1 collective-permute-start.2
  5.5 1.6 %collective-permute-start.3 = (f32[5,80,128]{2,1,0:T(8,128)S(1)}, f32[5,80,128]{2,1,0:T(8,128)S(1)}, u32[]{:S(2)}, u32[]{:S(2)}) collective-permute-start(f32[5,80,128]{2,1,0:T(8,128)S(1)} %get-tuple-element.29), channel_id=1, source_target_pairs={{0,8},{1,2},{2,1},{3,4},{4,3},{5,6},{6,5},{7,15},{8,0},{9,10},{10,... | collective-permute-start | bytes 614408 | tf_op jit(solution)/shard_map/ppermute | solution.py:474
  7.0 0.2 collective-permute-start
  7.2 1.5 %collective-permute-start.1 = (f32[5,128,128]{2,1,0:T(8,128)S(1)}, f32[5,128,128]{2,1,0:T(8,128)S(1)}, u32[]{:S(2)}, u32[]{:S(2)}) collective-permute-start(f32[5,128,128]{2,1,0:T(8,128)S(1)} %get-tuple-element.27), channel_id=1, source_target_pairs={{0,8},{1,2},{2,1},{3,4},{4,3},{5,6},{6,5},{7,15},{8,0},{9,10},{10,... | collective-permute-start | bytes 983048 | tf_op jit(solution)/shard_map/ppermute | solution.py:474
  8.7 0.0 collective-permute-done.2.near
  8.7 2.6 %collective-permute-done.3.far = f32[5,80,128]{2,1,0:T(8,128)S(1)} collective-permute-done((f32[5,80,128]{2,1,0:T(8,128)S(1)}, f32[5,80,128]{2,1,0:T(8,128)S(1)}, u32[]{:S(2)}, u32[]{:S(2)}) %collective-permute-start.3) | collective-permute-done | bytes 204832 | tf_op jit(solution)/shard_map/ppermute | solution.py:474
  11.3 0.5 %shard_map.48 = (f32[12,64,128]{2,1,0:T(8,128)S(1)}, f32[12,32,128]{2,1,0:T(8,128)S(1)}, f32[12,16,128]{2,1,0:T(8,128)S(1)}) custom-call(f32[8,128]{1,0:T(8,128)S(1)} %get-tuple-element.23.table, f32[6,2,256,128]{3,2,1,0:T(8,128)S(1)} %get-tuple-element.24.seeds, s32[2,256,128]{2,1,0:T(8,128)S(1)} %get-tuple-element.25.material, ...), custom_call_target="tpu_custom_call" | custom-call | tf_op jit(solution)/shard_map/pallas_call | solution.py:449
  11.9 0.1 collective-permute-start.5
  11.9 2.0 %collective-permute-start.6 = (f32[12,16,128]{2,1,0:T(8,128)S(1)}, f32[12,16,128]{2,1,0:T(8,128)S(1)}, u32[]{:S(2)}, u32[]{:S(2)}) collective-permute-start(f32[12,16,128]{2,1,0:T(8,128)S(1)} %get-tuple-element.34), channel_id=1, source_target_pairs={{0,8},{8,0},{16,24},{24,16},{1,9},{9,1},{17,25},{25,17},{2,10},{10... | collective-permute-start | bytes 294920 | tf_op jit(solution)/shard_map/ppermute | solution.py:478
  13.9 0.0 collective-permute-done.near
  13.9 0.9 %collective-permute-done.1.far = f32[5,128,128]{2,1,0:T(8,128)S(1)} collective-permute-done((f32[5,128,128]{2,1,0:T(8,128)S(1)}, f32[5,128,128]{2,1,0:T(8,128)S(1)}, u32[]{:S(2)}, u32[]{:S(2)}) %collective-permute-start.1) | collective-permute-done | bytes 327712 | tf_op jit(solution)/shard_map/ppermute | solution.py:474
  14.8 0.8 %shard_map.49 = (f32[12,96,128]{2,1,0:T(8,128)S(1)}, f32[12,48,128]{2,1,0:T(8,128)S(1)}, f32[12,16,128]{2,1,0:T(8,128)S(1)}) custom-call(f32[8,128]{1,0:T(8,128)S(1)} %get-tuple-element.23.table, f32[6,2,256,128]{3,2,1,0:T(8,128)S(1)} %get-tuple-element.24.seeds, s32[2,256,128]{2,1,0:T(8,128)S(1)} %get-tuple-element.25.material, ...), custom_call_target="tpu_custom_call" | custom-call | tf_op jit(solution)/shard_map/pallas_call | solution.py:449
  15.6 0.7 %collective-permute-start.4 = (f32[12,48,128]{2,1,0:T(8,128)S(1)}, f32[12,48,128]{2,1,0:T(8,128)S(1)}, u32[]{:S(2)}, u32[]{:S(2)}) collective-permute-start(f32[12,48,128]{2,1,0:T(8,128)S(1)} %get-tuple-element.32), channel_id=1, source_target_pairs={{0,16},{8,24},{16,0},{24,8},{1,17},{9,25},{17,1},{25,9},{2,18},{10... | collective-permute-start | bytes 884744 | tf_op jit(solution)/shard_map/ppermute | solution.py:478
  16.3 0.0 collective-permute-done.9.shared
  16.3 1.3 %shard_map.51 = (f32[5,168,128]{2,1,0:T(8,128)S(1)}, f32[5,168,128]{2,1,0:T(8,128)S(1)}) custom-call(f32[8,128]{1,0:T(8,128)S(1)} %get-tuple-element.23.table, f32[6,2,256,128]{3,2,1,0:T(8,128)S(1)} %get-tuple-element.24.seeds, s32[2,256,128]{2,1,0:T(8,128)S(1)} %get-tuple-element.25.material, f32[14,56,128]{2,1,0:T(8,128)S(1)} %collective-permute-done.9.shared, ...), custom_call_target="tpu_custom_call" | custom-call | tf_op jit(solution)/shard_map/pallas_call | solution.py:449
  17.6 0.1 collective-permute-start.10
  17.7 1.4 %collective-permute-start.11 = (f32[5,168,128]{2,1,0:T(8,128)S(1)}, f32[5,168,128]{2,1,0:T(8,128)S(1)}, u32[]{:S(2)}, u32[]{:S(2)}) collective-permute-start(f32[5,168,128]{2,1,0:T(8,128)S(1)} %get-tuple-element.40), channel_id=1, source_target_pairs={{0,8},{1,2},{2,1},{3,4},{4,3},{5,6},{6,5},{7,15},{8,0},{9,10},{10,... | collective-permute-start | bytes 1290248 | tf_op jit(solution)/shard_map/ppermute | solution.py:474
  19.2 0.0 collective-permute-done.6._.beside
  19.2 0.1 collective-permute-done.5.corner
  19.3 0.3 shard_map.50
  19.5 1.6 %collective-permute-start.7 = (f32[12,32,128]{2,1,0:T(8,128)S(1)}, f32[12,32,128]{2,1,0:T(8,128)S(1)}, u32[]{:S(2)}, u32[]{:S(2)}) collective-permute-start(f32[12,32,128]{2,1,0:T(8,128)S(1)} %get-tuple-element.36), channel_id=1, source_target_pairs={{0,8},{8,0},{16,24},{24,16},{1,9},{9,1},{17,25},{25,17},{2,10},{10... | collective-permute-start | bytes 589832 | tf_op jit(solution)/shard_map/ppermute | solution.py:478
  21.1 1.6 %collective-permute-start.8 = (f32[12,16,128]{2,1,0:T(8,128)S(1)}, f32[12,16,128]{2,1,0:T(8,128)S(1)}, u32[]{:S(2)}, u32[]{:S(2)}) collective-permute-start(f32[12,16,128]{2,1,0:T(8,128)S(1)} %get-tuple-element.37), channel_id=1, source_target_pairs={{0,24},{8,16},{16,8},{24,0},{1,25},{9,17},{17,9},{25,1},{2,26},{10... | collective-permute-start | bytes 294920 | tf_op jit(solution)/shard_map/ppermute | solution.py:478
  22.7 0.0 collective-permute-done.10.near
  22.7 6.4 %collective-permute-done.11.far = f32[5,168,128]{2,1,0:T(8,128)S(1)} collective-permute-done((f32[5,168,128]{2,1,0:T(8,128)S(1)}, f32[5,168,128]{2,1,0:T(8,128)S(1)}, u32[]{:S(2)}, u32[]{:S(2)}) %collective-permute-start.11) | collective-permute-done | bytes 430112 | tf_op jit(solution)/shard_map/ppermute | solution.py:474
  29.1 2.8 %shard_map.52._ = f32[1,6,2,256,128]{4,3,2,1,0:T(8,128)} custom-call(f32[8,128]{1,0:T(8,128)S(1)} %get-tuple-element.23.table, f32[6,2,256,128]{3,2,1,0:T(8,128)S(1)} %get-tuple-element.24.seeds, s32[2,256,128]{2,1,0:T(8,128)S(1)} %get-tuple-element.25.material, f32[14,56,128]{2,1,0:T(8,128)S(1)} %collective-permute-done.9.shared, ...), custom_call_target="tpu_custom_call" | custom-call | flops 1500000000 | tf_op jit(solution)/shard_map/pallas_call | solution.py:556
  31.9 1.2 %collective-permute-done.8.strip = f32[12,16,128]{2,1,0:T(8,128)S(1)} collective-permute-done((f32[12,16,128]{2,1,0:T(8,128)S(1)}, f32[12,16,128]{2,1,0:T(8,128)S(1)}, u32[]{:S(2)}, u32[]{:S(2)}) %collective-permute-start.8) | collective-permute-done | bytes 98336 | tf_op jit(solution)/shard_map/ppermute | solution.py:478
  33.1 0.0 collective-permute-done.7.got
  33.1 0.0 collective-permute-done.4.bands
  33.1 1.2 %shard_map.53 = f32[1,6,2,256,128]{4,3,2,1,0:T(8,128)} custom-call(f32[12,96,128]{2,1,0:T(8,128)S(1)} %get-tuple-element.31._.late, f32[12,48,128]{2,1,0:T(8,128)S(1)} %collective-permute-done.4.bands, f32[12,64,128]{2,1,0:T(8,128)S(1)} %get-tuple-element.35.summed, f32[12,32,128]{2,1,0:T(8,128)S(1)} %collective-permute-done.7.got, ...), custom_call_target="tpu_custom_call", output_to_operand_aliasing={{}: (6, {})} | custom-call | tf_op jit(solution)/shard_map/pallas_call | solution.py:565
Async XLA Ops:
  1.8 14.5 %collective-permute-start.9 = (f32[14,56,128]{2,1,0:T(8,128)S(1)}, f32[14,56,128]{2,1,0:T(8,128)S(1)}, u32[]{:S(2)}, u32[]{:S(2)}) collective-permute-start(f32[14,56,128]{2,1,0:T(8,128)S(1)} %get-tuple-element.38), channel_id=1, source_target_pairs={{0,16},{8,24},{16,0},{24,8},{1,17},{9,25},{17,1},{25,9},{2,18},{10... | collective-permute-start | bytes 1204232 | tf_op jit(solution)/shard_map/ppermute | solution.py:478
  5.4 3.3 %collective-permute-start.2 = (f32[5,80,128]{2,1,0:T(8,128)S(1)}, f32[5,80,128]{2,1,0:T(8,128)S(1)}, u32[]{:S(2)}, u32[]{:S(2)}) collective-permute-start(f32[5,80,128]{2,1,0:T(8,128)S(1)} %get-tuple-element.28), channel_id=1, source_target_pairs={{0,1},{1,0},{2,3},{3,2},{4,5},{5,4},{6,7},{7,6},{8,9},{9,8},{10,11... | collective-permute-start | bytes 614408 | tf_op jit(solution)/shard_map/ppermute | solution.py:464
  5.5 5.8 %collective-permute-start.3 = (f32[5,80,128]{2,1,0:T(8,128)S(1)}, f32[5,80,128]{2,1,0:T(8,128)S(1)}, u32[]{:S(2)}, u32[]{:S(2)}) collective-permute-start(f32[5,80,128]{2,1,0:T(8,128)S(1)} %get-tuple-element.29), channel_id=1, source_target_pairs={{0,8},{1,2},{2,1},{3,4},{4,3},{5,6},{6,5},{7,15},{8,0},{9,10},{10,... | collective-permute-start | bytes 614408 | tf_op jit(solution)/shard_map/ppermute | solution.py:474
  7.0 6.9 %collective-permute-start = (f32[5,128,128]{2,1,0:T(8,128)S(1)}, f32[5,128,128]{2,1,0:T(8,128)S(1)}, u32[]{:S(2)}, u32[]{:S(2)}) collective-permute-start(f32[5,128,128]{2,1,0:T(8,128)S(1)} %get-tuple-element.26), channel_id=1, source_target_pairs={{0,1},{1,0},{2,3},{3,2},{4,5},{5,4},{6,7},{7,6},{8,9},{9,8},{10,11... | collective-permute-start | bytes 983048 | tf_op jit(solution)/shard_map/ppermute | solution.py:464
  7.2 7.6 %collective-permute-start.1 = (f32[5,128,128]{2,1,0:T(8,128)S(1)}, f32[5,128,128]{2,1,0:T(8,128)S(1)}, u32[]{:S(2)}, u32[]{:S(2)}) collective-permute-start(f32[5,128,128]{2,1,0:T(8,128)S(1)} %get-tuple-element.27), channel_id=1, source_target_pairs={{0,8},{1,2},{2,1},{3,4},{4,3},{5,6},{6,5},{7,15},{8,0},{9,10},{10,... | collective-permute-start | bytes 983048 | tf_op jit(solution)/shard_map/ppermute | solution.py:474
  11.9 7.4 %collective-permute-start.5 = (f32[12,32,128]{2,1,0:T(8,128)S(1)}, f32[12,32,128]{2,1,0:T(8,128)S(1)}, u32[]{:S(2)}, u32[]{:S(2)}) collective-permute-start(f32[12,32,128]{2,1,0:T(8,128)S(1)} %get-tuple-element.33), channel_id=1, source_target_pairs={{0,16},{8,24},{16,0},{24,8},{1,17},{9,25},{17,1},{25,9},{2,18},{10... | collective-permute-start | bytes 589832 | tf_op jit(solution)/shard_map/ppermute | solution.py:478
  11.9 7.2 %collective-permute-start.6 = (f32[12,16,128]{2,1,0:T(8,128)S(1)}, f32[12,16,128]{2,1,0:T(8,128)S(1)}, u32[]{:S(2)}, u32[]{:S(2)}) collective-permute-start(f32[12,16,128]{2,1,0:T(8,128)S(1)} %get-tuple-element.34), channel_id=1, source_target_pairs={{0,8},{8,0},{16,24},{24,16},{1,9},{9,1},{17,25},{25,17},{2,10},{10... | collective-permute-start | bytes 294920 | tf_op jit(solution)/shard_map/ppermute | solution.py:478
  15.6 17.5 %collective-permute-start.4 = (f32[12,48,128]{2,1,0:T(8,128)S(1)}, f32[12,48,128]{2,1,0:T(8,128)S(1)}, u32[]{:S(2)}, u32[]{:S(2)}) collective-permute-start(f32[12,48,128]{2,1,0:T(8,128)S(1)} %get-tuple-element.32), channel_id=1, source_target_pairs={{0,16},{8,24},{16,0},{24,8},{1,17},{9,25},{17,1},{25,9},{2,18},{10... | collective-permute-start | bytes 884744 | tf_op jit(solution)/shard_map/ppermute | solution.py:478
  17.6 5.1 %collective-permute-start.10 = (f32[5,168,128]{2,1,0:T(8,128)S(1)}, f32[5,168,128]{2,1,0:T(8,128)S(1)}, u32[]{:S(2)}, u32[]{:S(2)}) collective-permute-start(f32[5,168,128]{2,1,0:T(8,128)S(1)} %get-tuple-element.39), channel_id=1, source_target_pairs={{0,1},{1,0},{2,3},{3,2},{4,5},{5,4},{6,7},{7,6},{8,9},{9,8},{10,11... | collective-permute-start | bytes 1290248 | tf_op jit(solution)/shard_map/ppermute | solution.py:464
  17.7 11.4 %collective-permute-start.11 = (f32[5,168,128]{2,1,0:T(8,128)S(1)}, f32[5,168,128]{2,1,0:T(8,128)S(1)}, u32[]{:S(2)}, u32[]{:S(2)}) collective-permute-start(f32[5,168,128]{2,1,0:T(8,128)S(1)} %get-tuple-element.40), channel_id=1, source_target_pairs={{0,8},{1,2},{2,1},{3,4},{4,3},{5,6},{6,5},{7,15},{8,0},{9,10},{10,... | collective-permute-start | bytes 1290248 | tf_op jit(solution)/shard_map/ppermute | solution.py:474
  19.5 13.6 %collective-permute-start.7 = (f32[12,32,128]{2,1,0:T(8,128)S(1)}, f32[12,32,128]{2,1,0:T(8,128)S(1)}, u32[]{:S(2)}, u32[]{:S(2)}) collective-permute-start(f32[12,32,128]{2,1,0:T(8,128)S(1)} %get-tuple-element.36), channel_id=1, source_target_pairs={{0,8},{8,0},{16,24},{24,16},{1,9},{9,1},{17,25},{25,17},{2,10},{10... | collective-permute-start | bytes 589832 | tf_op jit(solution)/shard_map/ppermute | solution.py:478
  21.1 12.0 %collective-permute-start.8 = (f32[12,16,128]{2,1,0:T(8,128)S(1)}, f32[12,16,128]{2,1,0:T(8,128)S(1)}, u32[]{:S(2)}, u32[]{:S(2)}) collective-permute-start(f32[12,16,128]{2,1,0:T(8,128)S(1)} %get-tuple-element.37), channel_id=1, source_target_pairs={{0,24},{8,16},{16,8},{24,0},{1,25},{9,17},{17,9},{25,1},{2,26},{10... | collective-permute-start | bytes 294920 | tf_op jit(solution)/shard_map/ppermute | solution.py:478

commit v14 on v12

--- a/solution.py
+++ b/solution.py
@@ -13,7 +13,7 @@
 PLANES = 5
 REACH = 2
 SHARED = 96
-LARGE, MEDIUM, SMALL = 10**10, 2 * 10**9, 0
+LARGE, MEDIUM, SMALL = 10**10, 2 * 10**9, 5 * 10**8
 
 magnetic_coeff = 0.5
 
@@ -346,7 +346,7 @@
     return results
 
 
-def edge_kernel(spans, sub, sub_size, tile, table, seeds, material, near, far, edge, corner, strip):
+def edge_kernel(spans, sub, sub_size, tile, table, seeds, material, near, far, edge, corner, beside):
     size_x = seeds.shape[2]
     keeps = ((0, BAND), (size_x - BAND, size_x))
     low, high = weighted_planes(seeds, material, table, near, far, spans, keeps, sub, sub_size)
@@ -354,14 +354,14 @@
     edge[:, :BAND] = low
     edge[:, BAND:] = high
     corner[...] = y_packed(low, high)
-    strip[...] = strip_packed(jnp.where(odd, high, low))
-
-
-def middle_kernel(spans, sub, sub_size, tile, table, seeds, material, near, far, edge, _, mid, bands, beside):
+    beside[...] = strip_packed(jnp.where(odd, low, high))
+
+
+def middle_kernel(spans, sub, sub_size, tile, table, seeds, material, near, far, edge, _, mid, bands, strip):
     size_x = seeds.shape[2]
     keep = (BAND, size_x - BAND)
     odd = lax.rem(lax.axis_index(tile), 2) == 1
-    beside[...] = strip_packed(jnp.where(odd, edge[:, :BAND], edge[:, BAND:]))
+    strip[...] = strip_packed(jnp.where(odd, edge[:, BAND:], edge[:, :BAND]))
     planes, = weighted_planes(seeds, material, table, near, far, spans, (keep,), sub, sub_size)
     half = bands.shape[1]
     mid[...] = planes
@@ -384,7 +384,7 @@
     part[...] = y_swapped(found)
 
 
-def corner_kernel(tile, edge, corner, summed, send):
+def corner_kernel(tile, edge, corner, _, summed, send):
     odd = lax.rem(lax.axis_index(tile), 2) == 1
     half = BAND // 2
     first, second = y_unpacked(corner[...])
@@ -520,13 +520,13 @@
     edge_far = far_exchange(edge_far, sub_size, tile_size)
     inner_far = far_exchange(inner_far, sub_size, tile_size)
 
-    edge, corner, strip = called(
+    edge, corner, beside = called(
         functools.partial(edge_kernel, edges, "sub", sub_size, "tile"),
         [(planes, 2 * BAND, size_y), (planes, BAND, size_y), (planes, BAND // 2, size_y)],
         table, seeds, material, edge_near, edge_far,
     )
     corner = swapped(corner, 2, tile_size)
-    strip = swapped(strip, 3, tile_size)
+    beside = swapped(beside, 1, tile_size)
 
     shape = (PLANES, packed_rows, size_y)
     shared_near, shared_far, done = called(
@@ -535,21 +535,20 @@
     shared_near = near_exchange(shared_near, sub_size)
     shared_far = far_exchange(shared_far, sub_size, tile_size)
 
-    mid, bands, beside = called(
+    mid, bands, strip = called(
         functools.partial(middle_kernel, inner, "sub", sub_size, "tile"),
         [(planes, rows, size_y), (planes, (rows - SHARED) // 2, size_y), (planes, BAND // 2, size_y)],
         table, seeds, material, inner_near, inner_far, edge, done,
     )
     bands = swapped(bands, 2, tile_size)
-    beside = swapped(beside, 1, tile_size)
-
-    corner, strip, mid = after(corner, strip, mid)
+    strip = swapped(strip, 3, tile_size)
+
+    corner, mid = after(corner, mid)
     summed, send = called(
         functools.partial(corner_kernel, "tile"), [(planes, 2 * BAND, size_y), (planes, BAND, size_y)],
-        edge, corner, flops=SMALL,
+        edge, corner, beside, flops=SMALL,
     )
     got = swapped(send, 1, tile_size)
-    beside, shared_near = after(beside, shared_near)
     part, = called(
         functools.partial(shared_kernel, span, size_x, "sub", sub_size),
         [(planes, SHARED + HALO, size_y)], table, shared, shared_near, shared_far, flops=MEDIUM,

time: 30.2 us -> 31 us (1.026)
  starting transfers between devices: 12.4 us -> 13.9 us
  waiting for transfers between devices: 8.36 us -> 7.69 us
    ppermute x3, starting transfers between devices: 3.89 us -> 4.82 us  [far_exchange(): return lax.ppermute(far, ('tile', 'sub'), pairs)]
    ppermute x6, waiting for transfers between devices: 4.59 us -> 3.92 us  [swapped(): lax.ppermute(value, 'tile', [(t, t ^ bits) for t in range(tile_size)])]
    ppermute x6, starting transfers between devices: 8.18 us -> 8.71 us  [swapped(): lax.ppermute(value, 'tile', [(t, t ^ bits) for t in range(tile_size)])]
  transfers between devices with their start and end apart: 12 -> 12, of which waited for: 5 -> 4; matrix products, arithmetic and copies ran while one was open for 0% -> 0% of each run, Pallas kernels for 21% -> 20%
where the time goes in v14:
time: 31 us; the launch traced here: 30.9 us
  starting transfers between devices  13.9 us (45%)
  Pallas kernels  9.25 us (30%)
  waiting for transfers between devices  7.69 us (25%)
    ppermute x6, starting transfers between devices, swapped(): lax.ppermute(value, 'tile', [(t, t ^ bits) for t in range(tile_size)])  8.71 us
    pallas_call x6, Pallas kernels, called(): pl.pallas_call(kernel, out_shape=outs, in_specs=[VMEM] * len(operands), o...  5.37 us
    ppermute x3, starting transfers between devices, far_exchange(): return lax.ppermute(far, ('tile', 'sub'), pairs)  4.82 us
    ppermute x6, waiting for transfers between devices, swapped(): lax.ppermute(value, 'tile', [(t, t ^ bits) for t in range(tile_size)])  3.92 us
    ppermute x3, waiting for transfers between devices, far_exchange(): return lax.ppermute(far, ('tile', 'sub'), pairs)  3.77 us
    pallas_call x1, Pallas kernels, two_by_two(): pl.pallas_call(functools.partial(first_kernel, fetched, HALO // 2), out_s...  1.81 us
    pallas_call x1, Pallas kernels, two_by_two(): pl.pallas_call(functools.partial(last_kernel, 'tile'), out_shape=whole, i...  1.16 us
    pallas_call x1, Pallas kernels, two_by_two(): pl.pallas_call(early_kernel, out_shape=whole, in_specs=[VMEM] * 2, out_sp...  0.91 us
  transfers between devices with their start and end apart: 12, of which 4 were waited for; matrix products, arithmetic and copies ran while one was open for 0% of the time, Pallas kernels for 20%

profile of v14, /device:TPU:0, one launch (start us, length us, event | category | flops | bytes accessed | tf_op | source)
XLA Modules:
  0.0 30.9 jit_solution(13150501548478829495)
XLA Ops:
  0.0 1.8 %shard_map.46 = (f32[14,56,128]{2,1,0:T(8,128)S(1)}, f32[6,2,256,128]{3,2,1,0:T(8,128)S(1)}, s32[2,256,128]{2,1,0:T(8,128)S(1)}, f32[8,128]{1,0:T(8,128)S(1)}) custom-call(f32[4]{0:T(128)} %decay.1, f32[4]{0:T(128)} %coupling.1, f32[1,6,2,256,128]{4,3,2,1,0:T(8,128)} %seeds.1, s32[1,2,256,128]{3,2,1,0:T(8,128)} %material.1), custom_call_target="tpu_custom_call" | custom-call | tf_op jit(solution)/shard_map/pallas_call | solution.py:500
  1.8 3.0 %collective-permute-start.5 = (f32[14,56,128]{2,1,0:T(8,128)S(1)}, f32[14,56,128]{2,1,0:T(8,128)S(1)}, u32[]{:S(2)}, u32[]{:S(2)}) collective-permute-start(f32[14,56,128]{2,1,0:T(8,128)S(1)} %get-tuple-element.35), channel_id=1, source_target_pairs={{0,16},{8,24},{16,0},{24,8},{1,17},{9,25},{17,1},{25,9},{2,18},{10... | collective-permute-start | bytes 1204232 | tf_op jit(solution)/shard_map/ppermute | solution.py:475
  4.9 0.8 %shard_map.47 = (f32[5,80,128]{2,1,0:T(8,128)S(1)}, f32[5,80,128]{2,1,0:T(8,128)S(1)}, f32[5,208,128]{2,1,0:T(8,128)S(1)}, f32[5,208,128]{2,1,0:T(8,128)S(1)}) custom-call(f32[8,128]{1,0:T(8,128)S(1)} %get-tuple-element.26.table, f32[6,2,256,128]{3,2,1,0:T(8,128)S(1)} %get-tuple-element.27.seeds, s32[2,256,128]{2,1,0:T(8,128)S(1)} %get-tuple-element.28.material), custom_call_target="tpu_custom_call" | custom-call | tf_op jit(solution)/shard_map/pallas_call | solution.py:446
  5.6 0.1 collective-permute-start
  5.7 1.6 %collective-permute-start.1 = (f32[5,80,128]{2,1,0:T(8,128)S(1)}, f32[5,80,128]{2,1,0:T(8,128)S(1)}, u32[]{:S(2)}, u32[]{:S(2)}) collective-permute-start(f32[5,80,128]{2,1,0:T(8,128)S(1)} %get-tuple-element.30), channel_id=1, source_target_pairs={{0,8},{1,2},{2,1},{3,4},{4,3},{5,6},{6,5},{7,15},{8,0},{9,10},{10,... | collective-permute-start | bytes 614408 | tf_op jit(solution)/shard_map/ppermute | solution.py:471
  7.2 0.2 collective-permute-start.3
  7.5 1.5 %collective-permute-start.4 = (f32[5,208,128]{2,1,0:T(8,128)S(1)}, f32[5,208,128]{2,1,0:T(8,128)S(1)}, u32[]{:S(2)}, u32[]{:S(2)}) collective-permute-start(f32[5,208,128]{2,1,0:T(8,128)S(1)} %get-tuple-element.33), channel_id=1, source_target_pairs={{0,8},{1,2},{2,1},{3,4},{4,3},{5,6},{6,5},{7,15},{8,0},{9,10},{10,... | collective-permute-start | bytes 1597448 | tf_op jit(solution)/shard_map/ppermute | solution.py:471
  8.9 0.0 collective-permute-done.near
  8.9 2.6 %collective-permute-done.1.far = f32[5,80,128]{2,1,0:T(8,128)S(1)} collective-permute-done((f32[5,80,128]{2,1,0:T(8,128)S(1)}, f32[5,80,128]{2,1,0:T(8,128)S(1)}, u32[]{:S(2)}, u32[]{:S(2)}) %collective-permute-start.1) | collective-permute-done | bytes 204832 | tf_op jit(solution)/shard_map/ppermute | solution.py:471
  11.5 0.5 %shard_map.48 = (f32[12,64,128]{2,1,0:T(8,128)S(1)}, f32[12,32,128]{2,1,0:T(8,128)S(1)}, f32[12,16,128]{2,1,0:T(8,128)S(1)}) custom-call(f32[8,128]{1,0:T(8,128)S(1)} %get-tuple-element.26.table, f32[6,2,256,128]{3,2,1,0:T(8,128)S(1)} %get-tuple-element.27.seeds, s32[2,256,128]{2,1,0:T(8,128)S(1)} %get-tuple-element.28.material, ...), custom_call_target="tpu_custom_call" | custom-call | tf_op jit(solution)/shard_map/pallas_call | solution.py:446
  12.1 1.6 %collective-permute-start.7 = (f32[12,16,128]{2,1,0:T(8,128)S(1)}, f32[12,16,128]{2,1,0:T(8,128)S(1)}, u32[]{:S(2)}, u32[]{:S(2)}) collective-permute-start(f32[12,16,128]{2,1,0:T(8,128)S(1)} %get-tuple-element.41), channel_id=1, source_target_pairs={{0,8},{8,0},{16,24},{24,16},{1,9},{9,1},{17,25},{25,17},{2,10},{10... | collective-permute-start | bytes 294920 | tf_op jit(solution)/shard_map/ppermute | solution.py:475
  13.6 0.5 %collective-permute-start.2 = (f32[12,32,128]{2,1,0:T(8,128)S(1)}, f32[12,32,128]{2,1,0:T(8,128)S(1)}, u32[]{:S(2)}, u32[]{:S(2)}) collective-permute-start(f32[12,32,128]{2,1,0:T(8,128)S(1)} %get-tuple-element.31), channel_id=1, source_target_pairs={{0,16},{8,24},{16,0},{24,8},{1,17},{9,25},{17,1},{25,9},{2,18},{10... | collective-permute-start | bytes 589832 | tf_op jit(solution)/shard_map/ppermute | solution.py:475
  14.1 0.0 collective-permute-done.5.shared
  14.1 1.1 %shard_map.49 = (f32[5,56,128]{2,1,0:T(8,128)S(1)}, f32[5,56,128]{2,1,0:T(8,128)S(1)}, f32[8,128]{1,0:T(8,128)S(1)}) custom-call(f32[8,128]{1,0:T(8,128)S(1)} %get-tuple-element.26.table, f32[14,56,128]{2,1,0:T(8,128)S(1)} %collective-permute-done.5.shared), custom_call_target="tpu_custom_call" | custom-call | flops 10000000000 | tf_op jit(solution)/shard_map/pallas_call | solution.py:446
  15.2 0.1 collective-permute-start.10
  15.3 0.0 collective-permute-done.3.near
  15.3 1.8 %collective-permute-start.11 = (f32[5,56,128]{2,1,0:T(8,128)S(1)}, f32[5,56,128]{2,1,0:T(8,128)S(1)}, u32[]{:S(2)}, u32[]{:S(2)}) collective-permute-start(f32[5,56,128]{2,1,0:T(8,128)S(1)} %get-tuple-element.46), channel_id=1, source_target_pairs={{0,8},{1,2},{2,1},{3,4},{4,3},{5,6},{6,5},{7,15},{8,0},{9,10},{10,... | collective-permute-start | bytes 430088 | tf_op jit(solution)/shard_map/ppermute | solution.py:471
  17.1 1.2 %collective-permute-done.4.far = f32[5,208,128]{2,1,0:T(8,128)S(1)} collective-permute-done((f32[5,208,128]{2,1,0:T(8,128)S(1)}, f32[5,208,128]{2,1,0:T(8,128)S(1)}, u32[]{:S(2)}, u32[]{:S(2)}) %collective-permute-start.4) | collective-permute-done | bytes 532512 | tf_op jit(solution)/shard_map/ppermute | solution.py:471
  18.3 1.3 %shard_map.50 = (f32[12,192,128]{2,1,0:T(8,128)S(1)}, f32[12,48,128]{2,1,0:T(8,128)S(1)}, f32[12,16,128]{2,1,0:T(8,128)S(1)}) custom-call(f32[8,128]{1,0:T(8,128)S(1)} %get-tuple-element.26.table, f32[6,2,256,128]{3,2,1,0:T(8,128)S(1)} %get-tuple-element.27.seeds, s32[2,256,128]{2,1,0:T(8,128)S(1)} %get-tuple-element.28.material, ...), custom_call_target="tpu_custom_call" | custom-call | tf_op jit(solution)/shard_map/pallas_call | solution.py:446
  19.6 0.7 %collective-permute-start.6 = (f32[12,48,128]{2,1,0:T(8,128)S(1)}, f32[12,48,128]{2,1,0:T(8,128)S(1)}, u32[]{:S(2)}, u32[]{:S(2)}) collective-permute-start(f32[12,48,128]{2,1,0:T(8,128)S(1)} %get-tuple-element.39), channel_id=1, source_target_pairs={{0,16},{8,24},{16,0},{24,8},{1,17},{9,25},{17,1},{25,9},{2,18},{10... | collective-permute-start | bytes 884744 | tf_op jit(solution)/shard_map/ppermute | solution.py:475
  20.3 0.0 collective-permute-done.2.corner
  20.3 0.0 collective-permute-done.7._.beside
  20.3 0.3 shard_map.51
  20.6 1.4 %collective-permute-start.8 = (f32[12,32,128]{2,1,0:T(8,128)S(1)}, f32[12,32,128]{2,1,0:T(8,128)S(1)}, u32[]{:S(2)}, u32[]{:S(2)}) collective-permute-start(f32[12,32,128]{2,1,0:T(8,128)S(1)} %get-tuple-element.43), channel_id=1, source_target_pairs={{0,8},{8,0},{16,24},{24,16},{1,9},{9,1},{17,25},{25,17},{2,10},{10... | collective-permute-start | bytes 589832 | tf_op jit(solution)/shard_map/ppermute | solution.py:475
  22.0 1.5 %collective-permute-start.9 = (f32[12,16,128]{2,1,0:T(8,128)S(1)}, f32[12,16,128]{2,1,0:T(8,128)S(1)}, u32[]{:S(2)}, u32[]{:S(2)}) collective-permute-start(f32[12,16,128]{2,1,0:T(8,128)S(1)} %get-tuple-element.44), channel_id=1, source_target_pairs={{0,24},{8,16},{16,8},{24,0},{1,25},{9,17},{17,9},{25,1},{2,26},{10... | collective-permute-start | bytes 294920 | tf_op jit(solution)/shard_map/ppermute | solution.py:475
  23.4 0.0 collective-permute-done.10.near
  23.5 1.5 %shard_map.52.part = f32[12,104,128]{2,1,0:T(8,128)S(1)} custom-call(f32[8,128]{1,0:T(8,128)S(1)} %get-tuple-element.26.table, f32[14,56,128]{2,1,0:T(8,128)S(1)} %collective-permute-done.5.shared, f32[5,56,128]{2,1,0:T(8,128)S(1)} %collective-permute-done.10.near, f32[5,56,128]{2,1,0:T(8,128)S(1)} %collective-permute-done.11.far), custom_call_target="tpu_custom_call" | custom-call | flops 2000000000 | tf_op jit(solution)/shard_map/pallas_call | solution.py:446
  24.9 0.9 %shard_map.53._ = f32[1,6,2,256,128]{4,3,2,1,0:T(8,128)} custom-call(f32[12,192,128]{2,1,0:T(8,128)S(1)} %get-tuple-element.38.mid, f32[12,104,128]{2,1,0:T(8,128)S(1)} %shard_map.52.part), custom_call_target="tpu_custom_call" | custom-call | tf_op jit(solution)/shard_map/pallas_call | solution.py:556
  25.9 3.5 %collective-permute-done.9.strip = f32[12,16,128]{2,1,0:T(8,128)S(1)} collective-permute-done((f32[12,16,128]{2,1,0:T(8,128)S(1)}, f32[12,16,128]{2,1,0:T(8,128)S(1)}, u32[]{:S(2)}, u32[]{:S(2)}) %collective-permute-start.9) | collective-permute-done | bytes 98336 | tf_op jit(solution)/shard_map/ppermute | solution.py:475
  29.3 0.0 collective-permute-done.8.got
  29.3 0.4 %collective-permute-done.6.bands = f32[12,48,128]{2,1,0:T(8,128)S(1)} collective-permute-done((f32[12,48,128]{2,1,0:T(8,128)S(1)}, f32[12,48,128]{2,1,0:T(8,128)S(1)}, u32[]{:S(2)}, u32[]{:S(2)}) %collective-permute-start.6) | collective-permute-done | bytes 294944 | tf_op jit(solution)/shard_map/ppermute | solution.py:475
  29.7 1.2 %shard_map.54 = f32[1,6,2,256,128]{4,3,2,1,0:T(8,128)} custom-call(f32[12,192,128]{2,1,0:T(8,128)S(1)} %get-tuple-element.38.mid, f32[12,48,128]{2,1,0:T(8,128)S(1)} %collective-permute-done.6.bands, f32[12,64,128]{2,1,0:T(8,128)S(1)} %get-tuple-element.42.summed, f32[12,32,128]{2,1,0:T(8,128)S(1)} %collective-permute-done.8.got, ...), custom_call_target="tpu_custom_call", output_to_operand_aliasing={{}: (6, {})} | custom-call | tf_op jit(solution)/shard_map/pallas_call | solution.py:565
  (1 shorter events, 0.0 us)
Async XLA Ops:
  1.8 12.3 %collective-permute-start.5 = (f32[14,56,128]{2,1,0:T(8,128)S(1)}, f32[14,56,128]{2,1,0:T(8,128)S(1)}, u32[]{:S(2)}, u32[]{:S(2)}) collective-permute-start(f32[14,56,128]{2,1,0:T(8,128)S(1)} %get-tuple-element.35), channel_id=1, source_target_pairs={{0,16},{8,24},{16,0},{24,8},{1,17},{9,25},{17,1},{25,9},{2,18},{10... | collective-permute-start | bytes 1204232 | tf_op jit(solution)/shard_map/ppermute | solution.py:475
  5.6 3.3 %collective-permute-start = (f32[5,80,128]{2,1,0:T(8,128)S(1)}, f32[5,80,128]{2,1,0:T(8,128)S(1)}, u32[]{:S(2)}, u32[]{:S(2)}) collective-permute-start(f32[5,80,128]{2,1,0:T(8,128)S(1)} %get-tuple-element.29), channel_id=1, source_target_pairs={{0,1},{1,0},{2,3},{3,2},{4,5},{5,4},{6,7},{7,6},{8,9},{9,8},{10,11... | collective-permute-start | bytes 614408 | tf_op jit(solution)/shard_map/ppermute | solution.py:461
  5.7 5.8 %collective-permute-start.1 = (f32[5,80,128]{2,1,0:T(8,128)S(1)}, f32[5,80,128]{2,1,0:T(8,128)S(1)}, u32[]{:S(2)}, u32[]{:S(2)}) collective-permute-start(f32[5,80,128]{2,1,0:T(8,128)S(1)} %get-tuple-element.30), channel_id=1, source_target_pairs={{0,8},{1,2},{2,1},{3,4},{4,3},{5,6},{6,5},{7,15},{8,0},{9,10},{10,... | collective-permute-start | bytes 614408 | tf_op jit(solution)/shard_map/ppermute | solution.py:471
  7.2 8.0 %collective-permute-start.3 = (f32[5,208,128]{2,1,0:T(8,128)S(1)}, f32[5,208,128]{2,1,0:T(8,128)S(1)}, u32[]{:S(2)}, u32[]{:S(2)}) collective-permute-start(f32[5,208,128]{2,1,0:T(8,128)S(1)} %get-tuple-element.32), channel_id=1, source_target_pairs={{0,1},{1,0},{2,3},{3,2},{4,5},{5,4},{6,7},{7,6},{8,9},{9,8},{10,11... | collective-permute-start | bytes 1597448 | tf_op jit(solution)/shard_map/ppermute | solution.py:461
  7.5 10.8 %collective-permute-start.4 = (f32[5,208,128]{2,1,0:T(8,128)S(1)}, f32[5,208,128]{2,1,0:T(8,128)S(1)}, u32[]{:S(2)}, u32[]{:S(2)}) collective-permute-start(f32[5,208,128]{2,1,0:T(8,128)S(1)} %get-tuple-element.33), channel_id=1, source_target_pairs={{0,8},{1,2},{2,1},{3,4},{4,3},{5,6},{6,5},{7,15},{8,0},{9,10},{10,... | collective-permute-start | bytes 1597448 | tf_op jit(solution)/shard_map/ppermute | solution.py:471
  12.1 8.3 %collective-permute-start.7 = (f32[12,16,128]{2,1,0:T(8,128)S(1)}, f32[12,16,128]{2,1,0:T(8,128)S(1)}, u32[]{:S(2)}, u32[]{:S(2)}) collective-permute-start(f32[12,16,128]{2,1,0:T(8,128)S(1)} %get-tuple-element.41), channel_id=1, source_target_pairs={{0,8},{8,0},{16,24},{24,16},{1,9},{9,1},{17,25},{25,17},{2,10},{10... | collective-permute-start | bytes 294920 | tf_op jit(solution)/shard_map/ppermute | solution.py:475
  13.6 6.7 %collective-permute-start.2 = (f32[12,32,128]{2,1,0:T(8,128)S(1)}, f32[12,32,128]{2,1,0:T(8,128)S(1)}, u32[]{:S(2)}, u32[]{:S(2)}) collective-permute-start(f32[12,32,128]{2,1,0:T(8,128)S(1)} %get-tuple-element.31), channel_id=1, source_target_pairs={{0,16},{8,24},{16,0},{24,8},{1,17},{9,25},{17,1},{25,9},{2,18},{10... | collective-permute-start | bytes 589832 | tf_op jit(solution)/shard_map/ppermute | solution.py:475
  15.2 8.2 %collective-permute-start.10 = (f32[5,56,128]{2,1,0:T(8,128)S(1)}, f32[5,56,128]{2,1,0:T(8,128)S(1)}, u32[]{:S(2)}, u32[]{:S(2)}) collective-permute-start(f32[5,56,128]{2,1,0:T(8,128)S(1)} %get-tuple-element.45), channel_id=1, source_target_pairs={{0,1},{1,0},{2,3},{3,2},{4,5},{5,4},{6,7},{7,6},{8,9},{9,8},{10,11... | collective-permute-start | bytes 430088 | tf_op jit(solution)/shard_map/ppermute | solution.py:461
  15.3 8.2 %collective-permute-start.11 = (f32[5,56,128]{2,1,0:T(8,128)S(1)}, f32[5,56,128]{2,1,0:T(8,128)S(1)}, u32[]{:S(2)}, u32[]{:S(2)}) collective-permute-start(f32[5,56,128]{2,1,0:T(8,128)S(1)} %get-tuple-element.46), channel_id=1, source_target_pairs={{0,8},{1,2},{2,1},{3,4},{4,3},{5,6},{6,5},{7,15},{8,0},{9,10},{10,... | collective-permute-start | bytes 430088 | tf_op jit(solution)/shard_map/ppermute | solution.py:471
  19.6 10.2 %collective-permute-start.6 = (f32[12,48,128]{2,1,0:T(8,128)S(1)}, f32[12,48,128]{2,1,0:T(8,128)S(1)}, u32[]{:S(2)}, u32[]{:S(2)}) collective-permute-start(f32[12,48,128]{2,1,0:T(8,128)S(1)} %get-tuple-element.39), channel_id=1, source_target_pairs={{0,16},{8,24},{16,0},{24,8},{1,17},{9,25},{17,1},{25,9},{2,18},{10... | collective-permute-start | bytes 884744 | tf_op jit(solution)/shard_map/ppermute | solution.py:475
  20.6 8.7 %collective-permute-start.8 = (f32[12,32,128]{2,1,0:T(8,128)S(1)}, f32[12,32,128]{2,1,0:T(8,128)S(1)}, u32[]{:S(2)}, u32[]{:S(2)}) collective-permute-start(f32[12,32,128]{2,1,0:T(8,128)S(1)} %get-tuple-element.43), channel_id=1, source_target_pairs={{0,8},{8,0},{16,24},{24,16},{1,9},{9,1},{17,25},{25,17},{2,10},{10... | collective-permute-start | bytes 589832 | tf_op jit(solution)/shard_map/ppermute | solution.py:475
  22.0 7.3 %collective-permute-start.9 = (f32[12,16,128]{2,1,0:T(8,128)S(1)}, f32[12,16,128]{2,1,0:T(8,128)S(1)}, u32[]{:S(2)}, u32[]{:S(2)}) collective-permute-start(f32[12,16,128]{2,1,0:T(8,128)S(1)} %get-tuple-element.44), channel_id=1, source_target_pairs={{0,24},{8,16},{16,8},{24,0},{1,25},{9,17},{17,9},{25,1},{2,26},{10... | collective-permute-start | bytes 294920 | tf_op jit(solution)/shard_map/ppermute | solution.py:475

commit v15 on v12

--- a/solution.py
+++ b/solution.py
@@ -13,7 +13,7 @@
 PLANES = 5
 REACH = 2
 SHARED = 96
-LARGE, MEDIUM, SMALL = 10**10, 2 * 10**9, 0
+LARGE, MEDIUM, SMALL = 10**10, 15 * 10**8, 0
 
 magnetic_coeff = 0.5
 

time: 30.2 us -> 32.4 us (1.073)
  waiting for transfers between devices: 8.36 us -> 10.4 us
    ppermute x6, waiting for transfers between devices: 4.59 us -> 5.74 us  [swapped(): lax.ppermute(value, 'tile', [(t, t ^ bits) for t in range(tile_size)])]
    ppermute x3, starting transfers between devices: 3.89 us -> 4.96 us  [far_exchange(): return lax.ppermute(far, ('tile', 'sub'), pairs)]
    ppermute x6, starting transfers between devices: 8.18 us -> 7.19 us  [swapped(): lax.ppermute(value, 'tile', [(t, t ^ bits) for t in range(tile_size)])]
    ppermute x3, waiting for transfers between devices: 3.76 us -> 4.68 us  [far_exchange(): return lax.ppermute(far, ('tile', 'sub'), pairs)]
  transfers between devices with their start and end apart: 12 -> 12, of which waited for: 5 -> 5; matrix products, arithmetic and copies ran while one was open for 0% -> 0% of each run, Pallas kernels for 21% -> 19%
where the time goes in v15:
time: 32.4 us; the launch traced here: 32.2 us
  starting transfers between devices  12.5 us (39%)
  waiting for transfers between devices  10.4 us (32%)
  Pallas kernels  9.22 us (28%)
    ppermute x6, starting transfers between devices, swapped(): lax.ppermute(value, 'tile', [(t, t ^ bits) for t in range(tile_size)])  7.19 us
    ppermute x6, waiting for transfers between devices, swapped(): lax.ppermute(value, 'tile', [(t, t ^ bits) for t in range(tile_size)])  5.74 us
    pallas_call x6, Pallas kernels, called(): pl.pallas_call(kernel, out_shape=outs, in_specs=[VMEM] * len(operands), o...  5.34 us
    ppermute x3, starting transfers between devices, far_exchange(): return lax.ppermute(far, ('tile', 'sub'), pairs)  4.96 us
    ppermute x3, waiting for transfers between devices, far_exchange(): return lax.ppermute(far, ('tile', 'sub'), pairs)  4.68 us
    pallas_call x1, Pallas kernels, two_by_two(): pl.pallas_call(functools.partial(first_kernel, fetched, HALO // 2), out_s...  1.81 us
    pallas_call x1, Pallas kernels, two_by_two(): pl.pallas_call(functools.partial(last_kernel, 'tile'), out_shape=whole, i...  1.16 us
    pallas_call x1, Pallas kernels, two_by_two(): pl.pallas_call(early_kernel, out_shape=whole, in_specs=[VMEM] * 2, out_sp...  0.91 us
  transfers between devices with their start and end apart: 12, of which 5 were waited for; matrix products, arithmetic and copies ran while one was open for 0% of the time, Pallas kernels for 19%

profile of v15, /device:TPU:0, one launch (start us, length us, event | category | flops | bytes accessed | tf_op | source)
XLA Modules:
  0.0 32.2 jit_solution(303780316481413622)
XLA Ops:
  0.0 1.8 %shard_map.46 = (f32[14,56,128]{2,1,0:T(8,128)S(1)}, f32[6,2,256,128]{3,2,1,0:T(8,128)S(1)}, s32[2,256,128]{2,1,0:T(8,128)S(1)}, f32[8,128]{1,0:T(8,128)S(1)}) custom-call(f32[4]{0:T(128)} %decay.1, f32[4]{0:T(128)} %coupling.1, f32[1,6,2,256,128]{4,3,2,1,0:T(8,128)} %seeds.1, s32[1,2,256,128]{3,2,1,0:T(8,128)} %material.1), custom_call_target="tpu_custom_call" | custom-call | tf_op jit(solution)/shard_map/pallas_call | solution.py:500
  1.8 3.0 %collective-permute-start.6 = (f32[14,56,128]{2,1,0:T(8,128)S(1)}, f32[14,56,128]{2,1,0:T(8,128)S(1)}, u32[]{:S(2)}, u32[]{:S(2)}) collective-permute-start(f32[14,56,128]{2,1,0:T(8,128)S(1)} %get-tuple-element.39), channel_id=1, source_target_pairs={{0,16},{8,24},{16,0},{24,8},{1,17},{9,25},{17,1},{25,9},{2,18},{10... | collective-permute-start | bytes 1204232 | tf_op jit(solution)/shard_map/ppermute | solution.py:475
  4.9 0.8 %shard_map.47 = (f32[5,80,128]{2,1,0:T(8,128)S(1)}, f32[5,80,128]{2,1,0:T(8,128)S(1)}, f32[5,208,128]{2,1,0:T(8,128)S(1)}, f32[5,208,128]{2,1,0:T(8,128)S(1)}) custom-call(f32[8,128]{1,0:T(8,128)S(1)} %get-tuple-element.29.table, f32[6,2,256,128]{3,2,1,0:T(8,128)S(1)} %get-tuple-element.30.seeds, s32[2,256,128]{2,1,0:T(8,128)S(1)} %get-tuple-element.31.material), custom_call_target="tpu_custom_call" | custom-call | tf_op jit(solution)/shard_map/pallas_call | solution.py:446
  5.6 0.1 collective-permute-start
  5.7 1.6 %collective-permute-start.1 = (f32[5,80,128]{2,1,0:T(8,128)S(1)}, f32[5,80,128]{2,1,0:T(8,128)S(1)}, u32[]{:S(2)}, u32[]{:S(2)}) collective-permute-start(f32[5,80,128]{2,1,0:T(8,128)S(1)} %get-tuple-element.33), channel_id=1, source_target_pairs={{0,8},{1,2},{2,1},{3,4},{4,3},{5,6},{6,5},{7,15},{8,0},{9,10},{10,... | collective-permute-start | bytes 614408 | tf_op jit(solution)/shard_map/ppermute | solution.py:471
  7.2 0.2 collective-permute-start.4
  7.4 1.5 %collective-permute-start.5 = (f32[5,208,128]{2,1,0:T(8,128)S(1)}, f32[5,208,128]{2,1,0:T(8,128)S(1)}, u32[]{:S(2)}, u32[]{:S(2)}) collective-permute-start(f32[5,208,128]{2,1,0:T(8,128)S(1)} %get-tuple-element.37), channel_id=1, source_target_pairs={{0,8},{1,2},{2,1},{3,4},{4,3},{5,6},{6,5},{7,15},{8,0},{9,10},{10,... | collective-permute-start | bytes 1597448 | tf_op jit(solution)/shard_map/ppermute | solution.py:471
  8.9 0.0 collective-permute-done.near
  8.9 2.6 %collective-permute-done.1.far = f32[5,80,128]{2,1,0:T(8,128)S(1)} collective-permute-done((f32[5,80,128]{2,1,0:T(8,128)S(1)}, f32[5,80,128]{2,1,0:T(8,128)S(1)}, u32[]{:S(2)}, u32[]{:S(2)}) %collective-permute-start.1) | collective-permute-done | bytes 204832 | tf_op jit(solution)/shard_map/ppermute | solution.py:471
  11.5 0.5 %shard_map.48 = (f32[12,64,128]{2,1,0:T(8,128)S(1)}, f32[12,32,128]{2,1,0:T(8,128)S(1)}, f32[12,16,128]{2,1,0:T(8,128)S(1)}) custom-call(f32[8,128]{1,0:T(8,128)S(1)} %get-tuple-element.29.table, f32[6,2,256,128]{3,2,1,0:T(8,128)S(1)} %get-tuple-element.30.seeds, s32[2,256,128]{2,1,0:T(8,128)S(1)} %get-tuple-element.31.material, ...), custom_call_target="tpu_custom_call" | custom-call | tf_op jit(solution)/shard_map/pallas_call | solution.py:446
  12.1 1.5 %collective-permute-start.3 = (f32[12,16,128]{2,1,0:T(8,128)S(1)}, f32[12,16,128]{2,1,0:T(8,128)S(1)}, u32[]{:S(2)}, u32[]{:S(2)}) collective-permute-start(f32[12,16,128]{2,1,0:T(8,128)S(1)} %get-tuple-element.35), channel_id=1, source_target_pairs={{0,24},{8,16},{16,8},{24,0},{1,25},{9,17},{17,9},{25,1},{2,26},{10... | collective-permute-start | bytes 294920 | tf_op jit(solution)/shard_map/ppermute | solution.py:475
  13.6 1.5 %collective-permute-start.2 = (f32[12,32,128]{2,1,0:T(8,128)S(1)}, f32[12,32,128]{2,1,0:T(8,128)S(1)}, u32[]{:S(2)}, u32[]{:S(2)}) collective-permute-start(f32[12,32,128]{2,1,0:T(8,128)S(1)} %get-tuple-element.34), channel_id=1, source_target_pairs={{0,16},{8,24},{16,0},{24,8},{1,17},{9,25},{17,1},{25,9},{2,18},{10... | collective-permute-start | bytes 589832 | tf_op jit(solution)/shard_map/ppermute | solution.py:475
  15.1 0.0 collective-permute-done.6.shared
  15.1 1.1 %shard_map.49 = (f32[5,56,128]{2,1,0:T(8,128)S(1)}, f32[5,56,128]{2,1,0:T(8,128)S(1)}, f32[8,128]{1,0:T(8,128)S(1)}) custom-call(f32[8,128]{1,0:T(8,128)S(1)} %get-tuple-element.29.table, f32[14,56,128]{2,1,0:T(8,128)S(1)} %collective-permute-done.6.shared), custom_call_target="tpu_custom_call" | custom-call | flops 10000000000 | tf_op jit(solution)/shard_map/pallas_call | solution.py:446
  16.2 0.0 collective-permute-done.4.near
  16.2 2.1 %collective-permute-done.5.far = f32[5,208,128]{2,1,0:T(8,128)S(1)} collective-permute-done((f32[5,208,128]{2,1,0:T(8,128)S(1)}, f32[5,208,128]{2,1,0:T(8,128)S(1)}, u32[]{:S(2)}, u32[]{:S(2)}) %collective-permute-start.5) | collective-permute-done | bytes 532512 | tf_op jit(solution)/shard_map/ppermute | solution.py:471
  18.3 1.3 %shard_map.50 = (f32[12,192,128]{2,1,0:T(8,128)S(1)}, f32[12,48,128]{2,1,0:T(8,128)S(1)}, f32[12,16,128]{2,1,0:T(8,128)S(1)}) custom-call(f32[8,128]{1,0:T(8,128)S(1)} %get-tuple-element.29.table, f32[6,2,256,128]{3,2,1,0:T(8,128)S(1)} %get-tuple-element.30.seeds, s32[2,256,128]{2,1,0:T(8,128)S(1)} %get-tuple-element.31.material, ...), custom_call_target="tpu_custom_call" | custom-call | tf_op jit(solution)/shard_map/pallas_call | solution.py:446
  19.5 0.1 collective-permute-start.7
  19.6 0.1 collective-permute-start.10
  19.7 1.9 %collective-permute-start.11 = (f32[5,56,128]{2,1,0:T(8,128)S(1)}, f32[5,56,128]{2,1,0:T(8,128)S(1)}, u32[]{:S(2)}, u32[]{:S(2)}) collective-permute-start(f32[5,56,128]{2,1,0:T(8,128)S(1)} %get-tuple-element.52), channel_id=1, source_target_pairs={{0,8},{1,2},{2,1},{3,4},{4,3},{5,6},{6,5},{7,15},{8,0},{9,10},{10,... | collective-permute-start | bytes 430088 | tf_op jit(solution)/shard_map/ppermute | solution.py:471
  21.6 0.0 collective-permute-done.3.strip
  21.6 0.2 collective-permute-start.9
  21.8 1.0 %collective-permute-done.2.corner = f32[12,32,128]{2,1,0:T(8,128)S(1)} collective-permute-done((f32[12,32,128]{2,1,0:T(8,128)S(1)}, f32[12,32,128]{2,1,0:T(8,128)S(1)}, u32[]{:S(2)}, u32[]{:S(2)}) %collective-permute-start.2) | collective-permute-done | bytes 196640 | tf_op jit(solution)/shard_map/ppermute | solution.py:475
  22.8 0.3 shard_map.51
  23.1 0.9 %collective-permute-start.8 = (f32[12,32,128]{2,1,0:T(8,128)S(1)}, f32[12,32,128]{2,1,0:T(8,128)S(1)}, u32[]{:S(2)}, u32[]{:S(2)}) collective-permute-start(f32[12,32,128]{2,1,0:T(8,128)S(1)} %get-tuple-element.46), channel_id=1, source_target_pairs={{0,8},{8,0},{16,24},{24,16},{1,9},{9,1},{17,25},{25,17},{2,10},{10... | collective-permute-start | bytes 589832 | tf_op jit(solution)/shard_map/ppermute | solution.py:475
  24.0 0.0 collective-permute-done.10.near
  24.0 4.5 %collective-permute-done.9.beside = f32[12,16,128]{2,1,0:T(8,128)S(1)} collective-permute-done((f32[12,16,128]{2,1,0:T(8,128)S(1)}, f32[12,16,128]{2,1,0:T(8,128)S(1)}, u32[]{:S(2)}, u32[]{:S(2)}) %collective-permute-start.9) | collective-permute-done | bytes 98336 | tf_op jit(solution)/shard_map/ppermute | solution.py:475
  28.5 0.0 collective-permute-done.11.far
  28.5 1.5 %shard_map.52.part = f32[12,104,128]{2,1,0:T(8,128)S(1)} custom-call(f32[8,128]{1,0:T(8,128)S(1)} %get-tuple-element.29.table, f32[14,56,128]{2,1,0:T(8,128)S(1)} %collective-permute-done.6.shared, f32[5,56,128]{2,1,0:T(8,128)S(1)} %collective-permute-done.10.near, f32[5,56,128]{2,1,0:T(8,128)S(1)} %collective-permute-done.11.far), custom_call_target="tpu_custom_call" | custom-call | flops 1500000000 | tf_op jit(solution)/shard_map/pallas_call | solution.py:446
  30.0 0.9 %shard_map.53._ = f32[1,6,2,256,128]{4,3,2,1,0:T(8,128)} custom-call(f32[12,192,128]{2,1,0:T(8,128)S(1)} %get-tuple-element.42.mid, f32[12,104,128]{2,1,0:T(8,128)S(1)} %shard_map.52.part), custom_call_target="tpu_custom_call" | custom-call | tf_op jit(solution)/shard_map/pallas_call | solution.py:557
  30.9 0.2 collective-permute-done.8.got
  31.1 1.2 %shard_map.54 = f32[1,6,2,256,128]{4,3,2,1,0:T(8,128)} custom-call(f32[12,192,128]{2,1,0:T(8,128)S(1)} %get-tuple-element.42.mid, f32[12,48,128]{2,1,0:T(8,128)S(1)} %collective-permute-done.7.bands, f32[12,64,128]{2,1,0:T(8,128)S(1)} %get-tuple-element.45.summed, f32[12,32,128]{2,1,0:T(8,128)S(1)} %collective-permute-done.8.got, ...), custom_call_target="tpu_custom_call", output_to_operand_aliasing={{}: (6, {})} | custom-call | tf_op jit(solution)/shard_map/pallas_call | solution.py:566
  (1 shorter events, 0.0 us)
Async XLA Ops:
  1.8 13.3 %collective-permute-start.6 = (f32[14,56,128]{2,1,0:T(8,128)S(1)}, f32[14,56,128]{2,1,0:T(8,128)S(1)}, u32[]{:S(2)}, u32[]{:S(2)}) collective-permute-start(f32[14,56,128]{2,1,0:T(8,128)S(1)} %get-tuple-element.39), channel_id=1, source_target_pairs={{0,16},{8,24},{16,0},{24,8},{1,17},{9,25},{17,1},{25,9},{2,18},{10... | collective-permute-start | bytes 1204232 | tf_op jit(solution)/shard_map/ppermute | solution.py:475
  5.6 3.3 %collective-permute-start = (f32[5,80,128]{2,1,0:T(8,128)S(1)}, f32[5,80,128]{2,1,0:T(8,128)S(1)}, u32[]{:S(2)}, u32[]{:S(2)}) collective-permute-start(f32[5,80,128]{2,1,0:T(8,128)S(1)} %get-tuple-element.32), channel_id=1, source_target_pairs={{0,1},{1,0},{2,3},{3,2},{4,5},{5,4},{6,7},{7,6},{8,9},{9,8},{10,11... | collective-permute-start | bytes 614408 | tf_op jit(solution)/shard_map/ppermute | solution.py:461
  5.7 5.8 %collective-permute-start.1 = (f32[5,80,128]{2,1,0:T(8,128)S(1)}, f32[5,80,128]{2,1,0:T(8,128)S(1)}, u32[]{:S(2)}, u32[]{:S(2)}) collective-permute-start(f32[5,80,128]{2,1,0:T(8,128)S(1)} %get-tuple-element.33), channel_id=1, source_target_pairs={{0,8},{1,2},{2,1},{3,4},{4,3},{5,6},{6,5},{7,15},{8,0},{9,10},{10,... | collective-permute-start | bytes 614408 | tf_op jit(solution)/shard_map/ppermute | solution.py:471
  7.2 8.9 %collective-permute-start.4 = (f32[5,208,128]{2,1,0:T(8,128)S(1)}, f32[5,208,128]{2,1,0:T(8,128)S(1)}, u32[]{:S(2)}, u32[]{:S(2)}) collective-permute-start(f32[5,208,128]{2,1,0:T(8,128)S(1)} %get-tuple-element.36), channel_id=1, source_target_pairs={{0,1},{1,0},{2,3},{3,2},{4,5},{5,4},{6,7},{7,6},{8,9},{9,8},{10,11... | collective-permute-start | bytes 1597448 | tf_op jit(solution)/shard_map/ppermute | solution.py:461
  7.4 10.8 %collective-permute-start.5 = (f32[5,208,128]{2,1,0:T(8,128)S(1)}, f32[5,208,128]{2,1,0:T(8,128)S(1)}, u32[]{:S(2)}, u32[]{:S(2)}) collective-permute-start(f32[5,208,128]{2,1,0:T(8,128)S(1)} %get-tuple-element.37), channel_id=1, source_target_pairs={{0,8},{1,2},{2,1},{3,4},{4,3},{5,6},{6,5},{7,15},{8,0},{9,10},{10,... | collective-permute-start | bytes 1597448 | tf_op jit(solution)/shard_map/ppermute | solution.py:471
  12.1 9.5 %collective-permute-start.3 = (f32[12,16,128]{2,1,0:T(8,128)S(1)}, f32[12,16,128]{2,1,0:T(8,128)S(1)}, u32[]{:S(2)}, u32[]{:S(2)}) collective-permute-start(f32[12,16,128]{2,1,0:T(8,128)S(1)} %get-tuple-element.35), channel_id=1, source_target_pairs={{0,24},{8,16},{16,8},{24,0},{1,25},{9,17},{17,9},{25,1},{2,26},{10... | collective-permute-start | bytes 294920 | tf_op jit(solution)/shard_map/ppermute | solution.py:475
  13.6 9.3 %collective-permute-start.2 = (f32[12,32,128]{2,1,0:T(8,128)S(1)}, f32[12,32,128]{2,1,0:T(8,128)S(1)}, u32[]{:S(2)}, u32[]{:S(2)}) collective-permute-start(f32[12,32,128]{2,1,0:T(8,128)S(1)} %get-tuple-element.34), channel_id=1, source_target_pairs={{0,16},{8,24},{16,0},{24,8},{1,17},{9,25},{17,1},{25,9},{2,18},{10... | collective-permute-start | bytes 589832 | tf_op jit(solution)/shard_map/ppermute | solution.py:475
  19.5 11.5 %collective-permute-start.7 = (f32[12,48,128]{2,1,0:T(8,128)S(1)}, f32[12,48,128]{2,1,0:T(8,128)S(1)}, u32[]{:S(2)}, u32[]{:S(2)}) collective-permute-start(f32[12,48,128]{2,1,0:T(8,128)S(1)} %get-tuple-element.43), channel_id=1, source_target_pairs={{0,16},{8,24},{16,0},{24,8},{1,17},{9,25},{17,1},{25,9},{2,18},{10... | collective-permute-start | bytes 884744 | tf_op jit(solution)/shard_map/ppermute | solution.py:475
  19.6 4.3 %collective-permute-start.10 = (f32[5,56,128]{2,1,0:T(8,128)S(1)}, f32[5,56,128]{2,1,0:T(8,128)S(1)}, u32[]{:S(2)}, u32[]{:S(2)}) collective-permute-start(f32[5,56,128]{2,1,0:T(8,128)S(1)} %get-tuple-element.49), channel_id=1, source_target_pairs={{0,1},{1,0},{2,3},{3,2},{4,5},{5,4},{6,7},{7,6},{8,9},{9,8},{10,11... | collective-permute-start | bytes 430088 | tf_op jit(solution)/shard_map/ppermute | solution.py:461
  19.7 8.8 %collective-permute-start.11 = (f32[5,56,128]{2,1,0:T(8,128)S(1)}, f32[5,56,128]{2,1,0:T(8,128)S(1)}, u32[]{:S(2)}, u32[]{:S(2)}) collective-permute-start(f32[5,56,128]{2,1,0:T(8,128)S(1)} %get-tuple-element.52), channel_id=1, source_target_pairs={{0,8},{1,2},{2,1},{3,4},{4,3},{5,6},{6,5},{7,15},{8,0},{9,10},{10,... | collective-permute-start | bytes 430088 | tf_op jit(solution)/shard_map/ppermute | solution.py:471
  21.6 6.9 %collective-permute-start.9 = (f32[12,16,128]{2,1,0:T(8,128)S(1)}, f32[12,16,128]{2,1,0:T(8,128)S(1)}, u32[]{:S(2)}, u32[]{:S(2)}) collective-permute-start(f32[12,16,128]{2,1,0:T(8,128)S(1)} %get-tuple-element.48), channel_id=1, source_target_pairs={{0,8},{8,0},{16,24},{24,16},{1,9},{9,1},{17,25},{25,17},{2,10},{10... | collective-permute-start | bytes 294920 | tf_op jit(solution)/shard_map/ppermute | solution.py:475
  23.1 8.0 %collective-permute-start.8 = (f32[12,32,128]{2,1,0:T(8,128)S(1)}, f32[12,32,128]{2,1,0:T(8,128)S(1)}, u32[]{:S(2)}, u32[]{:S(2)}) collective-permute-start(f32[12,32,128]{2,1,0:T(8,128)S(1)} %get-tuple-element.46), channel_id=1, source_target_pairs={{0,8},{8,0},{16,24},{24,16},{1,9},{9,1},{17,25},{25,17},{2,10},{10... | collective-permute-start | bytes 589832 | tf_op jit(solution)/shard_map/ppermute | solution.py:475

commit v16 on v15

--- a/solution.py
+++ b/solution.py
@@ -12,8 +12,8 @@
 HALO = 8
 PLANES = 5
 REACH = 2
-SHARED = 96
-LARGE, MEDIUM, SMALL = 10**10, 15 * 10**8, 0
+SHARED = 80
+LARGE, MEDIUM, SMALL = 10**10, 25 * 10**8, 0
 
 magnetic_coeff = 0.5
 

time: 32.4 us -> 30.8 us (0.951)
  waiting for transfers between devices: 10.4 us -> 9.58 us
  Pallas kernels: 9.22 us -> 8.85 us
    ppermute x3, starting transfers between devices: 4.96 us -> 3.65 us  [far_exchange(): return lax.ppermute(far, ('tile', 'sub'), pairs)]
    ppermute x6, starting transfers between devices: 7.19 us -> 8.17 us  [swapped(): lax.ppermute(value, 'tile', [(t, t ^ bits) for t in range(tile_size)])]
    ppermute x3, waiting for transfers between devices: 4.68 us -> 4.09 us  [far_exchange(): return lax.ppermute(far, ('tile', 'sub'), pairs)]
  transfers between devices with their start and end apart: 12 -> 12, of which waited for: 5 -> 6; matrix products, arithmetic and copies ran while one was open for 0% -> 0% of each run, Pallas kernels for 19% -> 19%
where the time goes in v16:
time: 30.8 us; the launch traced here: 30.7 us
  starting transfers between devices  12.2 us (40%)
  waiting for transfers between devices  9.58 us (31%)
  Pallas kernels  8.85 us (29%)
    ppermute x6, starting transfers between devices, swapped(): lax.ppermute(value, 'tile', [(t, t ^ bits) for t in range(tile_size)])  8.17 us
    ppermute x6, waiting for transfers between devices, swapped(): lax.ppermute(value, 'tile', [(t, t ^ bits) for t in range(tile_size)])  5.48 us
    pallas_call x6, Pallas kernels, called(): pl.pallas_call(kernel, out_shape=outs, in_specs=[VMEM] * len(operands), o...  5.1 us
    ppermute x3, waiting for transfers between devices, far_exchange(): return lax.ppermute(far, ('tile', 'sub'), pairs)  4.09 us
    ppermute x3, starting transfers between devices, far_exchange(): return lax.ppermute(far, ('tile', 'sub'), pairs)  3.65 us
    pallas_call x1, Pallas kernels, two_by_two(): pl.pallas_call(functools.partial(first_kernel, fetched, HALO // 2), out_s...  1.71 us
    pallas_call x1, Pallas kernels, two_by_two(): pl.pallas_call(functools.partial(last_kernel, 'tile'), out_shape=whole, i...  1.19 us
    pallas_call x1, Pallas kernels, two_by_two(): pl.pallas_call(early_kernel, out_shape=whole, in_specs=[VMEM] * 2, out_sp...  0.86 us
  transfers between devices with their start and end apart: 12, of which 6 were waited for; matrix products, arithmetic and copies ran while one was open for 0% of the time, Pallas kernels for 19%

profile of v16, /device:TPU:0, one launch (start us, length us, event | category | flops | bytes accessed | tf_op | source)
XLA Modules:
  0.0 30.7 jit_solution(2002045250773282154)
XLA Ops:
  0.0 1.7 %shard_map.46 = (f32[14,48,128]{2,1,0:T(8,128)S(1)}, f32[6,2,256,128]{3,2,1,0:T(8,128)S(1)}, s32[2,256,128]{2,1,0:T(8,128)S(1)}, f32[8,128]{1,0:T(8,128)S(1)}) custom-call(f32[4]{0:T(128)} %decay.1, f32[4]{0:T(128)} %coupling.1, f32[1,6,2,256,128]{4,3,2,1,0:T(8,128)} %seeds.1, s32[1,2,256,128]{3,2,1,0:T(8,128)} %material.1), custom_call_target="tpu_custom_call" | custom-call | tf_op jit(solution)/shard_map/pallas_call | solution.py:500
  1.7 3.0 %collective-permute-start.6 = (f32[14,48,128]{2,1,0:T(8,128)S(1)}, f32[14,48,128]{2,1,0:T(8,128)S(1)}, u32[]{:S(2)}, u32[]{:S(2)}) collective-permute-start(f32[14,48,128]{2,1,0:T(8,128)S(1)} %get-tuple-element.39), channel_id=1, source_target_pairs={{0,16},{8,24},{16,0},{24,8},{1,17},{9,25},{17,1},{25,9},{2,18},{10... | collective-permute-start | bytes 1032200 | tf_op jit(solution)/shard_map/ppermute | solution.py:475
  4.7 0.8 %shard_map.47 = (f32[5,80,128]{2,1,0:T(8,128)S(1)}, f32[5,80,128]{2,1,0:T(8,128)S(1)}, f32[5,208,128]{2,1,0:T(8,128)S(1)}, f32[5,208,128]{2,1,0:T(8,128)S(1)}) custom-call(f32[8,128]{1,0:T(8,128)S(1)} %get-tuple-element.29.table, f32[6,2,256,128]{3,2,1,0:T(8,128)S(1)} %get-tuple-element.30.seeds, s32[2,256,128]{2,1,0:T(8,128)S(1)} %get-tuple-element.31.material), custom_call_target="tpu_custom_call" | custom-call | tf_op jit(solution)/shard_map/pallas_call | solution.py:446
  5.5 0.1 collective-permute-start
  5.6 1.6 %collective-permute-start.1 = (f32[5,80,128]{2,1,0:T(8,128)S(1)}, f32[5,80,128]{2,1,0:T(8,128)S(1)}, u32[]{:S(2)}, u32[]{:S(2)}) collective-permute-start(f32[5,80,128]{2,1,0:T(8,128)S(1)} %get-tuple-element.33), channel_id=1, source_target_pairs={{0,8},{1,2},{2,1},{3,4},{4,3},{5,6},{6,5},{7,15},{8,0},{9,10},{10,... | collective-permute-start | bytes 614408 | tf_op jit(solution)/shard_map/ppermute | solution.py:471
  7.1 0.2 collective-permute-start.4
  7.3 1.5 %collective-permute-start.5 = (f32[5,208,128]{2,1,0:T(8,128)S(1)}, f32[5,208,128]{2,1,0:T(8,128)S(1)}, u32[]{:S(2)}, u32[]{:S(2)}) collective-permute-start(f32[5,208,128]{2,1,0:T(8,128)S(1)} %get-tuple-element.37), channel_id=1, source_target_pairs={{0,8},{1,2},{2,1},{3,4},{4,3},{5,6},{6,5},{7,15},{8,0},{9,10},{10,... | collective-permute-start | bytes 1597448 | tf_op jit(solution)/shard_map/ppermute | solution.py:471
  8.8 2.6 %collective-permute-done.1.far = f32[5,80,128]{2,1,0:T(8,128)S(1)} collective-permute-done((f32[5,80,128]{2,1,0:T(8,128)S(1)}, f32[5,80,128]{2,1,0:T(8,128)S(1)}, u32[]{:S(2)}, u32[]{:S(2)}) %collective-permute-start.1) | collective-permute-done | bytes 204832 | tf_op jit(solution)/shard_map/ppermute | solution.py:471
  11.4 0.5 %shard_map.48 = (f32[12,64,128]{2,1,0:T(8,128)S(1)}, f32[12,32,128]{2,1,0:T(8,128)S(1)}, f32[12,16,128]{2,1,0:T(8,128)S(1)}) custom-call(f32[8,128]{1,0:T(8,128)S(1)} %get-tuple-element.29.table, f32[6,2,256,128]{3,2,1,0:T(8,128)S(1)} %get-tuple-element.30.seeds, s32[2,256,128]{2,1,0:T(8,128)S(1)} %get-tuple-element.31.material, ...), custom_call_target="tpu_custom_call" | custom-call | tf_op jit(solution)/shard_map/pallas_call | solution.py:446
  11.9 1.5 %collective-permute-start.3 = (f32[12,16,128]{2,1,0:T(8,128)S(1)}, f32[12,16,128]{2,1,0:T(8,128)S(1)}, u32[]{:S(2)}, u32[]{:S(2)}) collective-permute-start(f32[12,16,128]{2,1,0:T(8,128)S(1)} %get-tuple-element.35), channel_id=1, source_target_pairs={{0,24},{8,16},{16,8},{24,0},{1,25},{9,17},{17,9},{25,1},{2,26},{10... | collective-permute-start | bytes 294920 | tf_op jit(solution)/shard_map/ppermute | solution.py:475
  13.4 1.5 %collective-permute-start.2 = (f32[12,32,128]{2,1,0:T(8,128)S(1)}, f32[12,32,128]{2,1,0:T(8,128)S(1)}, u32[]{:S(2)}, u32[]{:S(2)}) collective-permute-start(f32[12,32,128]{2,1,0:T(8,128)S(1)} %get-tuple-element.34), channel_id=1, source_target_pairs={{0,16},{8,24},{16,0},{24,8},{1,17},{9,25},{17,1},{25,9},{2,18},{10... | collective-permute-start | bytes 589832 | tf_op jit(solution)/shard_map/ppermute | solution.py:475
  15.0 0.0 collective-permute-done.6.shared
  15.0 1.0 %shard_map.49 = (f32[5,48,128]{2,1,0:T(8,128)S(1)}, f32[5,48,128]{2,1,0:T(8,128)S(1)}, f32[8,128]{1,0:T(8,128)S(1)}) custom-call(f32[8,128]{1,0:T(8,128)S(1)} %get-tuple-element.29.table, f32[14,48,128]{2,1,0:T(8,128)S(1)} %collective-permute-done.6.shared), custom_call_target="tpu_custom_call" | custom-call | flops 10000000000 | tf_op jit(solution)/shard_map/pallas_call | solution.py:446
  16.0 0.1 collective-permute-start.10
  16.0 0.0 collective-permute-done.4.near
  16.1 0.6 %collective-permute-start.11 = (f32[5,48,128]{2,1,0:T(8,128)S(1)}, f32[5,48,128]{2,1,0:T(8,128)S(1)}, u32[]{:S(2)}, u32[]{:S(2)}) collective-permute-start(f32[5,48,128]{2,1,0:T(8,128)S(1)} %get-tuple-element.52), channel_id=1, source_target_pairs={{0,8},{1,2},{2,1},{3,4},{4,3},{5,6},{6,5},{7,15},{8,0},{9,10},{10,... | collective-permute-start | bytes 368648 | tf_op jit(solution)/shard_map/ppermute | solution.py:471
  16.7 1.5 %collective-permute-done.5.far = f32[5,208,128]{2,1,0:T(8,128)S(1)} collective-permute-done((f32[5,208,128]{2,1,0:T(8,128)S(1)}, f32[5,208,128]{2,1,0:T(8,128)S(1)}, u32[]{:S(2)}, u32[]{:S(2)}) %collective-permute-start.5) | collective-permute-done | bytes 532512 | tf_op jit(solution)/shard_map/ppermute | solution.py:471
  18.2 1.3 %shard_map.50 = (f32[12,192,128]{2,1,0:T(8,128)S(1)}, f32[12,56,128]{2,1,0:T(8,128)S(1)}, f32[12,16,128]{2,1,0:T(8,128)S(1)}) custom-call(f32[8,128]{1,0:T(8,128)S(1)} %get-tuple-element.29.table, f32[6,2,256,128]{3,2,1,0:T(8,128)S(1)} %get-tuple-element.30.seeds, s32[2,256,128]{2,1,0:T(8,128)S(1)} %get-tuple-element.31.material, ...), custom_call_target="tpu_custom_call" | custom-call | tf_op jit(solution)/shard_map/pallas_call | solution.py:446
  19.4 0.1 collective-permute-start.7
  19.5 0.0 collective-permute-done.3.strip
  19.5 2.0 %collective-permute-start.9 = (f32[12,16,128]{2,1,0:T(8,128)S(1)}, f32[12,16,128]{2,1,0:T(8,128)S(1)}, u32[]{:S(2)}, u32[]{:S(2)}) collective-permute-start(f32[12,16,128]{2,1,0:T(8,128)S(1)} %get-tuple-element.48), channel_id=1, source_target_pairs={{0,8},{8,0},{16,24},{24,16},{1,9},{9,1},{17,25},{25,17},{2,10},{10... | collective-permute-start | bytes 294920 | tf_op jit(solution)/shard_map/ppermute | solution.py:475
  21.5 1.2 %collective-permute-done.2.corner = f32[12,32,128]{2,1,0:T(8,128)S(1)} collective-permute-done((f32[12,32,128]{2,1,0:T(8,128)S(1)}, f32[12,32,128]{2,1,0:T(8,128)S(1)}, u32[]{:S(2)}, u32[]{:S(2)}) %collective-permute-start.2) | collective-permute-done | bytes 196640 | tf_op jit(solution)/shard_map/ppermute | solution.py:475
  22.7 0.3 shard_map.51
  22.9 0.1 collective-permute-start.8
  23.0 0.0 collective-permute-done.10.near
  23.0 1.6 %collective-permute-done.9.beside = f32[12,16,128]{2,1,0:T(8,128)S(1)} collective-permute-done((f32[12,16,128]{2,1,0:T(8,128)S(1)}, f32[12,16,128]{2,1,0:T(8,128)S(1)}, u32[]{:S(2)}, u32[]{:S(2)}) %collective-permute-start.9) | collective-permute-done | bytes 98336 | tf_op jit(solution)/shard_map/ppermute | solution.py:475
  24.7 0.0 collective-permute-done.11.far
  24.7 1.3 %shard_map.52.part = f32[12,88,128]{2,1,0:T(8,128)S(1)} custom-call(f32[8,128]{1,0:T(8,128)S(1)} %get-tuple-element.29.table, f32[14,48,128]{2,1,0:T(8,128)S(1)} %collective-permute-done.6.shared, f32[5,48,128]{2,1,0:T(8,128)S(1)} %collective-permute-done.10.near, f32[5,48,128]{2,1,0:T(8,128)S(1)} %collective-permute-done.11.far), custom_call_target="tpu_custom_call" | custom-call | flops 2500000000 | tf_op jit(solution)/shard_map/pallas_call | solution.py:446
  26.0 0.9 %shard_map.53._ = f32[1,6,2,256,128]{4,3,2,1,0:T(8,128)} custom-call(f32[12,192,128]{2,1,0:T(8,128)S(1)} %get-tuple-element.42.mid, f32[12,88,128]{2,1,0:T(8,128)S(1)} %shard_map.52.part), custom_call_target="tpu_custom_call" | custom-call | tf_op jit(solution)/shard_map/pallas_call | solution.py:557
  26.9 1.9 %collective-permute-done.8.got = f32[12,32,128]{2,1,0:T(8,128)S(1)} collective-permute-done((f32[12,32,128]{2,1,0:T(8,128)S(1)}, f32[12,32,128]{2,1,0:T(8,128)S(1)}, u32[]{:S(2)}, u32[]{:S(2)}) %collective-permute-start.8) | collective-permute-done | bytes 196640 | tf_op jit(solution)/shard_map/ppermute | solution.py:475
  28.8 0.7 %collective-permute-done.7.bands = f32[12,56,128]{2,1,0:T(8,128)S(1)} collective-permute-done((f32[12,56,128]{2,1,0:T(8,128)S(1)}, f32[12,56,128]{2,1,0:T(8,128)S(1)}, u32[]{:S(2)}, u32[]{:S(2)}) %collective-permute-start.7) | collective-permute-done | bytes 344096 | tf_op jit(solution)/shard_map/ppermute | solution.py:475
  29.5 1.2 %shard_map.54 = f32[1,6,2,256,128]{4,3,2,1,0:T(8,128)} custom-call(f32[12,192,128]{2,1,0:T(8,128)S(1)} %get-tuple-element.42.mid, f32[12,56,128]{2,1,0:T(8,128)S(1)} %collective-permute-done.7.bands, f32[12,64,128]{2,1,0:T(8,128)S(1)} %get-tuple-element.45.summed, f32[12,32,128]{2,1,0:T(8,128)S(1)} %collective-permute-done.8.got, ...), custom_call_target="tpu_custom_call", output_to_operand_aliasing={{}: (6, {})} | custom-call | tf_op jit(solution)/shard_map/pallas_call | solution.py:566
  (1 shorter events, 0.0 us)
Async XLA Ops:
  1.7 13.3 %collective-permute-start.6 = (f32[14,48,128]{2,1,0:T(8,128)S(1)}, f32[14,48,128]{2,1,0:T(8,128)S(1)}, u32[]{:S(2)}, u32[]{:S(2)}) collective-permute-start(f32[14,48,128]{2,1,0:T(8,128)S(1)} %get-tuple-element.39), channel_id=1, source_target_pairs={{0,16},{8,24},{16,0},{24,8},{1,17},{9,25},{17,1},{25,9},{2,18},{10... | collective-permute-start | bytes 1032200 | tf_op jit(solution)/shard_map/ppermute | solution.py:475
  5.5 3.3 %collective-permute-start = (f32[5,80,128]{2,1,0:T(8,128)S(1)}, f32[5,80,128]{2,1,0:T(8,128)S(1)}, u32[]{:S(2)}, u32[]{:S(2)}) collective-permute-start(f32[5,80,128]{2,1,0:T(8,128)S(1)} %get-tuple-element.32), channel_id=1, source_target_pairs={{0,1},{1,0},{2,3},{3,2},{4,5},{5,4},{6,7},{7,6},{8,9},{9,8},{10,11... | collective-permute-start | bytes 614408 | tf_op jit(solution)/shard_map/ppermute | solution.py:461
  5.6 5.8 %collective-permute-start.1 = (f32[5,80,128]{2,1,0:T(8,128)S(1)}, f32[5,80,128]{2,1,0:T(8,128)S(1)}, u32[]{:S(2)}, u32[]{:S(2)}) collective-permute-start(f32[5,80,128]{2,1,0:T(8,128)S(1)} %get-tuple-element.33), channel_id=1, source_target_pairs={{0,8},{1,2},{2,1},{3,4},{4,3},{5,6},{6,5},{7,15},{8,0},{9,10},{10,... | collective-permute-start | bytes 614408 | tf_op jit(solution)/shard_map/ppermute | solution.py:471
  7.1 8.9 %collective-permute-start.4 = (f32[5,208,128]{2,1,0:T(8,128)S(1)}, f32[5,208,128]{2,1,0:T(8,128)S(1)}, u32[]{:S(2)}, u32[]{:S(2)}) collective-permute-start(f32[5,208,128]{2,1,0:T(8,128)S(1)} %get-tuple-element.36), channel_id=1, source_target_pairs={{0,1},{1,0},{2,3},{3,2},{4,5},{5,4},{6,7},{7,6},{8,9},{9,8},{10,11... | collective-permute-start | bytes 1597448 | tf_op jit(solution)/shard_map/ppermute | solution.py:461
  7.3 10.8 %collective-permute-start.5 = (f32[5,208,128]{2,1,0:T(8,128)S(1)}, f32[5,208,128]{2,1,0:T(8,128)S(1)}, u32[]{:S(2)}, u32[]{:S(2)}) collective-permute-start(f32[5,208,128]{2,1,0:T(8,128)S(1)} %get-tuple-element.37), channel_id=1, source_target_pairs={{0,8},{1,2},{2,1},{3,4},{4,3},{5,6},{6,5},{7,15},{8,0},{9,10},{10,... | collective-permute-start | bytes 1597448 | tf_op jit(solution)/shard_map/ppermute | solution.py:471
  11.9 7.6 %collective-permute-start.3 = (f32[12,16,128]{2,1,0:T(8,128)S(1)}, f32[12,16,128]{2,1,0:T(8,128)S(1)}, u32[]{:S(2)}, u32[]{:S(2)}) collective-permute-start(f32[12,16,128]{2,1,0:T(8,128)S(1)} %get-tuple-element.35), channel_id=1, source_target_pairs={{0,24},{8,16},{16,8},{24,0},{1,25},{9,17},{17,9},{25,1},{2,26},{10... | collective-permute-start | bytes 294920 | tf_op jit(solution)/shard_map/ppermute | solution.py:475
  13.4 9.2 %collective-permute-start.2 = (f32[12,32,128]{2,1,0:T(8,128)S(1)}, f32[12,32,128]{2,1,0:T(8,128)S(1)}, u32[]{:S(2)}, u32[]{:S(2)}) collective-permute-start(f32[12,32,128]{2,1,0:T(8,128)S(1)} %get-tuple-element.34), channel_id=1, source_target_pairs={{0,16},{8,24},{16,0},{24,8},{1,17},{9,25},{17,1},{25,9},{2,18},{10... | collective-permute-start | bytes 589832 | tf_op jit(solution)/shard_map/ppermute | solution.py:475
  16.0 7.1 %collective-permute-start.10 = (f32[5,48,128]{2,1,0:T(8,128)S(1)}, f32[5,48,128]{2,1,0:T(8,128)S(1)}, u32[]{:S(2)}, u32[]{:S(2)}) collective-permute-start(f32[5,48,128]{2,1,0:T(8,128)S(1)} %get-tuple-element.49), channel_id=1, source_target_pairs={{0,1},{1,0},{2,3},{3,2},{4,5},{5,4},{6,7},{7,6},{8,9},{9,8},{10,11... | collective-permute-start | bytes 368648 | tf_op jit(solution)/shard_map/ppermute | solution.py:461
  16.1 8.6 %collective-permute-start.11 = (f32[5,48,128]{2,1,0:T(8,128)S(1)}, f32[5,48,128]{2,1,0:T(8,128)S(1)}, u32[]{:S(2)}, u32[]{:S(2)}) collective-permute-start(f32[5,48,128]{2,1,0:T(8,128)S(1)} %get-tuple-element.52), channel_id=1, source_target_pairs={{0,8},{1,2},{2,1},{3,4},{4,3},{5,6},{6,5},{7,15},{8,0},{9,10},{10,... | collective-permute-start | bytes 368648 | tf_op jit(solution)/shard_map/ppermute | solution.py:471
  19.4 10.1 %collective-permute-start.7 = (f32[12,56,128]{2,1,0:T(8,128)S(1)}, f32[12,56,128]{2,1,0:T(8,128)S(1)}, u32[]{:S(2)}, u32[]{:S(2)}) collective-permute-start(f32[12,56,128]{2,1,0:T(8,128)S(1)} %get-tuple-element.43), channel_id=1, source_target_pairs={{0,16},{8,24},{16,0},{24,8},{1,17},{9,25},{17,1},{25,9},{2,18},{10... | collective-permute-start | bytes 1032200 | tf_op jit(solution)/shard_map/ppermute | solution.py:475
  19.5 5.2 %collective-permute-start.9 = (f32[12,16,128]{2,1,0:T(8,128)S(1)}, f32[12,16,128]{2,1,0:T(8,128)S(1)}, u32[]{:S(2)}, u32[]{:S(2)}) collective-permute-start(f32[12,16,128]{2,1,0:T(8,128)S(1)} %get-tuple-element.48), channel_id=1, source_target_pairs={{0,8},{8,0},{16,24},{24,16},{1,9},{9,1},{17,25},{25,17},{2,10},{10... | collective-permute-start | bytes 294920 | tf_op jit(solution)/shard_map/ppermute | solution.py:475
  22.9 5.9 %collective-permute-start.8 = (f32[12,32,128]{2,1,0:T(8,128)S(1)}, f32[12,32,128]{2,1,0:T(8,128)S(1)}, u32[]{:S(2)}, u32[]{:S(2)}) collective-permute-start(f32[12,32,128]{2,1,0:T(8,128)S(1)} %get-tuple-element.46), channel_id=1, source_target_pairs={{0,8},{8,0},{16,24},{24,16},{1,9},{9,1},{17,25},{25,17},{2,10},{10... | collective-permute-start | bytes 589832 | tf_op jit(solution)/shard_map/ppermute | solution.py:475

commit v17 on v12

--- a/solution.py
+++ b/solution.py
@@ -409,25 +409,44 @@
     copy.wait()
 
 
-def last_kernel(tile, mid, bands, summed, got, strip, beside, _, out, low, high, sems):
+def late_kernel(tile, mid, bands, summed, strip, beside, low, high):
     odd = lax.rem(lax.axis_index(tile), 2) == 1
-    half, count = bands.shape[1], low.shape[2]
-    quarter = BAND // 2
+    half = bands.shape[1]
+    first, second = y_unpacked(bands[...])
+    low[:, BAND:] = mid[:, :half] + first
+    high[:, :half] = mid[:, -half:] + second
+    nothing = (jnp.zeros(strip.shape, jnp.float32),) * 2
+    by, away = strip_of(nothing, beside[...]), strip_of(nothing, strip[...])
+    low[:, :BAND] = summed[:, :BAND] + jnp.where(odd, by, away)
+    high[:, half:] = summed[:, BAND:] + jnp.where(odd, away, by)
+
+
+def last_kernel(tile, low, high, got, _, out, edges, sems):
+    odd = lax.rem(lax.axis_index(tile), 2) == 1
     depth, size_x = out.shape[2:4]
+    count = low.shape[1]
+    half, quarter = count - BAND, BAND // 2
     copies = []
+
+    def write(source, target):
+        copies.append(pltpu.make_async_copy(source, target, sems.at[len(copies)]))
+        copies[-1].start()
+
     for c in range(6):
-        at = slice(depth * c, depth * (c + 1))
-        first, second = y_unpacked(bands[at])
-        low[c, :, BAND:] = mid[at, :half] + first
-        high[c, :, :half] = mid[at, -half:] + second
-        straight = got[at, :quarter]
-        by = strip_of((straight, middle_out(straight)), beside[at])
-        away = strip_of(y_unpacked(got[at, quarter:]), strip[at])
-        low[c, :, :BAND] = summed[at, :BAND] + jnp.where(odd, by, away)
-        high[c, :, half:] = summed[at, BAND:] + jnp.where(odd, away, by)
-        for k, (rows, start) in enumerate(((low, 0), (high, size_x - count))):
-            copies.append(pltpu.make_async_copy(rows.at[c], out.at[0, c, :, pl.ds(start, count)], sems.at[2 * c + k]))
-            copies[-1].start()
+        at = pl.ds(depth * c, depth)
+        write(low.at[at, pl.ds(BAND, half)], out.at[0, c, :, pl.ds(BAND, half)])
+        write(high.at[at, pl.ds(0, half)], out.at[0, c, :, pl.ds(size_x - count, half)])
+    straight = got[:, :quarter]
+    middle = inner_lanes(straight.shape)
+    by = jnp.where(middle, 0.0, straight), jnp.where(middle, 0.0, middle_out(straight))
+    by = jnp.concatenate(by, axis=1)
+    away = jnp.concatenate(y_unpacked(got[:, quarter:]), axis=1)
+    edges[0] = low[:, :BAND] + jnp.where(odd, by, away)
+    edges[1] = high[:, half:] + jnp.where(odd, away, by)
+    for c in range(6):
+        at = pl.ds(depth * c, depth)
+        write(edges.at[0, at], out.at[0, c, :, pl.ds(0, BAND)])
+        write(edges.at[1, at], out.at[0, c, :, pl.ds(size_x - BAND, BAND)])
     for copy in copies:
         copy.wait()
 
@@ -563,17 +582,20 @@
         compiler_params=PARAMS,
         cost_estimate=cost(0),
     )(mid, part)
+    low, high = called(
+        functools.partial(late_kernel, "tile"), [(planes, (size_x - SHARED) // 2, size_y)] * 2,
+        mid, bands, summed, strip, beside,
+    )
     return pl.pallas_call(
         functools.partial(last_kernel, "tile"),
         out_shape=whole,
-        in_specs=[VMEM] * 6 + [HBM],
+        in_specs=[VMEM] * 3 + [HBM],
         out_specs=HBM,
-        scratch_shapes=[pltpu.VMEM((6, depth, (size_x - SHARED) // 2, size_y), jnp.float32)] * 2
-        + [pltpu.SemaphoreType.DMA((12,))],
-        input_output_aliases={6: 0},
+        scratch_shapes=[pltpu.VMEM((2, planes, BAND, size_y), jnp.float32), pltpu.SemaphoreType.DMA((24,))],
+        input_output_aliases={3: 0},
         compiler_params=PARAMS,
         cost_estimate=cost(0),
-    )(mid, bands, summed, got, strip, beside, early)
+    )(low, high, got, early)
 
 
 def any_lattice(seeds, material, decay, coupling, sub_size, tile_size):

time: 30.2 us -> 30.2 us (level)
    pallas_call x6 -> x7, Pallas kernels: 5.34 us -> 5.63 us  [called(): pl.pallas_call(kernel, out_shape=outs, in_specs=[VMEM] * len(operands), o...]
  transfers between devices with their start and end apart: 12 -> 12, of which waited for: 5 -> 6; matrix products, arithmetic and copies ran while one was open for 0% -> 0% of each run, Pallas kernels for 21% -> 22%
where the time goes in v17:
time: 30.2 us; the launch traced here: 30.1 us
  starting transfers between devices  12.4 us (41%)
  Pallas kernels  9.51 us (31%)
  waiting for transfers between devices  8.06 us (27%)
    ppermute x6, starting transfers between devices, swapped(): lax.ppermute(value, 'tile', [(t, t ^ bits) for t in range(tile_size)])  8.18 us
    pallas_call x7, Pallas kernels, called(): pl.pallas_call(kernel, out_shape=outs, in_specs=[VMEM] * len(operands), o...  5.63 us
    ppermute x6, waiting for transfers between devices, swapped(): lax.ppermute(value, 'tile', [(t, t ^ bits) for t in range(tile_size)])  4.29 us
    ppermute x3, starting transfers between devices, far_exchange(): return lax.ppermute(far, ('tile', 'sub'), pairs)  3.89 us
    ppermute x3, waiting for transfers between devices, far_exchange(): return lax.ppermute(far, ('tile', 'sub'), pairs)  3.76 us
    pallas_call x1, Pallas kernels, two_by_two(): pl.pallas_call(functools.partial(first_kernel, fetched, HALO // 2), out_s...  1.81 us
    pallas_call x1, Pallas kernels, two_by_two(): pl.pallas_call(functools.partial(last_kernel, 'tile'), out_shape=whole, i...  1.16 us
    pallas_call x1, Pallas kernels, two_by_two(): pl.pallas_call(early_kernel, out_shape=whole, in_specs=[VMEM] * 2, out_sp...  0.91 us
  transfers between devices with their start and end apart: 12, of which 6 were waited for; matrix products, arithmetic and copies ran while one was open for 0% of the time, Pallas kernels for 22%

profile of v17, /device:TPU:0, one launch (start us, length us, event | category | flops | bytes accessed | tf_op | source)
XLA Modules:
  0.0 30.1 jit_solution(12050472882892844147)
XLA Ops:
  0.0 1.8 %shard_map.46 = (f32[14,56,128]{2,1,0:T(8,128)S(1)}, f32[6,2,256,128]{3,2,1,0:T(8,128)S(1)}, s32[2,256,128]{2,1,0:T(8,128)S(1)}, f32[8,128]{1,0:T(8,128)S(1)}) custom-call(f32[4]{0:T(128)} %decay.1, f32[4]{0:T(128)} %coupling.1, f32[1,6,2,256,128]{4,3,2,1,0:T(8,128)} %seeds.1, s32[1,2,256,128]{3,2,1,0:T(8,128)} %material.1), custom_call_target="tpu_custom_call" | custom-call | tf_op jit(solution)/shard_map/pallas_call | solution.py:519
  1.8 3.0 %collective-permute-start.6 = (f32[14,56,128]{2,1,0:T(8,128)S(1)}, f32[14,56,128]{2,1,0:T(8,128)S(1)}, u32[]{:S(2)}, u32[]{:S(2)}) collective-permute-start(f32[14,56,128]{2,1,0:T(8,128)S(1)} %get-tuple-element.41), channel_id=1, source_target_pairs={{0,16},{8,24},{16,0},{24,8},{1,17},{9,25},{17,1},{25,9},{2,18},{10... | collective-permute-start | bytes 1204232 | tf_op jit(solution)/shard_map/ppermute | solution.py:494
  4.9 0.8 %shard_map.47 = (f32[5,80,128]{2,1,0:T(8,128)S(1)}, f32[5,80,128]{2,1,0:T(8,128)S(1)}, f32[5,208,128]{2,1,0:T(8,128)S(1)}, f32[5,208,128]{2,1,0:T(8,128)S(1)}) custom-call(f32[8,128]{1,0:T(8,128)S(1)} %get-tuple-element.31.table, f32[6,2,256,128]{3,2,1,0:T(8,128)S(1)} %get-tuple-element.32.seeds, s32[2,256,128]{2,1,0:T(8,128)S(1)} %get-tuple-element.33.material), custom_call_target="tpu_custom_call" | custom-call | tf_op jit(solution)/shard_map/pallas_call | solution.py:465
  5.6 0.1 collective-permute-start
  5.7 1.6 %collective-permute-start.1 = (f32[5,80,128]{2,1,0:T(8,128)S(1)}, f32[5,80,128]{2,1,0:T(8,128)S(1)}, u32[]{:S(2)}, u32[]{:S(2)}) collective-permute-start(f32[5,80,128]{2,1,0:T(8,128)S(1)} %get-tuple-element.35), channel_id=1, source_target_pairs={{0,8},{1,2},{2,1},{3,4},{4,3},{5,6},{6,5},{7,15},{8,0},{9,10},{10,... | collective-permute-start | bytes 614408 | tf_op jit(solution)/shard_map/ppermute | solution.py:490
  7.2 0.2 collective-permute-start.4
  7.4 1.5 %collective-permute-start.5 = (f32[5,208,128]{2,1,0:T(8,128)S(1)}, f32[5,208,128]{2,1,0:T(8,128)S(1)}, u32[]{:S(2)}, u32[]{:S(2)}) collective-permute-start(f32[5,208,128]{2,1,0:T(8,128)S(1)} %get-tuple-element.39), channel_id=1, source_target_pairs={{0,8},{1,2},{2,1},{3,4},{4,3},{5,6},{6,5},{7,15},{8,0},{9,10},{10,... | collective-permute-start | bytes 1597448 | tf_op jit(solution)/shard_map/ppermute | solution.py:490
  8.9 0.0 collective-permute-done.near
  8.9 2.6 %collective-permute-done.1.far = f32[5,80,128]{2,1,0:T(8,128)S(1)} collective-permute-done((f32[5,80,128]{2,1,0:T(8,128)S(1)}, f32[5,80,128]{2,1,0:T(8,128)S(1)}, u32[]{:S(2)}, u32[]{:S(2)}) %collective-permute-start.1) | collective-permute-done | bytes 204832 | tf_op jit(solution)/shard_map/ppermute | solution.py:490
  11.5 0.5 %shard_map.48 = (f32[12,64,128]{2,1,0:T(8,128)S(1)}, f32[12,32,128]{2,1,0:T(8,128)S(1)}, f32[12,16,128]{2,1,0:T(8,128)S(1)}) custom-call(f32[8,128]{1,0:T(8,128)S(1)} %get-tuple-element.31.table, f32[6,2,256,128]{3,2,1,0:T(8,128)S(1)} %get-tuple-element.32.seeds, s32[2,256,128]{2,1,0:T(8,128)S(1)} %get-tuple-element.33.material, ...), custom_call_target="tpu_custom_call" | custom-call | tf_op jit(solution)/shard_map/pallas_call | solution.py:465
  12.1 1.5 %collective-permute-start.3 = (f32[12,16,128]{2,1,0:T(8,128)S(1)}, f32[12,16,128]{2,1,0:T(8,128)S(1)}, u32[]{:S(2)}, u32[]{:S(2)}) collective-permute-start(f32[12,16,128]{2,1,0:T(8,128)S(1)} %get-tuple-element.37), channel_id=1, source_target_pairs={{0,24},{8,16},{16,8},{24,0},{1,25},{9,17},{17,9},{25,1},{2,26},{10... | collective-permute-start | bytes 294920 | tf_op jit(solution)/shard_map/ppermute | solution.py:494
  13.6 1.5 %collective-permute-start.2 = (f32[12,32,128]{2,1,0:T(8,128)S(1)}, f32[12,32,128]{2,1,0:T(8,128)S(1)}, u32[]{:S(2)}, u32[]{:S(2)}) collective-permute-start(f32[12,32,128]{2,1,0:T(8,128)S(1)} %get-tuple-element.36), channel_id=1, source_target_pairs={{0,16},{8,24},{16,0},{24,8},{1,17},{9,25},{17,1},{25,9},{2,18},{10... | collective-permute-start | bytes 589832 | tf_op jit(solution)/shard_map/ppermute | solution.py:494
  15.1 0.0 collective-permute-done.6.shared
  15.1 1.1 %shard_map.49 = (f32[5,56,128]{2,1,0:T(8,128)S(1)}, f32[5,56,128]{2,1,0:T(8,128)S(1)}, f32[8,128]{1,0:T(8,128)S(1)}) custom-call(f32[8,128]{1,0:T(8,128)S(1)} %get-tuple-element.31.table, f32[14,56,128]{2,1,0:T(8,128)S(1)} %collective-permute-done.6.shared), custom_call_target="tpu_custom_call" | custom-call | flops 10000000000 | tf_op jit(solution)/shard_map/pallas_call | solution.py:465
  16.2 0.1 collective-permute-start.9
  16.2 0.8 %collective-permute-start.11 = (f32[5,56,128]{2,1,0:T(8,128)S(1)}, f32[5,56,128]{2,1,0:T(8,128)S(1)}, u32[]{:S(2)}, u32[]{:S(2)}) collective-permute-start(f32[5,56,128]{2,1,0:T(8,128)S(1)} %get-tuple-element.56), channel_id=1, source_target_pairs={{0,8},{1,2},{2,1},{3,4},{4,3},{5,6},{6,5},{7,15},{8,0},{9,10},{10,... | collective-permute-start | bytes 430088 | tf_op jit(solution)/shard_map/ppermute | solution.py:490
  17.1 1.2 %collective-permute-done.5.far = f32[5,208,128]{2,1,0:T(8,128)S(1)} collective-permute-done((f32[5,208,128]{2,1,0:T(8,128)S(1)}, f32[5,208,128]{2,1,0:T(8,128)S(1)}, u32[]{:S(2)}, u32[]{:S(2)}) %collective-permute-start.5) | collective-permute-done | bytes 532512 | tf_op jit(solution)/shard_map/ppermute | solution.py:490
  18.3 1.3 %shard_map.50 = (f32[12,192,128]{2,1,0:T(8,128)S(1)}, f32[12,48,128]{2,1,0:T(8,128)S(1)}, f32[12,16,128]{2,1,0:T(8,128)S(1)}) custom-call(f32[8,128]{1,0:T(8,128)S(1)} %get-tuple-element.31.table, f32[6,2,256,128]{3,2,1,0:T(8,128)S(1)} %get-tuple-element.32.seeds, s32[2,256,128]{2,1,0:T(8,128)S(1)} %get-tuple-element.33.material, ...), custom_call_target="tpu_custom_call" | custom-call | tf_op jit(solution)/shard_map/pallas_call | solution.py:465
  19.5 0.4 %collective-permute-start.7 = (f32[12,48,128]{2,1,0:T(8,128)S(1)}, f32[12,48,128]{2,1,0:T(8,128)S(1)}, u32[]{:S(2)}, u32[]{:S(2)}) collective-permute-start(f32[12,48,128]{2,1,0:T(8,128)S(1)} %get-tuple-element.45), channel_id=1, source_target_pairs={{0,16},{8,24},{16,0},{24,8},{1,17},{9,25},{17,1},{25,9},{2,18},{10... | collective-permute-start | bytes 884744 | tf_op jit(solution)/shard_map/ppermute | solution.py:494
  19.9 0.0 collective-permute-done.3.strip
  19.9 1.7 %collective-permute-start.8 = (f32[12,16,128]{2,1,0:T(8,128)S(1)}, f32[12,16,128]{2,1,0:T(8,128)S(1)}, u32[]{:S(2)}, u32[]{:S(2)}) collective-permute-start(f32[12,16,128]{2,1,0:T(8,128)S(1)} %get-tuple-element.49), channel_id=1, source_target_pairs={{0,8},{8,0},{16,24},{24,16},{1,9},{9,1},{17,25},{25,17},{2,10},{10... | collective-permute-start | bytes 294920 | tf_op jit(solution)/shard_map/ppermute | solution.py:494
  21.6 1.2 %collective-permute-done.2.corner = f32[12,32,128]{2,1,0:T(8,128)S(1)} collective-permute-done((f32[12,32,128]{2,1,0:T(8,128)S(1)}, f32[12,32,128]{2,1,0:T(8,128)S(1)}, u32[]{:S(2)}, u32[]{:S(2)}) %collective-permute-start.2) | collective-permute-done | bytes 196640 | tf_op jit(solution)/shard_map/ppermute | solution.py:494
  22.8 0.3 shard_map.51
  23.1 0.1 collective-permute-start.10
  23.1 0.0 collective-permute-done.9.near
  23.2 1.6 %collective-permute-done.8.beside = f32[12,16,128]{2,1,0:T(8,128)S(1)} collective-permute-done((f32[12,16,128]{2,1,0:T(8,128)S(1)}, f32[12,16,128]{2,1,0:T(8,128)S(1)}, u32[]{:S(2)}, u32[]{:S(2)}) %collective-permute-start.8) | collective-permute-done | bytes 98336 | tf_op jit(solution)/shard_map/ppermute | solution.py:494
  24.8 1.5 %shard_map.53.part = f32[12,104,128]{2,1,0:T(8,128)S(1)} custom-call(f32[8,128]{1,0:T(8,128)S(1)} %get-tuple-element.31.table, f32[14,56,128]{2,1,0:T(8,128)S(1)} %collective-permute-done.6.shared, f32[5,56,128]{2,1,0:T(8,128)S(1)} %collective-permute-done.9.near, f32[5,56,128]{2,1,0:T(8,128)S(1)} %collective-permute-done.11.far), custom_call_target="tpu_custom_call" | custom-call | flops 2000000000 | tf_op jit(solution)/shard_map/pallas_call | solution.py:465
  26.3 0.9 %shard_map.54._ = f32[1,6,2,256,128]{4,3,2,1,0:T(8,128)} custom-call(f32[12,192,128]{2,1,0:T(8,128)S(1)} %get-tuple-element.44.mid, f32[12,104,128]{2,1,0:T(8,128)S(1)} %shard_map.53.part), custom_call_target="tpu_custom_call" | custom-call | tf_op jit(solution)/shard_map/pallas_call | solution.py:576
  27.2 1.4 %collective-permute-done.7.bands = f32[12,48,128]{2,1,0:T(8,128)S(1)} collective-permute-done((f32[12,48,128]{2,1,0:T(8,128)S(1)}, f32[12,48,128]{2,1,0:T(8,128)S(1)}, u32[]{:S(2)}, u32[]{:S(2)}) %collective-permute-start.7) | collective-permute-done | bytes 294944 | tf_op jit(solution)/shard_map/ppermute | solution.py:494
  28.6 0.3 shard_map.52
  28.9 0.1 collective-permute-done.10.got
  28.9 1.2 %shard_map.55 = f32[1,6,2,256,128]{4,3,2,1,0:T(8,128)} custom-call(f32[12,80,128]{2,1,0:T(8,128)S(1)} %get-tuple-element.52.low, f32[12,80,128]{2,1,0:T(8,128)S(1)} %get-tuple-element.53.high, f32[12,32,128]{2,1,0:T(8,128)S(1)} %collective-permute-done.10.got, f32[1,6,2,256,128]{4,3,2,1,0:T(8,128)} %shard_map.54._), custom_call_target="tpu_custom_call", output_to_operand_aliasing={{}: (3, {})} | custom-call | tf_op jit(solution)/shard_map/pallas_call | solution.py:589
  (2 shorter events, 0.0 us)
Async XLA Ops:
  1.8 13.3 %collective-permute-start.6 = (f32[14,56,128]{2,1,0:T(8,128)S(1)}, f32[14,56,128]{2,1,0:T(8,128)S(1)}, u32[]{:S(2)}, u32[]{:S(2)}) collective-permute-start(f32[14,56,128]{2,1,0:T(8,128)S(1)} %get-tuple-element.41), channel_id=1, source_target_pairs={{0,16},{8,24},{16,0},{24,8},{1,17},{9,25},{17,1},{25,9},{2,18},{10... | collective-permute-start | bytes 1204232 | tf_op jit(solution)/shard_map/ppermute | solution.py:494
  5.6 3.3 %collective-permute-start = (f32[5,80,128]{2,1,0:T(8,128)S(1)}, f32[5,80,128]{2,1,0:T(8,128)S(1)}, u32[]{:S(2)}, u32[]{:S(2)}) collective-permute-start(f32[5,80,128]{2,1,0:T(8,128)S(1)} %get-tuple-element.34), channel_id=1, source_target_pairs={{0,1},{1,0},{2,3},{3,2},{4,5},{5,4},{6,7},{7,6},{8,9},{9,8},{10,11... | collective-permute-start | bytes 614408 | tf_op jit(solution)/shard_map/ppermute | solution.py:480
  5.7 5.8 %collective-permute-start.1 = (f32[5,80,128]{2,1,0:T(8,128)S(1)}, f32[5,80,128]{2,1,0:T(8,128)S(1)}, u32[]{:S(2)}, u32[]{:S(2)}) collective-permute-start(f32[5,80,128]{2,1,0:T(8,128)S(1)} %get-tuple-element.35), channel_id=1, source_target_pairs={{0,8},{1,2},{2,1},{3,4},{4,3},{5,6},{6,5},{7,15},{8,0},{9,10},{10,... | collective-permute-start | bytes 614408 | tf_op jit(solution)/shard_map/ppermute | solution.py:490
  7.2 9.0 %collective-permute-start.4 = (f32[5,208,128]{2,1,0:T(8,128)S(1)}, f32[5,208,128]{2,1,0:T(8,128)S(1)}, u32[]{:S(2)}, u32[]{:S(2)}) collective-permute-start(f32[5,208,128]{2,1,0:T(8,128)S(1)} %get-tuple-element.38), channel_id=1, source_target_pairs={{0,1},{1,0},{2,3},{3,2},{4,5},{5,4},{6,7},{7,6},{8,9},{9,8},{10,11... | collective-permute-start | bytes 1597448 | tf_op jit(solution)/shard_map/ppermute | solution.py:480
  7.4 10.8 %collective-permute-start.5 = (f32[5,208,128]{2,1,0:T(8,128)S(1)}, f32[5,208,128]{2,1,0:T(8,128)S(1)}, u32[]{:S(2)}, u32[]{:S(2)}) collective-permute-start(f32[5,208,128]{2,1,0:T(8,128)S(1)} %get-tuple-element.39), channel_id=1, source_target_pairs={{0,8},{1,2},{2,1},{3,4},{4,3},{5,6},{6,5},{7,15},{8,0},{9,10},{10,... | collective-permute-start | bytes 1597448 | tf_op jit(solution)/shard_map/ppermute | solution.py:490
  12.1 7.9 %collective-permute-start.3 = (f32[12,16,128]{2,1,0:T(8,128)S(1)}, f32[12,16,128]{2,1,0:T(8,128)S(1)}, u32[]{:S(2)}, u32[]{:S(2)}) collective-permute-start(f32[12,16,128]{2,1,0:T(8,128)S(1)} %get-tuple-element.37), channel_id=1, source_target_pairs={{0,24},{8,16},{16,8},{24,0},{1,25},{9,17},{17,9},{25,1},{2,26},{10... | collective-permute-start | bytes 294920 | tf_op jit(solution)/shard_map/ppermute | solution.py:494
  13.6 9.3 %collective-permute-start.2 = (f32[12,32,128]{2,1,0:T(8,128)S(1)}, f32[12,32,128]{2,1,0:T(8,128)S(1)}, u32[]{:S(2)}, u32[]{:S(2)}) collective-permute-start(f32[12,32,128]{2,1,0:T(8,128)S(1)} %get-tuple-element.36), channel_id=1, source_target_pairs={{0,16},{8,24},{16,0},{24,8},{1,17},{9,25},{17,1},{25,9},{2,18},{10... | collective-permute-start | bytes 589832 | tf_op jit(solution)/shard_map/ppermute | solution.py:494
  16.2 7.0 %collective-permute-start.9 = (f32[5,56,128]{2,1,0:T(8,128)S(1)}, f32[5,56,128]{2,1,0:T(8,128)S(1)}, u32[]{:S(2)}, u32[]{:S(2)}) collective-permute-start(f32[5,56,128]{2,1,0:T(8,128)S(1)} %get-tuple-element.50), channel_id=1, source_target_pairs={{0,1},{1,0},{2,3},{3,2},{4,5},{5,4},{6,7},{7,6},{8,9},{9,8},{10,11... | collective-permute-start | bytes 430088 | tf_op jit(solution)/shard_map/ppermute | solution.py:480
  16.2 8.5 %collective-permute-start.11 = (f32[5,56,128]{2,1,0:T(8,128)S(1)}, f32[5,56,128]{2,1,0:T(8,128)S(1)}, u32[]{:S(2)}, u32[]{:S(2)}) collective-permute-start(f32[5,56,128]{2,1,0:T(8,128)S(1)} %get-tuple-element.56), channel_id=1, source_target_pairs={{0,8},{1,2},{2,1},{3,4},{4,3},{5,6},{6,5},{7,15},{8,0},{9,10},{10,... | collective-permute-start | bytes 430088 | tf_op jit(solution)/shard_map/ppermute | solution.py:490
  19.5 9.0 %collective-permute-start.7 = (f32[12,48,128]{2,1,0:T(8,128)S(1)}, f32[12,48,128]{2,1,0:T(8,128)S(1)}, u32[]{:S(2)}, u32[]{:S(2)}) collective-permute-start(f32[12,48,128]{2,1,0:T(8,128)S(1)} %get-tuple-element.45), channel_id=1, source_target_pairs={{0,16},{8,24},{16,0},{24,8},{1,17},{9,25},{17,1},{25,9},{2,18},{10... | collective-permute-start | bytes 884744 | tf_op jit(solution)/shard_map/ppermute | solution.py:494
  19.9 4.8 %collective-permute-start.8 = (f32[12,16,128]{2,1,0:T(8,128)S(1)}, f32[12,16,128]{2,1,0:T(8,128)S(1)}, u32[]{:S(2)}, u32[]{:S(2)}) collective-permute-start(f32[12,16,128]{2,1,0:T(8,128)S(1)} %get-tuple-element.49), channel_id=1, source_target_pairs={{0,8},{8,0},{16,24},{24,16},{1,9},{9,1},{17,25},{25,17},{2,10},{10... | collective-permute-start | bytes 294920 | tf_op jit(solution)/shard_map/ppermute | solution.py:494
  23.1 5.9 %collective-permute-start.10 = (f32[12,32,128]{2,1,0:T(8,128)S(1)}, f32[12,32,128]{2,1,0:T(8,128)S(1)}, u32[]{:S(2)}, u32[]{:S(2)}) collective-permute-start(f32[12,32,128]{2,1,0:T(8,128)S(1)} %get-tuple-element.54), channel_id=1, source_target_pairs={{0,8},{8,0},{16,24},{24,16},{1,9},{9,1},{17,25},{25,17},{2,10},{10... | collective-permute-start | bytes 589832 | tf_op jit(solution)/shard_map/ppermute | solution.py:494

commit v18 on v17

--- a/solution.py
+++ b/solution.py
@@ -413,40 +413,41 @@
     odd = lax.rem(lax.axis_index(tile), 2) == 1
     half = bands.shape[1]
     first, second = y_unpacked(bands[...])
-    low[:, BAND:] = mid[:, :half] + first
-    high[:, :half] = mid[:, -half:] + second
     nothing = (jnp.zeros(strip.shape, jnp.float32),) * 2
     by, away = strip_of(nothing, beside[...]), strip_of(nothing, strip[...])
-    low[:, :BAND] = summed[:, :BAND] + jnp.where(odd, by, away)
-    high[:, half:] = summed[:, BAND:] + jnp.where(odd, away, by)
+
+    def by_component(rows):
+        return rows.reshape(*low.shape[:2], *rows.shape[1:])
+
+    low[:, :, BAND:] = by_component(mid[:, :half] + first)
+    high[:, :, :half] = by_component(mid[:, -half:] + second)
+    low[:, :, :BAND] = by_component(summed[:, :BAND] + jnp.where(odd, by, away))
+    high[:, :, half:] = by_component(summed[:, BAND:] + jnp.where(odd, away, by))
 
 
 def last_kernel(tile, low, high, got, _, out, edges, sems):
     odd = lax.rem(lax.axis_index(tile), 2) == 1
-    depth, size_x = out.shape[2:4]
-    count = low.shape[1]
+    size_x, count = out.shape[3], low.shape[2]
     half, quarter = count - BAND, BAND // 2
     copies = []
 
-    def write(source, target):
+    def write(source, start, rows):
+        target = out.at[0, :, :, pl.ds(start, rows)]
         copies.append(pltpu.make_async_copy(source, target, sems.at[len(copies)]))
         copies[-1].start()
 
-    for c in range(6):
-        at = pl.ds(depth * c, depth)
-        write(low.at[at, pl.ds(BAND, half)], out.at[0, c, :, pl.ds(BAND, half)])
-        write(high.at[at, pl.ds(0, half)], out.at[0, c, :, pl.ds(size_x - count, half)])
+    write(low.at[:, :, pl.ds(BAND, half)], BAND, half)
+    write(high.at[:, :, pl.ds(0, half)], size_x - count, half)
     straight = got[:, :quarter]
     middle = inner_lanes(straight.shape)
     by = jnp.where(middle, 0.0, straight), jnp.where(middle, 0.0, middle_out(straight))
     by = jnp.concatenate(by, axis=1)
     away = jnp.concatenate(y_unpacked(got[:, quarter:]), axis=1)
-    edges[0] = low[:, :BAND] + jnp.where(odd, by, away)
-    edges[1] = high[:, half:] + jnp.where(odd, away, by)
-    for c in range(6):
-        at = pl.ds(depth * c, depth)
-        write(edges.at[0, at], out.at[0, c, :, pl.ds(0, BAND)])
-        write(edges.at[1, at], out.at[0, c, :, pl.ds(size_x - BAND, BAND)])
+    shape = edges.shape[1:]
+    edges[0] = low[:, :, :BAND] + jnp.where(odd, by, away).reshape(shape)
+    write(edges.at[0], 0, BAND)
+    edges[1] = high[:, :, half:] + jnp.where(odd, away, by).reshape(shape)
+    write(edges.at[1], size_x - BAND, BAND)
     for copy in copies:
         copy.wait()
 
@@ -583,7 +584,7 @@
         cost_estimate=cost(0),
     )(mid, part)
     low, high = called(
-        functools.partial(late_kernel, "tile"), [(planes, (size_x - SHARED) // 2, size_y)] * 2,
+        functools.partial(late_kernel, "tile"), [(6, depth, (size_x - SHARED) // 2, size_y)] * 2,
         mid, bands, summed, strip, beside,
     )
     return pl.pallas_call(
@@ -591,7 +592,7 @@
         out_shape=whole,
         in_specs=[VMEM] * 3 + [HBM],
         out_specs=HBM,
-        scratch_shapes=[pltpu.VMEM((2, planes, BAND, size_y), jnp.float32), pltpu.SemaphoreType.DMA((24,))],
+        scratch_shapes=[pltpu.VMEM((2, 6, depth, BAND, size_y), jnp.float32), pltpu.SemaphoreType.DMA((4,))],
         input_output_aliases={3: 0},
         compiler_params=PARAMS,
         cost_estimate=cost(0),

time: 30.2 us -> 30.1 us (level)
  no operation moved by 1% of the time
where the time goes in v18:
time: 30.1 us; the launch traced here: 29.9 us
  starting transfers between devices  12.4 us (41%)
  Pallas kernels  9.33 us (31%)
  waiting for transfers between devices  8.06 us (27%)
    ppermute x6, starting transfers between devices, swapped(): lax.ppermute(value, 'tile', [(t, t ^ bits) for t in range(tile_size)])  8.18 us
    pallas_call x7, Pallas kernels, called(): pl.pallas_call(kernel, out_shape=outs, in_specs=[VMEM] * len(operands), o...  5.63 us
    ppermute x6, waiting for transfers between devices, swapped(): lax.ppermute(value, 'tile', [(t, t ^ bits) for t in range(tile_size)])  4.29 us
    ppermute x3, starting transfers between devices, far_exchange(): return lax.ppermute(far, ('tile', 'sub'), pairs)  3.89 us
    ppermute x3, waiting for transfers between devices, far_exchange(): return lax.ppermute(far, ('tile', 'sub'), pairs)  3.76 us
    pallas_call x1, Pallas kernels, two_by_two(): pl.pallas_call(functools.partial(first_kernel, fetched, HALO // 2), out_s...  1.81 us
    pallas_call x1, Pallas kernels, two_by_two(): pl.pallas_call(functools.partial(last_kernel, 'tile'), out_shape=whole, i...  0.98 us
    pallas_call x1, Pallas kernels, two_by_two(): pl.pallas_call(early_kernel, out_shape=whole, in_specs=[VMEM] * 2, out_sp...  0.91 us
  transfers between devices with their start and end apart: 12, of which 6 were waited for; matrix products, arithmetic and copies ran while one was open for 0% of the time, Pallas kernels for 22%

profile of v18, /device:TPU:0, one launch (start us, length us, event | category | flops | bytes accessed | tf_op | source)
XLA Modules:
  0.0 29.9 jit_solution(10335790523034098137)
XLA Ops:
  0.0 1.8 %shard_map.46 = (f32[14,56,128]{2,1,0:T(8,128)S(1)}, f32[6,2,256,128]{3,2,1,0:T(8,128)S(1)}, s32[2,256,128]{2,1,0:T(8,128)S(1)}, f32[8,128]{1,0:T(8,128)S(1)}) custom-call(f32[4]{0:T(128)} %decay.1, f32[4]{0:T(128)} %coupling.1, f32[1,6,2,256,128]{4,3,2,1,0:T(8,128)} %seeds.1, s32[1,2,256,128]{3,2,1,0:T(8,128)} %material.1), custom_call_target="tpu_custom_call" | custom-call | tf_op jit(solution)/shard_map/pallas_call | solution.py:520
  1.8 3.0 %collective-permute-start.6 = (f32[14,56,128]{2,1,0:T(8,128)S(1)}, f32[14,56,128]{2,1,0:T(8,128)S(1)}, u32[]{:S(2)}, u32[]{:S(2)}) collective-permute-start(f32[14,56,128]{2,1,0:T(8,128)S(1)} %get-tuple-element.41), channel_id=1, source_target_pairs={{0,16},{8,24},{16,0},{24,8},{1,17},{9,25},{17,1},{25,9},{2,18},{10... | collective-permute-start | bytes 1204232 | tf_op jit(solution)/shard_map/ppermute | solution.py:495
  4.9 0.8 %shard_map.47 = (f32[5,80,128]{2,1,0:T(8,128)S(1)}, f32[5,80,128]{2,1,0:T(8,128)S(1)}, f32[5,208,128]{2,1,0:T(8,128)S(1)}, f32[5,208,128]{2,1,0:T(8,128)S(1)}) custom-call(f32[8,128]{1,0:T(8,128)S(1)} %get-tuple-element.31.table, f32[6,2,256,128]{3,2,1,0:T(8,128)S(1)} %get-tuple-element.32.seeds, s32[2,256,128]{2,1,0:T(8,128)S(1)} %get-tuple-element.33.material), custom_call_target="tpu_custom_call" | custom-call | tf_op jit(solution)/shard_map/pallas_call | solution.py:466
  5.6 0.1 collective-permute-start
  5.7 1.6 %collective-permute-start.1 = (f32[5,80,128]{2,1,0:T(8,128)S(1)}, f32[5,80,128]{2,1,0:T(8,128)S(1)}, u32[]{:S(2)}, u32[]{:S(2)}) collective-permute-start(f32[5,80,128]{2,1,0:T(8,128)S(1)} %get-tuple-element.35), channel_id=1, source_target_pairs={{0,8},{1,2},{2,1},{3,4},{4,3},{5,6},{6,5},{7,15},{8,0},{9,10},{10,... | collective-permute-start | bytes 614408 | tf_op jit(solution)/shard_map/ppermute | solution.py:491
  7.2 0.2 collective-permute-start.4
  7.4 1.5 %collective-permute-start.5 = (f32[5,208,128]{2,1,0:T(8,128)S(1)}, f32[5,208,128]{2,1,0:T(8,128)S(1)}, u32[]{:S(2)}, u32[]{:S(2)}) collective-permute-start(f32[5,208,128]{2,1,0:T(8,128)S(1)} %get-tuple-element.39), channel_id=1, source_target_pairs={{0,8},{1,2},{2,1},{3,4},{4,3},{5,6},{6,5},{7,15},{8,0},{9,10},{10,... | collective-permute-start | bytes 1597448 | tf_op jit(solution)/shard_map/ppermute | solution.py:491
  8.9 0.0 collective-permute-done.near
  8.9 2.6 %collective-permute-done.1.far = f32[5,80,128]{2,1,0:T(8,128)S(1)} collective-permute-done((f32[5,80,128]{2,1,0:T(8,128)S(1)}, f32[5,80,128]{2,1,0:T(8,128)S(1)}, u32[]{:S(2)}, u32[]{:S(2)}) %collective-permute-start.1) | collective-permute-done | bytes 204832 | tf_op jit(solution)/shard_map/ppermute | solution.py:491
  11.5 0.5 %shard_map.48 = (f32[12,64,128]{2,1,0:T(8,128)S(1)}, f32[12,32,128]{2,1,0:T(8,128)S(1)}, f32[12,16,128]{2,1,0:T(8,128)S(1)}) custom-call(f32[8,128]{1,0:T(8,128)S(1)} %get-tuple-element.31.table, f32[6,2,256,128]{3,2,1,0:T(8,128)S(1)} %get-tuple-element.32.seeds, s32[2,256,128]{2,1,0:T(8,128)S(1)} %get-tuple-element.33.material, ...), custom_call_target="tpu_custom_call" | custom-call | tf_op jit(solution)/shard_map/pallas_call | solution.py:466
  12.1 1.5 %collective-permute-start.3 = (f32[12,16,128]{2,1,0:T(8,128)S(1)}, f32[12,16,128]{2,1,0:T(8,128)S(1)}, u32[]{:S(2)}, u32[]{:S(2)}) collective-permute-start(f32[12,16,128]{2,1,0:T(8,128)S(1)} %get-tuple-element.37), channel_id=1, source_target_pairs={{0,24},{8,16},{16,8},{24,0},{1,25},{9,17},{17,9},{25,1},{2,26},{10... | collective-permute-start | bytes 294920 | tf_op jit(solution)/shard_map/ppermute | solution.py:495
  13.6 1.5 %collective-permute-start.2 = (f32[12,32,128]{2,1,0:T(8,128)S(1)}, f32[12,32,128]{2,1,0:T(8,128)S(1)}, u32[]{:S(2)}, u32[]{:S(2)}) collective-permute-start(f32[12,32,128]{2,1,0:T(8,128)S(1)} %get-tuple-element.36), channel_id=1, source_target_pairs={{0,16},{8,24},{16,0},{24,8},{1,17},{9,25},{17,1},{25,9},{2,18},{10... | collective-permute-start | bytes 589832 | tf_op jit(solution)/shard_map/ppermute | solution.py:495
  15.1 0.0 collective-permute-done.6.shared
  15.1 1.1 %shard_map.49 = (f32[5,56,128]{2,1,0:T(8,128)S(1)}, f32[5,56,128]{2,1,0:T(8,128)S(1)}, f32[8,128]{1,0:T(8,128)S(1)}) custom-call(f32[8,128]{1,0:T(8,128)S(1)} %get-tuple-element.31.table, f32[14,56,128]{2,1,0:T(8,128)S(1)} %collective-permute-done.6.shared), custom_call_target="tpu_custom_call" | custom-call | flops 10000000000 | tf_op jit(solution)/shard_map/pallas_call | solution.py:466
  16.2 0.1 collective-permute-start.9
  16.2 0.8 %collective-permute-start.11 = (f32[5,56,128]{2,1,0:T(8,128)S(1)}, f32[5,56,128]{2,1,0:T(8,128)S(1)}, u32[]{:S(2)}, u32[]{:S(2)}) collective-permute-start(f32[5,56,128]{2,1,0:T(8,128)S(1)} %get-tuple-element.56), channel_id=1, source_target_pairs={{0,8},{1,2},{2,1},{3,4},{4,3},{5,6},{6,5},{7,15},{8,0},{9,10},{10,... | collective-permute-start | bytes 430088 | tf_op jit(solution)/shard_map/ppermute | solution.py:491
  17.1 1.2 %collective-permute-done.5.far = f32[5,208,128]{2,1,0:T(8,128)S(1)} collective-permute-done((f32[5,208,128]{2,1,0:T(8,128)S(1)}, f32[5,208,128]{2,1,0:T(8,128)S(1)}, u32[]{:S(2)}, u32[]{:S(2)}) %collective-permute-start.5) | collective-permute-done | bytes 532512 | tf_op jit(solution)/shard_map/ppermute | solution.py:491
  18.3 1.3 %shard_map.50 = (f32[12,192,128]{2,1,0:T(8,128)S(1)}, f32[12,48,128]{2,1,0:T(8,128)S(1)}, f32[12,16,128]{2,1,0:T(8,128)S(1)}) custom-call(f32[8,128]{1,0:T(8,128)S(1)} %get-tuple-element.31.table, f32[6,2,256,128]{3,2,1,0:T(8,128)S(1)} %get-tuple-element.32.seeds, s32[2,256,128]{2,1,0:T(8,128)S(1)} %get-tuple-element.33.material, ...), custom_call_target="tpu_custom_call" | custom-call | tf_op jit(solution)/shard_map/pallas_call | solution.py:466
  19.5 0.4 %collective-permute-start.7 = (f32[12,48,128]{2,1,0:T(8,128)S(1)}, f32[12,48,128]{2,1,0:T(8,128)S(1)}, u32[]{:S(2)}, u32[]{:S(2)}) collective-permute-start(f32[12,48,128]{2,1,0:T(8,128)S(1)} %get-tuple-element.45), channel_id=1, source_target_pairs={{0,16},{8,24},{16,0},{24,8},{1,17},{9,25},{17,1},{25,9},{2,18},{10... | collective-permute-start | bytes 884744 | tf_op jit(solution)/shard_map/ppermute | solution.py:495
  19.9 0.0 collective-permute-done.3.strip
  19.9 1.7 %collective-permute-start.8 = (f32[12,16,128]{2,1,0:T(8,128)S(1)}, f32[12,16,128]{2,1,0:T(8,128)S(1)}, u32[]{:S(2)}, u32[]{:S(2)}) collective-permute-start(f32[12,16,128]{2,1,0:T(8,128)S(1)} %get-tuple-element.49), channel_id=1, source_target_pairs={{0,8},{8,0},{16,24},{24,16},{1,9},{9,1},{17,25},{25,17},{2,10},{10... | collective-permute-start | bytes 294920 | tf_op jit(solution)/shard_map/ppermute | solution.py:495
  21.6 1.2 %collective-permute-done.2.corner = f32[12,32,128]{2,1,0:T(8,128)S(1)} collective-permute-done((f32[12,32,128]{2,1,0:T(8,128)S(1)}, f32[12,32,128]{2,1,0:T(8,128)S(1)}, u32[]{:S(2)}, u32[]{:S(2)}) %collective-permute-start.2) | collective-permute-done | bytes 196640 | tf_op jit(solution)/shard_map/ppermute | solution.py:495
  22.8 0.3 shard_map.51
  23.1 0.1 collective-permute-start.10
  23.1 0.0 collective-permute-done.9.near
  23.2 1.6 %collective-permute-done.8.beside = f32[12,16,128]{2,1,0:T(8,128)S(1)} collective-permute-done((f32[12,16,128]{2,1,0:T(8,128)S(1)}, f32[12,16,128]{2,1,0:T(8,128)S(1)}, u32[]{:S(2)}, u32[]{:S(2)}) %collective-permute-start.8) | collective-permute-done | bytes 98336 | tf_op jit(solution)/shard_map/ppermute | solution.py:495
  24.8 1.5 %shard_map.53.part = f32[12,104,128]{2,1,0:T(8,128)S(1)} custom-call(f32[8,128]{1,0:T(8,128)S(1)} %get-tuple-element.31.table, f32[14,56,128]{2,1,0:T(8,128)S(1)} %collective-permute-done.6.shared, f32[5,56,128]{2,1,0:T(8,128)S(1)} %collective-permute-done.9.near, f32[5,56,128]{2,1,0:T(8,128)S(1)} %collective-permute-done.11.far), custom_call_target="tpu_custom_call" | custom-call | flops 2000000000 | tf_op jit(solution)/shard_map/pallas_call | solution.py:466
  26.3 0.9 %shard_map.54._ = f32[1,6,2,256,128]{4,3,2,1,0:T(8,128)} custom-call(f32[12,192,128]{2,1,0:T(8,128)S(1)} %get-tuple-element.44.mid, f32[12,104,128]{2,1,0:T(8,128)S(1)} %shard_map.53.part), custom_call_target="tpu_custom_call" | custom-call | tf_op jit(solution)/shard_map/pallas_call | solution.py:577
  27.2 1.4 %collective-permute-done.7.bands = f32[12,48,128]{2,1,0:T(8,128)S(1)} collective-permute-done((f32[12,48,128]{2,1,0:T(8,128)S(1)}, f32[12,48,128]{2,1,0:T(8,128)S(1)}, u32[]{:S(2)}, u32[]{:S(2)}) %collective-permute-start.7) | collective-permute-done | bytes 294944 | tf_op jit(solution)/shard_map/ppermute | solution.py:495
  28.6 0.3 shard_map.52
  28.9 0.1 collective-permute-done.10.got
  28.9 1.0 %shard_map.55 = f32[1,6,2,256,128]{4,3,2,1,0:T(8,128)} custom-call(f32[6,2,80,128]{3,2,1,0:T(8,128)S(1)} %get-tuple-element.52.low, f32[6,2,80,128]{3,2,1,0:T(8,128)S(1)} %get-tuple-element.53.high, f32[12,32,128]{2,1,0:T(8,128)S(1)} %collective-permute-done.10.got, f32[1,6,2,256,128]{4,3,2,1,0:T(8,128)} %shard_map.54._), custom_call_target="tpu_custom_call", output_to_operand_aliasing={{}: (3, {})} | custom-call | tf_op jit(solution)/shard_map/pallas_call | solution.py:590
  (2 shorter events, 0.0 us)
Async XLA Ops:
  1.8 13.3 %collective-permute-start.6 = (f32[14,56,128]{2,1,0:T(8,128)S(1)}, f32[14,56,128]{2,1,0:T(8,128)S(1)}, u32[]{:S(2)}, u32[]{:S(2)}) collective-permute-start(f32[14,56,128]{2,1,0:T(8,128)S(1)} %get-tuple-element.41), channel_id=1, source_target_pairs={{0,16},{8,24},{16,0},{24,8},{1,17},{9,25},{17,1},{25,9},{2,18},{10... | collective-permute-start | bytes 1204232 | tf_op jit(solution)/shard_map/ppermute | solution.py:495
  5.6 3.3 %collective-permute-start = (f32[5,80,128]{2,1,0:T(8,128)S(1)}, f32[5,80,128]{2,1,0:T(8,128)S(1)}, u32[]{:S(2)}, u32[]{:S(2)}) collective-permute-start(f32[5,80,128]{2,1,0:T(8,128)S(1)} %get-tuple-element.34), channel_id=1, source_target_pairs={{0,1},{1,0},{2,3},{3,2},{4,5},{5,4},{6,7},{7,6},{8,9},{9,8},{10,11... | collective-permute-start | bytes 614408 | tf_op jit(solution)/shard_map/ppermute | solution.py:481
  5.7 5.8 %collective-permute-start.1 = (f32[5,80,128]{2,1,0:T(8,128)S(1)}, f32[5,80,128]{2,1,0:T(8,128)S(1)}, u32[]{:S(2)}, u32[]{:S(2)}) collective-permute-start(f32[5,80,128]{2,1,0:T(8,128)S(1)} %get-tuple-element.35), channel_id=1, source_target_pairs={{0,8},{1,2},{2,1},{3,4},{4,3},{5,6},{6,5},{7,15},{8,0},{9,10},{10,... | collective-permute-start | bytes 614408 | tf_op jit(solution)/shard_map/ppermute | solution.py:491
  7.2 9.0 %collective-permute-start.4 = (f32[5,208,128]{2,1,0:T(8,128)S(1)}, f32[5,208,128]{2,1,0:T(8,128)S(1)}, u32[]{:S(2)}, u32[]{:S(2)}) collective-permute-start(f32[5,208,128]{2,1,0:T(8,128)S(1)} %get-tuple-element.38), channel_id=1, source_target_pairs={{0,1},{1,0},{2,3},{3,2},{4,5},{5,4},{6,7},{7,6},{8,9},{9,8},{10,11... | collective-permute-start | bytes 1597448 | tf_op jit(solution)/shard_map/ppermute | solution.py:481
  7.4 10.8 %collective-permute-start.5 = (f32[5,208,128]{2,1,0:T(8,128)S(1)}, f32[5,208,128]{2,1,0:T(8,128)S(1)}, u32[]{:S(2)}, u32[]{:S(2)}) collective-permute-start(f32[5,208,128]{2,1,0:T(8,128)S(1)} %get-tuple-element.39), channel_id=1, source_target_pairs={{0,8},{1,2},{2,1},{3,4},{4,3},{5,6},{6,5},{7,15},{8,0},{9,10},{10,... | collective-permute-start | bytes 1597448 | tf_op jit(solution)/shard_map/ppermute | solution.py:491
  12.1 7.9 %collective-permute-start.3 = (f32[12,16,128]{2,1,0:T(8,128)S(1)}, f32[12,16,128]{2,1,0:T(8,128)S(1)}, u32[]{:S(2)}, u32[]{:S(2)}) collective-permute-start(f32[12,16,128]{2,1,0:T(8,128)S(1)} %get-tuple-element.37), channel_id=1, source_target_pairs={{0,24},{8,16},{16,8},{24,0},{1,25},{9,17},{17,9},{25,1},{2,26},{10... | collective-permute-start | bytes 294920 | tf_op jit(solution)/shard_map/ppermute | solution.py:495
  13.6 9.3 %collective-permute-start.2 = (f32[12,32,128]{2,1,0:T(8,128)S(1)}, f32[12,32,128]{2,1,0:T(8,128)S(1)}, u32[]{:S(2)}, u32[]{:S(2)}) collective-permute-start(f32[12,32,128]{2,1,0:T(8,128)S(1)} %get-tuple-element.36), channel_id=1, source_target_pairs={{0,16},{8,24},{16,0},{24,8},{1,17},{9,25},{17,1},{25,9},{2,18},{10... | collective-permute-start | bytes 589832 | tf_op jit(solution)/shard_map/ppermute | solution.py:495
  16.2 7.0 %collective-permute-start.9 = (f32[5,56,128]{2,1,0:T(8,128)S(1)}, f32[5,56,128]{2,1,0:T(8,128)S(1)}, u32[]{:S(2)}, u32[]{:S(2)}) collective-permute-start(f32[5,56,128]{2,1,0:T(8,128)S(1)} %get-tuple-element.50), channel_id=1, source_target_pairs={{0,1},{1,0},{2,3},{3,2},{4,5},{5,4},{6,7},{7,6},{8,9},{9,8},{10,11... | collective-permute-start | bytes 430088 | tf_op jit(solution)/shard_map/ppermute | solution.py:481
  16.2 8.5 %collective-permute-start.11 = (f32[5,56,128]{2,1,0:T(8,128)S(1)}, f32[5,56,128]{2,1,0:T(8,128)S(1)}, u32[]{:S(2)}, u32[]{:S(2)}) collective-permute-start(f32[5,56,128]{2,1,0:T(8,128)S(1)} %get-tuple-element.56), channel_id=1, source_target_pairs={{0,8},{1,2},{2,1},{3,4},{4,3},{5,6},{6,5},{7,15},{8,0},{9,10},{10,... | collective-permute-start | bytes 430088 | tf_op jit(solution)/shard_map/ppermute | solution.py:491
  19.5 9.0 %collective-permute-start.7 = (f32[12,48,128]{2,1,0:T(8,128)S(1)}, f32[12,48,128]{2,1,0:T(8,128)S(1)}, u32[]{:S(2)}, u32[]{:S(2)}) collective-permute-start(f32[12,48,128]{2,1,0:T(8,128)S(1)} %get-tuple-element.45), channel_id=1, source_target_pairs={{0,16},{8,24},{16,0},{24,8},{1,17},{9,25},{17,1},{25,9},{2,18},{10... | collective-permute-start | bytes 884744 | tf_op jit(solution)/shard_map/ppermute | solution.py:495
  19.9 4.8 %collective-permute-start.8 = (f32[12,16,128]{2,1,0:T(8,128)S(1)}, f32[12,16,128]{2,1,0:T(8,128)S(1)}, u32[]{:S(2)}, u32[]{:S(2)}) collective-permute-start(f32[12,16,128]{2,1,0:T(8,128)S(1)} %get-tuple-element.49), channel_id=1, source_target_pairs={{0,8},{8,0},{16,24},{24,16},{1,9},{9,1},{17,25},{25,17},{2,10},{10... | collective-permute-start | bytes 294920 | tf_op jit(solution)/shard_map/ppermute | solution.py:495
  23.1 5.9 %collective-permute-start.10 = (f32[12,32,128]{2,1,0:T(8,128)S(1)}, f32[12,32,128]{2,1,0:T(8,128)S(1)}, u32[]{:S(2)}, u32[]{:S(2)}) collective-permute-start(f32[12,32,128]{2,1,0:T(8,128)S(1)} %get-tuple-element.54), channel_id=1, source_target_pairs={{0,8},{8,0},{16,24},{24,16},{1,9},{9,1},{17,25},{25,17},{2,10},{10... | collective-permute-start | bytes 589832 | tf_op jit(solution)/shard_map/ppermute | solution.py:495

commit v19 on v18

--- a/solution.py
+++ b/solution.py
@@ -12,8 +12,8 @@
 HALO = 8
 PLANES = 5
 REACH = 2
-SHARED = 96
-LARGE, MEDIUM, SMALL = 10**10, 2 * 10**9, 0
+SHARED = 112
+LARGE, MEDIUM, SMALL = 10**10, 15 * 10**8, 0
 
 magnetic_coeff = 0.5
 

time: 30.1 us -> 33.7 us (1.12)
  starting transfers between devices: 12.4 us -> 16.4 us
  waiting for transfers between devices: 8.06 us -> 7.55 us
    ppermute x6, starting transfers between devices: 8.18 us -> 10.5 us  [swapped(): lax.ppermute(value, 'tile', [(t, t ^ bits) for t in range(tile_size)])]
    ppermute x3, starting transfers between devices: 3.89 us -> 5.61 us  [far_exchange(): return lax.ppermute(far, ('tile', 'sub'), pairs)]
    ppermute x3, waiting for transfers between devices: 3.76 us -> 2.58 us  [far_exchange(): return lax.ppermute(far, ('tile', 'sub'), pairs)]
    ppermute x6, waiting for transfers between devices: 4.29 us -> 4.97 us  [swapped(): lax.ppermute(value, 'tile', [(t, t ^ bits) for t in range(tile_size)])]
  transfers between devices with their start and end apart: 12 -> 12, of which waited for: 6 -> 4; matrix products, arithmetic and copies ran while one was open for 0% -> 0% of each run, Pallas kernels for 22% -> 20%
where the time goes in v19:
time: 33.7 us; the launch traced here: 33.6 us
  starting transfers between devices  16.4 us (49%)
  Pallas kernels  9.54 us (28%)
  waiting for transfers between devices  7.55 us (22%)
    ppermute x6, starting transfers between devices, swapped(): lax.ppermute(value, 'tile', [(t, t ^ bits) for t in range(tile_size)])  10.5 us
    pallas_call x7, Pallas kernels, called(): pl.pallas_call(kernel, out_shape=outs, in_specs=[VMEM] * len(operands), o...  5.83 us
    ppermute x3, starting transfers between devices, far_exchange(): return lax.ppermute(far, ('tile', 'sub'), pairs)  5.61 us
    ppermute x6, waiting for transfers between devices, swapped(): lax.ppermute(value, 'tile', [(t, t ^ bits) for t in range(tile_size)])  4.97 us
    ppermute x3, waiting for transfers between devices, far_exchange(): return lax.ppermute(far, ('tile', 'sub'), pairs)  2.58 us
    pallas_call x1, Pallas kernels, two_by_two(): pl.pallas_call(functools.partial(first_kernel, fetched, HALO // 2), out_s...  1.81 us
    pallas_call x1, Pallas kernels, two_by_two(): pl.pallas_call(early_kernel, out_shape=whole, in_specs=[VMEM] * 2, out_sp...  0.96 us
    pallas_call x1, Pallas kernels, two_by_two(): pl.pallas_call(functools.partial(last_kernel, 'tile'), out_shape=whole, i...  0.95 us
  transfers between devices with their start and end apart: 12, of which 4 were waited for; matrix products, arithmetic and copies ran while one was open for 0% of the time, Pallas kernels for 20%

profile of v19, /device:TPU:0, one launch (start us, length us, event | category | flops | bytes accessed | tf_op | source)
XLA Modules:
  0.0 33.6 jit_solution(7171376385548072733)
XLA Ops:
  0.0 1.8 %shard_map.46 = (f32[14,64,128]{2,1,0:T(8,128)S(1)}, f32[6,2,256,128]{3,2,1,0:T(8,128)S(1)}, s32[2,256,128]{2,1,0:T(8,128)S(1)}, f32[8,128]{1,0:T(8,128)S(1)}) custom-call(f32[4]{0:T(128)} %decay.1, f32[4]{0:T(128)} %coupling.1, f32[1,6,2,256,128]{4,3,2,1,0:T(8,128)} %seeds.1, s32[1,2,256,128]{3,2,1,0:T(8,128)} %material.1), custom_call_target="tpu_custom_call" | custom-call | tf_op jit(solution)/shard_map/pallas_call | solution.py:520
  1.8 3.0 %collective-permute-start.6 = (f32[14,64,128]{2,1,0:T(8,128)S(1)}, f32[14,64,128]{2,1,0:T(8,128)S(1)}, u32[]{:S(2)}, u32[]{:S(2)}) collective-permute-start(f32[14,64,128]{2,1,0:T(8,128)S(1)} %get-tuple-element.41), channel_id=1, source_target_pairs={{0,16},{8,24},{16,0},{24,8},{1,17},{9,25},{17,1},{25,9},{2,18},{10... | collective-permute-start | bytes 1376264 | tf_op jit(solution)/shard_map/ppermute | solution.py:495
  4.9 0.8 %shard_map.47 = (f32[5,80,128]{2,1,0:T(8,128)S(1)}, f32[5,80,128]{2,1,0:T(8,128)S(1)}, f32[5,208,128]{2,1,0:T(8,128)S(1)}, f32[5,208,128]{2,1,0:T(8,128)S(1)}) custom-call(f32[8,128]{1,0:T(8,128)S(1)} %get-tuple-element.31.table, f32[6,2,256,128]{3,2,1,0:T(8,128)S(1)} %get-tuple-element.32.seeds, s32[2,256,128]{2,1,0:T(8,128)S(1)} %get-tuple-element.33.material), custom_call_target="tpu_custom_call" | custom-call | tf_op jit(solution)/shard_map/pallas_call | solution.py:466
  5.6 0.1 collective-permute-start
  5.7 1.6 %collective-permute-start.1 = (f32[5,80,128]{2,1,0:T(8,128)S(1)}, f32[5,80,128]{2,1,0:T(8,128)S(1)}, u32[]{:S(2)}, u32[]{:S(2)}) collective-permute-start(f32[5,80,128]{2,1,0:T(8,128)S(1)} %get-tuple-element.35), channel_id=1, source_target_pairs={{0,8},{1,2},{2,1},{3,4},{4,3},{5,6},{6,5},{7,15},{8,0},{9,10},{10,... | collective-permute-start | bytes 614408 | tf_op jit(solution)/shard_map/ppermute | solution.py:491
  7.2 0.2 collective-permute-start.4
  7.5 1.5 %collective-permute-start.5 = (f32[5,208,128]{2,1,0:T(8,128)S(1)}, f32[5,208,128]{2,1,0:T(8,128)S(1)}, u32[]{:S(2)}, u32[]{:S(2)}) collective-permute-start(f32[5,208,128]{2,1,0:T(8,128)S(1)} %get-tuple-element.39), channel_id=1, source_target_pairs={{0,8},{1,2},{2,1},{3,4},{4,3},{5,6},{6,5},{7,15},{8,0},{9,10},{10,... | collective-permute-start | bytes 1597448 | tf_op jit(solution)/shard_map/ppermute | solution.py:491
  8.9 0.0 collective-permute-done.near
  8.9 2.6 %collective-permute-done.1.far = f32[5,80,128]{2,1,0:T(8,128)S(1)} collective-permute-done((f32[5,80,128]{2,1,0:T(8,128)S(1)}, f32[5,80,128]{2,1,0:T(8,128)S(1)}, u32[]{:S(2)}, u32[]{:S(2)}) %collective-permute-start.1) | collective-permute-done | bytes 204832 | tf_op jit(solution)/shard_map/ppermute | solution.py:491
  11.5 0.5 %shard_map.48 = (f32[12,64,128]{2,1,0:T(8,128)S(1)}, f32[12,32,128]{2,1,0:T(8,128)S(1)}, f32[12,16,128]{2,1,0:T(8,128)S(1)}) custom-call(f32[8,128]{1,0:T(8,128)S(1)} %get-tuple-element.31.table, f32[6,2,256,128]{3,2,1,0:T(8,128)S(1)} %get-tuple-element.32.seeds, s32[2,256,128]{2,1,0:T(8,128)S(1)} %get-tuple-element.33.material, ...), custom_call_target="tpu_custom_call" | custom-call | tf_op jit(solution)/shard_map/pallas_call | solution.py:466
  12.1 1.5 %collective-permute-start.3 = (f32[12,16,128]{2,1,0:T(8,128)S(1)}, f32[12,16,128]{2,1,0:T(8,128)S(1)}, u32[]{:S(2)}, u32[]{:S(2)}) collective-permute-start(f32[12,16,128]{2,1,0:T(8,128)S(1)} %get-tuple-element.37), channel_id=1, source_target_pairs={{0,24},{8,16},{16,8},{24,0},{1,25},{9,17},{17,9},{25,1},{2,26},{10... | collective-permute-start | bytes 294920 | tf_op jit(solution)/shard_map/ppermute | solution.py:495
  13.6 1.5 %collective-permute-start.2 = (f32[12,32,128]{2,1,0:T(8,128)S(1)}, f32[12,32,128]{2,1,0:T(8,128)S(1)}, u32[]{:S(2)}, u32[]{:S(2)}) collective-permute-start(f32[12,32,128]{2,1,0:T(8,128)S(1)} %get-tuple-element.36), channel_id=1, source_target_pairs={{0,16},{8,24},{16,0},{24,8},{1,17},{9,25},{17,1},{25,9},{2,18},{10... | collective-permute-start | bytes 589832 | tf_op jit(solution)/shard_map/ppermute | solution.py:495
  15.1 0.4 %collective-permute-done.6.shared = f32[14,64,128]{2,1,0:T(8,128)S(1)} collective-permute-done((f32[14,64,128]{2,1,0:T(8,128)S(1)}, f32[14,64,128]{2,1,0:T(8,128)S(1)}, u32[]{:S(2)}, u32[]{:S(2)}) %collective-permute-start.6) | collective-permute-done | bytes 458784 | tf_op jit(solution)/shard_map/ppermute | solution.py:495
  15.5 1.2 %shard_map.49 = (f32[5,64,128]{2,1,0:T(8,128)S(1)}, f32[5,64,128]{2,1,0:T(8,128)S(1)}, f32[8,128]{1,0:T(8,128)S(1)}) custom-call(f32[8,128]{1,0:T(8,128)S(1)} %get-tuple-element.31.table, f32[14,64,128]{2,1,0:T(8,128)S(1)} %collective-permute-done.6.shared), custom_call_target="tpu_custom_call" | custom-call | flops 10000000000 | tf_op jit(solution)/shard_map/pallas_call | solution.py:466
  16.7 0.1 collective-permute-start.9
  16.7 0.0 collective-permute-done.4.near
  16.7 2.6 %collective-permute-start.11 = (f32[5,64,128]{2,1,0:T(8,128)S(1)}, f32[5,64,128]{2,1,0:T(8,128)S(1)}, u32[]{:S(2)}, u32[]{:S(2)}) collective-permute-start(f32[5,64,128]{2,1,0:T(8,128)S(1)} %get-tuple-element.56), channel_id=1, source_target_pairs={{0,8},{1,2},{2,1},{3,4},{4,3},{5,6},{6,5},{7,15},{8,0},{9,10},{10,... | collective-permute-start | bytes 491528 | tf_op jit(solution)/shard_map/ppermute | solution.py:491
  19.3 0.0 collective-permute-done.5.far
  19.3 1.2 %shard_map.50 = (f32[12,192,128]{2,1,0:T(8,128)S(1)}, f32[12,40,128]{2,1,0:T(8,128)S(1)}, f32[12,16,128]{2,1,0:T(8,128)S(1)}) custom-call(f32[8,128]{1,0:T(8,128)S(1)} %get-tuple-element.31.table, f32[6,2,256,128]{3,2,1,0:T(8,128)S(1)} %get-tuple-element.32.seeds, s32[2,256,128]{2,1,0:T(8,128)S(1)} %get-tuple-element.33.material, ...), custom_call_target="tpu_custom_call" | custom-call | tf_op jit(solution)/shard_map/pallas_call | solution.py:466
  20.6 2.3 %collective-permute-start.7 = (f32[12,40,128]{2,1,0:T(8,128)S(1)}, f32[12,40,128]{2,1,0:T(8,128)S(1)}, u32[]{:S(2)}, u32[]{:S(2)}) collective-permute-start(f32[12,40,128]{2,1,0:T(8,128)S(1)} %get-tuple-element.45), channel_id=1, source_target_pairs={{0,16},{8,24},{16,0},{24,8},{1,17},{9,25},{17,1},{25,9},{2,18},{10... | collective-permute-start | bytes 737288 | tf_op jit(solution)/shard_map/ppermute | solution.py:495
  22.9 0.0 collective-permute-done.3.strip
  22.9 0.2 collective-permute-start.8
  23.0 0.0 collective-permute-done.2.corner
  23.0 0.3 shard_map.51
  23.3 1.9 %collective-permute-start.10 = (f32[12,32,128]{2,1,0:T(8,128)S(1)}, f32[12,32,128]{2,1,0:T(8,128)S(1)}, u32[]{:S(2)}, u32[]{:S(2)}) collective-permute-start(f32[12,32,128]{2,1,0:T(8,128)S(1)} %get-tuple-element.54), channel_id=1, source_target_pairs={{0,8},{8,0},{16,24},{24,16},{1,9},{9,1},{17,25},{25,17},{2,10},{10... | collective-permute-start | bytes 589832 | tf_op jit(solution)/shard_map/ppermute | solution.py:495
  25.2 3.2 %collective-permute-done.8.beside = f32[12,16,128]{2,1,0:T(8,128)S(1)} collective-permute-done((f32[12,16,128]{2,1,0:T(8,128)S(1)}, f32[12,16,128]{2,1,0:T(8,128)S(1)}, u32[]{:S(2)}, u32[]{:S(2)}) %collective-permute-start.8) | collective-permute-done | bytes 98336 | tf_op jit(solution)/shard_map/ppermute | solution.py:495
  28.4 1.6 %shard_map.53.part = f32[12,120,128]{2,1,0:T(8,128)S(1)} custom-call(f32[8,128]{1,0:T(8,128)S(1)} %get-tuple-element.31.table, f32[14,64,128]{2,1,0:T(8,128)S(1)} %collective-permute-done.6.shared, f32[5,64,128]{2,1,0:T(8,128)S(1)} %collective-permute-done.9.near, f32[5,64,128]{2,1,0:T(8,128)S(1)} %collective-permute-done.11.far), custom_call_target="tpu_custom_call" | custom-call | flops 1500000000 | tf_op jit(solution)/shard_map/pallas_call | solution.py:466
  30.1 1.0 %shard_map.54._ = f32[1,6,2,256,128]{4,3,2,1,0:T(8,128)} custom-call(f32[12,192,128]{2,1,0:T(8,128)S(1)} %get-tuple-element.44.mid, f32[12,120,128]{2,1,0:T(8,128)S(1)} %shard_map.53.part), custom_call_target="tpu_custom_call" | custom-call | tf_op jit(solution)/shard_map/pallas_call | solution.py:577
  31.1 0.0 collective-permute-done.7.bands
  31.1 0.3 shard_map.52
  31.3 1.3 %collective-permute-done.10.got = f32[12,32,128]{2,1,0:T(8,128)S(1)} collective-permute-done((f32[12,32,128]{2,1,0:T(8,128)S(1)}, f32[12,32,128]{2,1,0:T(8,128)S(1)}, u32[]{:S(2)}, u32[]{:S(2)}) %collective-permute-start.10) | collective-permute-done | bytes 196640 | tf_op jit(solution)/shard_map/ppermute | solution.py:495
  32.7 0.9 %shard_map.55 = f32[1,6,2,256,128]{4,3,2,1,0:T(8,128)} custom-call(f32[6,2,72,128]{3,2,1,0:T(8,128)S(1)} %get-tuple-element.52.low, f32[6,2,72,128]{3,2,1,0:T(8,128)S(1)} %get-tuple-element.53.high, f32[12,32,128]{2,1,0:T(8,128)S(1)} %collective-permute-done.10.got, f32[1,6,2,256,128]{4,3,2,1,0:T(8,128)} %shard_map.54._), custom_call_target="tpu_custom_call", output_to_operand_aliasing={{}: (3, {})} | custom-call | tf_op jit(solution)/shard_map/pallas_call | solution.py:590
  (2 shorter events, 0.0 us)
Async XLA Ops:
  1.8 13.7 %collective-permute-start.6 = (f32[14,64,128]{2,1,0:T(8,128)S(1)}, f32[14,64,128]{2,1,0:T(8,128)S(1)}, u32[]{:S(2)}, u32[]{:S(2)}) collective-permute-start(f32[14,64,128]{2,1,0:T(8,128)S(1)} %get-tuple-element.41), channel_id=1, source_target_pairs={{0,16},{8,24},{16,0},{24,8},{1,17},{9,25},{17,1},{25,9},{2,18},{10... | collective-permute-start | bytes 1376264 | tf_op jit(solution)/shard_map/ppermute | solution.py:495
  5.6 3.3 %collective-permute-start = (f32[5,80,128]{2,1,0:T(8,128)S(1)}, f32[5,80,128]{2,1,0:T(8,128)S(1)}, u32[]{:S(2)}, u32[]{:S(2)}) collective-permute-start(f32[5,80,128]{2,1,0:T(8,128)S(1)} %get-tuple-element.34), channel_id=1, source_target_pairs={{0,1},{1,0},{2,3},{3,2},{4,5},{5,4},{6,7},{7,6},{8,9},{9,8},{10,11... | collective-permute-start | bytes 614408 | tf_op jit(solution)/shard_map/ppermute | solution.py:481
  5.7 5.8 %collective-permute-start.1 = (f32[5,80,128]{2,1,0:T(8,128)S(1)}, f32[5,80,128]{2,1,0:T(8,128)S(1)}, u32[]{:S(2)}, u32[]{:S(2)}) collective-permute-start(f32[5,80,128]{2,1,0:T(8,128)S(1)} %get-tuple-element.35), channel_id=1, source_target_pairs={{0,8},{1,2},{2,1},{3,4},{4,3},{5,6},{6,5},{7,15},{8,0},{9,10},{10,... | collective-permute-start | bytes 614408 | tf_op jit(solution)/shard_map/ppermute | solution.py:491
  7.2 9.5 %collective-permute-start.4 = (f32[5,208,128]{2,1,0:T(8,128)S(1)}, f32[5,208,128]{2,1,0:T(8,128)S(1)}, u32[]{:S(2)}, u32[]{:S(2)}) collective-permute-start(f32[5,208,128]{2,1,0:T(8,128)S(1)} %get-tuple-element.38), channel_id=1, source_target_pairs={{0,1},{1,0},{2,3},{3,2},{4,5},{5,4},{6,7},{7,6},{8,9},{9,8},{10,11... | collective-permute-start | bytes 1597448 | tf_op jit(solution)/shard_map/ppermute | solution.py:481
  7.5 11.9 %collective-permute-start.5 = (f32[5,208,128]{2,1,0:T(8,128)S(1)}, f32[5,208,128]{2,1,0:T(8,128)S(1)}, u32[]{:S(2)}, u32[]{:S(2)}) collective-permute-start(f32[5,208,128]{2,1,0:T(8,128)S(1)} %get-tuple-element.39), channel_id=1, source_target_pairs={{0,8},{1,2},{2,1},{3,4},{4,3},{5,6},{6,5},{7,15},{8,0},{9,10},{10,... | collective-permute-start | bytes 1597448 | tf_op jit(solution)/shard_map/ppermute | solution.py:491
  12.1 10.8 %collective-permute-start.3 = (f32[12,16,128]{2,1,0:T(8,128)S(1)}, f32[12,16,128]{2,1,0:T(8,128)S(1)}, u32[]{:S(2)}, u32[]{:S(2)}) collective-permute-start(f32[12,16,128]{2,1,0:T(8,128)S(1)} %get-tuple-element.37), channel_id=1, source_target_pairs={{0,24},{8,16},{16,8},{24,0},{1,25},{9,17},{17,9},{25,1},{2,26},{10... | collective-permute-start | bytes 294920 | tf_op jit(solution)/shard_map/ppermute | solution.py:495
  13.6 9.5 %collective-permute-start.2 = (f32[12,32,128]{2,1,0:T(8,128)S(1)}, f32[12,32,128]{2,1,0:T(8,128)S(1)}, u32[]{:S(2)}, u32[]{:S(2)}) collective-permute-start(f32[12,32,128]{2,1,0:T(8,128)S(1)} %get-tuple-element.36), channel_id=1, source_target_pairs={{0,16},{8,24},{16,0},{24,8},{1,17},{9,25},{17,1},{25,9},{2,18},{10... | collective-permute-start | bytes 589832 | tf_op jit(solution)/shard_map/ppermute | solution.py:495
  16.7 8.6 %collective-permute-start.9 = (f32[5,64,128]{2,1,0:T(8,128)S(1)}, f32[5,64,128]{2,1,0:T(8,128)S(1)}, u32[]{:S(2)}, u32[]{:S(2)}) collective-permute-start(f32[5,64,128]{2,1,0:T(8,128)S(1)} %get-tuple-element.50), channel_id=1, source_target_pairs={{0,1},{1,0},{2,3},{3,2},{4,5},{5,4},{6,7},{7,6},{8,9},{9,8},{10,11... | collective-permute-start | bytes 491528 | tf_op jit(solution)/shard_map/ppermute | solution.py:481
  16.7 11.7 %collective-permute-start.11 = (f32[5,64,128]{2,1,0:T(8,128)S(1)}, f32[5,64,128]{2,1,0:T(8,128)S(1)}, u32[]{:S(2)}, u32[]{:S(2)}) collective-permute-start(f32[5,64,128]{2,1,0:T(8,128)S(1)} %get-tuple-element.56), channel_id=1, source_target_pairs={{0,8},{1,2},{2,1},{3,4},{4,3},{5,6},{6,5},{7,15},{8,0},{9,10},{10,... | collective-permute-start | bytes 491528 | tf_op jit(solution)/shard_map/ppermute | solution.py:491
  20.6 10.5 %collective-permute-start.7 = (f32[12,40,128]{2,1,0:T(8,128)S(1)}, f32[12,40,128]{2,1,0:T(8,128)S(1)}, u32[]{:S(2)}, u32[]{:S(2)}) collective-permute-start(f32[12,40,128]{2,1,0:T(8,128)S(1)} %get-tuple-element.45), channel_id=1, source_target_pairs={{0,16},{8,24},{16,0},{24,8},{1,17},{9,25},{17,1},{25,9},{2,18},{10... | collective-permute-start | bytes 737288 | tf_op jit(solution)/shard_map/ppermute | solution.py:495
  22.9 5.6 %collective-permute-start.8 = (f32[12,16,128]{2,1,0:T(8,128)S(1)}, f32[12,16,128]{2,1,0:T(8,128)S(1)}, u32[]{:S(2)}, u32[]{:S(2)}) collective-permute-start(f32[12,16,128]{2,1,0:T(8,128)S(1)} %get-tuple-element.49), channel_id=1, source_target_pairs={{0,8},{8,0},{16,24},{24,16},{1,9},{9,1},{17,25},{25,17},{2,10},{10... | collective-permute-start | bytes 294920 | tf_op jit(solution)/shard_map/ppermute | solution.py:495
  23.3 9.4 %collective-permute-start.10 = (f32[12,32,128]{2,1,0:T(8,128)S(1)}, f32[12,32,128]{2,1,0:T(8,128)S(1)}, u32[]{:S(2)}, u32[]{:S(2)}) collective-permute-start(f32[12,32,128]{2,1,0:T(8,128)S(1)} %get-tuple-element.54), channel_id=1, source_target_pairs={{0,8},{8,0},{16,24},{24,16},{1,9},{9,1},{17,25},{25,17},{2,10},{10... | collective-permute-start | bytes 589832 | tf_op jit(solution)/shard_map/ppermute | solution.py:495

commit v20 on v18

--- a/solution.py
+++ b/solution.py
@@ -13,7 +13,7 @@
 PLANES = 5
 REACH = 2
 SHARED = 96
-LARGE, MEDIUM, SMALL = 10**10, 2 * 10**9, 0
+LARGE, MEDIUM, SMALL = 10**10, 25 * 10**8, 0
 
 magnetic_coeff = 0.5
 

time: 30.1 us -> 30.3 us (level)
  starting transfers between devices: 12.4 us -> 12.9 us
    ppermute x6, starting transfers between devices: 8.18 us -> 8.69 us  [swapped(): lax.ppermute(value, 'tile', [(t, t ^ bits) for t in range(tile_size)])]
  transfers between devices with their start and end apart: 12 -> 12, of which waited for: 6 -> 5; matrix products, arithmetic and copies ran while one was open for 0% -> 0% of each run, Pallas kernels for 22% -> 22%
where the time goes in v20:
time: 30.3 us; the launch traced here: 30.1 us
  starting transfers between devices  12.9 us (43%)
  Pallas kernels  9.34 us (31%)
  waiting for transfers between devices  7.76 us (26%)
    ppermute x6, starting transfers between devices, swapped(): lax.ppermute(value, 'tile', [(t, t ^ bits) for t in range(tile_size)])  8.69 us
    pallas_call x7, Pallas kernels, called(): pl.pallas_call(kernel, out_shape=outs, in_specs=[VMEM] * len(operands), o...  5.63 us
    ppermute x6, waiting for transfers between devices, swapped(): lax.ppermute(value, 'tile', [(t, t ^ bits) for t in range(tile_size)])  3.99 us
    ppermute x3, starting transfers between devices, far_exchange(): return lax.ppermute(far, ('tile', 'sub'), pairs)  3.89 us
    ppermute x3, waiting for transfers between devices, far_exchange(): return lax.ppermute(far, ('tile', 'sub'), pairs)  3.76 us
    pallas_call x1, Pallas kernels, two_by_two(): pl.pallas_call(functools.partial(first_kernel, fetched, HALO // 2), out_s...  1.81 us
    pallas_call x1, Pallas kernels, two_by_two(): pl.pallas_call(functools.partial(last_kernel, 'tile'), out_shape=whole, i...  0.98 us
    pallas_call x1, Pallas kernels, two_by_two(): pl.pallas_call(early_kernel, out_shape=whole, in_specs=[VMEM] * 2, out_sp...  0.91 us
  transfers between devices with their start and end apart: 12, of which 5 were waited for; matrix products, arithmetic and copies ran while one was open for 0% of the time, Pallas kernels for 22%

profile of v20, /device:TPU:0, one launch (start us, length us, event | category | flops | bytes accessed | tf_op | source)
XLA Modules:
  0.0 30.1 jit_solution(4613023018536302584)
XLA Ops:
  0.0 1.8 %shard_map.46 = (f32[14,56,128]{2,1,0:T(8,128)S(1)}, f32[6,2,256,128]{3,2,1,0:T(8,128)S(1)}, s32[2,256,128]{2,1,0:T(8,128)S(1)}, f32[8,128]{1,0:T(8,128)S(1)}) custom-call(f32[4]{0:T(128)} %decay.1, f32[4]{0:T(128)} %coupling.1, f32[1,6,2,256,128]{4,3,2,1,0:T(8,128)} %seeds.1, s32[1,2,256,128]{3,2,1,0:T(8,128)} %material.1), custom_call_target="tpu_custom_call" | custom-call | tf_op jit(solution)/shard_map/pallas_call | solution.py:520
  1.8 3.0 %collective-permute-start.6 = (f32[14,56,128]{2,1,0:T(8,128)S(1)}, f32[14,56,128]{2,1,0:T(8,128)S(1)}, u32[]{:S(2)}, u32[]{:S(2)}) collective-permute-start(f32[14,56,128]{2,1,0:T(8,128)S(1)} %get-tuple-element.41), channel_id=1, source_target_pairs={{0,16},{8,24},{16,0},{24,8},{1,17},{9,25},{17,1},{25,9},{2,18},{10... | collective-permute-start | bytes 1204232 | tf_op jit(solution)/shard_map/ppermute | solution.py:495
  4.9 0.8 %shard_map.47 = (f32[5,80,128]{2,1,0:T(8,128)S(1)}, f32[5,80,128]{2,1,0:T(8,128)S(1)}, f32[5,208,128]{2,1,0:T(8,128)S(1)}, f32[5,208,128]{2,1,0:T(8,128)S(1)}) custom-call(f32[8,128]{1,0:T(8,128)S(1)} %get-tuple-element.31.table, f32[6,2,256,128]{3,2,1,0:T(8,128)S(1)} %get-tuple-element.32.seeds, s32[2,256,128]{2,1,0:T(8,128)S(1)} %get-tuple-element.33.material), custom_call_target="tpu_custom_call" | custom-call | tf_op jit(solution)/shard_map/pallas_call | solution.py:466
  5.6 0.1 collective-permute-start
  5.7 1.6 %collective-permute-start.1 = (f32[5,80,128]{2,1,0:T(8,128)S(1)}, f32[5,80,128]{2,1,0:T(8,128)S(1)}, u32[]{:S(2)}, u32[]{:S(2)}) collective-permute-start(f32[5,80,128]{2,1,0:T(8,128)S(1)} %get-tuple-element.35), channel_id=1, source_target_pairs={{0,8},{1,2},{2,1},{3,4},{4,3},{5,6},{6,5},{7,15},{8,0},{9,10},{10,... | collective-permute-start | bytes 614408 | tf_op jit(solution)/shard_map/ppermute | solution.py:491
  7.2 0.2 collective-permute-start.4
  7.4 1.5 %collective-permute-start.5 = (f32[5,208,128]{2,1,0:T(8,128)S(1)}, f32[5,208,128]{2,1,0:T(8,128)S(1)}, u32[]{:S(2)}, u32[]{:S(2)}) collective-permute-start(f32[5,208,128]{2,1,0:T(8,128)S(1)} %get-tuple-element.39), channel_id=1, source_target_pairs={{0,8},{1,2},{2,1},{3,4},{4,3},{5,6},{6,5},{7,15},{8,0},{9,10},{10,... | collective-permute-start | bytes 1597448 | tf_op jit(solution)/shard_map/ppermute | solution.py:491
  8.9 0.0 collective-permute-done.near
  8.9 2.6 %collective-permute-done.1.far = f32[5,80,128]{2,1,0:T(8,128)S(1)} collective-permute-done((f32[5,80,128]{2,1,0:T(8,128)S(1)}, f32[5,80,128]{2,1,0:T(8,128)S(1)}, u32[]{:S(2)}, u32[]{:S(2)}) %collective-permute-start.1) | collective-permute-done | bytes 204832 | tf_op jit(solution)/shard_map/ppermute | solution.py:491
  11.5 0.5 %shard_map.48 = (f32[12,64,128]{2,1,0:T(8,128)S(1)}, f32[12,32,128]{2,1,0:T(8,128)S(1)}, f32[12,16,128]{2,1,0:T(8,128)S(1)}) custom-call(f32[8,128]{1,0:T(8,128)S(1)} %get-tuple-element.31.table, f32[6,2,256,128]{3,2,1,0:T(8,128)S(1)} %get-tuple-element.32.seeds, s32[2,256,128]{2,1,0:T(8,128)S(1)} %get-tuple-element.33.material, ...), custom_call_target="tpu_custom_call" | custom-call | tf_op jit(solution)/shard_map/pallas_call | solution.py:466
  12.1 1.5 %collective-permute-start.3 = (f32[12,16,128]{2,1,0:T(8,128)S(1)}, f32[12,16,128]{2,1,0:T(8,128)S(1)}, u32[]{:S(2)}, u32[]{:S(2)}) collective-permute-start(f32[12,16,128]{2,1,0:T(8,128)S(1)} %get-tuple-element.37), channel_id=1, source_target_pairs={{0,24},{8,16},{16,8},{24,0},{1,25},{9,17},{17,9},{25,1},{2,26},{10... | collective-permute-start | bytes 294920 | tf_op jit(solution)/shard_map/ppermute | solution.py:495
  13.6 1.5 %collective-permute-start.2 = (f32[12,32,128]{2,1,0:T(8,128)S(1)}, f32[12,32,128]{2,1,0:T(8,128)S(1)}, u32[]{:S(2)}, u32[]{:S(2)}) collective-permute-start(f32[12,32,128]{2,1,0:T(8,128)S(1)} %get-tuple-element.36), channel_id=1, source_target_pairs={{0,16},{8,24},{16,0},{24,8},{1,17},{9,25},{17,1},{25,9},{2,18},{10... | collective-permute-start | bytes 589832 | tf_op jit(solution)/shard_map/ppermute | solution.py:495
  15.1 0.0 collective-permute-done.6.shared
  15.1 1.1 %shard_map.49 = (f32[5,56,128]{2,1,0:T(8,128)S(1)}, f32[5,56,128]{2,1,0:T(8,128)S(1)}, f32[8,128]{1,0:T(8,128)S(1)}) custom-call(f32[8,128]{1,0:T(8,128)S(1)} %get-tuple-element.31.table, f32[14,56,128]{2,1,0:T(8,128)S(1)} %collective-permute-done.6.shared), custom_call_target="tpu_custom_call" | custom-call | flops 10000000000 | tf_op jit(solution)/shard_map/pallas_call | solution.py:466
  16.2 0.1 collective-permute-start.9
  16.2 0.0 collective-permute-done.4.near
  16.2 0.8 %collective-permute-start.11 = (f32[5,56,128]{2,1,0:T(8,128)S(1)}, f32[5,56,128]{2,1,0:T(8,128)S(1)}, u32[]{:S(2)}, u32[]{:S(2)}) collective-permute-start(f32[5,56,128]{2,1,0:T(8,128)S(1)} %get-tuple-element.56), channel_id=1, source_target_pairs={{0,8},{1,2},{2,1},{3,4},{4,3},{5,6},{6,5},{7,15},{8,0},{9,10},{10,... | collective-permute-start | bytes 430088 | tf_op jit(solution)/shard_map/ppermute | solution.py:491
  17.1 1.2 %collective-permute-done.5.far = f32[5,208,128]{2,1,0:T(8,128)S(1)} collective-permute-done((f32[5,208,128]{2,1,0:T(8,128)S(1)}, f32[5,208,128]{2,1,0:T(8,128)S(1)}, u32[]{:S(2)}, u32[]{:S(2)}) %collective-permute-start.5) | collective-permute-done | bytes 532512 | tf_op jit(solution)/shard_map/ppermute | solution.py:491
  18.3 1.3 %shard_map.50 = (f32[12,192,128]{2,1,0:T(8,128)S(1)}, f32[12,48,128]{2,1,0:T(8,128)S(1)}, f32[12,16,128]{2,1,0:T(8,128)S(1)}) custom-call(f32[8,128]{1,0:T(8,128)S(1)} %get-tuple-element.31.table, f32[6,2,256,128]{3,2,1,0:T(8,128)S(1)} %get-tuple-element.32.seeds, s32[2,256,128]{2,1,0:T(8,128)S(1)} %get-tuple-element.33.material, ...), custom_call_target="tpu_custom_call" | custom-call | tf_op jit(solution)/shard_map/pallas_call | solution.py:466
  19.5 1.6 %collective-permute-start.8 = (f32[12,16,128]{2,1,0:T(8,128)S(1)}, f32[12,16,128]{2,1,0:T(8,128)S(1)}, u32[]{:S(2)}, u32[]{:S(2)}) collective-permute-start(f32[12,16,128]{2,1,0:T(8,128)S(1)} %get-tuple-element.49), channel_id=1, source_target_pairs={{0,8},{8,0},{16,24},{24,16},{1,9},{9,1},{17,25},{25,17},{2,10},{10... | collective-permute-start | bytes 294920 | tf_op jit(solution)/shard_map/ppermute | solution.py:495
  21.1 0.0 collective-permute-done.3.strip
  21.1 0.5 %collective-permute-start.7 = (f32[12,48,128]{2,1,0:T(8,128)S(1)}, f32[12,48,128]{2,1,0:T(8,128)S(1)}, u32[]{:S(2)}, u32[]{:S(2)}) collective-permute-start(f32[12,48,128]{2,1,0:T(8,128)S(1)} %get-tuple-element.45), channel_id=1, source_target_pairs={{0,16},{8,24},{16,0},{24,8},{1,17},{9,25},{17,1},{25,9},{2,18},{10... | collective-permute-start | bytes 884744 | tf_op jit(solution)/shard_map/ppermute | solution.py:495
  21.6 0.7 %collective-permute-done.2.corner = f32[12,32,128]{2,1,0:T(8,128)S(1)} collective-permute-done((f32[12,32,128]{2,1,0:T(8,128)S(1)}, f32[12,32,128]{2,1,0:T(8,128)S(1)}, u32[]{:S(2)}, u32[]{:S(2)}) %collective-permute-start.2) | collective-permute-done | bytes 196640 | tf_op jit(solution)/shard_map/ppermute | solution.py:495
  22.2 0.3 shard_map.51
  22.5 0.6 %collective-permute-start.10 = (f32[12,32,128]{2,1,0:T(8,128)S(1)}, f32[12,32,128]{2,1,0:T(8,128)S(1)}, u32[]{:S(2)}, u32[]{:S(2)}) collective-permute-start(f32[12,32,128]{2,1,0:T(8,128)S(1)} %get-tuple-element.54), channel_id=1, source_target_pairs={{0,8},{8,0},{16,24},{24,16},{1,9},{9,1},{17,25},{25,17},{2,10},{10... | collective-permute-start | bytes 589832 | tf_op jit(solution)/shard_map/ppermute | solution.py:495
  23.1 1.1 %collective-permute-done.8.beside = f32[12,16,128]{2,1,0:T(8,128)S(1)} collective-permute-done((f32[12,16,128]{2,1,0:T(8,128)S(1)}, f32[12,16,128]{2,1,0:T(8,128)S(1)}, u32[]{:S(2)}, u32[]{:S(2)}) %collective-permute-start.8) | collective-permute-done | bytes 98336 | tf_op jit(solution)/shard_map/ppermute | solution.py:495
  24.2 0.0 collective-permute-done.11.far
  24.2 1.5 %shard_map.53.part = f32[12,104,128]{2,1,0:T(8,128)S(1)} custom-call(f32[8,128]{1,0:T(8,128)S(1)} %get-tuple-element.31.table, f32[14,56,128]{2,1,0:T(8,128)S(1)} %collective-permute-done.6.shared, f32[5,56,128]{2,1,0:T(8,128)S(1)} %collective-permute-done.9.near, f32[5,56,128]{2,1,0:T(8,128)S(1)} %collective-permute-done.11.far), custom_call_target="tpu_custom_call" | custom-call | flops 2500000000 | tf_op jit(solution)/shard_map/pallas_call | solution.py:466
  25.7 0.9 %shard_map.54._ = f32[1,6,2,256,128]{4,3,2,1,0:T(8,128)} custom-call(f32[12,192,128]{2,1,0:T(8,128)S(1)} %get-tuple-element.44.mid, f32[12,104,128]{2,1,0:T(8,128)S(1)} %shard_map.53.part), custom_call_target="tpu_custom_call" | custom-call | tf_op jit(solution)/shard_map/pallas_call | solution.py:577
  26.6 2.2 %collective-permute-done.7.bands = f32[12,48,128]{2,1,0:T(8,128)S(1)} collective-permute-done((f32[12,48,128]{2,1,0:T(8,128)S(1)}, f32[12,48,128]{2,1,0:T(8,128)S(1)}, u32[]{:S(2)}, u32[]{:S(2)}) %collective-permute-start.7) | collective-permute-done | bytes 294944 | tf_op jit(solution)/shard_map/ppermute | solution.py:495
  28.8 0.3 shard_map.52
  29.1 1.0 %shard_map.55 = f32[1,6,2,256,128]{4,3,2,1,0:T(8,128)} custom-call(f32[6,2,80,128]{3,2,1,0:T(8,128)S(1)} %get-tuple-element.52.low, f32[6,2,80,128]{3,2,1,0:T(8,128)S(1)} %get-tuple-element.53.high, f32[12,32,128]{2,1,0:T(8,128)S(1)} %collective-permute-done.10.got, f32[1,6,2,256,128]{4,3,2,1,0:T(8,128)} %shard_map.54._), custom_call_target="tpu_custom_call", output_to_operand_aliasing={{}: (3, {})} | custom-call | tf_op jit(solution)/shard_map/pallas_call | solution.py:590
  (2 shorter events, 0.0 us)
Async XLA Ops:
  1.8 13.3 %collective-permute-start.6 = (f32[14,56,128]{2,1,0:T(8,128)S(1)}, f32[14,56,128]{2,1,0:T(8,128)S(1)}, u32[]{:S(2)}, u32[]{:S(2)}) collective-permute-start(f32[14,56,128]{2,1,0:T(8,128)S(1)} %get-tuple-element.41), channel_id=1, source_target_pairs={{0,16},{8,24},{16,0},{24,8},{1,17},{9,25},{17,1},{25,9},{2,18},{10... | collective-permute-start | bytes 1204232 | tf_op jit(solution)/shard_map/ppermute | solution.py:495
  5.6 3.3 %collective-permute-start = (f32[5,80,128]{2,1,0:T(8,128)S(1)}, f32[5,80,128]{2,1,0:T(8,128)S(1)}, u32[]{:S(2)}, u32[]{:S(2)}) collective-permute-start(f32[5,80,128]{2,1,0:T(8,128)S(1)} %get-tuple-element.34), channel_id=1, source_target_pairs={{0,1},{1,0},{2,3},{3,2},{4,5},{5,4},{6,7},{7,6},{8,9},{9,8},{10,11... | collective-permute-start | bytes 614408 | tf_op jit(solution)/shard_map/ppermute | solution.py:481
  5.7 5.8 %collective-permute-start.1 = (f32[5,80,128]{2,1,0:T(8,128)S(1)}, f32[5,80,128]{2,1,0:T(8,128)S(1)}, u32[]{:S(2)}, u32[]{:S(2)}) collective-permute-start(f32[5,80,128]{2,1,0:T(8,128)S(1)} %get-tuple-element.35), channel_id=1, source_target_pairs={{0,8},{1,2},{2,1},{3,4},{4,3},{5,6},{6,5},{7,15},{8,0},{9,10},{10,... | collective-permute-start | bytes 614408 | tf_op jit(solution)/shard_map/ppermute | solution.py:491
  7.2 9.0 %collective-permute-start.4 = (f32[5,208,128]{2,1,0:T(8,128)S(1)}, f32[5,208,128]{2,1,0:T(8,128)S(1)}, u32[]{:S(2)}, u32[]{:S(2)}) collective-permute-start(f32[5,208,128]{2,1,0:T(8,128)S(1)} %get-tuple-element.38), channel_id=1, source_target_pairs={{0,1},{1,0},{2,3},{3,2},{4,5},{5,4},{6,7},{7,6},{8,9},{9,8},{10,11... | collective-permute-start | bytes 1597448 | tf_op jit(solution)/shard_map/ppermute | solution.py:481
  7.4 10.8 %collective-permute-start.5 = (f32[5,208,128]{2,1,0:T(8,128)S(1)}, f32[5,208,128]{2,1,0:T(8,128)S(1)}, u32[]{:S(2)}, u32[]{:S(2)}) collective-permute-start(f32[5,208,128]{2,1,0:T(8,128)S(1)} %get-tuple-element.39), channel_id=1, source_target_pairs={{0,8},{1,2},{2,1},{3,4},{4,3},{5,6},{6,5},{7,15},{8,0},{9,10},{10,... | collective-permute-start | bytes 1597448 | tf_op jit(solution)/shard_map/ppermute | solution.py:491
  12.1 9.0 %collective-permute-start.3 = (f32[12,16,128]{2,1,0:T(8,128)S(1)}, f32[12,16,128]{2,1,0:T(8,128)S(1)}, u32[]{:S(2)}, u32[]{:S(2)}) collective-permute-start(f32[12,16,128]{2,1,0:T(8,128)S(1)} %get-tuple-element.37), channel_id=1, source_target_pairs={{0,24},{8,16},{16,8},{24,0},{1,25},{9,17},{17,9},{25,1},{2,26},{10... | collective-permute-start | bytes 294920 | tf_op jit(solution)/shard_map/ppermute | solution.py:495
  13.6 8.7 %collective-permute-start.2 = (f32[12,32,128]{2,1,0:T(8,128)S(1)}, f32[12,32,128]{2,1,0:T(8,128)S(1)}, u32[]{:S(2)}, u32[]{:S(2)}) collective-permute-start(f32[12,32,128]{2,1,0:T(8,128)S(1)} %get-tuple-element.36), channel_id=1, source_target_pairs={{0,16},{8,24},{16,0},{24,8},{1,17},{9,25},{17,1},{25,9},{2,18},{10... | collective-permute-start | bytes 589832 | tf_op jit(solution)/shard_map/ppermute | solution.py:495
  16.2 6.9 %collective-permute-start.9 = (f32[5,56,128]{2,1,0:T(8,128)S(1)}, f32[5,56,128]{2,1,0:T(8,128)S(1)}, u32[]{:S(2)}, u32[]{:S(2)}) collective-permute-start(f32[5,56,128]{2,1,0:T(8,128)S(1)} %get-tuple-element.50), channel_id=1, source_target_pairs={{0,1},{1,0},{2,3},{3,2},{4,5},{5,4},{6,7},{7,6},{8,9},{9,8},{10,11... | collective-permute-start | bytes 430088 | tf_op jit(solution)/shard_map/ppermute | solution.py:481
  16.2 8.0 %collective-permute-start.11 = (f32[5,56,128]{2,1,0:T(8,128)S(1)}, f32[5,56,128]{2,1,0:T(8,128)S(1)}, u32[]{:S(2)}, u32[]{:S(2)}) collective-permute-start(f32[5,56,128]{2,1,0:T(8,128)S(1)} %get-tuple-element.56), channel_id=1, source_target_pairs={{0,8},{1,2},{2,1},{3,4},{4,3},{5,6},{6,5},{7,15},{8,0},{9,10},{10,... | collective-permute-start | bytes 430088 | tf_op jit(solution)/shard_map/ppermute | solution.py:491
  19.5 4.7 %collective-permute-start.8 = (f32[12,16,128]{2,1,0:T(8,128)S(1)}, f32[12,16,128]{2,1,0:T(8,128)S(1)}, u32[]{:S(2)}, u32[]{:S(2)}) collective-permute-start(f32[12,16,128]{2,1,0:T(8,128)S(1)} %get-tuple-element.49), channel_id=1, source_target_pairs={{0,8},{8,0},{16,24},{24,16},{1,9},{9,1},{17,25},{25,17},{2,10},{10... | collective-permute-start | bytes 294920 | tf_op jit(solution)/shard_map/ppermute | solution.py:495
  21.1 7.7 %collective-permute-start.7 = (f32[12,48,128]{2,1,0:T(8,128)S(1)}, f32[12,48,128]{2,1,0:T(8,128)S(1)}, u32[]{:S(2)}, u32[]{:S(2)}) collective-permute-start(f32[12,48,128]{2,1,0:T(8,128)S(1)} %get-tuple-element.45), channel_id=1, source_target_pairs={{0,16},{8,24},{16,0},{24,8},{1,17},{9,25},{17,1},{25,9},{2,18},{10... | collective-permute-start | bytes 884744 | tf_op jit(solution)/shard_map/ppermute | solution.py:495
  22.5 6.6 %collective-permute-start.10 = (f32[12,32,128]{2,1,0:T(8,128)S(1)}, f32[12,32,128]{2,1,0:T(8,128)S(1)}, u32[]{:S(2)}, u32[]{:S(2)}) collective-permute-start(f32[12,32,128]{2,1,0:T(8,128)S(1)} %get-tuple-element.54), channel_id=1, source_target_pairs={{0,8},{8,0},{16,24},{24,16},{1,9},{9,1},{17,25},{25,17},{2,10},{10... | collective-permute-start | bytes 589832 | tf_op jit(solution)/shard_map/ppermute | solution.py:495

commit v21 on v18

--- a/solution.py
+++ b/solution.py
@@ -148,7 +148,8 @@
     far[...] = jnp.where(odd, up, down)
 
 
-def halo_kernel(spans, sub, table, seeds, material, near, far):
+def halo_kernel(spans, sub, table, seeds, material, *rest):
+    near, far = rest[-2:]
     send_halos(sub, loaded(seeds, material, table, spans), near, far)
 
 
@@ -313,11 +314,6 @@
             table[k * count + m : k * count + m + 1] = jnp.full((1, table.shape[1]), entries[k, m], jnp.float32)
 
 
-def halo_pair_kernel(edges, inner, sub, table, seeds, material, near_edge, far_edge, near, far):
-    send_halos(sub, loaded(seeds, material, table, edges), near_edge, far_edge)
-    send_halos(sub, loaded(seeds, material, table, inner), near, far)
-
-
 def shared_fields(table, shared):
     depth = shared.shape[0] // 7
     planes = bands_unpacked(shared[...])
@@ -532,9 +528,12 @@
         cost_estimate=cost(0),
     )(*(pltpu.with_memory_space_constraint(x, pltpu.HBM) for x in (decay, coupling, seeds, material)))
     shared = swapped(shared, 2, tile_size)
-    edge_near, edge_far, inner_near, inner_far = called(
-        functools.partial(halo_pair_kernel, edges, inner, "sub"),
-        [(PLANES, edge_rows, size_y)] * 2 + [(PLANES, inner_rows, size_y)] * 2, table, seeds, material,
+    edge_near, edge_far = called(
+        functools.partial(halo_kernel, edges, "sub"), [(PLANES, edge_rows, size_y)] * 2, table, seeds, material
+    )
+    inner_near, inner_far = called(
+        functools.partial(halo_kernel, inner, "sub"), [(PLANES, inner_rows, size_y)] * 2,
+        table, seeds, material, edge_near,
     )
     edge_near, inner_near = near_exchange(edge_near, sub_size), near_exchange(inner_near, sub_size)
     edge_far = far_exchange(edge_far, sub_size, tile_size)

time: 30.1 us -> 32.3 us (1.073)
  starting transfers between devices: 12.4 us -> 15.3 us
  waiting for transfers between devices: 8.06 us -> 7.32 us
    ppermute x6, starting transfers between devices: 8.18 us -> 10.2 us  [swapped(): lax.ppermute(value, 'tile', [(t, t ^ bits) for t in range(tile_size)])]
    ppermute x3, waiting for transfers between devices: 3.76 us -> 2.61 us  [far_exchange(): return lax.ppermute(far, ('tile', 'sub'), pairs)]
    ppermute x3, starting transfers between devices: 3.89 us -> 4.54 us  [far_exchange(): return lax.ppermute(far, ('tile', 'sub'), pairs)]
    ppermute x6, waiting for transfers between devices: 4.29 us -> 4.7 us  [swapped(): lax.ppermute(value, 'tile', [(t, t ^ bits) for t in range(tile_size)])]
    pallas_call x7 -> x8, Pallas kernels: 5.63 us -> 5.66 us  [called(): pl.pallas_call(kernel, out_shape=outs, in_specs=[VMEM] * len(operands), o...]
  transfers between devices with their start and end apart: 12 -> 12, of which waited for: 6 -> 4; matrix products, arithmetic and copies ran while one was open for 0% -> 0% of each run, Pallas kernels for 22% -> 20%
where the time goes in v21:
time: 32.3 us; the launch traced here: 32.1 us
  starting transfers between devices  15.3 us (47%)
  Pallas kernels  9.36 us (29%)
  waiting for transfers between devices  7.32 us (23%)
    ppermute x6, starting transfers between devices, swapped(): lax.ppermute(value, 'tile', [(t, t ^ bits) for t in range(tile_size)])  10.2 us
    pallas_call x8, Pallas kernels, called(): pl.pallas_call(kernel, out_shape=outs, in_specs=[VMEM] * len(operands), o...  5.66 us
    ppermute x6, waiting for transfers between devices, swapped(): lax.ppermute(value, 'tile', [(t, t ^ bits) for t in range(tile_size)])  4.7 us
    ppermute x3, starting transfers between devices, far_exchange(): return lax.ppermute(far, ('tile', 'sub'), pairs)  4.54 us
    ppermute x3, waiting for transfers between devices, far_exchange(): return lax.ppermute(far, ('tile', 'sub'), pairs)  2.61 us
    pallas_call x1, Pallas kernels, two_by_two(): pl.pallas_call(functools.partial(first_kernel, fetched, HALO // 2), out_s...  1.81 us
    pallas_call x1, Pallas kernels, two_by_two(): pl.pallas_call(functools.partial(last_kernel, 'tile'), out_shape=whole, i...  0.98 us
    pallas_call x1, Pallas kernels, two_by_two(): pl.pallas_call(early_kernel, out_shape=whole, in_specs=[VMEM] * 2, out_sp...  0.91 us
  transfers between devices with their start and end apart: 12, of which 4 were waited for; matrix products, arithmetic and copies ran while one was open for 0% of the time, Pallas kernels for 20%

profile of v21, /device:TPU:0, one launch (start us, length us, event | category | flops | bytes accessed | tf_op | source)
XLA Modules:
  0.0 32.1 jit_solution(9356477649888132856)
XLA Ops:
  0.0 1.8 %shard_map.46 = (f32[14,56,128]{2,1,0:T(8,128)S(1)}, f32[6,2,256,128]{3,2,1,0:T(8,128)S(1)}, s32[2,256,128]{2,1,0:T(8,128)S(1)}, f32[8,128]{1,0:T(8,128)S(1)}) custom-call(f32[4]{0:T(128)} %decay.1, f32[4]{0:T(128)} %coupling.1, f32[1,6,2,256,128]{4,3,2,1,0:T(8,128)} %seeds.1, s32[1,2,256,128]{3,2,1,0:T(8,128)} %material.1), custom_call_target="tpu_custom_call" | custom-call | tf_op jit(solution)/shard_map/pallas_call | solution.py:516
  1.8 3.0 %collective-permute-start.6 = (f32[14,56,128]{2,1,0:T(8,128)S(1)}, f32[14,56,128]{2,1,0:T(8,128)S(1)}, u32[]{:S(2)}, u32[]{:S(2)}) collective-permute-start(f32[14,56,128]{2,1,0:T(8,128)S(1)} %get-tuple-element.41), channel_id=1, source_target_pairs={{0,16},{8,24},{16,0},{24,8},{1,17},{9,25},{17,1},{25,9},{2,18},{10... | collective-permute-start | bytes 1204232 | tf_op jit(solution)/shard_map/ppermute | solution.py:491
  4.9 0.2 shard_map.47
  5.1 1.6 %collective-permute-start.1 = (f32[5,80,128]{2,1,0:T(8,128)S(1)}, f32[5,80,128]{2,1,0:T(8,128)S(1)}, u32[]{:S(2)}, u32[]{:S(2)}) collective-permute-start(f32[5,80,128]{2,1,0:T(8,128)S(1)} %get-tuple-element.35), channel_id=1, source_target_pairs={{0,8},{1,2},{2,1},{3,4},{4,3},{5,6},{6,5},{7,15},{8,0},{9,10},{10,... | collective-permute-start | bytes 614408 | tf_op jit(solution)/shard_map/ppermute | solution.py:487
  6.7 0.2 collective-permute-start
  6.9 0.5 %shard_map.49 = (f32[5,208,128]{2,1,0:T(8,128)S(1)}, f32[5,208,128]{2,1,0:T(8,128)S(1)}) custom-call(f32[8,128]{1,0:T(8,128)S(1)} %get-tuple-element.31.table, f32[6,2,256,128]{3,2,1,0:T(8,128)S(1)} %get-tuple-element.32.seeds, s32[2,256,128]{2,1,0:T(8,128)S(1)} %get-tuple-element.33.material, f32[5,80,128]{2,1,0:T(8,128)S(1)} %get-tuple-element.34.rest_0_), custom_call_target="tpu_custom_call" | custom-call | tf_op jit(solution)/shard_map/pallas_call | solution.py:462
  7.4 0.4 %collective-permute-start.4 = (f32[5,208,128]{2,1,0:T(8,128)S(1)}, f32[5,208,128]{2,1,0:T(8,128)S(1)}, u32[]{:S(2)}, u32[]{:S(2)}) collective-permute-start(f32[5,208,128]{2,1,0:T(8,128)S(1)} %get-tuple-element.38), channel_id=1, source_target_pairs={{0,1},{1,0},{2,3},{3,2},{4,5},{5,4},{6,7},{7,6},{8,9},{9,8},{10,11... | collective-permute-start | bytes 1597448 | tf_op jit(solution)/shard_map/ppermute | solution.py:477
  7.8 1.3 %collective-permute-start.5 = (f32[5,208,128]{2,1,0:T(8,128)S(1)}, f32[5,208,128]{2,1,0:T(8,128)S(1)}, u32[]{:S(2)}, u32[]{:S(2)}) collective-permute-start(f32[5,208,128]{2,1,0:T(8,128)S(1)} %get-tuple-element.39), channel_id=1, source_target_pairs={{0,8},{1,2},{2,1},{3,4},{4,3},{5,6},{6,5},{7,15},{8,0},{9,10},{10,... | collective-permute-start | bytes 1597448 | tf_op jit(solution)/shard_map/ppermute | solution.py:487
  9.0 1.9 %collective-permute-done.1.far = f32[5,80,128]{2,1,0:T(8,128)S(1)} collective-permute-done((f32[5,80,128]{2,1,0:T(8,128)S(1)}, f32[5,80,128]{2,1,0:T(8,128)S(1)}, u32[]{:S(2)}, u32[]{:S(2)}) %collective-permute-start.1) | collective-permute-done | bytes 204832 | tf_op jit(solution)/shard_map/ppermute | solution.py:487
  10.9 0.0 collective-permute-done.near
  10.9 0.5 %shard_map.48 = (f32[12,64,128]{2,1,0:T(8,128)S(1)}, f32[12,32,128]{2,1,0:T(8,128)S(1)}, f32[12,16,128]{2,1,0:T(8,128)S(1)}) custom-call(f32[8,128]{1,0:T(8,128)S(1)} %get-tuple-element.31.table, f32[6,2,256,128]{3,2,1,0:T(8,128)S(1)} %get-tuple-element.32.seeds, s32[2,256,128]{2,1,0:T(8,128)S(1)} %get-tuple-element.33.material, ...), custom_call_target="tpu_custom_call" | custom-call | tf_op jit(solution)/shard_map/pallas_call | solution.py:462
  11.5 1.5 %collective-permute-start.3 = (f32[12,16,128]{2,1,0:T(8,128)S(1)}, f32[12,16,128]{2,1,0:T(8,128)S(1)}, u32[]{:S(2)}, u32[]{:S(2)}) collective-permute-start(f32[12,16,128]{2,1,0:T(8,128)S(1)} %get-tuple-element.37), channel_id=1, source_target_pairs={{0,24},{8,16},{16,8},{24,0},{1,25},{9,17},{17,9},{25,1},{2,26},{10... | collective-permute-start | bytes 294920 | tf_op jit(solution)/shard_map/ppermute | solution.py:491
  13.0 1.5 %collective-permute-start.2 = (f32[12,32,128]{2,1,0:T(8,128)S(1)}, f32[12,32,128]{2,1,0:T(8,128)S(1)}, u32[]{:S(2)}, u32[]{:S(2)}) collective-permute-start(f32[12,32,128]{2,1,0:T(8,128)S(1)} %get-tuple-element.36), channel_id=1, source_target_pairs={{0,16},{8,24},{16,0},{24,8},{1,17},{9,25},{17,1},{25,9},{2,18},{10... | collective-permute-start | bytes 589832 | tf_op jit(solution)/shard_map/ppermute | solution.py:491
  14.5 0.0 collective-permute-done.6.shared
  14.5 1.1 %shard_map.50 = (f32[5,56,128]{2,1,0:T(8,128)S(1)}, f32[5,56,128]{2,1,0:T(8,128)S(1)}, f32[8,128]{1,0:T(8,128)S(1)}) custom-call(f32[8,128]{1,0:T(8,128)S(1)} %get-tuple-element.31.table, f32[14,56,128]{2,1,0:T(8,128)S(1)} %collective-permute-done.6.shared), custom_call_target="tpu_custom_call" | custom-call | flops 10000000000 | tf_op jit(solution)/shard_map/pallas_call | solution.py:462
  15.6 0.1 collective-permute-start.9
  15.6 0.0 collective-permute-done.4.near
  15.7 1.7 %collective-permute-start.11 = (f32[5,56,128]{2,1,0:T(8,128)S(1)}, f32[5,56,128]{2,1,0:T(8,128)S(1)}, u32[]{:S(2)}, u32[]{:S(2)}) collective-permute-start(f32[5,56,128]{2,1,0:T(8,128)S(1)} %get-tuple-element.56), channel_id=1, source_target_pairs={{0,8},{1,2},{2,1},{3,4},{4,3},{5,6},{6,5},{7,15},{8,0},{9,10},{10,... | collective-permute-start | bytes 430088 | tf_op jit(solution)/shard_map/ppermute | solution.py:487
  17.4 0.7 %collective-permute-done.5.far = f32[5,208,128]{2,1,0:T(8,128)S(1)} collective-permute-done((f32[5,208,128]{2,1,0:T(8,128)S(1)}, f32[5,208,128]{2,1,0:T(8,128)S(1)}, u32[]{:S(2)}, u32[]{:S(2)}) %collective-permute-start.5) | collective-permute-done | bytes 532512 | tf_op jit(solution)/shard_map/ppermute | solution.py:487
  18.1 1.3 %shard_map.51 = (f32[12,192,128]{2,1,0:T(8,128)S(1)}, f32[12,48,128]{2,1,0:T(8,128)S(1)}, f32[12,16,128]{2,1,0:T(8,128)S(1)}) custom-call(f32[8,128]{1,0:T(8,128)S(1)} %get-tuple-element.31.table, f32[6,2,256,128]{3,2,1,0:T(8,128)S(1)} %get-tuple-element.32.seeds, s32[2,256,128]{2,1,0:T(8,128)S(1)} %get-tuple-element.33.material, ...), custom_call_target="tpu_custom_call" | custom-call | tf_op jit(solution)/shard_map/pallas_call | solution.py:462
  19.4 2.0 %collective-permute-start.7 = (f32[12,48,128]{2,1,0:T(8,128)S(1)}, f32[12,48,128]{2,1,0:T(8,128)S(1)}, u32[]{:S(2)}, u32[]{:S(2)}) collective-permute-start(f32[12,48,128]{2,1,0:T(8,128)S(1)} %get-tuple-element.45), channel_id=1, source_target_pairs={{0,16},{8,24},{16,0},{24,8},{1,17},{9,25},{17,1},{25,9},{2,18},{10... | collective-permute-start | bytes 884744 | tf_op jit(solution)/shard_map/ppermute | solution.py:491
  21.4 0.0 collective-permute-done.3.strip
  21.4 0.0 collective-permute-start.8
  21.4 0.3 shard_map.52
  21.7 2.1 %collective-permute-start.10 = (f32[12,32,128]{2,1,0:T(8,128)S(1)}, f32[12,32,128]{2,1,0:T(8,128)S(1)}, u32[]{:S(2)}, u32[]{:S(2)}) collective-permute-start(f32[12,32,128]{2,1,0:T(8,128)S(1)} %get-tuple-element.54), channel_id=1, source_target_pairs={{0,8},{8,0},{16,24},{24,16},{1,9},{9,1},{17,25},{25,17},{2,10},{10... | collective-permute-start | bytes 589832 | tf_op jit(solution)/shard_map/ppermute | solution.py:491
  23.7 0.0 collective-permute-done.9.near
  23.7 3.2 %collective-permute-done.8.beside = f32[12,16,128]{2,1,0:T(8,128)S(1)} collective-permute-done((f32[12,16,128]{2,1,0:T(8,128)S(1)}, f32[12,16,128]{2,1,0:T(8,128)S(1)}, u32[]{:S(2)}, u32[]{:S(2)}) %collective-permute-start.8) | collective-permute-done | bytes 98336 | tf_op jit(solution)/shard_map/ppermute | solution.py:491
  26.9 1.5 %shard_map.54.part = f32[12,104,128]{2,1,0:T(8,128)S(1)} custom-call(f32[8,128]{1,0:T(8,128)S(1)} %get-tuple-element.31.table, f32[14,56,128]{2,1,0:T(8,128)S(1)} %collective-permute-done.6.shared, f32[5,56,128]{2,1,0:T(8,128)S(1)} %collective-permute-done.9.near, f32[5,56,128]{2,1,0:T(8,128)S(1)} %collective-permute-done.11.far), custom_call_target="tpu_custom_call" | custom-call | flops 2000000000 | tf_op jit(solution)/shard_map/pallas_call | solution.py:462
  28.4 0.9 %shard_map.55._ = f32[1,6,2,256,128]{4,3,2,1,0:T(8,128)} custom-call(f32[12,192,128]{2,1,0:T(8,128)S(1)} %get-tuple-element.44.mid, f32[12,104,128]{2,1,0:T(8,128)S(1)} %shard_map.54.part), custom_call_target="tpu_custom_call" | custom-call | tf_op jit(solution)/shard_map/pallas_call | solution.py:576
  29.3 0.3 shard_map.53
  29.6 1.5 %collective-permute-done.10.got = f32[12,32,128]{2,1,0:T(8,128)S(1)} collective-permute-done((f32[12,32,128]{2,1,0:T(8,128)S(1)}, f32[12,32,128]{2,1,0:T(8,128)S(1)}, u32[]{:S(2)}, u32[]{:S(2)}) %collective-permute-start.10) | collective-permute-done | bytes 196640 | tf_op jit(solution)/shard_map/ppermute | solution.py:491
  31.1 1.0 %shard_map.56 = f32[1,6,2,256,128]{4,3,2,1,0:T(8,128)} custom-call(f32[6,2,80,128]{3,2,1,0:T(8,128)S(1)} %get-tuple-element.52.low, f32[6,2,80,128]{3,2,1,0:T(8,128)S(1)} %get-tuple-element.53.high, f32[12,32,128]{2,1,0:T(8,128)S(1)} %collective-permute-done.10.got, f32[1,6,2,256,128]{4,3,2,1,0:T(8,128)} %shard_map.55._), custom_call_target="tpu_custom_call", output_to_operand_aliasing={{}: (3, {})} | custom-call | tf_op jit(solution)/shard_map/pallas_call | solution.py:589
  (3 shorter events, 0.0 us)
Async XLA Ops:
  1.8 12.7 %collective-permute-start.6 = (f32[14,56,128]{2,1,0:T(8,128)S(1)}, f32[14,56,128]{2,1,0:T(8,128)S(1)}, u32[]{:S(2)}, u32[]{:S(2)}) collective-permute-start(f32[14,56,128]{2,1,0:T(8,128)S(1)} %get-tuple-element.41), channel_id=1, source_target_pairs={{0,16},{8,24},{16,0},{24,8},{1,17},{9,25},{17,1},{25,9},{2,18},{10... | collective-permute-start | bytes 1204232 | tf_op jit(solution)/shard_map/ppermute | solution.py:491
  5.1 5.8 %collective-permute-start.1 = (f32[5,80,128]{2,1,0:T(8,128)S(1)}, f32[5,80,128]{2,1,0:T(8,128)S(1)}, u32[]{:S(2)}, u32[]{:S(2)}) collective-permute-start(f32[5,80,128]{2,1,0:T(8,128)S(1)} %get-tuple-element.35), channel_id=1, source_target_pairs={{0,8},{1,2},{2,1},{3,4},{4,3},{5,6},{6,5},{7,15},{8,0},{9,10},{10,... | collective-permute-start | bytes 614408 | tf_op jit(solution)/shard_map/ppermute | solution.py:487
  6.7 4.3 %collective-permute-start = (f32[5,80,128]{2,1,0:T(8,128)S(1)}, f32[5,80,128]{2,1,0:T(8,128)S(1)}, u32[]{:S(2)}, u32[]{:S(2)}) collective-permute-start(f32[5,80,128]{2,1,0:T(8,128)S(1)} %get-tuple-element.34.rest_0_), channel_id=1, source_target_pairs={{0,1},{1,0},{2,3},{3,2},{4,5},{5,4},{6,7},{7,6},{8,9},{9,8},{10,11... | collective-permute-start | bytes 614408 | tf_op jit(solution)/shard_map/ppermute | solution.py:477
  7.4 8.3 %collective-permute-start.4 = (f32[5,208,128]{2,1,0:T(8,128)S(1)}, f32[5,208,128]{2,1,0:T(8,128)S(1)}, u32[]{:S(2)}, u32[]{:S(2)}) collective-permute-start(f32[5,208,128]{2,1,0:T(8,128)S(1)} %get-tuple-element.38), channel_id=1, source_target_pairs={{0,1},{1,0},{2,3},{3,2},{4,5},{5,4},{6,7},{7,6},{8,9},{9,8},{10,11... | collective-permute-start | bytes 1597448 | tf_op jit(solution)/shard_map/ppermute | solution.py:477
  7.8 10.3 %collective-permute-start.5 = (f32[5,208,128]{2,1,0:T(8,128)S(1)}, f32[5,208,128]{2,1,0:T(8,128)S(1)}, u32[]{:S(2)}, u32[]{:S(2)}) collective-permute-start(f32[5,208,128]{2,1,0:T(8,128)S(1)} %get-tuple-element.39), channel_id=1, source_target_pairs={{0,8},{1,2},{2,1},{3,4},{4,3},{5,6},{6,5},{7,15},{8,0},{9,10},{10,... | collective-permute-start | bytes 1597448 | tf_op jit(solution)/shard_map/ppermute | solution.py:487
  11.5 9.9 %collective-permute-start.3 = (f32[12,16,128]{2,1,0:T(8,128)S(1)}, f32[12,16,128]{2,1,0:T(8,128)S(1)}, u32[]{:S(2)}, u32[]{:S(2)}) collective-permute-start(f32[12,16,128]{2,1,0:T(8,128)S(1)} %get-tuple-element.37), channel_id=1, source_target_pairs={{0,24},{8,16},{16,8},{24,0},{1,25},{9,17},{17,9},{25,1},{2,26},{10... | collective-permute-start | bytes 294920 | tf_op jit(solution)/shard_map/ppermute | solution.py:491
  13.0 8.4 %collective-permute-start.2 = (f32[12,32,128]{2,1,0:T(8,128)S(1)}, f32[12,32,128]{2,1,0:T(8,128)S(1)}, u32[]{:S(2)}, u32[]{:S(2)}) collective-permute-start(f32[12,32,128]{2,1,0:T(8,128)S(1)} %get-tuple-element.36), channel_id=1, source_target_pairs={{0,16},{8,24},{16,0},{24,8},{1,17},{9,25},{17,1},{25,9},{2,18},{10... | collective-permute-start | bytes 589832 | tf_op jit(solution)/shard_map/ppermute | solution.py:491
  15.6 8.2 %collective-permute-start.9 = (f32[5,56,128]{2,1,0:T(8,128)S(1)}, f32[5,56,128]{2,1,0:T(8,128)S(1)}, u32[]{:S(2)}, u32[]{:S(2)}) collective-permute-start(f32[5,56,128]{2,1,0:T(8,128)S(1)} %get-tuple-element.50), channel_id=1, source_target_pairs={{0,1},{1,0},{2,3},{3,2},{4,5},{5,4},{6,7},{7,6},{8,9},{9,8},{10,11... | collective-permute-start | bytes 430088 | tf_op jit(solution)/shard_map/ppermute | solution.py:477
  15.7 11.3 %collective-permute-start.11 = (f32[5,56,128]{2,1,0:T(8,128)S(1)}, f32[5,56,128]{2,1,0:T(8,128)S(1)}, u32[]{:S(2)}, u32[]{:S(2)}) collective-permute-start(f32[5,56,128]{2,1,0:T(8,128)S(1)} %get-tuple-element.56), channel_id=1, source_target_pairs={{0,8},{1,2},{2,1},{3,4},{4,3},{5,6},{6,5},{7,15},{8,0},{9,10},{10,... | collective-permute-start | bytes 430088 | tf_op jit(solution)/shard_map/ppermute | solution.py:487
  19.4 10.0 %collective-permute-start.7 = (f32[12,48,128]{2,1,0:T(8,128)S(1)}, f32[12,48,128]{2,1,0:T(8,128)S(1)}, u32[]{:S(2)}, u32[]{:S(2)}) collective-permute-start(f32[12,48,128]{2,1,0:T(8,128)S(1)} %get-tuple-element.45), channel_id=1, source_target_pairs={{0,16},{8,24},{16,0},{24,8},{1,17},{9,25},{17,1},{25,9},{2,18},{10... | collective-permute-start | bytes 884744 | tf_op jit(solution)/shard_map/ppermute | solution.py:491
  21.4 5.5 %collective-permute-start.8 = (f32[12,16,128]{2,1,0:T(8,128)S(1)}, f32[12,16,128]{2,1,0:T(8,128)S(1)}, u32[]{:S(2)}, u32[]{:S(2)}) collective-permute-start(f32[12,16,128]{2,1,0:T(8,128)S(1)} %get-tuple-element.49), channel_id=1, source_target_pairs={{0,8},{8,0},{16,24},{24,16},{1,9},{9,1},{17,25},{25,17},{2,10},{10... | collective-permute-start | bytes 294920 | tf_op jit(solution)/shard_map/ppermute | solution.py:491
  21.7 9.5 %collective-permute-start.10 = (f32[12,32,128]{2,1,0:T(8,128)S(1)}, f32[12,32,128]{2,1,0:T(8,128)S(1)}, u32[]{:S(2)}, u32[]{:S(2)}) collective-permute-start(f32[12,32,128]{2,1,0:T(8,128)S(1)} %get-tuple-element.54), channel_id=1, source_target_pairs={{0,8},{8,0},{16,24},{24,16},{1,9},{9,1},{17,25},{25,17},{2,10},{10... | collective-permute-start | bytes 589832 | tf_op jit(solution)/shard_map/ppermute | solution.py:491

commit v22 on v18

--- a/solution.py
+++ b/solution.py
@@ -305,12 +305,14 @@
         copy.wait()
     planes = [held[c, :, rows] for c in range(6)] + [labels[:, rows].astype(jnp.float32)]
     shared[...] = bands_packed(jnp.concatenate(planes, axis=0))
-    for copy in copies[early:]:
+    for copy in copies[early : early + 2]:
         copy.wait()
     count = entries.shape[1]
     for k in range(2):
         for m in range(count):
             table[k * count + m : k * count + m + 1] = jnp.full((1, table.shape[1]), entries[k, m], jnp.float32)
+    for copy in copies[early + 2 :]:
+        copy.wait()
 
 
 def halo_pair_kernel(edges, inner, sub, table, seeds, material, near_edge, far_edge, near, far):

time: 30.1 us -> 30.1 us (level)
  no operation moved by 1% of the time
where the time goes in v22:
time: 30.1 us; the launch traced here: 29.9 us
  starting transfers between devices  12.4 us (41%)
  Pallas kernels  9.33 us (31%)
  waiting for transfers between devices  8.06 us (27%)
    ppermute x6, starting transfers between devices, swapped(): lax.ppermute(value, 'tile', [(t, t ^ bits) for t in range(tile_size)])  8.18 us
    pallas_call x7, Pallas kernels, called(): pl.pallas_call(kernel, out_shape=outs, in_specs=[VMEM] * len(operands), o...  5.63 us
    ppermute x6, waiting for transfers between devices, swapped(): lax.ppermute(value, 'tile', [(t, t ^ bits) for t in range(tile_size)])  4.29 us
    ppermute x3, starting transfers between devices, far_exchange(): return lax.ppermute(far, ('tile', 'sub'), pairs)  3.89 us
    ppermute x3, waiting for transfers between devices, far_exchange(): return lax.ppermute(far, ('tile', 'sub'), pairs)  3.76 us
    pallas_call x1, Pallas kernels, two_by_two(): pl.pallas_call(functools.partial(first_kernel, fetched, HALO // 2), out_s...  1.81 us
    pallas_call x1, Pallas kernels, two_by_two(): pl.pallas_call(functools.partial(last_kernel, 'tile'), out_shape=whole, i...  0.98 us
    pallas_call x1, Pallas kernels, two_by_two(): pl.pallas_call(early_kernel, out_shape=whole, in_specs=[VMEM] * 2, out_sp...  0.91 us
  transfers between devices with their start and end apart: 12, of which 6 were waited for; matrix products, arithmetic and copies ran while one was open for 0% of the time, Pallas kernels for 22%

profile of v22, /device:TPU:0, one launch (start us, length us, event | category | flops | bytes accessed | tf_op | source)
XLA Modules:
  0.0 29.9 jit_solution(13255521747803082177)
XLA Ops:
  0.0 1.8 %shard_map.46 = (f32[14,56,128]{2,1,0:T(8,128)S(1)}, f32[6,2,256,128]{3,2,1,0:T(8,128)S(1)}, s32[2,256,128]{2,1,0:T(8,128)S(1)}, f32[8,128]{1,0:T(8,128)S(1)}) custom-call(f32[4]{0:T(128)} %decay.1, f32[4]{0:T(128)} %coupling.1, f32[1,6,2,256,128]{4,3,2,1,0:T(8,128)} %seeds.1, s32[1,2,256,128]{3,2,1,0:T(8,128)} %material.1), custom_call_target="tpu_custom_call" | custom-call | tf_op jit(solution)/shard_map/pallas_call | solution.py:522
  1.8 3.0 %collective-permute-start.6 = (f32[14,56,128]{2,1,0:T(8,128)S(1)}, f32[14,56,128]{2,1,0:T(8,128)S(1)}, u32[]{:S(2)}, u32[]{:S(2)}) collective-permute-start(f32[14,56,128]{2,1,0:T(8,128)S(1)} %get-tuple-element.41), channel_id=1, source_target_pairs={{0,16},{8,24},{16,0},{24,8},{1,17},{9,25},{17,1},{25,9},{2,18},{10... | collective-permute-start | bytes 1204232 | tf_op jit(solution)/shard_map/ppermute | solution.py:497
  4.9 0.8 %shard_map.47 = (f32[5,80,128]{2,1,0:T(8,128)S(1)}, f32[5,80,128]{2,1,0:T(8,128)S(1)}, f32[5,208,128]{2,1,0:T(8,128)S(1)}, f32[5,208,128]{2,1,0:T(8,128)S(1)}) custom-call(f32[8,128]{1,0:T(8,128)S(1)} %get-tuple-element.31.table, f32[6,2,256,128]{3,2,1,0:T(8,128)S(1)} %get-tuple-element.32.seeds, s32[2,256,128]{2,1,0:T(8,128)S(1)} %get-tuple-element.33.material), custom_call_target="tpu_custom_call" | custom-call | tf_op jit(solution)/shard_map/pallas_call | solution.py:468
  5.6 0.1 collective-permute-start
  5.7 1.6 %collective-permute-start.1 = (f32[5,80,128]{2,1,0:T(8,128)S(1)}, f32[5,80,128]{2,1,0:T(8,128)S(1)}, u32[]{:S(2)}, u32[]{:S(2)}) collective-permute-start(f32[5,80,128]{2,1,0:T(8,128)S(1)} %get-tuple-element.35), channel_id=1, source_target_pairs={{0,8},{1,2},{2,1},{3,4},{4,3},{5,6},{6,5},{7,15},{8,0},{9,10},{10,... | collective-permute-start | bytes 614408 | tf_op jit(solution)/shard_map/ppermute | solution.py:493
  7.2 0.2 collective-permute-start.4
  7.4 1.5 %collective-permute-start.5 = (f32[5,208,128]{2,1,0:T(8,128)S(1)}, f32[5,208,128]{2,1,0:T(8,128)S(1)}, u32[]{:S(2)}, u32[]{:S(2)}) collective-permute-start(f32[5,208,128]{2,1,0:T(8,128)S(1)} %get-tuple-element.39), channel_id=1, source_target_pairs={{0,8},{1,2},{2,1},{3,4},{4,3},{5,6},{6,5},{7,15},{8,0},{9,10},{10,... | collective-permute-start | bytes 1597448 | tf_op jit(solution)/shard_map/ppermute | solution.py:493
  8.9 0.0 collective-permute-done.near
  8.9 2.6 %collective-permute-done.1.far = f32[5,80,128]{2,1,0:T(8,128)S(1)} collective-permute-done((f32[5,80,128]{2,1,0:T(8,128)S(1)}, f32[5,80,128]{2,1,0:T(8,128)S(1)}, u32[]{:S(2)}, u32[]{:S(2)}) %collective-permute-start.1) | collective-permute-done | bytes 204832 | tf_op jit(solution)/shard_map/ppermute | solution.py:493
  11.5 0.5 %shard_map.48 = (f32[12,64,128]{2,1,0:T(8,128)S(1)}, f32[12,32,128]{2,1,0:T(8,128)S(1)}, f32[12,16,128]{2,1,0:T(8,128)S(1)}) custom-call(f32[8,128]{1,0:T(8,128)S(1)} %get-tuple-element.31.table, f32[6,2,256,128]{3,2,1,0:T(8,128)S(1)} %get-tuple-element.32.seeds, s32[2,256,128]{2,1,0:T(8,128)S(1)} %get-tuple-element.33.material, ...), custom_call_target="tpu_custom_call" | custom-call | tf_op jit(solution)/shard_map/pallas_call | solution.py:468
  12.1 1.5 %collective-permute-start.3 = (f32[12,16,128]{2,1,0:T(8,128)S(1)}, f32[12,16,128]{2,1,0:T(8,128)S(1)}, u32[]{:S(2)}, u32[]{:S(2)}) collective-permute-start(f32[12,16,128]{2,1,0:T(8,128)S(1)} %get-tuple-element.37), channel_id=1, source_target_pairs={{0,24},{8,16},{16,8},{24,0},{1,25},{9,17},{17,9},{25,1},{2,26},{10... | collective-permute-start | bytes 294920 | tf_op jit(solution)/shard_map/ppermute | solution.py:497
  13.6 1.5 %collective-permute-start.2 = (f32[12,32,128]{2,1,0:T(8,128)S(1)}, f32[12,32,128]{2,1,0:T(8,128)S(1)}, u32[]{:S(2)}, u32[]{:S(2)}) collective-permute-start(f32[12,32,128]{2,1,0:T(8,128)S(1)} %get-tuple-element.36), channel_id=1, source_target_pairs={{0,16},{8,24},{16,0},{24,8},{1,17},{9,25},{17,1},{25,9},{2,18},{10... | collective-permute-start | bytes 589832 | tf_op jit(solution)/shard_map/ppermute | solution.py:497
  15.1 0.0 collective-permute-done.6.shared
  15.1 1.1 %shard_map.49 = (f32[5,56,128]{2,1,0:T(8,128)S(1)}, f32[5,56,128]{2,1,0:T(8,128)S(1)}, f32[8,128]{1,0:T(8,128)S(1)}) custom-call(f32[8,128]{1,0:T(8,128)S(1)} %get-tuple-element.31.table, f32[14,56,128]{2,1,0:T(8,128)S(1)} %collective-permute-done.6.shared), custom_call_target="tpu_custom_call" | custom-call | flops 10000000000 | tf_op jit(solution)/shard_map/pallas_call | solution.py:468
  16.2 0.1 collective-permute-start.9
  16.2 0.0 collective-permute-done.4.near
  16.2 0.8 %collective-permute-start.11 = (f32[5,56,128]{2,1,0:T(8,128)S(1)}, f32[5,56,128]{2,1,0:T(8,128)S(1)}, u32[]{:S(2)}, u32[]{:S(2)}) collective-permute-start(f32[5,56,128]{2,1,0:T(8,128)S(1)} %get-tuple-element.56), channel_id=1, source_target_pairs={{0,8},{1,2},{2,1},{3,4},{4,3},{5,6},{6,5},{7,15},{8,0},{9,10},{10,... | collective-permute-start | bytes 430088 | tf_op jit(solution)/shard_map/ppermute | solution.py:493
  17.1 1.2 %collective-permute-done.5.far = f32[5,208,128]{2,1,0:T(8,128)S(1)} collective-permute-done((f32[5,208,128]{2,1,0:T(8,128)S(1)}, f32[5,208,128]{2,1,0:T(8,128)S(1)}, u32[]{:S(2)}, u32[]{:S(2)}) %collective-permute-start.5) | collective-permute-done | bytes 532512 | tf_op jit(solution)/shard_map/ppermute | solution.py:493
  18.3 1.3 %shard_map.50 = (f32[12,192,128]{2,1,0:T(8,128)S(1)}, f32[12,48,128]{2,1,0:T(8,128)S(1)}, f32[12,16,128]{2,1,0:T(8,128)S(1)}) custom-call(f32[8,128]{1,0:T(8,128)S(1)} %get-tuple-element.31.table, f32[6,2,256,128]{3,2,1,0:T(8,128)S(1)} %get-tuple-element.32.seeds, s32[2,256,128]{2,1,0:T(8,128)S(1)} %get-tuple-element.33.material, ...), custom_call_target="tpu_custom_call" | custom-call | tf_op jit(solution)/shard_map/pallas_call | solution.py:468
  19.5 0.4 %collective-permute-start.7 = (f32[12,48,128]{2,1,0:T(8,128)S(1)}, f32[12,48,128]{2,1,0:T(8,128)S(1)}, u32[]{:S(2)}, u32[]{:S(2)}) collective-permute-start(f32[12,48,128]{2,1,0:T(8,128)S(1)} %get-tuple-element.45), channel_id=1, source_target_pairs={{0,16},{8,24},{16,0},{24,8},{1,17},{9,25},{17,1},{25,9},{2,18},{10... | collective-permute-start | bytes 884744 | tf_op jit(solution)/shard_map/ppermute | solution.py:497
  19.9 1.7 %collective-permute-start.8 = (f32[12,16,128]{2,1,0:T(8,128)S(1)}, f32[12,16,128]{2,1,0:T(8,128)S(1)}, u32[]{:S(2)}, u32[]{:S(2)}) collective-permute-start(f32[12,16,128]{2,1,0:T(8,128)S(1)} %get-tuple-element.49), channel_id=1, source_target_pairs={{0,8},{8,0},{16,24},{24,16},{1,9},{9,1},{17,25},{25,17},{2,10},{10... | collective-permute-start | bytes 294920 | tf_op jit(solution)/shard_map/ppermute | solution.py:497
  21.6 1.2 %collective-permute-done.2.corner = f32[12,32,128]{2,1,0:T(8,128)S(1)} collective-permute-done((f32[12,32,128]{2,1,0:T(8,128)S(1)}, f32[12,32,128]{2,1,0:T(8,128)S(1)}, u32[]{:S(2)}, u32[]{:S(2)}) %collective-permute-start.2) | collective-permute-done | bytes 196640 | tf_op jit(solution)/shard_map/ppermute | solution.py:497
  22.8 0.3 shard_map.51
  23.1 0.1 collective-permute-start.10
  23.2 1.6 %collective-permute-done.8.beside = f32[12,16,128]{2,1,0:T(8,128)S(1)} collective-permute-done((f32[12,16,128]{2,1,0:T(8,128)S(1)}, f32[12,16,128]{2,1,0:T(8,128)S(1)}, u32[]{:S(2)}, u32[]{:S(2)}) %collective-permute-start.8) | collective-permute-done | bytes 98336 | tf_op jit(solution)/shard_map/ppermute | solution.py:497
  24.8 0.0 collective-permute-done.11.far
  24.8 1.5 %shard_map.53.part = f32[12,104,128]{2,1,0:T(8,128)S(1)} custom-call(f32[8,128]{1,0:T(8,128)S(1)} %get-tuple-element.31.table, f32[14,56,128]{2,1,0:T(8,128)S(1)} %collective-permute-done.6.shared, f32[5,56,128]{2,1,0:T(8,128)S(1)} %collective-permute-done.9.near, f32[5,56,128]{2,1,0:T(8,128)S(1)} %collective-permute-done.11.far), custom_call_target="tpu_custom_call" | custom-call | flops 2000000000 | tf_op jit(solution)/shard_map/pallas_call | solution.py:468
  26.3 0.9 %shard_map.54._ = f32[1,6,2,256,128]{4,3,2,1,0:T(8,128)} custom-call(f32[12,192,128]{2,1,0:T(8,128)S(1)} %get-tuple-element.44.mid, f32[12,104,128]{2,1,0:T(8,128)S(1)} %shard_map.53.part), custom_call_target="tpu_custom_call" | custom-call | tf_op jit(solution)/shard_map/pallas_call | solution.py:579
  27.2 1.4 %collective-permute-done.7.bands = f32[12,48,128]{2,1,0:T(8,128)S(1)} collective-permute-done((f32[12,48,128]{2,1,0:T(8,128)S(1)}, f32[12,48,128]{2,1,0:T(8,128)S(1)}, u32[]{:S(2)}, u32[]{:S(2)}) %collective-permute-start.7) | collective-permute-done | bytes 294944 | tf_op jit(solution)/shard_map/ppermute | solution.py:497
  28.6 0.3 shard_map.52
  28.9 0.1 collective-permute-done.10.got
  28.9 1.0 %shard_map.55 = f32[1,6,2,256,128]{4,3,2,1,0:T(8,128)} custom-call(f32[6,2,80,128]{3,2,1,0:T(8,128)S(1)} %get-tuple-element.52.low, f32[6,2,80,128]{3,2,1,0:T(8,128)S(1)} %get-tuple-element.53.high, f32[12,32,128]{2,1,0:T(8,128)S(1)} %collective-permute-done.10.got, f32[1,6,2,256,128]{4,3,2,1,0:T(8,128)} %shard_map.54._), custom_call_target="tpu_custom_call", output_to_operand_aliasing={{}: (3, {})} | custom-call | tf_op jit(solution)/shard_map/pallas_call | solution.py:592
  (2 shorter events, 0.0 us)
Async XLA Ops:
  1.8 13.3 %collective-permute-start.6 = (f32[14,56,128]{2,1,0:T(8,128)S(1)}, f32[14,56,128]{2,1,0:T(8,128)S(1)}, u32[]{:S(2)}, u32[]{:S(2)}) collective-permute-start(f32[14,56,128]{2,1,0:T(8,128)S(1)} %get-tuple-element.41), channel_id=1, source_target_pairs={{0,16},{8,24},{16,0},{24,8},{1,17},{9,25},{17,1},{25,9},{2,18},{10... | collective-permute-start | bytes 1204232 | tf_op jit(solution)/shard_map/ppermute | solution.py:497
  5.6 3.3 %collective-permute-start = (f32[5,80,128]{2,1,0:T(8,128)S(1)}, f32[5,80,128]{2,1,0:T(8,128)S(1)}, u32[]{:S(2)}, u32[]{:S(2)}) collective-permute-start(f32[5,80,128]{2,1,0:T(8,128)S(1)} %get-tuple-element.34), channel_id=1, source_target_pairs={{0,1},{1,0},{2,3},{3,2},{4,5},{5,4},{6,7},{7,6},{8,9},{9,8},{10,11... | collective-permute-start | bytes 614408 | tf_op jit(solution)/shard_map/ppermute | solution.py:483
  5.7 5.8 %collective-permute-start.1 = (f32[5,80,128]{2,1,0:T(8,128)S(1)}, f32[5,80,128]{2,1,0:T(8,128)S(1)}, u32[]{:S(2)}, u32[]{:S(2)}) collective-permute-start(f32[5,80,128]{2,1,0:T(8,128)S(1)} %get-tuple-element.35), channel_id=1, source_target_pairs={{0,8},{1,2},{2,1},{3,4},{4,3},{5,6},{6,5},{7,15},{8,0},{9,10},{10,... | collective-permute-start | bytes 614408 | tf_op jit(solution)/shard_map/ppermute | solution.py:493
  7.2 9.0 %collective-permute-start.4 = (f32[5,208,128]{2,1,0:T(8,128)S(1)}, f32[5,208,128]{2,1,0:T(8,128)S(1)}, u32[]{:S(2)}, u32[]{:S(2)}) collective-permute-start(f32[5,208,128]{2,1,0:T(8,128)S(1)} %get-tuple-element.38), channel_id=1, source_target_pairs={{0,1},{1,0},{2,3},{3,2},{4,5},{5,4},{6,7},{7,6},{8,9},{9,8},{10,11... | collective-permute-start | bytes 1597448 | tf_op jit(solution)/shard_map/ppermute | solution.py:483
  7.4 10.8 %collective-permute-start.5 = (f32[5,208,128]{2,1,0:T(8,128)S(1)}, f32[5,208,128]{2,1,0:T(8,128)S(1)}, u32[]{:S(2)}, u32[]{:S(2)}) collective-permute-start(f32[5,208,128]{2,1,0:T(8,128)S(1)} %get-tuple-element.39), channel_id=1, source_target_pairs={{0,8},{1,2},{2,1},{3,4},{4,3},{5,6},{6,5},{7,15},{8,0},{9,10},{10,... | collective-permute-start | bytes 1597448 | tf_op jit(solution)/shard_map/ppermute | solution.py:493
  12.1 7.9 %collective-permute-start.3 = (f32[12,16,128]{2,1,0:T(8,128)S(1)}, f32[12,16,128]{2,1,0:T(8,128)S(1)}, u32[]{:S(2)}, u32[]{:S(2)}) collective-permute-start(f32[12,16,128]{2,1,0:T(8,128)S(1)} %get-tuple-element.37), channel_id=1, source_target_pairs={{0,24},{8,16},{16,8},{24,0},{1,25},{9,17},{17,9},{25,1},{2,26},{10... | collective-permute-start | bytes 294920 | tf_op jit(solution)/shard_map/ppermute | solution.py:497
  13.6 9.3 %collective-permute-start.2 = (f32[12,32,128]{2,1,0:T(8,128)S(1)}, f32[12,32,128]{2,1,0:T(8,128)S(1)}, u32[]{:S(2)}, u32[]{:S(2)}) collective-permute-start(f32[12,32,128]{2,1,0:T(8,128)S(1)} %get-tuple-element.36), channel_id=1, source_target_pairs={{0,16},{8,24},{16,0},{24,8},{1,17},{9,25},{17,1},{25,9},{2,18},{10... | collective-permute-start | bytes 589832 | tf_op jit(solution)/shard_map/ppermute | solution.py:497
  16.2 7.0 %collective-permute-start.9 = (f32[5,56,128]{2,1,0:T(8,128)S(1)}, f32[5,56,128]{2,1,0:T(8,128)S(1)}, u32[]{:S(2)}, u32[]{:S(2)}) collective-permute-start(f32[5,56,128]{2,1,0:T(8,128)S(1)} %get-tuple-element.50), channel_id=1, source_target_pairs={{0,1},{1,0},{2,3},{3,2},{4,5},{5,4},{6,7},{7,6},{8,9},{9,8},{10,11... | collective-permute-start | bytes 430088 | tf_op jit(solution)/shard_map/ppermute | solution.py:483
  16.2 8.5 %collective-permute-start.11 = (f32[5,56,128]{2,1,0:T(8,128)S(1)}, f32[5,56,128]{2,1,0:T(8,128)S(1)}, u32[]{:S(2)}, u32[]{:S(2)}) collective-permute-start(f32[5,56,128]{2,1,0:T(8,128)S(1)} %get-tuple-element.56), channel_id=1, source_target_pairs={{0,8},{1,2},{2,1},{3,4},{4,3},{5,6},{6,5},{7,15},{8,0},{9,10},{10,... | collective-permute-start | bytes 430088 | tf_op jit(solution)/shard_map/ppermute | solution.py:493
  19.5 9.0 %collective-permute-start.7 = (f32[12,48,128]{2,1,0:T(8,128)S(1)}, f32[12,48,128]{2,1,0:T(8,128)S(1)}, u32[]{:S(2)}, u32[]{:S(2)}) collective-permute-start(f32[12,48,128]{2,1,0:T(8,128)S(1)} %get-tuple-element.45), channel_id=1, source_target_pairs={{0,16},{8,24},{16,0},{24,8},{1,17},{9,25},{17,1},{25,9},{2,18},{10... | collective-permute-start | bytes 884744 | tf_op jit(solution)/shard_map/ppermute | solution.py:497
  19.9 4.8 %collective-permute-start.8 = (f32[12,16,128]{2,1,0:T(8,128)S(1)}, f32[12,16,128]{2,1,0:T(8,128)S(1)}, u32[]{:S(2)}, u32[]{:S(2)}) collective-permute-start(f32[12,16,128]{2,1,0:T(8,128)S(1)} %get-tuple-element.49), channel_id=1, source_target_pairs={{0,8},{8,0},{16,24},{24,16},{1,9},{9,1},{17,25},{25,17},{2,10},{10... | collective-permute-start | bytes 294920 | tf_op jit(solution)/shard_map/ppermute | solution.py:497
  23.1 5.9 %collective-permute-start.10 = (f32[12,32,128]{2,1,0:T(8,128)S(1)}, f32[12,32,128]{2,1,0:T(8,128)S(1)}, u32[]{:S(2)}, u32[]{:S(2)}) collective-permute-start(f32[12,32,128]{2,1,0:T(8,128)S(1)} %get-tuple-element.54), channel_id=1, source_target_pairs={{0,8},{8,0},{16,24},{24,16},{1,9},{9,1},{17,25},{25,17},{2,10},{10... | collective-permute-start | bytes 589832 | tf_op jit(solution)/shard_map/ppermute | solution.py:497
